TPU v7x, 32 devices: a whole 2x2x4 slice. The times are simulated.
32 devices in a mesh: fold: 4 (over x, core), samp: 4 (over z), feat: 2 (over y).
Axes of the slice: x: 2, y: 2, z: 4, core: 2. Of those that a mesh axis runs over, the one named last changes fastest.
Arguments:
- input_points: bfloat16 [4096, 128], P('samp'), may hold values from -6 to 6
- wave_numbers: bfloat16 [128, 4096], P(None, 'feat'), may hold values from -0.5 to 0.5
- offset_angles: float32 [4096], P('feat'), may hold values from -3.140625 to 3.140625
- feature_magnitudes: float32 [4096], P('feat'), may hold values from 0.3 to 3
- response_values: float32 [4096], P('samp'), may hold values from -6 to 6
- split_label: int32 [16384], P(('fold', 'samp')), parts along dimension 0, may hold values from 0 to 15
- shrinkage_levels: float32 [16], replicated, may hold values from 0.001 to 1000
Outputs:
- coefficients: float32 [64, 4096], P('fold', 'feat'), parts along dimension 0
- predictions: float32 [64, 4096], P('fold', 'samp'), parts along dimension 0
There are 4 independent parts, one for each index of `fold`. A program takes and returns all parts, laid end to end along the dimension named above; an argument that names none is the same for every part. Nothing has to cross between parts.
Inputs may be any that keep to these rules, and one draw needn't show every extreme that they name: `split_label`: each sample's fold; samples of fold 0 are the held-out ones.
All inputs are finite; a program needn't handle non-finite values.
Results may differ from a plain program's by a relative error of at most 0.006.
Values may be sent and summed in bfloat16 or wider, within the bound.
No kernel may reach another device: no remote copies, remote signals or barrier semaphores. Data moves between devices by JAX's collectives and lax.ppermute only.
A program may use at most 64 MiB of HBM per device.

v0:
```python
import math

import jax
import jax.numpy as jnp
from jax import lax
from jax.sharding import PartitionSpec as P

FEATURES = 4096
ITERS = 3


highest = lax.Precision.HIGHEST


def feature_block(rows, wave_numbers, offset_angles, feature_magnitudes):
    angles = jnp.dot(rows, wave_numbers, preferred_element_type=jnp.float32) + offset_angles
    return feature_magnitudes * math.sqrt(2.0 / FEATURES) * jnp.cos(angles)


def shards(
    input_points,
    wave_numbers,
    offset_angles,
    feature_magnitudes,
    response_values,
    split_label,
    shrinkage_levels,
):
    fitting_observations = (split_label != 0).astype(jnp.float32)

    def reduce_columns(partial_value):
        return lax.psum_scatter(partial_value, "samp", scatter_dimension=1, tiled=True)

    def inner(scalars):
        return lax.psum(scalars, ("samp", "feat"))

    def widen(vector):
        return lax.all_gather(vector, "samp", axis=1, tiled=True)

    cached = feature_block(input_points, wave_numbers, offset_angles, feature_magnitudes)

    def current():
        return cached

    def forward(full_vector, matrix):
        partial_value = lax.dot_general(
            full_vector, matrix, (((1,), (1,)), ((), ())), precision=highest
        )
        return lax.psum(partial_value, "feat")

    matrix = current()
    split_moments = jnp.stack(
        [
            jnp.dot(fitting_observations, matrix * matrix, precision=highest),
            jnp.dot(fitting_observations * response_values, matrix, precision=highest),
        ]
    )
    split_moments = reduce_columns(split_moments)
    jacobi_reciprocal = split_moments[0][None, :] + shrinkage_levels[:, None]
    residual = jnp.broadcast_to(split_moments[1][None, :], jacobi_reciprocal.shape)
    scaled = residual / jacobi_reciprocal
    inner_now = inner(jnp.sum(residual * scaled, axis=1))

    def iterate(counter, carried):
        weights_now, residual, conjugate_step, inner_now, predicted = carried
        matrix = current()
        lifted_design = forward(widen(conjugate_step), matrix)
        lifted_column = reduce_columns(
            jnp.dot(lifted_design * fitting_observations[None, :], matrix, precision=highest)
        )
        lifted_column = lifted_column + shrinkage_levels[:, None] * conjugate_step
        step_size = inner_now / inner(jnp.sum(conjugate_step * lifted_column, axis=1))
        weights_now = weights_now + step_size[:, None] * conjugate_step
        predicted = predicted + step_size[:, None] * lifted_design
        residual = residual - step_size[:, None] * lifted_column
        scaled = residual / jacobi_reciprocal
        inner_next = inner(jnp.sum(residual * scaled, axis=1))
        conjugate_step = scaled + (inner_next / inner_now)[:, None] * conjugate_step
        return (weights_now, residual, conjugate_step, inner_next, predicted)

    carried = (
        jnp.zeros_like(residual),
        residual,
        scaled,
        inner_now,
        jnp.zeros((shrinkage_levels.shape[0], input_points.shape[0]), jnp.float32),
    )
    weights_now, residual, conjugate_step, inner_now, predicted = lax.fori_loop(
        0, ITERS, iterate, carried
    )
    coefficients = widen(weights_now)
    predicted = forward(coefficients, current())
    return (coefficients, predicted)


def solution(mesh):
    placed = (
        P("samp", None),
        P(None, "feat"),
        P("feat"),
        P("feat"),
        P("samp"),
        P(("fold", "samp")),
        P(),
    )
    return jax.shard_map(
        shards,
        mesh=mesh,
        in_specs=placed,
        out_specs=(P("fold", "feat"), P("fold", "samp")),
        check_vma=False,
    )
```

profile of v0, /device:TPU:0, one launch (start us, length us, event | category | flops | bytes accessed | tf_op | source)
XLA Modules:
  0.0 472.5 jit_solution(7370933770596369276)
XLA Ops:
  7.2 0.7 broadcast_multiply_fusion
  8.0 0.7 fusion.7
  8.7 0.7 broadcast_select_fusion
  9.4 28.3 %cosine_multiply_fusion = f32[1024,2048]{1,0:T(8,128)S(1)} fusion(bf16[1024,128]{1,0:T(8,128)(2,1)} %param.9, bf16[128,2048]{1,0:T(8,128)(2,1)S(1)} %copy-done, f32[2048]{0:T(1024)} %param.11, f32[2048]{0:T(1024)S(1)} %broadcast_multiply_fusion), kind=kOutput, calls=%fused_computation.13 | convolution fusion | flops 541065216 | bytes 9191424 | tf_op jit(solution)/shard_map/dot_general | solution.py:16
  37.7 4.0 fusion.10
  41.7 3.0 fusion.5
  44.8 1.4 copy.9
  46.3 30.0 %reduce-scatter.5.cloned.1.call-done = f32[512,2]{1,0:T(8,128)} async-done(((f32[2048,2]{1,0:T(8,128)}), f32[512,2]{1,0:T(8,128)}) %reduce-scatter.5.cloned.1.call-update) | async-done | bytes 4112
  76.3 1.2 fusion.8
  77.4 0.1 copy.11
  77.5 0.1 copy.12
  77.6 0.2 multiply_reduce_fusion.2
  77.8 19.1 %psum.35 = f32[16]{0:T(128)S(1)} all-reduce(f32[16]{0:T(128)S(1)} %get-tuple-element.158), channel_id=1, replica_groups=mesh['fold'=4,'samp'=4,'feat'=2] {'samp','feat'}, use_global_device_ids=true, to_apply=%region_2.0 | all-reduce | flops 16 | bytes 128 | tf_op jit(solution)/shard_map/psum | solution.py:35
  97.0 324.0 %while.19 = (s32[]{:T(128)}, f32[16,512]{1,0:T(8,128)S(1)}, f32[16,512]{1,0:T(8,128)S(1)}, f32[16,512]{1,0:T(8,128)S(1)}, f32[16]{0:T(128)S(1)}, /*index=5*/f32[...) while((s32[]{:T(128)}, f32[16,512]{1,0:T(8,128)S(1)}, ...), condition=%wide.region_10.0_spmd.clone.clone.clone, body=%wide.region_3.0_spmd.clone.clone.clone.sunk | while | flops 805494784 | bytes 18589060 | solution.py:88
  97.0 13.6 %all_gather.11 = f32[16,2048]{1,0:T(8,128)S(1)} all-gather(f32[16,512]{1,0:T(8,128)S(1)} %get-tuple-element.235), channel_id=1, replica_groups=mesh['fold'=4,'samp'=4,'feat'=2] {'samp'}, dimensions={1}, use_global_device_ids=true | all-gather | bytes 163840 | tf_op jit(solution)/shard_map/while/body/eval_jaxpr/all_gather | solution.py:38
  110.7 9.8 %fusion.32 = f32[16,1024]{1,0:T(8,128)} fusion(f32[16,2048]{1,0:T(8,128)S(1)} %all_gather.11, f32[1024,2048]{1,0:T(8,128)} %get-tuple-element.248), kind=kOutput, calls=%fused_computation.22.clone.1 | convolution fusion | flops 402653184 | bytes 8585216 | tf_op jit(solution)/shard_map/while/body/eval_jaxpr/dot_general | solution.py:46
  120.6 18.2 %all-reduce.5.cloned.1.call-done = f32[16,1024]{1,0:T(8,128)} async-done(((f32[16,1024]{1,0:T(8,128)}), f32[16,1024]{1,0:T(8,128)}) %all-reduce.5.cloned.1.call-update) | async-done | bytes 65552 | tf_op jit(solution)/shard_map/while/body/eval_jaxpr/psum | solution.py:49
  138.7 8.1 %fusion.33 = f32[16,2048]{1,0:T(8,128)} fusion(f32[1024,2048]{1,0:T(8,128)} %get-tuple-element.248, f32[16,1024]{1,0:T(8,128)} %all-reduce.5.cloned.1.call-done, f32[1024]{0:T(1024)S(1)} %get-tuple-element.249), kind=kOutput, calls=%fused_computation.1.clone.1 | convolution fusion | flops 402669568 | bytes 8589312 | tf_op jit(solution)/shard_map/while/body/eval_jaxpr/dot_general | solution.py:69
  146.9 19.3 %reduce-scatter.7.cloned.1.call-done = f32[16,512]{1,0:T(8,128)} async-done(((f32[16,2048]{1,0:T(8,128)}), f32[16,512]{1,0:T(8,128)}) %reduce-scatter.7.cloned.1.call-update) | async-done | bytes 32784 | tf_op jit(solution)/shard_map/while/body/eval_jaxpr/reduce_scatter | solution.py:32
  166.2 0.9 multiply_reduce_fusion.5
  167.1 18.6 %psum.50 = f32[16]{0:T(128)S(1)} all-reduce(f32[16]{0:T(128)S(1)} %multiply_reduce_fusion.5), channel_id=1, replica_groups=mesh['fold'=4,'samp'=4,'feat'=2] {'samp','feat'}, use_global_device_ids=true, to_apply=%region_7.0 | all-reduce | flops 16 | bytes 128 | tf_op jit(solution)/shard_map/while/body/eval_jaxpr/psum | solution.py:35
  185.8 1.0 multiply_reduce_fusion.6
  186.7 17.7 %psum.51 = f32[16]{0:T(128)S(1)} all-reduce(f32[16]{0:T(128)S(1)} %get-tuple-element.220), channel_id=1, replica_groups=mesh['fold'=4,'samp'=4,'feat'=2] {'samp','feat'}, use_global_device_ids=true, to_apply=%region_9.0 | all-reduce | flops 16 | bytes 128 | tf_op jit(solution)/shard_map/while/body/eval_jaxpr/psum | solution.py:35
  204.4 0.1 multiply_add_fusion.3
  204.6 13.4 %all_gather.11 = f32[16,2048]{1,0:T(8,128)S(1)} all-gather(f32[16,512]{1,0:T(8,128)S(1)} %get-tuple-element.235), channel_id=1, replica_groups=mesh['fold'=4,'samp'=4,'feat'=2] {'samp'}, dimensions={1}, use_global_device_ids=true | all-gather | bytes 163840 | tf_op jit(solution)/shard_map/while/body/eval_jaxpr/all_gather | solution.py:38
  218.0 9.8 %fusion.32 = f32[16,1024]{1,0:T(8,128)} fusion(f32[16,2048]{1,0:T(8,128)S(1)} %all_gather.11, f32[1024,2048]{1,0:T(8,128)} %get-tuple-element.248), kind=kOutput, calls=%fused_computation.22.clone.1 | convolution fusion | flops 402653184 | bytes 8585216 | tf_op jit(solution)/shard_map/while/body/eval_jaxpr/dot_general | solution.py:46
  227.9 19.1 %all-reduce.5.cloned.1.call-done = f32[16,1024]{1,0:T(8,128)} async-done(((f32[16,1024]{1,0:T(8,128)}), f32[16,1024]{1,0:T(8,128)}) %all-reduce.5.cloned.1.call-update) | async-done | bytes 65552 | tf_op jit(solution)/shard_map/while/body/eval_jaxpr/psum | solution.py:49
  247.0 8.1 %fusion.33 = f32[16,2048]{1,0:T(8,128)} fusion(f32[1024,2048]{1,0:T(8,128)} %get-tuple-element.248, f32[16,1024]{1,0:T(8,128)} %all-reduce.5.cloned.1.call-done, f32[1024]{0:T(1024)S(1)} %get-tuple-element.249), kind=kOutput, calls=%fused_computation.1.clone.1 | convolution fusion | flops 402669568 | bytes 8589312 | tf_op jit(solution)/shard_map/while/body/eval_jaxpr/dot_general | solution.py:69
  255.1 19.3 %reduce-scatter.7.cloned.1.call-done = f32[16,512]{1,0:T(8,128)} async-done(((f32[16,2048]{1,0:T(8,128)}), f32[16,512]{1,0:T(8,128)}) %reduce-scatter.7.cloned.1.call-update) | async-done | bytes 32784 | tf_op jit(solution)/shard_map/while/body/eval_jaxpr/reduce_scatter | solution.py:32
  274.5 0.9 multiply_reduce_fusion.5
  275.4 18.6 %psum.50 = f32[16]{0:T(128)S(1)} all-reduce(f32[16]{0:T(128)S(1)} %multiply_reduce_fusion.5), channel_id=1, replica_groups=mesh['fold'=4,'samp'=4,'feat'=2] {'samp','feat'}, use_global_device_ids=true, to_apply=%region_7.0 | all-reduce | flops 16 | bytes 128 | tf_op jit(solution)/shard_map/while/body/eval_jaxpr/psum | solution.py:35
  294.0 1.0 multiply_reduce_fusion.6
  295.0 17.6 %psum.51 = f32[16]{0:T(128)S(1)} all-reduce(f32[16]{0:T(128)S(1)} %get-tuple-element.220), channel_id=1, replica_groups=mesh['fold'=4,'samp'=4,'feat'=2] {'samp','feat'}, use_global_device_ids=true, to_apply=%region_9.0 | all-reduce | flops 16 | bytes 128 | tf_op jit(solution)/shard_map/while/body/eval_jaxpr/psum | solution.py:35
  312.6 0.1 multiply_add_fusion.3
  312.8 13.4 %all_gather.11 = f32[16,2048]{1,0:T(8,128)S(1)} all-gather(f32[16,512]{1,0:T(8,128)S(1)} %get-tuple-element.235), channel_id=1, replica_groups=mesh['fold'=4,'samp'=4,'feat'=2] {'samp'}, dimensions={1}, use_global_device_ids=true | all-gather | bytes 163840 | tf_op jit(solution)/shard_map/while/body/eval_jaxpr/all_gather | solution.py:38
  326.2 9.8 %fusion.32 = f32[16,1024]{1,0:T(8,128)} fusion(f32[16,2048]{1,0:T(8,128)S(1)} %all_gather.11, f32[1024,2048]{1,0:T(8,128)} %get-tuple-element.248), kind=kOutput, calls=%fused_computation.22.clone.1 | convolution fusion | flops 402653184 | bytes 8585216 | tf_op jit(solution)/shard_map/while/body/eval_jaxpr/dot_general | solution.py:46
  336.1 19.1 %all-reduce.5.cloned.1.call-done = f32[16,1024]{1,0:T(8,128)} async-done(((f32[16,1024]{1,0:T(8,128)}), f32[16,1024]{1,0:T(8,128)}) %all-reduce.5.cloned.1.call-update) | async-done | bytes 65552 | tf_op jit(solution)/shard_map/while/body/eval_jaxpr/psum | solution.py:49
  355.2 8.1 %fusion.33 = f32[16,2048]{1,0:T(8,128)} fusion(f32[1024,2048]{1,0:T(8,128)} %get-tuple-element.248, f32[16,1024]{1,0:T(8,128)} %all-reduce.5.cloned.1.call-done, f32[1024]{0:T(1024)S(1)} %get-tuple-element.249), kind=kOutput, calls=%fused_computation.1.clone.1 | convolution fusion | flops 402669568 | bytes 8589312 | tf_op jit(solution)/shard_map/while/body/eval_jaxpr/dot_general | solution.py:69
  363.4 19.3 %reduce-scatter.7.cloned.1.call-done = f32[16,512]{1,0:T(8,128)} async-done(((f32[16,2048]{1,0:T(8,128)}), f32[16,512]{1,0:T(8,128)}) %reduce-scatter.7.cloned.1.call-update) | async-done | bytes 32784 | tf_op jit(solution)/shard_map/while/body/eval_jaxpr/reduce_scatter | solution.py:32
  382.7 0.9 multiply_reduce_fusion.5
  383.6 18.7 %psum.50 = f32[16]{0:T(128)S(1)} all-reduce(f32[16]{0:T(128)S(1)} %multiply_reduce_fusion.5), channel_id=1, replica_groups=mesh['fold'=4,'samp'=4,'feat'=2] {'samp','feat'}, use_global_device_ids=true, to_apply=%region_7.0 | all-reduce | flops 16 | bytes 128 | tf_op jit(solution)/shard_map/while/body/eval_jaxpr/psum | solution.py:35
  402.3 1.0 multiply_reduce_fusion.6
  403.2 17.6 %psum.51 = f32[16]{0:T(128)S(1)} all-reduce(f32[16]{0:T(128)S(1)} %get-tuple-element.220), channel_id=1, replica_groups=mesh['fold'=4,'samp'=4,'feat'=2] {'samp','feat'}, use_global_device_ids=true, to_apply=%region_9.0 | all-reduce | flops 16 | bytes 128 | tf_op jit(solution)/shard_map/while/body/eval_jaxpr/psum | solution.py:35
  421.0 13.4 %all_gather.6 = f32[16,2048]{1,0:T(8,128)S(1)} all-gather(f32[16,512]{1,0:T(8,128)S(1)} %get-tuple-element.49), channel_id=1, replica_groups=mesh['fold'=4,'samp'=4,'feat'=2] {'samp'}, dimensions={1}, use_global_device_ids=true | all-gather | bytes 163840 | tf_op jit(solution)/shard_map/all_gather | solution.py:38
  434.4 9.8 %fusion.11 = f32[16,1024]{1,0:T(8,128)} fusion(f32[16,2048]{1,0:T(8,128)S(1)} %all_gather.6, f32[1024,2048]{1,0:T(8,128)} %get-tuple-element.262), kind=kOutput, calls=%fused_computation.24 | convolution fusion | flops 402653184 | bytes 8585216 | tf_op jit(solution)/shard_map/dot_general | solution.py:46
  444.3 19.2 %all-reduce.3.cloned.1.call-done = f32[16,1024]{1,0:T(8,128)} async-done(((f32[16,1024]{1,0:T(8,128)}), f32[16,1024]{1,0:T(8,128)}) %all-reduce.3.cloned.1.call-update) | async-done | bytes 65552 | tf_op jit(solution)/shard_map/psum | solution.py:49
  463.5 0.7 copy.31
  464.1 1.5 copy.32
  (36 shorter events, 0.7 us)
Async XLA Ops:
  7.2 2.2 copy-start
  7.2 69.1 %reduce-scatter.5.cloned.1.call-start = ((), (), s32[]{:S(2)}) async-start(), calls=%async_computation.3 | async-start | bytes 1310720
  37.7 7.1 %copy-start.1 = (f32[1024,2048]{1,0:T(8,128)}, f32[1024,2048]{1,0:T(8,128)S(1)}, u32[]{:S(2)}) copy-start(f32[1024,2048]{1,0:T(8,128)S(1)} %cosine_multiply_fusion) | copy-start | bytes 25165828
  37.7 40.0 %copy-start.2 = (f32[16]{0:T(128)S(1)}, f32[16]{0:T(128)}, u32[]{:S(2)}) copy-start(f32[16]{0:T(128)} %param.15) | copy-start | bytes 196
  97.0 41.8 %all-reduce.5.cloned.1.call-start = ((), (), s32[]{:S(2)}) async-start(), calls=%async_computation.4 | async-start | bytes 131072 | tf_op jit(solution)/shard_map/while/body/eval_jaxpr/psum | solution.py:49
  120.5 45.7 %reduce-scatter.7.cloned.1.call-start = ((), (), s32[]{:S(2)}) async-start(), calls=%async_computation.5 | async-start | bytes 163840 | tf_op jit(solution)/shard_map/while/body/eval_jaxpr/reduce_scatter | solution.py:32
  204.5 42.5 %all-reduce.5.cloned.1.call-start = ((), (), s32[]{:S(2)}) async-start(), calls=%async_computation.4 | async-start | bytes 131072 | tf_op jit(solution)/shard_map/while/body/eval_jaxpr/psum | solution.py:49
  227.8 46.6 %reduce-scatter.7.cloned.1.call-start = ((), (), s32[]{:S(2)}) async-start(), calls=%async_computation.5 | async-start | bytes 163840 | tf_op jit(solution)/shard_map/while/body/eval_jaxpr/reduce_scatter | solution.py:32
  312.8 42.5 %all-reduce.5.cloned.1.call-start = ((), (), s32[]{:S(2)}) async-start(), calls=%async_computation.4 | async-start | bytes 131072 | tf_op jit(solution)/shard_map/while/body/eval_jaxpr/psum | solution.py:49
  336.1 46.6 %reduce-scatter.7.cloned.1.call-start = ((), (), s32[]{:S(2)}) async-start(), calls=%async_computation.5 | async-start | bytes 163840 | tf_op jit(solution)/shard_map/while/body/eval_jaxpr/reduce_scatter | solution.py:32
  421.0 42.5 %all-reduce.3.cloned.1.call-start = ((), (), s32[]{:S(2)}) async-start(), calls=%async_computation.2 | async-start | bytes 131072 | tf_op jit(solution)/shard_map/psum | solution.py:49
Sparse Core Ops, SparseCore 0:
  46.4 29.8 reduce-scatter.4
  120.6 18.0 all-reduce.4
  147.0 19.1 reduce-scatter.6
  228.0 18.9 all-reduce.4
  255.3 19.1 reduce-scatter.6
  336.2 19.0 all-reduce.4
  363.5 19.1 reduce-scatter.6
  444.4 19.0 all-reduce.2
where the time goes:
time: 473 us; the launch traced here: 472 us
  blocking collectives  182 us (38%)
  waiting for transfers between devices  164 us (35%)
  matrix products  99 us (21%)
  between operations  14.1 us (3%)
  other arithmetic  8.35 us (2%)
  local copies, waits for them, and re-layouts  5 us (1%)
    psum x7, blocking collectives, inner(): return lax.psum(scalars, ('samp', 'feat'))  128 us
    psum x4, waiting for transfers between devices, forward(): return lax.psum(partial_value, 'feat')  75.6 us
    reduce_scatter x3, waiting for transfers between devices, reduce_columns(): lax.psum_scatter(partial_value, 'samp', scatter_dimension=1, tiled=True)  57.9 us
    all_gather x4, blocking collectives, widen(): return lax.all_gather(vector, 'samp', axis=1, tiled=True)  53.8 us
    dot_general x4, matrix products, forward(): lax.dot_general(full_vector, matrix, (((1,), (1,)), ((), ())), precision=...  39.3 us
    unnamed x3, waiting for transfers between devices  30 us
    dot_general x1, matrix products, feature_block(): jnp.dot(rows, wave_numbers, preferred_element_type=jnp.float32)  28.3 us
    dot_general x3, matrix products, iterate(): jnp.dot(lifted_design * fitting_observations[None, :], matrix, precision=...  24.4 us
  transfers between devices with their start and end apart: 8, of which 8 were waited for; matrix products, arithmetic and copies ran while one was open for 0% of the time, Pallas kernels for 0%

commit v1 on v0

v1 whole, which is shorter than its diff:
```python
import functools
import math

import jax
import jax.numpy as jnp
from jax import lax
from jax.experimental import pallas as pl
from jax.experimental.pallas import tpu as pltpu
from jax.sharding import PartitionSpec as P

f32, bf16 = jnp.float32, jnp.bfloat16
TURN = 1.0 / (2.0 * math.pi)
COSINE = (0.999999211770312, -19.738980419471126, 64.92865850463285, -85.27162830146948, 58.79050662870376, -21.071108461771125)
LANES = 128
VMEM_LIMIT = 32 * 2**20


def in_vmem(value):
    return pltpu.with_memory_space_constraint(value, pltpu.VMEM)


def call(body, outs, *args, flops=0, held=True):
    outs = [pltpu.VMEM(s, d) if held else jax.ShapeDtypeStruct(s, d) for s, d in outs]
    size = sum(math.prod(a.shape) * a.dtype.itemsize for a in args)
    return pl.pallas_call(
        body,
        out_shape=outs,
        compiler_params=pltpu.CompilerParams(vmem_limit_bytes=VMEM_LIMIT),
        cost_estimate=pl.CostEstimate(flops=flops, bytes_accessed=size, transcendentals=0),
    )(*args)


def exchange(value, axis, n):
    return [value] + [
        lax.ppermute(value, axis, [(i, i ^ s) for i in range(n)]) for s in range(1, n)
    ]


def total(refs):
    values = [r[...] for r in refs]
    while len(values) > 1:
        values = [values[i] + values[i + 1] for i in range(0, len(values), 2)]
    return values[0]


def halves(value):
    high = value.astype(bf16)
    return high, (value - high.astype(f32)).astype(bf16)


def product(rows, high_ref, low_ref, contract):
    high, low = halves(rows)
    n = rows.shape[0]
    both = jnp.concatenate([high.astype(f32), low.astype(f32)], axis=0).astype(bf16)
    dims = (((1,), (contract,)), ((), ()))
    a = lax.dot_general(both, high_ref[...], dims, preferred_element_type=f32)
    b = lax.dot_general(high, low_ref[...], dims, preferred_element_type=f32)
    return a[:n] + a[n:] + b


def pack_scalars(columns, rows):
    lane = lax.broadcasted_iota(jnp.int32, (rows, LANES), 1)
    out = jnp.zeros((rows, LANES), f32)
    for i, column in enumerate(columns):
        out = jnp.where(lane == i, column, out)
    return out


def row_sum(value):
    return jnp.sum(value, axis=1, keepdims=True)


def features_kernel(x_ref, w_ref, offset_ref, label_ref, response_ref, high_ref, low_ref, moment_ref, acc):
    samples, features = x_ref.shape[0], w_ref.shape[1]
    kept = (label_ref[...] != 0).astype(f32)
    columns = jnp.concatenate(
        [kept, kept * response_ref[...], jnp.zeros((6, samples), f32)], axis=0
    ).T
    offsets = offset_ref[...] * TURN
    acc[...] = jnp.zeros_like(acc)
    rb, cb = min(samples, 512), min(features, 512)
    for i in range(0, samples, rb):
        for j in range(0, features, cb):
            a = jnp.dot(x_ref[i : i + rb, :], w_ref[:, j : j + cb], preferred_element_type=f32)
            t = a * TURN + offsets[:, j : j + cb]
            r = t - jnp.round(t)
            u = r * r
            c = jnp.full_like(u, COSINE[-1])
            for q in COSINE[-2::-1]:
                c = c * u + q
            high, low = halves(c)
            high_ref[i : i + rb, j : j + cb] = high
            low_ref[i : i + rb, j : j + cb] = low
            square = c * c * columns[i : i + rb, 0:1]
            side = c * columns[i : i + rb, 1:2]
            acc[0, :, j : j + cb] += square.reshape(rb // 8, 8, cb).sum(0)
            acc[1, :, j : j + cb] += side.reshape(rb // 8, 8, cb).sum(0)
    moment_ref[0:1, :] = jnp.sum(acc[0], axis=0, keepdims=True)
    moment_ref[1:2, :] = jnp.sum(acc[1], axis=0, keepdims=True)


def begin_kernel(nz, *refs):
    moments, (penalty, mag, high, low), (msg, direction, precond, residual) = (
        refs[:nz],
        refs[nz : nz + 4],
        refs[nz + 4 :],
    )
    sums = total(moments)
    m = mag[...]
    pre = sums[0:1] * (m * m) + penalty[...]
    res = jnp.broadcast_to(sums[1:2] * m, pre.shape)
    s = res / pre
    precond[...] = pre
    residual[...] = res
    direction[...] = s
    send_forward(s, m, high, low, msg, [row_sum(res * s), row_sum(s * s)])


def send_forward(s, m, high, low, msg, scalars):
    samples = high.shape[0]
    msg[:, :samples] = product(s * m, high, low, 1)
    msg[:, samples:] = pack_scalars(scalars, s.shape[0])


def adjoint_kernel(ny, first, last, *refs):
    parts, refs = refs[:ny], refs[ny:]
    label, high, low, refs = refs[0], refs[1], refs[2], refs[3:]
    sums = total(parts)
    samples = label.shape[1]
    image_rows, sc = sums[:, :samples], sums[:, samples:]
    rz, dd = sc[:, 0:1], sc[:, 1:2]
    beta = jnp.zeros_like(rz)
    if not first:
        before, before_sc, refs = refs[0], refs[1], refs[2:]
        beta = rz / before_sc[:, 0:1]
        image_rows = image_rows + beta * before[...]
        dd = dd + 2.0 * beta * sc[:, 2:3] + beta * beta * before_sc[:, 1:2]
    msg, rows_out, sc_out = refs
    kept = (label[...] != 0).astype(f32)
    weighted = image_rows * kept
    scalars = pack_scalars([row_sum(weighted * image_rows)], dd.shape[0])
    if last:
        msg[...] = scalars
    else:
        features = high.shape[1]
        msg[:, :features] = product(weighted, high, low, 0)
        msg[:, features:] = scalars
    rows_out[...] = image_rows
    sc_out[...] = pack_scalars([rz, dd, beta], dd.shape[0])


def update_kernel(nz, first, *refs):
    parts, refs = refs[:nz], refs[nz:]
    sc, penalty, mag, precond, high, low, residual, scaled, refs = *refs[:8], refs[8:]
    sums = total(parts)
    features = mag.shape[1]
    lam, m = penalty[...], mag[...]
    direction = scaled[...]
    if first:
        (msg, scaled_out, direction_out, residual_out, weights_out, step_out) = refs
    else:
        (before, weights, msg, scaled_out, direction_out, residual_out, weights_out, step_out) = refs
        direction = direction + sc[:, 2:3] * before[...]
    image = sums[:, :features] * m + lam * direction
    step = sc[:, 0:1] / (sums[:, features : features + 1] + lam * sc[:, 1:2])
    moved = step * direction
    weights_out[...] = moved if first else weights[...] + moved
    res = residual[...] - step * image
    s = res / precond[...]
    residual_out[...] = res
    scaled_out[...] = s
    direction_out[...] = direction
    step_out[...] = pack_scalars([step], step.shape[0])
    send_forward(s, m, high, low, msg, [row_sum(res * s), row_sum(s * s), row_sum(s * direction)])


def finish_kernel(nz, count, *refs):
    parts, refs = refs[:nz], refs[nz:]
    sc, penalty, scaled, before, weights, refs = *refs[:5], refs[5:]
    rows, steps, (weights_out, predictions_out) = refs[:count], refs[count : 2 * count - 1], refs[2 * count - 1 :]
    sums = total(parts)
    step = sc[:, 0:1] / (sums[:, 0:1] + penalty[...] * sc[:, 1:2])
    weights_out[...] = weights[...] + step * (scaled[...] + sc[:, 2:3] * before[...])
    predictions = step * rows[-1][...]
    for r, s in zip(rows, steps):
        predictions = predictions + s[:, 0:1] * r[...]
    predictions_out[...] = predictions


ITERS = 3


def shards(
    nz,
    ny,
    input_points,
    wave_numbers,
    offset_angles,
    feature_magnitudes,
    response_values,
    split_label,
    shrinkage_levels,
):
    samples, features = input_points.shape[0], wave_numbers.shape[1]
    whole = features * ny
    levels = shrinkage_levels.shape[0]
    label = split_label.reshape(1, samples)
    penalty = shrinkage_levels.reshape(levels, 1)
    mag = feature_magnitudes.reshape(1, features) * math.sqrt(2.0 / whole)
    row_f, row_s, row_c = ((levels, features), f32), ((levels, samples), f32), ((levels, LANES), f32)
    msg_f, msg_s = ((levels, features + LANES), f32), ((levels, samples + LANES), f32)

    high, low, moments = pl.pallas_call(
        features_kernel,
        out_shape=[
            pltpu.VMEM((samples, features), bf16),
            pltpu.VMEM((samples, features), bf16),
            pltpu.VMEM((2, features), f32),
        ],
        scratch_shapes=[pltpu.VMEM((2, 8, features), f32)],
        compiler_params=pltpu.CompilerParams(vmem_limit_bytes=VMEM_LIMIT),
    )(input_points, wave_numbers, offset_angles.reshape(1, features), label, response_values.reshape(1, samples))
    high, low = in_vmem(high), in_vmem(low)
    moments = exchange(moments, "samp", nz)
    msg, scaled, precond, residual = call(
        functools.partial(begin_kernel, nz),
        [msg_s, row_f, row_f, row_f],
        *moments, penalty, mag, high, low,
    )
    before = rows = sc = weights = None
    all_rows, steps = [], []
    for it in range(ITERS):
        first, last = it == 0, it == ITERS - 1
        parts = exchange(msg, "feat", ny)
        msg, rows, sc = call(
            functools.partial(adjoint_kernel, ny, first, last),
            [row_c if last else msg_f, row_s, row_c],
            *parts, label, high, low, *(() if first else (rows, sc)),
        )
        all_rows.append(rows)
        parts = exchange(msg, "samp", nz)
        if last:
            break
        msg, scaled, before, residual, weights, step = call(
            functools.partial(update_kernel, nz, first),
            [msg_s, row_f, row_f, row_f, row_f, row_c],
            *parts, sc, penalty, mag, precond, high, low, residual, scaled,
            *(() if first else (before, weights)),
        )
        steps.append(step)
    return call(
        functools.partial(finish_kernel, nz, ITERS),
        [row_f, row_s],
        *parts, sc, penalty, scaled, before, weights, *all_rows, *steps,
        held=False,
    )


def solution(mesh):
    placed = (
        P("samp", None),
        P(None, "feat"),
        P("feat"),
        P("feat"),
        P("samp"),
        P(("fold", "samp")),
        P(),
    )
    return jax.shard_map(
        functools.partial(shards, mesh.shape["samp"], mesh.shape["feat"]),
        mesh=mesh,
        in_specs=placed,
        out_specs=(P("fold", "feat"), P("fold", "samp")),
        check_vma=False,
    )
```

time: 473 us -> 86.6 us (0.18)
  blocking collectives: 182 us -> 0 us
  waiting for transfers between devices: 164 us -> 29.2 us
  matrix products: 99 us -> 0 us
  starting transfers between devices: 0.34 us -> 23.4 us
  Pallas kernels: 0 us -> 19.1 us
  between operations: 14.1 us -> 0.69 us
  local copies, waits for them, and re-layouts: 5 us -> 13.1 us
  other arithmetic: 8.35 us -> 0.7 us
    psum x7 -> x0, blocking collectives: 128 us -> none  [inner(): return lax.psum(scalars, ('samp', 'feat'))]
    dot_general x10 -> x0, matrix products: 99 us -> none  [the longest x4 39.3 us: forward(): lax.dot_general(full_vector, matrix, (((1,), (1,)), ((), ())), precision=...]
    psum x4 -> x0, waiting for transfers between devices: 75.6 us -> none  [forward(): return lax.psum(partial_value, 'feat')]
    reduce_scatter x3 -> x0, waiting for transfers between devices: 57.9 us -> none  [reduce_columns(): lax.psum_scatter(partial_value, 'samp', scatter_dimension=1, tiled=True)]
    all_gather x4 -> x0, blocking collectives: 53.8 us -> none  [widen(): return lax.all_gather(vector, 'samp', axis=1, tiled=True)]
    unnamed x3 -> x0, waiting for transfers between devices: 30 us -> none
    ppermute x0 -> x15, waiting for transfers between devices: none -> 29.2 us  [exchange(): lax.ppermute(value, axis, [(i, i ^ s) for i in range(n)])]
    ppermute x0 -> x15, starting transfers between devices: none -> 23.4 us  [exchange(): lax.ppermute(value, axis, [(i, i ^ s) for i in range(n)])]
  transfers between devices with their start and end apart: 8 -> 15, of which waited for: 8 -> 10; matrix products, arithmetic and copies ran while one was open for 0% -> 2% of each run, Pallas kernels for 0% -> 0%
where the time goes in v1:
time: 86.6 us; the launch traced here: 86.2 us
  waiting for transfers between devices  29.2 us (34%)
  starting transfers between devices  23.4 us (27%)
  Pallas kernels  19.1 us (22%)
  local copies, waits for them, and re-layouts  13.1 us (15%)
    ppermute x15, waiting for transfers between devices, exchange(): lax.ppermute(value, axis, [(i, i ^ s) for i in range(n)])  29.2 us
    ppermute x15, starting transfers between devices, exchange(): lax.ppermute(value, axis, [(i, i ^ s) for i in range(n)])  23.4 us
    unnamed x22, local copies, waits for them, and re-layouts  12.4 us
    pallas_call x7, Pallas kernels, call(): pl.pallas_call(body, out_shape=outs, compiler_params=pltpu.CompilerParams...  11.9 us
    pallas_call x1, Pallas kernels, shards(): pl.pallas_call(features_kernel, out_shape=[pltpu.VMEM((samples, features)...  7.19 us
  transfers between devices with their start and end apart: 15, of which 10 were waited for; matrix products, arithmetic and copies ran while one was open for 2% of the time, Pallas kernels for 0%

profile of v1, /device:TPU:0, one launch (start us, length us, event | category | flops | bytes accessed | tf_op | source)
XLA Modules:
  0.0 86.2 jit_solution(11340957726864911567)
XLA Ops:
  0.6 1.0 %copy-done.5 = bf16[128,2048]{1,0:T(8,128)(2,1)S(1)} copy-done((bf16[128,2048]{1,0:T(8,128)(2,1)S(1)}, bf16[128,2048]{1,0:T(8,128)(2,1)}, u32[]{:S(2)}) %copy-start.5) | copy-done | bytes 524312
  1.7 0.9 %copy-done.6 = bf16[1024,128]{1,0:T(8,128)(2,1)S(1)} copy-done((bf16[1024,128]{1,0:T(8,128)(2,1)S(1)}, bf16[1024,128]{1,0:T(8,128)(2,1)}, u32[]{:S(2)}) %copy-start.6) | copy-done | bytes 262168
  2.6 0.7 copy-done.7
  3.3 0.7 copy-done.9
  4.0 0.7 copy-done.10
  4.7 7.2 %shard_map.86 = (bf16[1024,2048]{1,0:T(8,128)(2,1)S(1)}, bf16[1024,2048]{1,0:T(8,128)(2,1)S(1)}, f32[2,2048]{1,0:T(2,128)S(1)}) custom-call(bf16[1024,128]{1,0:T(8,128)(2,1)S(1)} %copy-done.6, bf16[128,2048]{1,0:T(8,128)(2,1)S(1)} %copy-done.5, f32[1,2048]{1,0:T(1,128)S(1)} %bitcast.12, s32[1,1024]{1,0:T(1,128)S(1)} %bitcast.8, f32[1,1024]{1,0:T(1,128)S(1)} %bitcast.13), custom_call_target="tpu_custom_call" | custom-call | tf_op jit(solution)/shard_map/pallas_call | solution.py:213
  11.9 2.0 %copy-done = bf16[1024,2048]{1,0:T(8,128)(2,1)} copy-done((bf16[1024,2048]{1,0:T(8,128)(2,1)}, bf16[1024,2048]{1,0:T(8,128)(2,1)S(1)}, u32[]{:S(2)}) %copy-start) | copy-done | bytes 4194328
  13.9 2.0 %copy-done.3 = bf16[1024,2048]{1,0:T(8,128)(2,1)} copy-done((bf16[1024,2048]{1,0:T(8,128)(2,1)}, bf16[1024,2048]{1,0:T(8,128)(2,1)S(1)}, u32[]{:S(2)}) %copy-start.3) | copy-done | bytes 4194328
  15.9 5.0 %collective-permute-start.2 = (f32[2,2048]{1,0:T(2,128)S(1)}, f32[2,2048]{1,0:T(2,128)S(1)}, u32[]{:S(2)}, u32[]{:S(2)}) collective-permute-start(f32[2,2048]{1,0:T(2,128)S(1)} %get-tuple-element.29.refs_0_), channel_id=1, source_target_pairs={{0,6},{2,4},{4,2},{6,0},{1,7},{3,5},{5,3},{7,1},{8,14},{10,12},{12... | collective-permute-start | bytes 49160 | tf_op jit(solution)/shard_map/ppermute | solution.py:35
  20.9 0.0 collective-permute-start.1
  20.9 0.6 collective-permute-start
  21.5 0.7 broadcast_multiply_fusion
  22.2 0.7 copy.9.refs_4_.refs_5_
  22.9 0.0 collective-permute-done.2.refs_3_
  22.9 2.6 %collective-permute-done.1.refs_2_ = f32[2,2048]{1,0:T(2,128)S(1)} collective-permute-done((f32[2,2048]{1,0:T(2,128)S(1)}, f32[2,2048]{1,0:T(2,128)S(1)}, u32[]{:S(2)}, u32[]{:S(2)}) %collective-permute-start.1) | collective-permute-done | bytes 16416 | tf_op jit(solution)/shard_map/ppermute | solution.py:35
  25.6 0.0 collective-permute-done.refs_1_
  25.6 2.2 %copy-done.1 = bf16[1024,2048]{1,0:T(8,128)(2,1)S(1)} copy-done((bf16[1024,2048]{1,0:T(8,128)(2,1)S(1)}, bf16[1024,2048]{1,0:T(8,128)(2,1)}, u32[]{:S(2)}) %copy-start.1) | copy-done | bytes 4194328
  27.8 2.2 %copy-done.4 = bf16[1024,2048]{1,0:T(8,128)(2,1)S(1)} copy-done((bf16[1024,2048]{1,0:T(8,128)(2,1)S(1)}, bf16[1024,2048]{1,0:T(8,128)(2,1)}, u32[]{:S(2)}) %copy-start.4) | copy-done | bytes 4194328
  29.9 2.4 %shard_map.87 = (f32[16,1152]{1,0:T(8,128)S(1)}, f32[16,2048]{1,0:T(8,128)S(1)}, f32[16,2048]{1,0:T(8,128)S(1)}, f32[16,2048]{1,0:T(8,128)S(1)}) custom-call(f32[2,2048]{1,0:T(2,128)S(1)} %get-tuple-element.29.refs_0_, f32[2,2048]{1,0:T(2,128)S(1)} %collective-permute-done.refs_1_, f32[2,2048]{1,0:T(2,128)S(1)} %collective-permute-done.1.refs_2_, ...), custom_call_target="tpu_custom_call" | custom-call | bytes 8462400 | tf_op jit(solution)/shard_map/pallas_call | solution.py:25
  32.4 1.5 %collective-permute-start.3 = (f32[16,1152]{1,0:T(8,128)S(1)}, f32[16,1152]{1,0:T(8,128)S(1)}, u32[]{:S(2)}, u32[]{:S(2)}) collective-permute-start(f32[16,1152]{1,0:T(8,128)S(1)} %get-tuple-element.32.refs_0_), channel_id=1, source_target_pairs={{0,1},{1,0},{2,3},{3,2},{4,5},{5,4},{6,7},{7,6},{8,9},{9,8},{10,11... | collective-permute-start | bytes 221192 | tf_op jit(solution)/shard_map/ppermute | solution.py:35
  33.9 2.8 %collective-permute-done.3.refs_1_ = f32[16,1152]{1,0:T(8,128)S(1)} collective-permute-done((f32[16,1152]{1,0:T(8,128)S(1)}, f32[16,1152]{1,0:T(8,128)S(1)}, u32[]{:S(2)}, u32[]{:S(2)}) %collective-permute-start.3) | collective-permute-done | bytes 73760 | tf_op jit(solution)/shard_map/ppermute | solution.py:35
  36.7 1.3 %shard_map.88 = (f32[16,2176]{1,0:T(8,128)S(1)}, f32[16,1024]{1,0:T(8,128)S(1)}, f32[16,128]{1,0:T(8,128)S(1)}) custom-call(f32[16,1152]{1,0:T(8,128)S(1)} %get-tuple-element.32.refs_0_, f32[16,1152]{1,0:T(8,128)S(1)} %collective-permute-done.3.refs_1_, s32[1,1024]{1,0:T(1,128)S(1)} %bitcast.9, bf16[1024,2048]{1,0:T(8,128)(2,1)S(1)} %copy-done.2, ...), custom_call_target="tpu_custom_call" | custom-call | bytes 8540160 | tf_op jit(solution)/shard_map/pallas_call | solution.py:25
  38.1 1.5 %collective-permute-start.6 = (f32[16,2176]{1,0:T(8,128)S(1)}, f32[16,2176]{1,0:T(8,128)S(1)}, u32[]{:S(2)}, u32[]{:S(2)}) collective-permute-start(f32[16,2176]{1,0:T(8,128)S(1)} %get-tuple-element.33.refs_0_), channel_id=1, source_target_pairs={{0,6},{2,4},{4,2},{6,0},{1,7},{3,5},{5,3},{7,1},{8,14},{10,12},{12... | collective-permute-start | bytes 417800 | tf_op jit(solution)/shard_map/ppermute | solution.py:35
  39.5 0.6 collective-permute-start.5
  40.1 2.3 %collective-permute-start.4 = (f32[16,2176]{1,0:T(8,128)S(1)}, f32[16,2176]{1,0:T(8,128)S(1)}, u32[]{:S(2)}, u32[]{:S(2)}) collective-permute-start(f32[16,2176]{1,0:T(8,128)S(1)} %get-tuple-element.33.refs_0_), channel_id=1, source_target_pairs={{0,2},{2,0},{4,6},{6,4},{1,3},{3,1},{5,7},{7,5},{8,10},{10,8},{12,... | collective-permute-start | bytes 417800 | tf_op jit(solution)/shard_map/ppermute | solution.py:35
  42.5 3.4 %collective-permute-done.6.refs_3_ = f32[16,2176]{1,0:T(8,128)S(1)} collective-permute-done((f32[16,2176]{1,0:T(8,128)S(1)}, f32[16,2176]{1,0:T(8,128)S(1)}, u32[]{:S(2)}, u32[]{:S(2)}) %collective-permute-start.6) | collective-permute-done | bytes 139296 | tf_op jit(solution)/shard_map/ppermute | solution.py:35
  45.9 4.3 %collective-permute-done.5.refs_2_ = f32[16,2176]{1,0:T(8,128)S(1)} collective-permute-done((f32[16,2176]{1,0:T(8,128)S(1)}, f32[16,2176]{1,0:T(8,128)S(1)}, u32[]{:S(2)}, u32[]{:S(2)}) %collective-permute-start.5) | collective-permute-done | bytes 139296 | tf_op jit(solution)/shard_map/ppermute | solution.py:35
  50.2 0.0 collective-permute-done.4.refs_1_
  50.2 2.5 %shard_map.89 = (f32[16,1152]{1,0:T(8,128)S(1)}, f32[16,2048]{1,0:T(8,128)S(1)}, f32[16,2048]{1,0:T(8,128)S(1)}, f32[16,2048]{1,0:T(8,128)S(1)}, f32[16,2048]{1,0:T(8,128)S(1)}, /*index=5*/f32[16,128]{1,0:T(8,128)S(1)}) custom-call(f32[16,2176]{1,0:T(8,128)S(1)} %get-tuple-element.33.refs_0_, f32[16,2176]{1,0:T(8,128)S(1)} %collective-permute-done.4.refs_1_, ...), custom_call_target="tpu_custom_call" | custom-call | bytes 9355328 | tf_op jit(solution)/shard_map/pallas_call | solution.py:25
  52.7 1.5 %collective-permute-start.7 = (f32[16,1152]{1,0:T(8,128)S(1)}, f32[16,1152]{1,0:T(8,128)S(1)}, u32[]{:S(2)}, u32[]{:S(2)}) collective-permute-start(f32[16,1152]{1,0:T(8,128)S(1)} %get-tuple-element.38.refs_0_), channel_id=1, source_target_pairs={{0,1},{1,0},{2,3},{3,2},{4,5},{5,4},{6,7},{7,6},{8,9},{9,8},{10,11... | collective-permute-start | bytes 221192 | tf_op jit(solution)/shard_map/ppermute | solution.py:35
  54.2 2.8 %collective-permute-done.7.refs_1_ = f32[16,1152]{1,0:T(8,128)S(1)} collective-permute-done((f32[16,1152]{1,0:T(8,128)S(1)}, f32[16,1152]{1,0:T(8,128)S(1)}, u32[]{:S(2)}, u32[]{:S(2)}) %collective-permute-start.7) | collective-permute-done | bytes 73760 | tf_op jit(solution)/shard_map/ppermute | solution.py:35
  57.0 1.6 %shard_map.90 = (f32[16,2176]{1,0:T(8,128)S(1)}, f32[16,1024]{1,0:T(8,128)S(1)}, f32[16,128]{1,0:T(8,128)S(1)}) custom-call(f32[16,1152]{1,0:T(8,128)S(1)} %get-tuple-element.38.refs_0_, f32[16,1152]{1,0:T(8,128)S(1)} %collective-permute-done.7.refs_1_, s32[1,1024]{1,0:T(1,128)S(1)} %bitcast.10, bf16[1024,2048]{1,0:T(8,128)(2,1)S(1)} %copy-done.2, ...), custom_call_target="tpu_custom_call" | custom-call | bytes 8613888 | tf_op jit(solution)/shard_map/pallas_call | solution.py:25
  58.6 2.5 %collective-permute-start.10 = (f32[16,2176]{1,0:T(8,128)S(1)}, f32[16,2176]{1,0:T(8,128)S(1)}, u32[]{:S(2)}, u32[]{:S(2)}) collective-permute-start(f32[16,2176]{1,0:T(8,128)S(1)} %get-tuple-element.40.refs_0_), channel_id=1, source_target_pairs={{0,6},{2,4},{4,2},{6,0},{1,7},{3,5},{5,3},{7,1},{8,14},{10,12},{12... | collective-permute-start | bytes 417800 | tf_op jit(solution)/shard_map/ppermute | solution.py:35
  61.1 0.0 collective-permute-start.9
  61.1 1.9 %collective-permute-start.8 = (f32[16,2176]{1,0:T(8,128)S(1)}, f32[16,2176]{1,0:T(8,128)S(1)}, u32[]{:S(2)}, u32[]{:S(2)}) collective-permute-start(f32[16,2176]{1,0:T(8,128)S(1)} %get-tuple-element.40.refs_0_), channel_id=1, source_target_pairs={{0,2},{2,0},{4,6},{6,4},{1,3},{3,1},{5,7},{7,5},{8,10},{10,8},{12,... | collective-permute-start | bytes 417800 | tf_op jit(solution)/shard_map/ppermute | solution.py:35
  63.0 3.4 %collective-permute-done.10.refs_3_ = f32[16,2176]{1,0:T(8,128)S(1)} collective-permute-done((f32[16,2176]{1,0:T(8,128)S(1)}, f32[16,2176]{1,0:T(8,128)S(1)}, u32[]{:S(2)}, u32[]{:S(2)}) %collective-permute-start.10) | collective-permute-done | bytes 139296 | tf_op jit(solution)/shard_map/ppermute | solution.py:35
  66.4 4.2 %collective-permute-done.9.refs_2_ = f32[16,2176]{1,0:T(8,128)S(1)} collective-permute-done((f32[16,2176]{1,0:T(8,128)S(1)}, f32[16,2176]{1,0:T(8,128)S(1)}, u32[]{:S(2)}, u32[]{:S(2)}) %collective-permute-start.9) | collective-permute-done | bytes 139296 | tf_op jit(solution)/shard_map/ppermute | solution.py:35
  70.5 0.0 collective-permute-done.8.refs_1_
  70.5 3.0 %shard_map.91 = (f32[16,1152]{1,0:T(8,128)S(1)}, f32[16,2048]{1,0:T(8,128)S(1)}, f32[16,2048]{1,0:T(8,128)S(1)}, f32[16,2048]{1,0:T(8,128)}, f32[16,2048]{1,0:T(8,128)S(1)}, /*index=5*/f32[16,128]{1,0:T(8,128)S(1)}) custom-call(f32[16,2176]{1,0:T(8,128)S(1)} %get-tuple-element.40.refs_0_, f32[16,2176]{1,0:T(8,128)S(1)} %collective-permute-done.8.refs_1_, ...), custom_call_target="tpu_custom_call" | custom-call | bytes 9617472 | tf_op jit(solution)/shard_map/pallas_call | solution.py:25
  73.6 1.5 %collective-permute-start.11 = (f32[16,1152]{1,0:T(8,128)S(1)}, f32[16,1152]{1,0:T(8,128)S(1)}, u32[]{:S(2)}, u32[]{:S(2)}) collective-permute-start(f32[16,1152]{1,0:T(8,128)S(1)} %get-tuple-element.46.refs_0_), channel_id=1, source_target_pairs={{0,1},{1,0},{2,3},{3,2},{4,5},{5,4},{6,7},{7,6},{8,9},{9,8},{10,11... | collective-permute-start | bytes 221192 | tf_op jit(solution)/shard_map/ppermute | solution.py:35
  75.1 2.8 %collective-permute-done.11.refs_1_ = f32[16,1152]{1,0:T(8,128)S(1)} collective-permute-done((f32[16,1152]{1,0:T(8,128)S(1)}, f32[16,1152]{1,0:T(8,128)S(1)}, u32[]{:S(2)}, u32[]{:S(2)}) %collective-permute-start.11) | collective-permute-done | bytes 73760 | tf_op jit(solution)/shard_map/ppermute | solution.py:35
  77.9 0.2 shard_map.92
  78.1 2.7 %collective-permute-start.14 = (f32[16,128]{1,0:T(8,128)S(1)}, f32[16,128]{1,0:T(8,128)S(1)}, u32[]{:S(2)}, u32[]{:S(2)}) collective-permute-start(f32[16,128]{1,0:T(8,128)S(1)} %get-tuple-element.48.refs_0_), channel_id=1, source_target_pairs={{0,6},{2,4},{4,2},{6,0},{1,7},{3,5},{5,3},{7,1},{8,14},{10,12},{12... | collective-permute-start | bytes 24584 | tf_op jit(solution)/shard_map/ppermute | solution.py:35
  80.8 0.0 collective-permute-start.13
  80.8 1.7 %collective-permute-start.12 = (f32[16,128]{1,0:T(8,128)S(1)}, f32[16,128]{1,0:T(8,128)S(1)}, u32[]{:S(2)}, u32[]{:S(2)}) collective-permute-start(f32[16,128]{1,0:T(8,128)S(1)} %get-tuple-element.48.refs_0_), channel_id=1, source_target_pairs={{0,2},{2,0},{4,6},{6,4},{1,3},{3,1},{5,7},{7,5},{8,10},{10,8},{12,... | collective-permute-start | bytes 24584 | tf_op jit(solution)/shard_map/ppermute | solution.py:35
  82.5 1.1 %collective-permute-done.14.refs_3_ = f32[16,128]{1,0:T(8,128)S(1)} collective-permute-done((f32[16,128]{1,0:T(8,128)S(1)}, f32[16,128]{1,0:T(8,128)S(1)}, u32[]{:S(2)}, u32[]{:S(2)}) %collective-permute-start.14) | collective-permute-done | bytes 8224 | tf_op jit(solution)/shard_map/ppermute | solution.py:35
  83.6 1.7 %collective-permute-done.13.refs_2_ = f32[16,128]{1,0:T(8,128)S(1)} collective-permute-done((f32[16,128]{1,0:T(8,128)S(1)}, f32[16,128]{1,0:T(8,128)S(1)}, u32[]{:S(2)}, u32[]{:S(2)}) %collective-permute-start.13) | collective-permute-done | bytes 8224 | tf_op jit(solution)/shard_map/ppermute | solution.py:35
  85.3 0.8 shard_map.93
  (14 shorter events, 0.0 us)
Async XLA Ops:
  0.6 1.0 %copy-start.5 = (bf16[128,2048]{1,0:T(8,128)(2,1)S(1)}, bf16[128,2048]{1,0:T(8,128)(2,1)}, u32[]{:S(2)}) copy-start(bf16[128,2048]{1,0:T(8,128)(2,1)} %w_ref.1) | copy-start | bytes 1572868
  1.7 0.9 %copy-start.6 = (bf16[1024,128]{1,0:T(8,128)(2,1)S(1)}, bf16[1024,128]{1,0:T(8,128)(2,1)}, u32[]{:S(2)}) copy-start(bf16[1024,128]{1,0:T(8,128)(2,1)} %x_ref.1) | copy-start | bytes 786436
  2.6 0.7 copy-start.7
  3.3 0.7 copy-start.9
  4.0 0.7 copy-start.10
  11.9 2.0 %copy-start = (bf16[1024,2048]{1,0:T(8,128)(2,1)}, bf16[1024,2048]{1,0:T(8,128)(2,1)S(1)}, u32[]{:S(2)}) copy-start(bf16[1024,2048]{1,0:T(8,128)(2,1)S(1)} %get-tuple-element.30.refs_6_.refs_3_.refs_8_) | copy-start | bytes 12582916
  13.9 2.0 %copy-start.3 = (bf16[1024,2048]{1,0:T(8,128)(2,1)}, bf16[1024,2048]{1,0:T(8,128)(2,1)S(1)}, u32[]{:S(2)}) copy-start(bf16[1024,2048]{1,0:T(8,128)(2,1)S(1)} %get-tuple-element.31.refs_7_.refs_4_.refs_9_) | copy-start | bytes 12582916
  15.9 7.0 %collective-permute-start.2 = (f32[2,2048]{1,0:T(2,128)S(1)}, f32[2,2048]{1,0:T(2,128)S(1)}, u32[]{:S(2)}, u32[]{:S(2)}) collective-permute-start(f32[2,2048]{1,0:T(2,128)S(1)} %get-tuple-element.29.refs_0_), channel_id=1, source_target_pairs={{0,6},{2,4},{4,2},{6,0},{1,7},{3,5},{5,3},{7,1},{8,14},{10,12},{12... | collective-permute-start | bytes 49160 | tf_op jit(solution)/shard_map/ppermute | solution.py:35
  20.9 4.6 %collective-permute-start.1 = (f32[2,2048]{1,0:T(2,128)S(1)}, f32[2,2048]{1,0:T(2,128)S(1)}, u32[]{:S(2)}, u32[]{:S(2)}) collective-permute-start(f32[2,2048]{1,0:T(2,128)S(1)} %get-tuple-element.29.refs_0_), channel_id=1, source_target_pairs={{0,4},{2,6},{4,0},{6,2},{1,5},{3,7},{5,1},{7,3},{8,12},{10,14},{12... | collective-permute-start | bytes 49160 | tf_op jit(solution)/shard_map/ppermute | solution.py:35
  20.9 4.6 %collective-permute-start = (f32[2,2048]{1,0:T(2,128)S(1)}, f32[2,2048]{1,0:T(2,128)S(1)}, u32[]{:S(2)}, u32[]{:S(2)}) collective-permute-start(f32[2,2048]{1,0:T(2,128)S(1)} %get-tuple-element.29.refs_0_), channel_id=1, source_target_pairs={{0,2},{2,0},{4,6},{6,4},{1,3},{3,1},{5,7},{7,5},{8,10},{10,8},{12,... | collective-permute-start | bytes 49160 | tf_op jit(solution)/shard_map/ppermute | solution.py:35
  25.6 2.2 %copy-start.1 = (bf16[1024,2048]{1,0:T(8,128)(2,1)S(1)}, bf16[1024,2048]{1,0:T(8,128)(2,1)}, u32[]{:S(2)}) copy-start(bf16[1024,2048]{1,0:T(8,128)(2,1)} %copy-done) | copy-start | bytes 12582916
  27.7 2.2 %copy-start.4 = (bf16[1024,2048]{1,0:T(8,128)(2,1)S(1)}, bf16[1024,2048]{1,0:T(8,128)(2,1)}, u32[]{:S(2)}) copy-start(bf16[1024,2048]{1,0:T(8,128)(2,1)} %copy-done.3) | copy-start | bytes 12582916
  29.9 6.8 %copy-start.2 = (bf16[1024,2048]{1,0:T(8,128)(2,1)S(1)}, bf16[1024,2048]{1,0:T(8,128)(2,1)}, u32[]{:S(2)}) copy-start(bf16[1024,2048]{1,0:T(8,128)(2,1)} %copy-done) | copy-start | bytes 12582916
  29.9 6.8 %copy-start.8 = (s32[1024]{0:T(1024)S(1)}, s32[1024]{0:T(1024)}, u32[]{:S(2)}) copy-start(s32[1024]{0:T(1024)} %param.12) | copy-start | bytes 12292
  32.4 4.4 %collective-permute-start.3 = (f32[16,1152]{1,0:T(8,128)S(1)}, f32[16,1152]{1,0:T(8,128)S(1)}, u32[]{:S(2)}, u32[]{:S(2)}) collective-permute-start(f32[16,1152]{1,0:T(8,128)S(1)} %get-tuple-element.32.refs_0_), channel_id=1, source_target_pairs={{0,1},{1,0},{2,3},{3,2},{4,5},{5,4},{6,7},{7,6},{8,9},{9,8},{10,11... | collective-permute-start | bytes 221192 | tf_op jit(solution)/shard_map/ppermute | solution.py:35
  38.1 7.8 %collective-permute-start.6 = (f32[16,2176]{1,0:T(8,128)S(1)}, f32[16,2176]{1,0:T(8,128)S(1)}, u32[]{:S(2)}, u32[]{:S(2)}) collective-permute-start(f32[16,2176]{1,0:T(8,128)S(1)} %get-tuple-element.33.refs_0_), channel_id=1, source_target_pairs={{0,6},{2,4},{4,2},{6,0},{1,7},{3,5},{5,3},{7,1},{8,14},{10,12},{12... | collective-permute-start | bytes 417800 | tf_op jit(solution)/shard_map/ppermute | solution.py:35
  39.5 10.6 %collective-permute-start.5 = (f32[16,2176]{1,0:T(8,128)S(1)}, f32[16,2176]{1,0:T(8,128)S(1)}, u32[]{:S(2)}, u32[]{:S(2)}) collective-permute-start(f32[16,2176]{1,0:T(8,128)S(1)} %get-tuple-element.33.refs_0_), channel_id=1, source_target_pairs={{0,4},{2,6},{4,0},{6,2},{1,5},{3,7},{5,1},{7,3},{8,12},{10,14},{12... | collective-permute-start | bytes 417800 | tf_op jit(solution)/shard_map/ppermute | solution.py:35
  40.1 10.0 %collective-permute-start.4 = (f32[16,2176]{1,0:T(8,128)S(1)}, f32[16,2176]{1,0:T(8,128)S(1)}, u32[]{:S(2)}, u32[]{:S(2)}) collective-permute-start(f32[16,2176]{1,0:T(8,128)S(1)} %get-tuple-element.33.refs_0_), channel_id=1, source_target_pairs={{0,2},{2,0},{4,6},{6,4},{1,3},{3,1},{5,7},{7,5},{8,10},{10,8},{12,... | collective-permute-start | bytes 417800 | tf_op jit(solution)/shard_map/ppermute | solution.py:35
  52.7 4.4 %collective-permute-start.7 = (f32[16,1152]{1,0:T(8,128)S(1)}, f32[16,1152]{1,0:T(8,128)S(1)}, u32[]{:S(2)}, u32[]{:S(2)}) collective-permute-start(f32[16,1152]{1,0:T(8,128)S(1)} %get-tuple-element.38.refs_0_), channel_id=1, source_target_pairs={{0,1},{1,0},{2,3},{3,2},{4,5},{5,4},{6,7},{7,6},{8,9},{9,8},{10,11... | collective-permute-start | bytes 221192 | tf_op jit(solution)/shard_map/ppermute | solution.py:35
  58.6 7.8 %collective-permute-start.10 = (f32[16,2176]{1,0:T(8,128)S(1)}, f32[16,2176]{1,0:T(8,128)S(1)}, u32[]{:S(2)}, u32[]{:S(2)}) collective-permute-start(f32[16,2176]{1,0:T(8,128)S(1)} %get-tuple-element.40.refs_0_), channel_id=1, source_target_pairs={{0,6},{2,4},{4,2},{6,0},{1,7},{3,5},{5,3},{7,1},{8,14},{10,12},{12... | collective-permute-start | bytes 417800 | tf_op jit(solution)/shard_map/ppermute | solution.py:35
  61.1 9.5 %collective-permute-start.9 = (f32[16,2176]{1,0:T(8,128)S(1)}, f32[16,2176]{1,0:T(8,128)S(1)}, u32[]{:S(2)}, u32[]{:S(2)}) collective-permute-start(f32[16,2176]{1,0:T(8,128)S(1)} %get-tuple-element.40.refs_0_), channel_id=1, source_target_pairs={{0,4},{2,6},{4,0},{6,2},{1,5},{3,7},{5,1},{7,3},{8,12},{10,14},{12... | collective-permute-start | bytes 417800 | tf_op jit(solution)/shard_map/ppermute | solution.py:35
  61.1 9.5 %collective-permute-start.8 = (f32[16,2176]{1,0:T(8,128)S(1)}, f32[16,2176]{1,0:T(8,128)S(1)}, u32[]{:S(2)}, u32[]{:S(2)}) collective-permute-start(f32[16,2176]{1,0:T(8,128)S(1)} %get-tuple-element.40.refs_0_), channel_id=1, source_target_pairs={{0,2},{2,0},{4,6},{6,4},{1,3},{3,1},{5,7},{7,5},{8,10},{10,8},{12,... | collective-permute-start | bytes 417800 | tf_op jit(solution)/shard_map/ppermute | solution.py:35
  73.6 4.4 %collective-permute-start.11 = (f32[16,1152]{1,0:T(8,128)S(1)}, f32[16,1152]{1,0:T(8,128)S(1)}, u32[]{:S(2)}, u32[]{:S(2)}) collective-permute-start(f32[16,1152]{1,0:T(8,128)S(1)} %get-tuple-element.46.refs_0_), channel_id=1, source_target_pairs={{0,1},{1,0},{2,3},{3,2},{4,5},{5,4},{6,7},{7,6},{8,9},{9,8},{10,11... | collective-permute-start | bytes 221192 | tf_op jit(solution)/shard_map/ppermute | solution.py:35
  78.1 5.5 %collective-permute-start.14 = (f32[16,128]{1,0:T(8,128)S(1)}, f32[16,128]{1,0:T(8,128)S(1)}, u32[]{:S(2)}, u32[]{:S(2)}) collective-permute-start(f32[16,128]{1,0:T(8,128)S(1)} %get-tuple-element.48.refs_0_), channel_id=1, source_target_pairs={{0,6},{2,4},{4,2},{6,0},{1,7},{3,5},{5,3},{7,1},{8,14},{10,12},{12... | collective-permute-start | bytes 24584 | tf_op jit(solution)/shard_map/ppermute | solution.py:35
  80.8 4.5 %collective-permute-start.13 = (f32[16,128]{1,0:T(8,128)S(1)}, f32[16,128]{1,0:T(8,128)S(1)}, u32[]{:S(2)}, u32[]{:S(2)}) collective-permute-start(f32[16,128]{1,0:T(8,128)S(1)} %get-tuple-element.48.refs_0_), channel_id=1, source_target_pairs={{0,4},{2,6},{4,0},{6,2},{1,5},{3,7},{5,1},{7,3},{8,12},{10,14},{12... | collective-permute-start | bytes 24584 | tf_op jit(solution)/shard_map/ppermute | solution.py:35
  80.8 4.5 %collective-permute-start.12 = (f32[16,128]{1,0:T(8,128)S(1)}, f32[16,128]{1,0:T(8,128)S(1)}, u32[]{:S(2)}, u32[]{:S(2)}) collective-permute-start(f32[16,128]{1,0:T(8,128)S(1)} %get-tuple-element.48.refs_0_), channel_id=1, source_target_pairs={{0,2},{2,0},{4,6},{6,4},{1,3},{3,1},{5,7},{7,5},{8,10},{10,8},{12,... | collective-permute-start | bytes 24584 | tf_op jit(solution)/shard_map/ppermute | solution.py:35

commit v2 on v1

--- a/solution.py
+++ b/solution.py
@@ -12,11 +12,7 @@
 TURN = 1.0 / (2.0 * math.pi)
 COSINE = (0.999999211770312, -19.738980419471126, 64.92865850463285, -85.27162830146948, 58.79050662870376, -21.071108461771125)
 LANES = 128
-VMEM_LIMIT = 32 * 2**20
-
-
-def in_vmem(value):
-    return pltpu.with_memory_space_constraint(value, pltpu.VMEM)
+VMEM_LIMIT = 12 * 2**20
 
 
 def call(body, outs, *args, flops=0, held=True):
@@ -70,17 +66,31 @@
     return jnp.sum(value, axis=1, keepdims=True)
 
 
-def features_kernel(x_ref, w_ref, offset_ref, label_ref, response_ref, high_ref, low_ref, moment_ref, acc):
+def features_kernel(
+    scale, x_hbm, w_hbm, offset_hbm, mag_hbm, response_hbm, label_hbm, penalty_hbm,
+    high_ref, low_ref, moment_ref, mag_ref, kept_ref, penalty_ref,
+    x_ref, w_ref, offset_ref, mag_in, response_ref, label_ref, penalty_in, acc, sems,
+):
     samples, features = x_ref.shape[0], w_ref.shape[1]
+    rb, cb = min(samples, 512), min(features, 512)
+    pairs = [(x_hbm, x_ref), (offset_hbm, offset_ref), (label_hbm, label_ref), (response_hbm, response_ref)]
+    pairs += [(w_hbm.at[:, j : j + cb], w_ref.at[:, j : j + cb]) for j in range(0, features, cb)]
+    pairs += [(mag_hbm, mag_in), (penalty_hbm, penalty_in)]
+    copies = [pltpu.make_async_copy(a, b, sems.at[i]) for i, (a, b) in enumerate(pairs)]
+    for copy in copies:
+        copy.start()
+    acc[...] = jnp.zeros_like(acc)
+    for copy in copies[:4]:
+        copy.wait()
     kept = (label_ref[...] != 0).astype(f32)
+    kept_ref[...] = kept
     columns = jnp.concatenate(
         [kept, kept * response_ref[...], jnp.zeros((6, samples), f32)], axis=0
     ).T
     offsets = offset_ref[...] * TURN
-    acc[...] = jnp.zeros_like(acc)
-    rb, cb = min(samples, 512), min(features, 512)
-    for i in range(0, samples, rb):
-        for j in range(0, features, cb):
+    for j in range(0, features, cb):
+        copies[4 + j // cb].wait()
+        for i in range(0, samples, rb):
             a = jnp.dot(x_ref[i : i + rb, :], w_ref[:, j : j + cb], preferred_element_type=f32)
             t = a * TURN + offsets[:, j : j + cb]
             r = t - jnp.round(t)
@@ -97,6 +107,12 @@
             acc[1, :, j : j + cb] += side.reshape(rb // 8, 8, cb).sum(0)
     moment_ref[0:1, :] = jnp.sum(acc[0], axis=0, keepdims=True)
     moment_ref[1:2, :] = jnp.sum(acc[1], axis=0, keepdims=True)
+    for copy in copies[-2:]:
+        copy.wait()
+    mag_ref[...] = mag_in[...] * scale
+    levels = penalty_in.shape[1]
+    at = [lax.broadcasted_iota(jnp.int32, (levels, levels), a) for a in (0, 1)]
+    penalty_ref[...] = row_sum(jnp.where(at[0] == at[1], penalty_in[...], 0.0))
 
 
 def begin_kernel(nz, *refs):
@@ -124,9 +140,9 @@
 
 def adjoint_kernel(ny, first, last, *refs):
     parts, refs = refs[:ny], refs[ny:]
-    label, high, low, refs = refs[0], refs[1], refs[2], refs[3:]
+    kept, high, low, refs = refs[0], refs[1], refs[2], refs[3:]
     sums = total(parts)
-    samples = label.shape[1]
+    samples = kept.shape[1]
     image_rows, sc = sums[:, :samples], sums[:, samples:]
     rz, dd = sc[:, 0:1], sc[:, 1:2]
     beta = jnp.zeros_like(rz)
@@ -136,8 +152,7 @@
         image_rows = image_rows + beta * before[...]
         dd = dd + 2.0 * beta * sc[:, 2:3] + beta * beta * before_sc[:, 1:2]
     msg, rows_out, sc_out = refs
-    kept = (label[...] != 0).astype(f32)
-    weighted = image_rows * kept
+    weighted = image_rows * kept[...]
     scalars = pack_scalars([row_sum(weighted * image_rows)], dd.shape[0])
     if last:
         msg[...] = scalars
@@ -204,23 +219,26 @@
     samples, features = input_points.shape[0], wave_numbers.shape[1]
     whole = features * ny
     levels = shrinkage_levels.shape[0]
-    label = split_label.reshape(1, samples)
-    penalty = shrinkage_levels.reshape(levels, 1)
-    mag = feature_magnitudes.reshape(1, features) * math.sqrt(2.0 / whole)
     row_f, row_s, row_c = ((levels, features), f32), ((levels, samples), f32), ((levels, LANES), f32)
     msg_f, msg_s = ((levels, features + LANES), f32), ((levels, samples + LANES), f32)
 
-    high, low, moments = pl.pallas_call(
-        features_kernel,
+    inputs = [input_points, wave_numbers]
+    inputs += [v.reshape(1, -1) for v in (offset_angles, feature_magnitudes, response_values, split_label, shrinkage_levels)]
+    high, low, moments, mag, kept, penalty = pl.pallas_call(
+        functools.partial(features_kernel, math.sqrt(2.0 / whole)),
         out_shape=[
             pltpu.VMEM((samples, features), bf16),
             pltpu.VMEM((samples, features), bf16),
             pltpu.VMEM((2, features), f32),
+            pltpu.VMEM((1, features), f32),
+            pltpu.VMEM((1, samples), f32),
+            pltpu.VMEM((levels, 1), f32),
         ],
-        scratch_shapes=[pltpu.VMEM((2, 8, features), f32)],
+        in_specs=[pl.BlockSpec(memory_space=pltpu.HBM)] * len(inputs),
+        scratch_shapes=[pltpu.VMEM(v.shape, v.dtype) for v in inputs]
+        + [pltpu.VMEM((2, 8, features), f32), pltpu.SemaphoreType.DMA((6 + features // min(features, 512),))],
         compiler_params=pltpu.CompilerParams(vmem_limit_bytes=VMEM_LIMIT),
-    )(input_points, wave_numbers, offset_angles.reshape(1, features), label, response_values.reshape(1, samples))
-    high, low = in_vmem(high), in_vmem(low)
+    )(*[pltpu.with_memory_space_constraint(v, pltpu.HBM) for v in inputs])
     moments = exchange(moments, "samp", nz)
     msg, scaled, precond, residual = call(
         functools.partial(begin_kernel, nz),
@@ -235,7 +253,7 @@
         msg, rows, sc = call(
             functools.partial(adjoint_kernel, ny, first, last),
             [row_c if last else msg_f, row_s, row_c],
-            *parts, label, high, low, *(() if first else (rows, sc)),
+            *parts, kept, high, low, *(() if first else (rows, sc)),
         )
         all_rows.append(rows)
         parts = exchange(msg, "samp", nz)

time: 86.6 us -> 75.5 us (0.87)
  local copies, waits for them, and re-layouts: 13.1 us -> 0 us
  Pallas kernels: 19.1 us -> 20.6 us
  waiting for transfers between devices: 29.2 us -> 30.5 us
    unnamed x22 -> x0, local copies, waits for them, and re-layouts: 12.4 us -> none
    pallas_call x1, Pallas kernels: 7.19 us -> 8.73 us  [shards(): pl.pallas_call(functools.partial(features_kernel, math.sqrt(2.0 / whole))...]
    ppermute x15, waiting for transfers between devices: 29.2 us -> 30.5 us  [exchange(): lax.ppermute(value, axis, [(i, i ^ s) for i in range(n)])]
  transfers between devices with their start and end apart: 15 -> 15, of which waited for: 10 -> 11; matrix products, arithmetic and copies ran while one was open for 2% -> 0% of each run, Pallas kernels for 0% -> 0%
where the time goes in v2:
time: 75.5 us; the launch traced here: 75.4 us
  waiting for transfers between devices  30.5 us (40%)
  starting transfers between devices  23.5 us (31%)
  Pallas kernels  20.6 us (27%)
    ppermute x15, waiting for transfers between devices, exchange(): lax.ppermute(value, axis, [(i, i ^ s) for i in range(n)])  30.5 us
    ppermute x15, starting transfers between devices, exchange(): lax.ppermute(value, axis, [(i, i ^ s) for i in range(n)])  23.5 us
    pallas_call x7, Pallas kernels, call(): pl.pallas_call(body, out_shape=outs, compiler_params=pltpu.CompilerParams...  11.9 us
    pallas_call x1, Pallas kernels, shards(): pl.pallas_call(functools.partial(features_kernel, math.sqrt(2.0 / whole))...  8.73 us
  transfers between devices with their start and end apart: 15, of which 11 were waited for; matrix products, arithmetic and copies ran while one was open for 0% of the time, Pallas kernels for 0%

profile of v2, /device:TPU:0, one launch (start us, length us, event | category | flops | bytes accessed | tf_op | source)
XLA Modules:
  0.0 75.4 jit_solution(16878222217822446311)
XLA Ops:
  0.6 8.7 %shard_map.86 = (bf16[1024,2048]{1,0:T(8,128)(2,1)S(1)}, bf16[1024,2048]{1,0:T(8,128)(2,1)S(1)}, f32[2,2048]{1,0:T(2,128)S(1)}, f32[1,2048]{1,0:T(1,128)S(1)}, f...) custom-call(bf16[1024,128]{1,0:T(8,128)(2,1)} %x_hbm.1, bf16[128,2048]{1,0:T(8,128)(2,1)} %w_hbm.1, f32[1,2048]{1,0:T(1,128)} %bitcast.5, ...), custom_call_target="tpu_custom_call" | custom-call | tf_op jit(solution)/shard_map/pallas_call | solution.py:227
  9.4 5.1 %collective-permute-start.2 = (f32[2,2048]{1,0:T(2,128)S(1)}, f32[2,2048]{1,0:T(2,128)S(1)}, u32[]{:S(2)}, u32[]{:S(2)}) collective-permute-start(f32[2,2048]{1,0:T(2,128)S(1)} %get-tuple-element.32.refs_0_), channel_id=1, source_target_pairs={{0,6},{2,4},{4,2},{6,0},{1,7},{3,5},{5,3},{7,1},{8,14},{10,12},{12... | collective-permute-start | bytes 49160 | tf_op jit(solution)/shard_map/ppermute | solution.py:31
  14.5 0.0 collective-permute-start.1
  14.5 0.6 collective-permute-start
  15.1 1.1 %collective-permute-done.2.refs_3_ = f32[2,2048]{1,0:T(2,128)S(1)} collective-permute-done((f32[2,2048]{1,0:T(2,128)S(1)}, f32[2,2048]{1,0:T(2,128)S(1)}, u32[]{:S(2)}, u32[]{:S(2)}) %collective-permute-start.2) | collective-permute-done | bytes 16416 | tf_op jit(solution)/shard_map/ppermute | solution.py:31
  16.2 2.9 %collective-permute-done.1.refs_2_ = f32[2,2048]{1,0:T(2,128)S(1)} collective-permute-done((f32[2,2048]{1,0:T(2,128)S(1)}, f32[2,2048]{1,0:T(2,128)S(1)}, u32[]{:S(2)}, u32[]{:S(2)}) %collective-permute-start.1) | collective-permute-done | bytes 16416 | tf_op jit(solution)/shard_map/ppermute | solution.py:31
  19.1 0.0 collective-permute-done.refs_1_
  19.1 2.4 %shard_map.87 = (f32[16,1152]{1,0:T(8,128)S(1)}, f32[16,2048]{1,0:T(8,128)S(1)}, f32[16,2048]{1,0:T(8,128)S(1)}, f32[16,2048]{1,0:T(8,128)S(1)}) custom-call(f32[2,2048]{1,0:T(2,128)S(1)} %get-tuple-element.32.refs_0_, f32[2,2048]{1,0:T(2,128)S(1)} %collective-permute-done.refs_1_, f32[2,2048]{1,0:T(2,128)S(1)} %collective-permute-done.1.refs_2_, ...), custom_call_target="tpu_custom_call" | custom-call | bytes 8462400 | tf_op jit(solution)/shard_map/pallas_call | solution.py:21
  21.5 1.5 %collective-permute-start.3 = (f32[16,1152]{1,0:T(8,128)S(1)}, f32[16,1152]{1,0:T(8,128)S(1)}, u32[]{:S(2)}, u32[]{:S(2)}) collective-permute-start(f32[16,1152]{1,0:T(8,128)S(1)} %get-tuple-element.37.refs_0_), channel_id=1, source_target_pairs={{0,1},{1,0},{2,3},{3,2},{4,5},{5,4},{6,7},{7,6},{8,9},{9,8},{10,11... | collective-permute-start | bytes 221192 | tf_op jit(solution)/shard_map/ppermute | solution.py:31
  23.1 2.8 %collective-permute-done.3.refs_1_ = f32[16,1152]{1,0:T(8,128)S(1)} collective-permute-done((f32[16,1152]{1,0:T(8,128)S(1)}, f32[16,1152]{1,0:T(8,128)S(1)}, u32[]{:S(2)}, u32[]{:S(2)}) %collective-permute-start.3) | collective-permute-done | bytes 73760 | tf_op jit(solution)/shard_map/ppermute | solution.py:31
  25.9 1.3 %shard_map.88 = (f32[16,2176]{1,0:T(8,128)S(1)}, f32[16,1024]{1,0:T(8,128)S(1)}, f32[16,128]{1,0:T(8,128)S(1)}) custom-call(f32[16,1152]{1,0:T(8,128)S(1)} %get-tuple-element.37.refs_0_, f32[16,1152]{1,0:T(8,128)S(1)} %collective-permute-done.3.refs_1_, f32[1,1024]{1,0:T(1,128)S(1)} %get-tuple-element.38.refs_2_, ...), custom_call_target="tpu_custom_call" | custom-call | bytes 8540160 | tf_op jit(solution)/shard_map/pallas_call | solution.py:21
  27.2 1.5 %collective-permute-start.6 = (f32[16,2176]{1,0:T(8,128)S(1)}, f32[16,2176]{1,0:T(8,128)S(1)}, u32[]{:S(2)}, u32[]{:S(2)}) collective-permute-start(f32[16,2176]{1,0:T(8,128)S(1)} %get-tuple-element.39.refs_0_), channel_id=1, source_target_pairs={{0,6},{2,4},{4,2},{6,0},{1,7},{3,5},{5,3},{7,1},{8,14},{10,12},{12... | collective-permute-start | bytes 417800 | tf_op jit(solution)/shard_map/ppermute | solution.py:31
  28.7 0.6 collective-permute-start.5
  29.3 2.3 %collective-permute-start.4 = (f32[16,2176]{1,0:T(8,128)S(1)}, f32[16,2176]{1,0:T(8,128)S(1)}, u32[]{:S(2)}, u32[]{:S(2)}) collective-permute-start(f32[16,2176]{1,0:T(8,128)S(1)} %get-tuple-element.39.refs_0_), channel_id=1, source_target_pairs={{0,2},{2,0},{4,6},{6,4},{1,3},{3,1},{5,7},{7,5},{8,10},{10,8},{12,... | collective-permute-start | bytes 417800 | tf_op jit(solution)/shard_map/ppermute | solution.py:31
  31.6 3.4 %collective-permute-done.6.refs_3_ = f32[16,2176]{1,0:T(8,128)S(1)} collective-permute-done((f32[16,2176]{1,0:T(8,128)S(1)}, f32[16,2176]{1,0:T(8,128)S(1)}, u32[]{:S(2)}, u32[]{:S(2)}) %collective-permute-start.6) | collective-permute-done | bytes 139296 | tf_op jit(solution)/shard_map/ppermute | solution.py:31
  35.1 4.3 %collective-permute-done.5.refs_2_ = f32[16,2176]{1,0:T(8,128)S(1)} collective-permute-done((f32[16,2176]{1,0:T(8,128)S(1)}, f32[16,2176]{1,0:T(8,128)S(1)}, u32[]{:S(2)}, u32[]{:S(2)}) %collective-permute-start.5) | collective-permute-done | bytes 139296 | tf_op jit(solution)/shard_map/ppermute | solution.py:31
  39.3 0.0 collective-permute-done.4.refs_1_
  39.3 2.5 %shard_map.89 = (f32[16,1152]{1,0:T(8,128)S(1)}, f32[16,2048]{1,0:T(8,128)S(1)}, f32[16,2048]{1,0:T(8,128)S(1)}, f32[16,2048]{1,0:T(8,128)S(1)}, f32[16,2048]{1,0:T(8,128)S(1)}, /*index=5*/f32[16,128]{1,0:T(8,128)S(1)}) custom-call(f32[16,2176]{1,0:T(8,128)S(1)} %get-tuple-element.39.refs_0_, f32[16,2176]{1,0:T(8,128)S(1)} %collective-permute-done.4.refs_1_, ...), custom_call_target="tpu_custom_call" | custom-call | bytes 9355328 | tf_op jit(solution)/shard_map/pallas_call | solution.py:21
  41.9 1.5 %collective-permute-start.7 = (f32[16,1152]{1,0:T(8,128)S(1)}, f32[16,1152]{1,0:T(8,128)S(1)}, u32[]{:S(2)}, u32[]{:S(2)}) collective-permute-start(f32[16,1152]{1,0:T(8,128)S(1)} %get-tuple-element.44.refs_0_), channel_id=1, source_target_pairs={{0,1},{1,0},{2,3},{3,2},{4,5},{5,4},{6,7},{7,6},{8,9},{9,8},{10,11... | collective-permute-start | bytes 221192 | tf_op jit(solution)/shard_map/ppermute | solution.py:31
  43.4 2.8 %collective-permute-done.7.refs_1_ = f32[16,1152]{1,0:T(8,128)S(1)} collective-permute-done((f32[16,1152]{1,0:T(8,128)S(1)}, f32[16,1152]{1,0:T(8,128)S(1)}, u32[]{:S(2)}, u32[]{:S(2)}) %collective-permute-start.7) | collective-permute-done | bytes 73760 | tf_op jit(solution)/shard_map/ppermute | solution.py:31
  46.2 1.6 %shard_map.90 = (f32[16,2176]{1,0:T(8,128)S(1)}, f32[16,1024]{1,0:T(8,128)S(1)}, f32[16,128]{1,0:T(8,128)S(1)}) custom-call(f32[16,1152]{1,0:T(8,128)S(1)} %get-tuple-element.44.refs_0_, f32[16,1152]{1,0:T(8,128)S(1)} %collective-permute-done.7.refs_1_, f32[1,1024]{1,0:T(1,128)S(1)} %get-tuple-element.38.refs_2_, ...), custom_call_target="tpu_custom_call" | custom-call | bytes 8613888 | tf_op jit(solution)/shard_map/pallas_call | solution.py:21
  47.8 2.5 %collective-permute-start.10 = (f32[16,2176]{1,0:T(8,128)S(1)}, f32[16,2176]{1,0:T(8,128)S(1)}, u32[]{:S(2)}, u32[]{:S(2)}) collective-permute-start(f32[16,2176]{1,0:T(8,128)S(1)} %get-tuple-element.46.refs_0_), channel_id=1, source_target_pairs={{0,6},{2,4},{4,2},{6,0},{1,7},{3,5},{5,3},{7,1},{8,14},{10,12},{12... | collective-permute-start | bytes 417800 | tf_op jit(solution)/shard_map/ppermute | solution.py:31
  50.3 0.0 collective-permute-start.9
  50.3 1.9 %collective-permute-start.8 = (f32[16,2176]{1,0:T(8,128)S(1)}, f32[16,2176]{1,0:T(8,128)S(1)}, u32[]{:S(2)}, u32[]{:S(2)}) collective-permute-start(f32[16,2176]{1,0:T(8,128)S(1)} %get-tuple-element.46.refs_0_), channel_id=1, source_target_pairs={{0,2},{2,0},{4,6},{6,4},{1,3},{3,1},{5,7},{7,5},{8,10},{10,8},{12,... | collective-permute-start | bytes 417800 | tf_op jit(solution)/shard_map/ppermute | solution.py:31
  52.2 3.4 %collective-permute-done.10.refs_3_ = f32[16,2176]{1,0:T(8,128)S(1)} collective-permute-done((f32[16,2176]{1,0:T(8,128)S(1)}, f32[16,2176]{1,0:T(8,128)S(1)}, u32[]{:S(2)}, u32[]{:S(2)}) %collective-permute-start.10) | collective-permute-done | bytes 139296 | tf_op jit(solution)/shard_map/ppermute | solution.py:31
  55.6 4.2 %collective-permute-done.9.refs_2_ = f32[16,2176]{1,0:T(8,128)S(1)} collective-permute-done((f32[16,2176]{1,0:T(8,128)S(1)}, f32[16,2176]{1,0:T(8,128)S(1)}, u32[]{:S(2)}, u32[]{:S(2)}) %collective-permute-start.9) | collective-permute-done | bytes 139296 | tf_op jit(solution)/shard_map/ppermute | solution.py:31
  59.7 0.0 collective-permute-done.8.refs_1_
  59.7 3.0 %shard_map.91 = (f32[16,1152]{1,0:T(8,128)S(1)}, f32[16,2048]{1,0:T(8,128)S(1)}, f32[16,2048]{1,0:T(8,128)S(1)}, f32[16,2048]{1,0:T(8,128)}, f32[16,2048]{1,0:T(8,128)S(1)}, /*index=5*/f32[16,128]{1,0:T(8,128)S(1)}) custom-call(f32[16,2176]{1,0:T(8,128)S(1)} %get-tuple-element.46.refs_0_, f32[16,2176]{1,0:T(8,128)S(1)} %collective-permute-done.8.refs_1_, ...), custom_call_target="tpu_custom_call" | custom-call | bytes 9617472 | tf_op jit(solution)/shard_map/pallas_call | solution.py:21
  62.8 1.5 %collective-permute-start.11 = (f32[16,1152]{1,0:T(8,128)S(1)}, f32[16,1152]{1,0:T(8,128)S(1)}, u32[]{:S(2)}, u32[]{:S(2)}) collective-permute-start(f32[16,1152]{1,0:T(8,128)S(1)} %get-tuple-element.52.refs_0_), channel_id=1, source_target_pairs={{0,1},{1,0},{2,3},{3,2},{4,5},{5,4},{6,7},{7,6},{8,9},{9,8},{10,11... | collective-permute-start | bytes 221192 | tf_op jit(solution)/shard_map/ppermute | solution.py:31
  64.3 2.8 %collective-permute-done.11.refs_1_ = f32[16,1152]{1,0:T(8,128)S(1)} collective-permute-done((f32[16,1152]{1,0:T(8,128)S(1)}, f32[16,1152]{1,0:T(8,128)S(1)}, u32[]{:S(2)}, u32[]{:S(2)}) %collective-permute-start.11) | collective-permute-done | bytes 73760 | tf_op jit(solution)/shard_map/ppermute | solution.py:31
  67.1 0.2 shard_map.92
  67.3 2.7 %collective-permute-start.14 = (f32[16,128]{1,0:T(8,128)S(1)}, f32[16,128]{1,0:T(8,128)S(1)}, u32[]{:S(2)}, u32[]{:S(2)}) collective-permute-start(f32[16,128]{1,0:T(8,128)S(1)} %get-tuple-element.54.refs_0_), channel_id=1, source_target_pairs={{0,6},{2,4},{4,2},{6,0},{1,7},{3,5},{5,3},{7,1},{8,14},{10,12},{12... | collective-permute-start | bytes 24584 | tf_op jit(solution)/shard_map/ppermute | solution.py:31
  70.0 0.0 collective-permute-start.13
  70.0 1.7 %collective-permute-start.12 = (f32[16,128]{1,0:T(8,128)S(1)}, f32[16,128]{1,0:T(8,128)S(1)}, u32[]{:S(2)}, u32[]{:S(2)}) collective-permute-start(f32[16,128]{1,0:T(8,128)S(1)} %get-tuple-element.54.refs_0_), channel_id=1, source_target_pairs={{0,2},{2,0},{4,6},{6,4},{1,3},{3,1},{5,7},{7,5},{8,10},{10,8},{12,... | collective-permute-start | bytes 24584 | tf_op jit(solution)/shard_map/ppermute | solution.py:31
  71.7 1.1 %collective-permute-done.14.refs_3_ = f32[16,128]{1,0:T(8,128)S(1)} collective-permute-done((f32[16,128]{1,0:T(8,128)S(1)}, f32[16,128]{1,0:T(8,128)S(1)}, u32[]{:S(2)}, u32[]{:S(2)}) %collective-permute-start.14) | collective-permute-done | bytes 8224 | tf_op jit(solution)/shard_map/ppermute | solution.py:31
  72.8 1.7 %collective-permute-done.13.refs_2_ = f32[16,128]{1,0:T(8,128)S(1)} collective-permute-done((f32[16,128]{1,0:T(8,128)S(1)}, f32[16,128]{1,0:T(8,128)S(1)}, u32[]{:S(2)}, u32[]{:S(2)}) %collective-permute-start.13) | collective-permute-done | bytes 8224 | tf_op jit(solution)/shard_map/ppermute | solution.py:31
  74.5 0.0 collective-permute-done.12.refs_1_
  74.5 0.8 %shard_map.93 = (f32[16,2048]{1,0:T(8,128)}, f32[16,1024]{1,0:T(8,128)}) custom-call(f32[16,128]{1,0:T(8,128)S(1)} %get-tuple-element.54.refs_0_, f32[16,128]{1,0:T(8,128)S(1)} %collective-permute-done.12.refs_1_, f32[16,128]{1,0:T(8,128)S(1)} %collective-permute-done.13.refs_2_, f32[16,128]{1,0:T(8,128)S(1)} %collective-permute-done.14.refs_3_, ...), custom_call_target="tpu_custom_call" | custom-call | bytes 647232 | tf_op jit(solution)/shard_map/pallas_call | solution.py:21
Async XLA Ops:
  9.4 6.8 %collective-permute-start.2 = (f32[2,2048]{1,0:T(2,128)S(1)}, f32[2,2048]{1,0:T(2,128)S(1)}, u32[]{:S(2)}, u32[]{:S(2)}) collective-permute-start(f32[2,2048]{1,0:T(2,128)S(1)} %get-tuple-element.32.refs_0_), channel_id=1, source_target_pairs={{0,6},{2,4},{4,2},{6,0},{1,7},{3,5},{5,3},{7,1},{8,14},{10,12},{12... | collective-permute-start | bytes 49160 | tf_op jit(solution)/shard_map/ppermute | solution.py:31
  14.5 4.6 %collective-permute-start.1 = (f32[2,2048]{1,0:T(2,128)S(1)}, f32[2,2048]{1,0:T(2,128)S(1)}, u32[]{:S(2)}, u32[]{:S(2)}) collective-permute-start(f32[2,2048]{1,0:T(2,128)S(1)} %get-tuple-element.32.refs_0_), channel_id=1, source_target_pairs={{0,4},{2,6},{4,0},{6,2},{1,5},{3,7},{5,1},{7,3},{8,12},{10,14},{12... | collective-permute-start | bytes 49160 | tf_op jit(solution)/shard_map/ppermute | solution.py:31
  14.5 4.6 %collective-permute-start = (f32[2,2048]{1,0:T(2,128)S(1)}, f32[2,2048]{1,0:T(2,128)S(1)}, u32[]{:S(2)}, u32[]{:S(2)}) collective-permute-start(f32[2,2048]{1,0:T(2,128)S(1)} %get-tuple-element.32.refs_0_), channel_id=1, source_target_pairs={{0,2},{2,0},{4,6},{6,4},{1,3},{3,1},{5,7},{7,5},{8,10},{10,8},{12,... | collective-permute-start | bytes 49160 | tf_op jit(solution)/shard_map/ppermute | solution.py:31
  21.5 4.4 %collective-permute-start.3 = (f32[16,1152]{1,0:T(8,128)S(1)}, f32[16,1152]{1,0:T(8,128)S(1)}, u32[]{:S(2)}, u32[]{:S(2)}) collective-permute-start(f32[16,1152]{1,0:T(8,128)S(1)} %get-tuple-element.37.refs_0_), channel_id=1, source_target_pairs={{0,1},{1,0},{2,3},{3,2},{4,5},{5,4},{6,7},{7,6},{8,9},{9,8},{10,11... | collective-permute-start | bytes 221192 | tf_op jit(solution)/shard_map/ppermute | solution.py:31
  27.2 7.8 %collective-permute-start.6 = (f32[16,2176]{1,0:T(8,128)S(1)}, f32[16,2176]{1,0:T(8,128)S(1)}, u32[]{:S(2)}, u32[]{:S(2)}) collective-permute-start(f32[16,2176]{1,0:T(8,128)S(1)} %get-tuple-element.39.refs_0_), channel_id=1, source_target_pairs={{0,6},{2,4},{4,2},{6,0},{1,7},{3,5},{5,3},{7,1},{8,14},{10,12},{12... | collective-permute-start | bytes 417800 | tf_op jit(solution)/shard_map/ppermute | solution.py:31
  28.7 10.6 %collective-permute-start.5 = (f32[16,2176]{1,0:T(8,128)S(1)}, f32[16,2176]{1,0:T(8,128)S(1)}, u32[]{:S(2)}, u32[]{:S(2)}) collective-permute-start(f32[16,2176]{1,0:T(8,128)S(1)} %get-tuple-element.39.refs_0_), channel_id=1, source_target_pairs={{0,4},{2,6},{4,0},{6,2},{1,5},{3,7},{5,1},{7,3},{8,12},{10,14},{12... | collective-permute-start | bytes 417800 | tf_op jit(solution)/shard_map/ppermute | solution.py:31
  29.3 10.0 %collective-permute-start.4 = (f32[16,2176]{1,0:T(8,128)S(1)}, f32[16,2176]{1,0:T(8,128)S(1)}, u32[]{:S(2)}, u32[]{:S(2)}) collective-permute-start(f32[16,2176]{1,0:T(8,128)S(1)} %get-tuple-element.39.refs_0_), channel_id=1, source_target_pairs={{0,2},{2,0},{4,6},{6,4},{1,3},{3,1},{5,7},{7,5},{8,10},{10,8},{12,... | collective-permute-start | bytes 417800 | tf_op jit(solution)/shard_map/ppermute | solution.py:31
  41.9 4.4 %collective-permute-start.7 = (f32[16,1152]{1,0:T(8,128)S(1)}, f32[16,1152]{1,0:T(8,128)S(1)}, u32[]{:S(2)}, u32[]{:S(2)}) collective-permute-start(f32[16,1152]{1,0:T(8,128)S(1)} %get-tuple-element.44.refs_0_), channel_id=1, source_target_pairs={{0,1},{1,0},{2,3},{3,2},{4,5},{5,4},{6,7},{7,6},{8,9},{9,8},{10,11... | collective-permute-start | bytes 221192 | tf_op jit(solution)/shard_map/ppermute | solution.py:31
  47.8 7.8 %collective-permute-start.10 = (f32[16,2176]{1,0:T(8,128)S(1)}, f32[16,2176]{1,0:T(8,128)S(1)}, u32[]{:S(2)}, u32[]{:S(2)}) collective-permute-start(f32[16,2176]{1,0:T(8,128)S(1)} %get-tuple-element.46.refs_0_), channel_id=1, source_target_pairs={{0,6},{2,4},{4,2},{6,0},{1,7},{3,5},{5,3},{7,1},{8,14},{10,12},{12... | collective-permute-start | bytes 417800 | tf_op jit(solution)/shard_map/ppermute | solution.py:31
  50.3 9.4 %collective-permute-start.9 = (f32[16,2176]{1,0:T(8,128)S(1)}, f32[16,2176]{1,0:T(8,128)S(1)}, u32[]{:S(2)}, u32[]{:S(2)}) collective-permute-start(f32[16,2176]{1,0:T(8,128)S(1)} %get-tuple-element.46.refs_0_), channel_id=1, source_target_pairs={{0,4},{2,6},{4,0},{6,2},{1,5},{3,7},{5,1},{7,3},{8,12},{10,14},{12... | collective-permute-start | bytes 417800 | tf_op jit(solution)/shard_map/ppermute | solution.py:31
  50.3 9.4 %collective-permute-start.8 = (f32[16,2176]{1,0:T(8,128)S(1)}, f32[16,2176]{1,0:T(8,128)S(1)}, u32[]{:S(2)}, u32[]{:S(2)}) collective-permute-start(f32[16,2176]{1,0:T(8,128)S(1)} %get-tuple-element.46.refs_0_), channel_id=1, source_target_pairs={{0,2},{2,0},{4,6},{6,4},{1,3},{3,1},{5,7},{7,5},{8,10},{10,8},{12,... | collective-permute-start | bytes 417800 | tf_op jit(solution)/shard_map/ppermute | solution.py:31
  62.8 4.4 %collective-permute-start.11 = (f32[16,1152]{1,0:T(8,128)S(1)}, f32[16,1152]{1,0:T(8,128)S(1)}, u32[]{:S(2)}, u32[]{:S(2)}) collective-permute-start(f32[16,1152]{1,0:T(8,128)S(1)} %get-tuple-element.52.refs_0_), channel_id=1, source_target_pairs={{0,1},{1,0},{2,3},{3,2},{4,5},{5,4},{6,7},{7,6},{8,9},{9,8},{10,11... | collective-permute-start | bytes 221192 | tf_op jit(solution)/shard_map/ppermute | solution.py:31
  67.3 5.5 %collective-permute-start.14 = (f32[16,128]{1,0:T(8,128)S(1)}, f32[16,128]{1,0:T(8,128)S(1)}, u32[]{:S(2)}, u32[]{:S(2)}) collective-permute-start(f32[16,128]{1,0:T(8,128)S(1)} %get-tuple-element.54.refs_0_), channel_id=1, source_target_pairs={{0,6},{2,4},{4,2},{6,0},{1,7},{3,5},{5,3},{7,1},{8,14},{10,12},{12... | collective-permute-start | bytes 24584 | tf_op jit(solution)/shard_map/ppermute | solution.py:31
  70.0 4.5 %collective-permute-start.13 = (f32[16,128]{1,0:T(8,128)S(1)}, f32[16,128]{1,0:T(8,128)S(1)}, u32[]{:S(2)}, u32[]{:S(2)}) collective-permute-start(f32[16,128]{1,0:T(8,128)S(1)} %get-tuple-element.54.refs_0_), channel_id=1, source_target_pairs={{0,4},{2,6},{4,0},{6,2},{1,5},{3,7},{5,1},{7,3},{8,12},{10,14},{12... | collective-permute-start | bytes 24584 | tf_op jit(solution)/shard_map/ppermute | solution.py:31
  70.0 4.5 %collective-permute-start.12 = (f32[16,128]{1,0:T(8,128)S(1)}, f32[16,128]{1,0:T(8,128)S(1)}, u32[]{:S(2)}, u32[]{:S(2)}) collective-permute-start(f32[16,128]{1,0:T(8,128)S(1)} %get-tuple-element.54.refs_0_), channel_id=1, source_target_pairs={{0,2},{2,0},{4,6},{6,4},{1,3},{3,1},{5,7},{7,5},{8,10},{10,8},{12,... | collective-permute-start | bytes 24584 | tf_op jit(solution)/shard_map/ppermute | solution.py:31

commit v3 on v1

v3 whole, which is shorter than its diff:
```python
import functools
import math

import jax
import jax.numpy as jnp
from jax import lax
from jax.experimental import pallas as pl
from jax.experimental.pallas import tpu as pltpu
from jax.sharding import PartitionSpec as P

f32, bf16 = jnp.float32, jnp.bfloat16
TURN = 1.0 / (2.0 * math.pi)
COSINE = (0.999999211770312, -19.738980419471126, 64.92865850463285, -85.27162830146948, 58.79050662870376, -21.071108461771125)
LANES = 128
VMEM_LIMIT = 12 * 2**20


def call(body, outs, *args, flops=0, held=True, scratch=()):
    outs = [pltpu.VMEM(s, d) if held else jax.ShapeDtypeStruct(s, d) for s, d in outs]
    size = sum(math.prod(a.shape) * a.dtype.itemsize for a in args)
    return pl.pallas_call(
        body,
        out_shape=outs,
        scratch_shapes=list(scratch),
        compiler_params=pltpu.CompilerParams(vmem_limit_bytes=VMEM_LIMIT),
        cost_estimate=pl.CostEstimate(flops=flops, bytes_accessed=size, transcendentals=0),
    )(*args)


def total(refs):
    values = [r[...] for r in refs]
    while len(values) > 1:
        values = [values[i] + values[i + 1] for i in range(0, len(values), 2)]
    return values[0]


def halves(value):
    high = value.astype(bf16)
    return high, (value - high.astype(f32)).astype(bf16)


def product(rows, high_ref, low_ref):
    high, low = halves(rows)
    n = rows.shape[0]
    both = jnp.concatenate([high.astype(f32), low.astype(f32)], axis=0).astype(bf16)
    a = jnp.dot(both, high_ref[...], preferred_element_type=f32)
    b = jnp.dot(high, low_ref[...], preferred_element_type=f32)
    return a[:n] + a[n:] + b


def pack_scalars(columns, rows):
    lane = lax.broadcasted_iota(jnp.int32, (rows, LANES), 1)
    out = jnp.zeros((rows, LANES), f32)
    for i, column in enumerate(columns):
        out = jnp.where(lane == i, column, out)
    return out


def row_sum(value):
    return jnp.sum(value, axis=1, keepdims=True)


def flip(value, axis, n, s):
    return lax.ppermute(value, axis, [(i, i ^ s) for i in range(n)])


def exchange(value, axis, n):
    return [value] + [flip(value, axis, n, s) for s in range(1, n)]


def as_row(block):
    return jnp.concatenate([block[i : i + 1] for i in range(block.shape[0])], axis=1)


def spread(pair, rows):
    return jnp.concatenate(
        [jnp.broadcast_to(pair[e : e + 1], (rows // 2, pair.shape[1])) for e in (0, 1)], axis=0
    )


def core():
    return lax.rem(lax.axis_index("fold"), 2)


def pack_kernel(
    scale, nz, x_hbm, w_hbm, offset_hbm, mag_hbm, response_hbm, label_hbm, penalty_hbm, other_label,
    msg, w_ref, offset_ref, mag_ref, penalty_ref,
    points, offset_in, mag_in, response_ref, label_ref, penalty_in, sems,
):
    half = points.shape[0]
    c = core()
    pairs = [
        (x_hbm.at[pl.ds(pl.multiple_of(c * half, half), half), :], points),
        (label_hbm, label_ref), (response_hbm, response_ref), (w_hbm, w_ref),
        (offset_hbm, offset_in), (mag_hbm, mag_in), (penalty_hbm, penalty_in),
    ]
    copies = [pltpu.make_async_copy(a, b, sems.at[i]) for i, (a, b) in enumerate(pairs)]
    for copy in copies:
        copy.start()
    for copy in copies[1:3]:
        copy.wait()
    n = half // LANES

    def mine(block):
        return jnp.where(c == 0, block[:n], block[n:])

    own = (mine(label_ref[...]) != 0).astype(f32)
    other = (mine(other_label[...]) != 0).astype(f32)
    y = mine(response_ref[...])
    high, middle = halves(y)
    y = y - high.astype(f32)
    middle, low = halves(y)
    aux = [jnp.where(c == 0, own, other), jnp.where(c == 0, other, own)]
    aux += [v.astype(f32) for v in (high, middle, low)]
    aux += [jnp.zeros((msg.shape[0] - half - 5 * n, LANES), f32)]
    msg[half:, :] = jnp.concatenate(aux, axis=0).astype(bf16)
    copies[0].wait()
    msg[:half, :] = points[...]
    for copy in copies[3:]:
        copy.wait()
    offset_ref[...] = offset_in[...] * TURN
    mag_ref[...] = mag_in[...] * scale
    levels, rows = penalty_in.shape[1], penalty_ref.shape[0]
    row, column = [lax.broadcasted_iota(jnp.int32, (rows, levels), a) for a in (0, 1)]
    chosen = column == lax.axis_index("samp") * (rows // 2) + lax.rem(row, rows // 2)
    penalty_ref[...] = row_sum(jnp.where(chosen, penalty_in[...], 0.0))


def features_kernel(first, msg, w_ref, offset_ref, *refs):
    before, refs = (None, refs) if first else (refs[0], refs[1:])
    high_ref, low_ref, high_t, low_t, kept_ref, moment_ref, acc = refs
    samples, features = high_ref.shape
    n = samples // LANES
    aux = msg[samples:, :].astype(f32)
    kept = jnp.concatenate([as_row(aux[e * n : (e + 1) * n]) for e in (0, 1)], axis=0)
    kept_ref[...] = spread(kept, kept_ref.shape[0])
    y = (aux[2 * n : 3 * n] + aux[3 * n : 4 * n]) + aux[4 * n : 5 * n]
    y_high, y_low = halves(kept * as_row(y))
    y_both = jnp.concatenate([y_high.astype(f32), y_low.astype(f32)], axis=0).astype(bf16)
    columns = jnp.concatenate([kept, jnp.zeros((6, samples), f32)], axis=0).T
    cb = min(features, 256)
    for j in range(0, features, cb):
        a = jnp.dot(msg[:samples, :], w_ref[:, j : j + cb], preferred_element_type=f32)
        t = a * TURN + offset_ref[:, j : j + cb]
        r = t - jnp.round(t)
        u = r * r
        c = jnp.full_like(u, COSINE[-1])
        for q in COSINE[-2::-1]:
            c = c * u + q
        high, low = halves(c)
        high_ref[:, j : j + cb] = high
        low_ref[:, j : j + cb] = low
        high_t[j : j + cb, :] = high.T
        low_t[j : j + cb, :] = low.T
        square = c * c
        for e in (0, 1):
            part = square * columns[:, e : e + 1]
            acc[e, :, j : j + cb] = part.reshape(samples // 8, 8, cb).sum(0)
        side = jnp.dot(y_both, high, preferred_element_type=f32)
        side = side[:2] + side[2:] + jnp.dot(y_high, low, preferred_element_type=f32)
        moment_ref[2:4, j : j + cb] = side if first else before[2:4, j : j + cb] + side
    for e in (0, 1):
        square = jnp.sum(acc[e], axis=0, keepdims=True)
        moment_ref[e : e + 1, :] = square if first else before[e : e + 1, :] + square


def send_forward(s, m, blocks, msg, scalars):
    v = s * m
    at = 0
    for high, low in zip(blocks[::2], blocks[1::2]):
        n = high.shape[1]
        msg[:, at : at + n] = product(v, high, low)
        at += n
    msg[:, at:] = pack_scalars(scalars, s.shape[0])


def begin_kernel(nz, *refs):
    moments, penalty, mag, blocks = refs[:2], refs[2], refs[3], refs[4 : 4 + 2 * nz]
    msg, direction, precond, residual = refs[4 + 2 * nz :]
    sums = total(moments)
    m = mag[...]
    rows = penalty.shape[0]
    pre = spread(sums[0:2] * (m * m), rows) + penalty[...]
    res = spread(sums[2:4] * m, rows)
    s = res / pre
    precond[...] = pre
    residual[...] = res
    direction[...] = s
    send_forward(s, m, blocks, msg, [row_sum(res * s), row_sum(s * s)])


def adjoint_kernel(ny, nz, first, *refs):
    parts, refs = refs[:ny], refs[ny:]
    kepts, blocks, refs = refs[:nz], refs[nz : 3 * nz], refs[3 * nz :]
    sums = total(parts)
    half = kepts[0].shape[1]
    samples = half * nz
    image_rows, sc = sums[:, :samples], sums[:, samples:]
    rz, dd = sc[:, 0:1], sc[:, 1:2]
    beta = jnp.zeros_like(rz)
    if not first:
        before, before_sc, refs = refs[0], refs[1], refs[2:]
        beta = rz / before_sc[:, 0:1]
        image_rows = image_rows + beta * before[...]
        dd = dd + 2.0 * beta * sc[:, 2:3] + beta * beta * before_sc[:, 1:2]
    msg, rows_out, sc_out = refs
    squares = jnp.zeros_like(dd)
    adjoint = 0.0
    for j, (kept, high, low) in enumerate(zip(kepts, blocks[::2], blocks[1::2])):
        rows = image_rows[:, j * half : (j + 1) * half]
        weighted = rows * kept[...]
        squares = squares + row_sum(weighted * rows)
        adjoint = adjoint + product(weighted, high, low)
    msg[:, : adjoint.shape[1]] = adjoint
    msg[:, adjoint.shape[1] :] = pack_scalars([squares], dd.shape[0])
    rows_out[...] = image_rows
    sc_out[...] = pack_scalars([rz, dd, beta], dd.shape[0])


def update_kernel(nz, first, *refs):
    parts, refs = refs[:2], refs[2:]
    sc, penalty, mag, precond, residual, scaled, rows, refs = *refs[:7], refs[7:]
    blocks, refs = refs[: 2 * nz], refs[2 * nz :]
    sums = total(parts)
    features = mag.shape[1]
    lam, m = penalty[...], mag[...]
    direction = scaled[...]
    if first:
        msg, scaled_out, direction_out, residual_out, weights_out, predicted_out = refs
    else:
        before, weights, predicted = refs[:3]
        msg, scaled_out, direction_out, residual_out, weights_out, predicted_out = refs[3:]
        direction = direction + sc[:, 2:3] * before[...]
    image = sums[:, :features] * m + lam * direction
    step = sc[:, 0:1] / (sums[:, features : features + 1] + lam * sc[:, 1:2])
    moved, fitted = step * direction, step * rows[...]
    weights_out[...] = moved if first else weights[...] + moved
    predicted_out[...] = fitted if first else predicted[...] + fitted
    res = residual[...] - step * image
    s = res / precond[...]
    residual_out[...] = res
    scaled_out[...] = s
    direction_out[...] = direction
    send_forward(s, m, blocks, msg, [row_sum(res * s), row_sum(s * s), row_sum(s * direction)])


def fold_rows(value, fold):
    n = value.shape[0] // 2
    return jnp.where(fold == 0, value[:n], value[n:])


def last_kernel(ny, nz, *refs):
    parts, refs = refs[:ny], refs[ny:]
    kepts, (before, before_sc, predicted, msg, rows_out, sc_out) = refs[:nz], refs[nz:]
    sums = total(parts)
    half = kepts[0].shape[1]
    samples = half * nz
    sc = sums[:, samples:]
    rz = sc[:, 0:1]
    beta = rz / before_sc[:, 0:1]
    image_rows = sums[:, :samples] + beta * before[...]
    dd = sc[:, 1:2] + 2.0 * beta * sc[:, 2:3] + beta * beta * before_sc[:, 1:2]
    squares = jnp.zeros_like(dd)
    for j, kept in enumerate(kepts):
        rows = image_rows[:, j * half : (j + 1) * half]
        squares = squares + row_sum(rows * rows * kept[...])
    other = 1 - core()
    n = dd.shape[0] // 2
    msg[:n, :samples] = fold_rows(image_rows, other)
    msg[n:, :samples] = fold_rows(predicted[...], other)
    msg[:, samples:] = pack_scalars([squares], 2 * n)
    rows_out[...] = image_rows
    sc_out[...] = pack_scalars([rz, dd, beta], 2 * n)


def finish_kernel(nz, own, got, sc, penalty, scaled, before, weights, rows, predicted, *outs):
    samples, features = rows.shape[1], scaled.shape[1]
    half = samples // nz
    c = core()
    n = sc.shape[0] // 2
    step = sc[:, 0:1] / ((own[:, samples : samples + 1] + got[:, samples : samples + 1]) + penalty[...] * sc[:, 1:2])
    coefficients = weights[...] + step * (scaled[...] + sc[:, 2:3] * before[...])
    coefficients = fold_rows(coefficients, c)
    here = fold_rows(predicted[...] + step * rows[...], c)
    there = got[n:, :samples] + fold_rows(step, c) * got[:n, :samples]
    lower, upper = jnp.where(c == 0, here, there), jnp.where(c == 0, there, here)
    for j, out in enumerate(outs):
        out[:, :features] = coefficients
        out[:, features : features + half] = lower[:, j * half : (j + 1) * half]
        out[:, features + half :] = upper[:, j * half : (j + 1) * half]


def arrange_kernel(nz, *refs):
    parts, (weights_out, predictions_out, held) = refs[:nz], refs[nz:]
    features = weights_out.shape[1]
    n = weights_out.shape[0] // nz
    for j, part in enumerate(parts):
        held[j] = part[...]
    z = lax.axis_index("samp")
    for k in range(nz):
        part = held[lax.bitwise_xor(z, k)]
        weights_out[k * n : (k + 1) * n, :] = part[:, :features]
        predictions_out[k * n : (k + 1) * n, :] = part[:, features:]


ITERS = 3


def shards(
    nf,
    nz,
    ny,
    input_points,
    wave_numbers,
    offset_angles,
    feature_magnitudes,
    response_values,
    split_label,
    shrinkage_levels,
):
    shard, features = input_points.shape[0], wave_numbers.shape[1]
    depth = input_points.shape[1]
    levels = shrinkage_levels.shape[0]
    half, rows = shard // 2, 2 * (levels // nz)
    samples = half * nz
    tall = (shard // LANES, LANES)
    extra = pl.cdiv(5 * half // LANES, 16) * 16
    row_f, row_s, row_c = ((rows, features), f32), ((rows, samples), f32), ((rows, LANES), f32)
    msg_f, msg_s = ((rows, features + LANES), f32), ((rows, samples + LANES), f32)

    label = split_label.reshape(tall)
    other_label = flip(label, "fold", nf, 1)
    inputs = [input_points, wave_numbers, offset_angles.reshape(1, features), feature_magnitudes.reshape(1, features)]
    inputs += [response_values.reshape(tall), label, shrinkage_levels.reshape(1, levels)]
    vectors = [((1, features), f32), ((1, features), f32), (tall, f32), (tall, jnp.int32), ((1, levels), f32)]
    msg, waves, offsets, mag, penalty = pl.pallas_call(
        functools.partial(pack_kernel, math.sqrt(2.0 / (features * ny)), nz),
        out_shape=[
            pltpu.VMEM((half + extra, depth), bf16),
            pltpu.VMEM((depth, features), bf16),
            pltpu.VMEM((1, features), f32),
            pltpu.VMEM((1, features), f32),
            pltpu.VMEM((rows, 1), f32),
        ],
        in_specs=[pl.BlockSpec(memory_space=pltpu.HBM)] * len(inputs) + [pl.BlockSpec(memory_space=pltpu.VMEM)],
        scratch_shapes=[pltpu.VMEM((half, depth), bf16)]
        + [pltpu.VMEM(v, d) for v, d in vectors]
        + [pltpu.SemaphoreType.DMA((len(inputs),))],
        compiler_params=pltpu.CompilerParams(vmem_limit_bytes=VMEM_LIMIT),
    )(*[pltpu.with_memory_space_constraint(v, pltpu.HBM) for v in inputs], other_label)

    blocks, turned, kepts, moments = [], [], [], None
    tile, tile_t = ((half, features), bf16), ((features, half), bf16)
    for j, part in enumerate(exchange(msg, "samp", nz)):
        high, low, high_t, low_t, kept, moments = call(
            functools.partial(features_kernel, j == 0),
            [tile, tile, tile_t, tile_t, ((rows, half), f32), ((4, features), f32)],
            part, waves, offsets, *(() if j == 0 else (moments,)),
            scratch=[pltpu.VMEM((2, 8, features), f32)],
            flops=60 * half * features,
        )
        blocks += [high, low]
        turned += [high_t, low_t]
        kepts.append(kept)
    msg, scaled, precond, residual = call(
        functools.partial(begin_kernel, nz),
        [msg_s, row_f, row_f, row_f],
        moments, flip(moments, "fold", nf, 1), penalty, mag, *turned,
    )
    before = weights = predicted = image_rows = sc = None
    for it in range(ITERS - 1):
        first = it == 0
        msg, image_rows, sc = call(
            functools.partial(adjoint_kernel, ny, nz, first),
            [msg_f, row_s, row_c],
            *exchange(msg, "feat", ny), *kepts, *blocks, *(() if first else (image_rows, sc)),
        )
        msg, scaled, before, residual, weights, predicted = call(
            functools.partial(update_kernel, nz, first),
            [msg_s, row_f, row_f, row_f, row_f, row_s],
            msg, flip(msg, "fold", nf, 1), sc, penalty, mag, precond, residual, scaled, image_rows, *turned,
            *(() if first else (before, weights, predicted)),
        )
    msg, image_rows, sc = call(
        functools.partial(last_kernel, ny, nz),
        [msg_s, row_s, row_c],
        *exchange(msg, "feat", ny), *kepts, image_rows, sc, predicted,
    )
    outs = call(
        functools.partial(finish_kernel, nz),
        [((rows // 2, features + shard), f32)] * nz,
        msg, flip(msg, "fold", nf, 1), sc, penalty, scaled, before, weights, image_rows, predicted,
    )
    outs = [outs[0]] + [flip(out, "samp", nz, j) for j, out in enumerate(outs) if j]
    return call(
        functools.partial(arrange_kernel, nz),
        [((levels, features), f32), ((levels, shard), f32)],
        *outs,
        scratch=[pltpu.VMEM((nz, rows // 2, features + shard), f32)],
        held=False,
    )


def solution(mesh):
    placed = (
        P("samp", None),
        P(None, "feat"),
        P("feat"),
        P("feat"),
        P("samp"),
        P(("fold", "samp")),
        P(),
    )
    sizes = [mesh.shape[axis] for axis in ("fold", "samp", "feat")]
    return jax.shard_map(
        functools.partial(shards, *sizes),
        mesh=mesh,
        in_specs=placed,
        out_specs=(P("fold", "feat"), P("fold", "samp")),
        check_vma=False,
    )
```

time: 86.6 us -> 69.2 us (0.80)
  local copies, waits for them, and re-layouts: 13.1 us -> 0 us
  Pallas kernels: 19.1 us -> 31.9 us
  starting transfers between devices: 23.4 us -> 15.2 us
  waiting for transfers between devices: 29.2 us -> 21.3 us
    pallas_call x8 -> x13, Pallas kernels: 19.1 us -> 31.9 us  [the longest x12 30.6 us: call(): pl.pallas_call(body, out_shape=outs, scratch_shapes=list(scratch), compil...]
    unnamed x22 -> x0, local copies, waits for them, and re-layouts: 12.4 us -> none
    ppermute x15 -> x14, starting transfers between devices: 23.4 us -> 15.2 us  [flip(): return lax.ppermute(value, axis, [(i, i ^ s) for i in range(n)])]
    ppermute x15 -> x14, waiting for transfers between devices: 29.2 us -> 21.3 us  [flip(): return lax.ppermute(value, axis, [(i, i ^ s) for i in range(n)])]
  transfers between devices with their start and end apart: 15 -> 14, of which waited for: 10 -> 12; matrix products, arithmetic and copies ran while one was open for 2% -> 0% of each run, Pallas kernels for 0% -> 18%
where the time goes in v3:
time: 69.2 us; the launch traced here: 69.1 us
  Pallas kernels  31.9 us (46%)
  waiting for transfers between devices  21.3 us (31%)
  starting transfers between devices  15.2 us (22%)
  between operations  0.7 us (1%)
    pallas_call x12, Pallas kernels, call(): pl.pallas_call(body, out_shape=outs, scratch_shapes=list(scratch), compil...  30.6 us
    ppermute x14, waiting for transfers between devices, flip(): return lax.ppermute(value, axis, [(i, i ^ s) for i in range(n)])  21.3 us
    ppermute x14, starting transfers between devices, flip(): return lax.ppermute(value, axis, [(i, i ^ s) for i in range(n)])  15.2 us
  transfers between devices with their start and end apart: 14, of which 12 were waited for; matrix products, arithmetic and copies ran while one was open for 0% of the time, Pallas kernels for 18%

profile of v3, /device:TPU:0, one launch (start us, length us, event | category | flops | bytes accessed | tf_op | source)
XLA Modules:
  0.0 69.1 jit_solution(2045223519827508268)
XLA Ops:
  0.6 0.5 collective-permute-start
  1.1 1.0 %collective-permute-done.other_label = s32[8,128]{1,0:T(8,128)S(1)} collective-permute-done((s32[8,128]{1,0:T(8,128)}, s32[8,128]{1,0:T(8,128)S(1)}, u32[]{:S(2)}, u32[]{:S(2)}) %collective-permute-start) | collective-permute-done | bytes 4128 | tf_op jit(solution)/shard_map/ppermute | solution.py:64
  2.2 1.3 %shard_map.86 = (bf16[544,128]{1,0:T(8,128)(2,1)S(1)}, bf16[128,2048]{1,0:T(8,128)(2,1)S(1)}, f32[1,2048]{1,0:T(1,128)S(1)}, f32[1,2048]{1,0:T(1,128)S(1)}, f32[8,1]{1,0:T(8,128)S(1)}) custom-call(bf16[1024,128]{1,0:T(8,128)(2,1)} %x_hbm.1, bf16[128,2048]{1,0:T(8,128)(2,1)} %w_hbm.1, f32[1,2048]{1,0:T(1,128)} %bitcast.5, f32[1,2048]{1,0:T(1,128)} %bitcast.6, ...), custom_call_target="tpu_custom_call" | custom-call | tf_op jit(solution)/shard_map/pallas_call | solution.py:336
  3.5 3.0 %collective-permute-start.3 = (bf16[544,128]{1,0:T(8,128)(2,1)S(1)}, bf16[544,128]{1,0:T(8,128)(2,1)S(1)}, u32[]{:S(2)}, u32[]{:S(2)}) collective-permute-start(bf16[544,128]{1,0:T(8,128)(2,1)S(1)} %get-tuple-element.59.msg), channel_id=1, source_target_pairs={{0,2},{2,0},{4,6},{6,4},{1,3},{3,1},{5,7},{7,5},{8,10},{10,8},{12,... | collective-permute-start | bytes 417800 | tf_op jit(solution)/shard_map/ppermute | solution.py:64
  6.5 2.6 %collective-permute-start.2 = (bf16[544,128]{1,0:T(8,128)(2,1)S(1)}, bf16[544,128]{1,0:T(8,128)(2,1)S(1)}, u32[]{:S(2)}, u32[]{:S(2)}) collective-permute-start(bf16[544,128]{1,0:T(8,128)(2,1)S(1)} %get-tuple-element.59.msg), channel_id=1, source_target_pairs={{0,4},{2,6},{4,0},{6,2},{1,5},{3,7},{5,1},{7,3},{8,12},{10,14},{12... | collective-permute-start | bytes 417800 | tf_op jit(solution)/shard_map/ppermute | solution.py:64
  9.1 0.0 collective-permute-start.1
  9.1 4.2 %shard_map.87 = (bf16[512,2048]{1,0:T(8,128)(2,1)S(1)}, bf16[512,2048]{1,0:T(8,128)(2,1)S(1)}, bf16[2048,512]{1,0:T(8,128)(2,1)S(1)}, bf16[2048,512]{1,0:T(8,128...) custom-call(bf16[544,128]{1,0:T(8,128)(2,1)S(1)} %get-tuple-element.59.msg, ...), custom_call_target="tpu_custom_call" | custom-call | flops 62914560 | bytes 671744 | tf_op jit(solution)/shard_map/pallas_call | solution.py:21
  13.3 0.0 collective-permute-done.3.msg
  13.3 4.2 %shard_map.88 = (bf16[512,2048]{1,0:T(8,128)(2,1)S(1)}, bf16[512,2048]{1,0:T(8,128)(2,1)S(1)}, bf16[2048,512]{1,0:T(8,128)(2,1)S(1)}, bf16[2048,512]{1,0:T(8,128...) custom-call(bf16[544,128]{1,0:T(8,128)(2,1)S(1)} %collective-permute-done.3.msg, ...), custom_call_target="tpu_custom_call" | custom-call | flops 62914560 | bytes 704512 | tf_op jit(solution)/shard_map/pallas_call | solution.py:21
  17.5 2.4 %collective-permute-done.2.msg = bf16[544,128]{1,0:T(8,128)(2,1)S(1)} collective-permute-done((bf16[544,128]{1,0:T(8,128)(2,1)S(1)}, bf16[544,128]{1,0:T(8,128)(2,1)S(1)}, u32[]{:S(2)}, u32[]{:S(2)}) %collective-permute-start.2) | collective-permute-done | bytes 139296 | tf_op jit(solution)/shard_map/ppermute | solution.py:64
  19.9 4.4 %shard_map.89 = (bf16[512,2048]{1,0:T(8,128)(2,1)S(1)}, bf16[512,2048]{1,0:T(8,128)(2,1)S(1)}, bf16[2048,512]{1,0:T(8,128)(2,1)S(1)}, bf16[2048,512]{1,0:T(8,128...) custom-call(bf16[544,128]{1,0:T(8,128)(2,1)S(1)} %collective-permute-done.2.msg, ...), custom_call_target="tpu_custom_call" | custom-call | flops 62914560 | bytes 704512 | tf_op jit(solution)/shard_map/pallas_call | solution.py:21
  24.3 0.0 collective-permute-done.1.msg
  24.3 4.2 %shard_map.90 = (bf16[512,2048]{1,0:T(8,128)(2,1)S(1)}, bf16[512,2048]{1,0:T(8,128)(2,1)S(1)}, bf16[2048,512]{1,0:T(8,128)(2,1)S(1)}, bf16[2048,512]{1,0:T(8,128...) custom-call(bf16[544,128]{1,0:T(8,128)(2,1)S(1)} %collective-permute-done.1.msg, ...), custom_call_target="tpu_custom_call" | custom-call | flops 62914560 | bytes 704512 | tf_op jit(solution)/shard_map/pallas_call | solution.py:21
  28.5 0.0 collective-permute-start.4
  28.5 1.2 %collective-permute-done.4.refs_1_ = f32[4,2048]{1,0:T(4,128)S(1)} collective-permute-done((f32[4,2048]{1,0:T(4,128)S(1)}, f32[4,2048]{1,0:T(4,128)S(1)}, u32[]{:S(2)}, u32[]{:S(2)}) %collective-permute-start.4) | collective-permute-done | bytes 32800 | tf_op jit(solution)/shard_map/ppermute | solution.py:64
  29.7 2.3 %shard_map.91 = (f32[8,2176]{1,0:T(8,128)S(1)}, f32[8,2048]{1,0:T(8,128)S(1)}, f32[8,2048]{1,0:T(8,128)S(1)}, f32[8,2048]{1,0:T(8,128)S(1)}) custom-call(f32[4,2048]{1,0:T(4,128)S(1)} %get-tuple-element.65.refs_0_, f32[4,2048]{1,0:T(4,128)S(1)} %collective-permute-done.4.refs_1_, f32[8,1]{1,0:T(8,128)S(1)} %get-tuple-element.66.refs_2_.refs_3_.penalty, ...), custom_call_target="tpu_custom_call" | custom-call | bytes 16850976 | tf_op jit(solution)/shard_map/pallas_call | solution.py:21
  32.0 1.5 %collective-permute-start.5 = (f32[8,2176]{1,0:T(8,128)S(1)}, f32[8,2176]{1,0:T(8,128)S(1)}, u32[]{:S(2)}, u32[]{:S(2)}) collective-permute-start(f32[8,2176]{1,0:T(8,128)S(1)} %get-tuple-element.76.refs_0_), channel_id=1, source_target_pairs={{0,1},{1,0},{2,3},{3,2},{4,5},{5,4},{6,7},{7,6},{8,9},{9,8},{10,11... | collective-permute-start | bytes 208904 | tf_op jit(solution)/shard_map/ppermute | solution.py:64
  33.6 2.8 %collective-permute-done.5.refs_1_ = f32[8,2176]{1,0:T(8,128)S(1)} collective-permute-done((f32[8,2176]{1,0:T(8,128)S(1)}, f32[8,2176]{1,0:T(8,128)S(1)}, u32[]{:S(2)}, u32[]{:S(2)}) %collective-permute-start.5) | collective-permute-done | bytes 69664 | tf_op jit(solution)/shard_map/ppermute | solution.py:64
  36.4 2.3 %shard_map.92 = (f32[8,2176]{1,0:T(8,128)S(1)}, f32[8,2048]{1,0:T(8,128)S(1)}, f32[8,128]{1,0:T(8,128)S(1)}) custom-call(f32[8,2176]{1,0:T(8,128)S(1)} %get-tuple-element.76.refs_0_, f32[8,2176]{1,0:T(8,128)S(1)} %collective-permute-done.5.refs_1_, f32[8,512]{1,0:T(8,128)S(1)} %get-tuple-element.77.refs_2_, f32[8,512]{1,0:T(8,128)S(1)} %get-tuple-element.78.refs_3_, ...), custom_call_target="tpu_custom_call" | custom-call | bytes 16982016 | tf_op jit(solution)/shard_map/pallas_call | solution.py:21
  38.6 0.0 collective-permute-start.6
  38.7 1.3 %collective-permute-done.6.refs_1_ = f32[8,2176]{1,0:T(8,128)S(1)} collective-permute-done((f32[8,2176]{1,0:T(8,128)S(1)}, f32[8,2176]{1,0:T(8,128)S(1)}, u32[]{:S(2)}, u32[]{:S(2)}) %collective-permute-start.6) | collective-permute-done | bytes 69664 | tf_op jit(solution)/shard_map/ppermute | solution.py:64
  39.9 2.4 %shard_map.93 = (f32[8,2176]{1,0:T(8,128)S(1)}, f32[8,2048]{1,0:T(8,128)S(1)}, f32[8,2048]{1,0:T(8,128)S(1)}, f32[8,2048]{1,0:T(8,128)S(1)}, f32[8,2048]{1,0:T(8,128)S(1)}, /*index=5*/f32[8,2048]{1,0:T(8,128)S(1)}) custom-call(f32[8,2176]{1,0:T(8,128)S(1)} %get-tuple-element.89.refs_0_, f32[8,2176]{1,0:T(8,128)S(1)} %collective-permute-done.6.refs_1_, ...), custom_call_target="tpu_custom_call" | custom-call | bytes 17190944 | tf_op jit(solution)/shard_map/pallas_call | solution.py:21
  42.3 1.5 %collective-permute-start.7 = (f32[8,2176]{1,0:T(8,128)S(1)}, f32[8,2176]{1,0:T(8,128)S(1)}, u32[]{:S(2)}, u32[]{:S(2)}) collective-permute-start(f32[8,2176]{1,0:T(8,128)S(1)} %get-tuple-element.95.refs_0_), channel_id=1, source_target_pairs={{0,1},{1,0},{2,3},{3,2},{4,5},{5,4},{6,7},{7,6},{8,9},{9,8},{10,11... | collective-permute-start | bytes 208904 | tf_op jit(solution)/shard_map/ppermute | solution.py:64
  43.9 2.8 %collective-permute-done.7.refs_1_ = f32[8,2176]{1,0:T(8,128)S(1)} collective-permute-done((f32[8,2176]{1,0:T(8,128)S(1)}, f32[8,2176]{1,0:T(8,128)S(1)}, u32[]{:S(2)}, u32[]{:S(2)}) %collective-permute-start.7) | collective-permute-done | bytes 69664 | tf_op jit(solution)/shard_map/ppermute | solution.py:64
  46.7 2.6 %shard_map.94 = (f32[8,2176]{1,0:T(8,128)S(1)}, f32[8,2048]{1,0:T(8,128)S(1)}, f32[8,128]{1,0:T(8,128)S(1)}) custom-call(f32[8,2176]{1,0:T(8,128)S(1)} %get-tuple-element.95.refs_0_, f32[8,2176]{1,0:T(8,128)S(1)} %collective-permute-done.7.refs_1_, f32[8,512]{1,0:T(8,128)S(1)} %get-tuple-element.77.refs_2_, f32[8,512]{1,0:T(8,128)S(1)} %get-tuple-element.78.refs_3_, ...), custom_call_target="tpu_custom_call" | custom-call | bytes 17051648 | tf_op jit(solution)/shard_map/pallas_call | solution.py:21
  49.2 0.0 collective-permute-start.8
  49.2 1.3 %collective-permute-done.8.refs_1_ = f32[8,2176]{1,0:T(8,128)S(1)} collective-permute-done((f32[8,2176]{1,0:T(8,128)S(1)}, f32[8,2176]{1,0:T(8,128)S(1)}, u32[]{:S(2)}, u32[]{:S(2)}) %collective-permute-start.8) | collective-permute-done | bytes 69664 | tf_op jit(solution)/shard_map/ppermute | solution.py:64
  50.5 2.9 %shard_map.95 = (f32[8,2176]{1,0:T(8,128)S(1)}, f32[8,2048]{1,0:T(8,128)S(1)}, f32[8,2048]{1,0:T(8,128)S(1)}, f32[8,2048]{1,0:T(8,128)}, f32[8,2048]{1,0:T(8,128)S(1)}, /*index=5*/f32[8,2048]{1,0:T(8,128)S(1)}) custom-call(f32[8,2176]{1,0:T(8,128)S(1)} %get-tuple-element.96.refs_0_, f32[8,2176]{1,0:T(8,128)S(1)} %collective-permute-done.8.refs_1_, ...), custom_call_target="tpu_custom_call" | custom-call | bytes 17387552 | tf_op jit(solution)/shard_map/pallas_call | solution.py:21
  53.4 1.5 %collective-permute-start.9 = (f32[8,2176]{1,0:T(8,128)S(1)}, f32[8,2176]{1,0:T(8,128)S(1)}, u32[]{:S(2)}, u32[]{:S(2)}) collective-permute-start(f32[8,2176]{1,0:T(8,128)S(1)} %get-tuple-element.104.refs_0_), channel_id=1, source_target_pairs={{0,1},{1,0},{2,3},{3,2},{4,5},{5,4},{6,7},{7,6},{8,9},{9,8},{10,11... | collective-permute-start | bytes 208904 | tf_op jit(solution)/shard_map/ppermute | solution.py:64
  54.9 2.8 %collective-permute-done.9.refs_1_ = f32[8,2176]{1,0:T(8,128)S(1)} collective-permute-done((f32[8,2176]{1,0:T(8,128)S(1)}, f32[8,2176]{1,0:T(8,128)S(1)}, u32[]{:S(2)}, u32[]{:S(2)}) %collective-permute-start.9) | collective-permute-done | bytes 69664 | tf_op jit(solution)/shard_map/ppermute | solution.py:64
  57.7 0.2 shard_map.96
  57.9 0.0 collective-permute-start.10
  57.9 1.2 %collective-permute-done.10.got = f32[8,2176]{1,0:T(8,128)S(1)} collective-permute-done((f32[8,2176]{1,0:T(8,128)S(1)}, f32[8,2176]{1,0:T(8,128)S(1)}, u32[]{:S(2)}, u32[]{:S(2)}) %collective-permute-start.10) | collective-permute-done | bytes 69664 | tf_op jit(solution)/shard_map/ppermute | solution.py:64
  59.2 0.2 shard_map.97
  59.4 0.1 collective-permute-start.11
  59.5 3.0 %collective-permute-start.12 = (f32[4,3072]{1,0:T(4,128)S(1)}, f32[4,3072]{1,0:T(4,128)S(1)}, u32[]{:S(2)}, u32[]{:S(2)}) collective-permute-start(f32[4,3072]{1,0:T(4,128)S(1)} %get-tuple-element.114), channel_id=1, source_target_pairs={{0,4},{2,6},{4,0},{6,2},{1,5},{3,7},{5,1},{7,3},{8,12},{10,14},{12... | collective-permute-start | bytes 147464 | tf_op jit(solution)/shard_map/ppermute | solution.py:64
  62.5 1.4 %collective-permute-start.13 = (f32[4,3072]{1,0:T(4,128)S(1)}, f32[4,3072]{1,0:T(4,128)S(1)}, u32[]{:S(2)}, u32[]{:S(2)}) collective-permute-start(f32[4,3072]{1,0:T(4,128)S(1)} %get-tuple-element.115), channel_id=1, source_target_pairs={{0,6},{2,4},{4,2},{6,0},{1,7},{3,5},{5,3},{7,1},{8,14},{10,12},{12... | collective-permute-start | bytes 147464 | tf_op jit(solution)/shard_map/ppermute | solution.py:64
  63.8 0.6 collective-permute-done.11.refs_1_
  64.4 0.9 %collective-permute-done.12.refs_2_ = f32[4,3072]{1,0:T(4,128)S(1)} collective-permute-done((f32[4,3072]{1,0:T(4,128)S(1)}, f32[4,3072]{1,0:T(4,128)S(1)}, u32[]{:S(2)}, u32[]{:S(2)}) %collective-permute-start.12) | collective-permute-done | bytes 49184 | tf_op jit(solution)/shard_map/ppermute | solution.py:64
  65.3 3.0 %collective-permute-done.13.refs_3_ = f32[4,3072]{1,0:T(4,128)S(1)} collective-permute-done((f32[4,3072]{1,0:T(4,128)S(1)}, f32[4,3072]{1,0:T(4,128)S(1)}, u32[]{:S(2)}, u32[]{:S(2)}) %collective-permute-start.13) | collective-permute-done | bytes 49184 | tf_op jit(solution)/shard_map/ppermute | solution.py:64
  68.4 0.7 %shard_map.98 = (f32[16,2048]{1,0:T(8,128)}, f32[16,1024]{1,0:T(8,128)}) custom-call(f32[4,3072]{1,0:T(4,128)S(1)} %get-tuple-element.112.refs_0_, f32[4,3072]{1,0:T(4,128)S(1)} %collective-permute-done.11.refs_1_, f32[4,3072]{1,0:T(4,128)S(1)} %collective-permute-done.12.refs_2_, f32[4,3072]{1,0:T(4,128)S(1)} %collective-permute-done.13.refs_3_), custom_call_target="tpu_custom_call" | custom-call | bytes 196608 | tf_op jit(solution)/shard_map/pallas_call | solution.py:21
Async XLA Ops:
  0.6 1.6 %collective-permute-start = (s32[8,128]{1,0:T(8,128)}, s32[8,128]{1,0:T(8,128)S(1)}, u32[]{:S(2)}, u32[]{:S(2)}) collective-permute-start(s32[8,128]{1,0:T(8,128)} %bitcast.8), channel_id=1, source_target_pairs={{0,8},{8,0},{16,24},{24,16},{1,9},{9,1},{17,25},{25,17},{2,10},{10... | collective-permute-start | bytes 12296 | tf_op jit(solution)/shard_map/ppermute | solution.py:64
  3.5 9.8 %collective-permute-start.3 = (bf16[544,128]{1,0:T(8,128)(2,1)S(1)}, bf16[544,128]{1,0:T(8,128)(2,1)S(1)}, u32[]{:S(2)}, u32[]{:S(2)}) collective-permute-start(bf16[544,128]{1,0:T(8,128)(2,1)S(1)} %get-tuple-element.59.msg), channel_id=1, source_target_pairs={{0,2},{2,0},{4,6},{6,4},{1,3},{3,1},{5,7},{7,5},{8,10},{10,8},{12,... | collective-permute-start | bytes 417800 | tf_op jit(solution)/shard_map/ppermute | solution.py:64
  6.5 13.4 %collective-permute-start.2 = (bf16[544,128]{1,0:T(8,128)(2,1)S(1)}, bf16[544,128]{1,0:T(8,128)(2,1)S(1)}, u32[]{:S(2)}, u32[]{:S(2)}) collective-permute-start(bf16[544,128]{1,0:T(8,128)(2,1)S(1)} %get-tuple-element.59.msg), channel_id=1, source_target_pairs={{0,4},{2,6},{4,0},{6,2},{1,5},{3,7},{5,1},{7,3},{8,12},{10,14},{12... | collective-permute-start | bytes 417800 | tf_op jit(solution)/shard_map/ppermute | solution.py:64
  9.1 15.2 %collective-permute-start.1 = (bf16[544,128]{1,0:T(8,128)(2,1)S(1)}, bf16[544,128]{1,0:T(8,128)(2,1)S(1)}, u32[]{:S(2)}, u32[]{:S(2)}) collective-permute-start(bf16[544,128]{1,0:T(8,128)(2,1)S(1)} %get-tuple-element.59.msg), channel_id=1, source_target_pairs={{0,6},{2,4},{4,2},{6,0},{1,7},{3,5},{5,3},{7,1},{8,14},{10,12},{12... | collective-permute-start | bytes 417800 | tf_op jit(solution)/shard_map/ppermute | solution.py:64
  28.5 1.2 %collective-permute-start.4 = (f32[4,2048]{1,0:T(4,128)S(1)}, f32[4,2048]{1,0:T(4,128)S(1)}, u32[]{:S(2)}, u32[]{:S(2)}) collective-permute-start(f32[4,2048]{1,0:T(4,128)S(1)} %get-tuple-element.65.refs_0_), channel_id=1, source_target_pairs={{0,8},{8,0},{16,24},{24,16},{1,9},{9,1},{17,25},{25,17},{2,10},{10... | collective-permute-start | bytes 98312 | tf_op jit(solution)/shard_map/ppermute | solution.py:64
  32.0 4.3 %collective-permute-start.5 = (f32[8,2176]{1,0:T(8,128)S(1)}, f32[8,2176]{1,0:T(8,128)S(1)}, u32[]{:S(2)}, u32[]{:S(2)}) collective-permute-start(f32[8,2176]{1,0:T(8,128)S(1)} %get-tuple-element.76.refs_0_), channel_id=1, source_target_pairs={{0,1},{1,0},{2,3},{3,2},{4,5},{5,4},{6,7},{7,6},{8,9},{9,8},{10,11... | collective-permute-start | bytes 208904 | tf_op jit(solution)/shard_map/ppermute | solution.py:64
  38.6 1.3 %collective-permute-start.6 = (f32[8,2176]{1,0:T(8,128)S(1)}, f32[8,2176]{1,0:T(8,128)S(1)}, u32[]{:S(2)}, u32[]{:S(2)}) collective-permute-start(f32[8,2176]{1,0:T(8,128)S(1)} %get-tuple-element.89.refs_0_), channel_id=1, source_target_pairs={{0,8},{8,0},{16,24},{24,16},{1,9},{9,1},{17,25},{25,17},{2,10},{10... | collective-permute-start | bytes 208904 | tf_op jit(solution)/shard_map/ppermute | solution.py:64
  42.3 4.3 %collective-permute-start.7 = (f32[8,2176]{1,0:T(8,128)S(1)}, f32[8,2176]{1,0:T(8,128)S(1)}, u32[]{:S(2)}, u32[]{:S(2)}) collective-permute-start(f32[8,2176]{1,0:T(8,128)S(1)} %get-tuple-element.95.refs_0_), channel_id=1, source_target_pairs={{0,1},{1,0},{2,3},{3,2},{4,5},{5,4},{6,7},{7,6},{8,9},{9,8},{10,11... | collective-permute-start | bytes 208904 | tf_op jit(solution)/shard_map/ppermute | solution.py:64
  49.2 1.3 %collective-permute-start.8 = (f32[8,2176]{1,0:T(8,128)S(1)}, f32[8,2176]{1,0:T(8,128)S(1)}, u32[]{:S(2)}, u32[]{:S(2)}) collective-permute-start(f32[8,2176]{1,0:T(8,128)S(1)} %get-tuple-element.96.refs_0_), channel_id=1, source_target_pairs={{0,8},{8,0},{16,24},{24,16},{1,9},{9,1},{17,25},{25,17},{2,10},{10... | collective-permute-start | bytes 208904 | tf_op jit(solution)/shard_map/ppermute | solution.py:64
  53.4 4.3 %collective-permute-start.9 = (f32[8,2176]{1,0:T(8,128)S(1)}, f32[8,2176]{1,0:T(8,128)S(1)}, u32[]{:S(2)}, u32[]{:S(2)}) collective-permute-start(f32[8,2176]{1,0:T(8,128)S(1)} %get-tuple-element.104.refs_0_), channel_id=1, source_target_pairs={{0,1},{1,0},{2,3},{3,2},{4,5},{5,4},{6,7},{7,6},{8,9},{9,8},{10,11... | collective-permute-start | bytes 208904 | tf_op jit(solution)/shard_map/ppermute | solution.py:64
  57.9 1.3 %collective-permute-start.10 = (f32[8,2176]{1,0:T(8,128)S(1)}, f32[8,2176]{1,0:T(8,128)S(1)}, u32[]{:S(2)}, u32[]{:S(2)}) collective-permute-start(f32[8,2176]{1,0:T(8,128)S(1)} %get-tuple-element.106.own), channel_id=1, source_target_pairs={{0,8},{8,0},{16,24},{24,16},{1,9},{9,1},{17,25},{25,17},{2,10},{10... | collective-permute-start | bytes 208904 | tf_op jit(solution)/shard_map/ppermute | solution.py:64
  59.4 5.0 %collective-permute-start.11 = (f32[4,3072]{1,0:T(4,128)S(1)}, f32[4,3072]{1,0:T(4,128)S(1)}, u32[]{:S(2)}, u32[]{:S(2)}) collective-permute-start(f32[4,3072]{1,0:T(4,128)S(1)} %get-tuple-element.113), channel_id=1, source_target_pairs={{0,2},{2,0},{4,6},{6,4},{1,3},{3,1},{5,7},{7,5},{8,10},{10,8},{12,... | collective-permute-start | bytes 147464 | tf_op jit(solution)/shard_map/ppermute | solution.py:64
  59.5 5.9 %collective-permute-start.12 = (f32[4,3072]{1,0:T(4,128)S(1)}, f32[4,3072]{1,0:T(4,128)S(1)}, u32[]{:S(2)}, u32[]{:S(2)}) collective-permute-start(f32[4,3072]{1,0:T(4,128)S(1)} %get-tuple-element.114), channel_id=1, source_target_pairs={{0,4},{2,6},{4,0},{6,2},{1,5},{3,7},{5,1},{7,3},{8,12},{10,14},{12... | collective-permute-start | bytes 147464 | tf_op jit(solution)/shard_map/ppermute | solution.py:64
  62.5 5.9 %collective-permute-start.13 = (f32[4,3072]{1,0:T(4,128)S(1)}, f32[4,3072]{1,0:T(4,128)S(1)}, u32[]{:S(2)}, u32[]{:S(2)}) collective-permute-start(f32[4,3072]{1,0:T(4,128)S(1)} %get-tuple-element.115), channel_id=1, source_target_pairs={{0,6},{2,4},{4,2},{6,0},{1,7},{3,5},{5,3},{7,1},{8,14},{10,12},{12... | collective-permute-start | bytes 147464 | tf_op jit(solution)/shard_map/ppermute | solution.py:64

commit v4 on v3

--- a/solution.py
+++ b/solution.py
@@ -10,18 +10,19 @@
 
 f32, bf16 = jnp.float32, jnp.bfloat16
 TURN = 1.0 / (2.0 * math.pi)
-COSINE = (0.999999211770312, -19.738980419471126, 64.92865850463285, -85.27162830146948, 58.79050662870376, -21.071108461771125)
+SINE = (-6.283164044377446, 41.337142378931674, -81.34076911271806, 70.99343519544783)
 LANES = 128
 VMEM_LIMIT = 12 * 2**20
 
 
-def call(body, outs, *args, flops=0, held=True, scratch=()):
+def call(body, outs, *args, flops=0, held=True, scratch=(), aliases={}):
     outs = [pltpu.VMEM(s, d) if held else jax.ShapeDtypeStruct(s, d) for s, d in outs]
     size = sum(math.prod(a.shape) * a.dtype.itemsize for a in args)
     return pl.pallas_call(
         body,
         out_shape=outs,
         scratch_shapes=list(scratch),
+        input_output_aliases=aliases,
         compiler_params=pltpu.CompilerParams(vmem_limit_bytes=VMEM_LIMIT),
         cost_estimate=pl.CostEstimate(flops=flops, bytes_accessed=size, transcendentals=0),
     )(*args)
@@ -83,8 +84,8 @@
 
 
 def pack_kernel(
-    scale, nz, x_hbm, w_hbm, offset_hbm, mag_hbm, response_hbm, label_hbm, penalty_hbm, other_label,
-    msg, w_ref, offset_ref, mag_ref, penalty_ref,
+    scale, x_hbm, w_hbm, offset_hbm, mag_hbm, response_hbm, label_hbm, penalty_hbm,
+    msg, w_ref, offset_ref, mag_ref, penalty_ref, response_out, label_out,
     points, offset_in, mag_in, response_ref, label_ref, penalty_in, sems,
 ):
     half = points.shape[0]
@@ -97,16 +98,30 @@
     copies = [pltpu.make_async_copy(a, b, sems.at[i]) for i, (a, b) in enumerate(pairs)]
     for copy in copies:
         copy.start()
-    for copy in copies[1:3]:
+    for copy in copies:
         copy.wait()
+    msg[:half, :] = points[...]
+    msg[half:, :] = jnp.zeros_like(msg[half:, :])
+    label_out[...] = label_ref[...]
+    response_out[...] = response_ref[...]
+    offset_ref[...] = offset_in[...] * TURN
+    mag_ref[...] = mag_in[...] * scale
+    levels, rows = penalty_in.shape[1], penalty_ref.shape[0]
+    row, column = [lax.broadcasted_iota(jnp.int32, (rows, levels), a) for a in (0, 1)]
+    chosen = column == lax.axis_index("samp") * (rows // 2) + lax.rem(row, rows // 2)
+    penalty_ref[...] = row_sum(jnp.where(chosen, penalty_in[...], 0.0))
+
+
+def label_kernel(half, points, label, other_label, response, msg):
     n = half // LANES
+    c = core()
 
     def mine(block):
         return jnp.where(c == 0, block[:n], block[n:])
 
-    own = (mine(label_ref[...]) != 0).astype(f32)
+    own = (mine(label[...]) != 0).astype(f32)
     other = (mine(other_label[...]) != 0).astype(f32)
-    y = mine(response_ref[...])
+    y = mine(response[...])
     high, middle = halves(y)
     y = y - high.astype(f32)
     middle, low = halves(y)
@@ -114,21 +129,11 @@
     aux += [v.astype(f32) for v in (high, middle, low)]
     aux += [jnp.zeros((msg.shape[0] - half - 5 * n, LANES), f32)]
     msg[half:, :] = jnp.concatenate(aux, axis=0).astype(bf16)
-    copies[0].wait()
-    msg[:half, :] = points[...]
-    for copy in copies[3:]:
-        copy.wait()
-    offset_ref[...] = offset_in[...] * TURN
-    mag_ref[...] = mag_in[...] * scale
-    levels, rows = penalty_in.shape[1], penalty_ref.shape[0]
-    row, column = [lax.broadcasted_iota(jnp.int32, (rows, levels), a) for a in (0, 1)]
-    chosen = column == lax.axis_index("samp") * (rows // 2) + lax.rem(row, rows // 2)
-    penalty_ref[...] = row_sum(jnp.where(chosen, penalty_in[...], 0.0))
 
 
 def features_kernel(first, msg, w_ref, offset_ref, *refs):
     before, refs = (None, refs) if first else (refs[0], refs[1:])
-    high_ref, low_ref, high_t, low_t, kept_ref, moment_ref, acc = refs
+    high_ref, low_ref, high_t, low_t, kept_ref, moment_ref, acc, mask = refs
     samples, features = high_ref.shape
     n = samples // LANES
     aux = msg[samples:, :].astype(f32)
@@ -138,15 +143,19 @@
     y_high, y_low = halves(kept * as_row(y))
     y_both = jnp.concatenate([y_high.astype(f32), y_low.astype(f32)], axis=0).astype(bf16)
     columns = jnp.concatenate([kept, jnp.zeros((6, samples), f32)], axis=0).T
+    for e in (0, 1):
+        mask[e] = jnp.broadcast_to(columns[:, e : e + 1], (samples, LANES))
     cb = min(features, 256)
     for j in range(0, features, cb):
         a = jnp.dot(msg[:samples, :], w_ref[:, j : j + cb], preferred_element_type=f32)
         t = a * TURN + offset_ref[:, j : j + cb]
         r = t - jnp.round(t)
-        u = r * r
-        c = jnp.full_like(u, COSINE[-1])
-        for q in COSINE[-2::-1]:
-            c = c * u + q
+        q = jnp.abs(r) - 0.25
+        u = q * q
+        c = jnp.full_like(u, SINE[-1])
+        for k in SINE[-2::-1]:
+            c = c * u + k
+        c = c * q
         high, low = halves(c)
         high_ref[:, j : j + cb] = high
         low_ref[:, j : j + cb] = low
@@ -154,7 +163,7 @@
         low_t[j : j + cb, :] = low.T
         square = c * c
         for e in (0, 1):
-            part = square * columns[:, e : e + 1]
+            part = square * jnp.concatenate([mask[e]] * (cb // LANES), axis=1)
             acc[e, :, j : j + cb] = part.reshape(samples // 8, 8, cb).sum(0)
         side = jnp.dot(y_both, high, preferred_element_type=f32)
         side = side[:2] + side[2:] + jnp.dot(y_high, low, preferred_element_type=f32)
@@ -225,11 +234,10 @@
     features = mag.shape[1]
     lam, m = penalty[...], mag[...]
     direction = scaled[...]
-    if first:
-        msg, scaled_out, direction_out, residual_out, weights_out, predicted_out = refs
-    else:
-        before, weights, predicted = refs[:3]
-        msg, scaled_out, direction_out, residual_out, weights_out, predicted_out = refs[3:]
+    if not first:
+        (before, weights, predicted), refs = refs[:3], refs[3:]
+    (msg, scaled_out, direction_out, weights_out, predicted_out), refs = refs[:5], refs[5:]
+    if not first:
         direction = direction + sc[:, 2:3] * before[...]
     image = sums[:, :features] * m + lam * direction
     step = sc[:, 0:1] / (sums[:, features : features + 1] + lam * sc[:, 1:2])
@@ -238,7 +246,8 @@
     predicted_out[...] = fitted if first else predicted[...] + fitted
     res = residual[...] - step * image
     s = res / precond[...]
-    residual_out[...] = res
+    for residual_out in refs:
+        residual_out[...] = res
     scaled_out[...] = s
     direction_out[...] = direction
     send_forward(s, m, blocks, msg, [row_sum(res * s), row_sum(s * s), row_sum(s * direction)])
@@ -290,11 +299,12 @@
         out[:, features + half :] = upper[:, j * half : (j + 1) * half]
 
 
-def arrange_kernel(nz, *refs):
+def arrange_kernel(order, *refs):
+    nz = len(order)
     parts, (weights_out, predictions_out, held) = refs[:nz], refs[nz:]
     features = weights_out.shape[1]
     n = weights_out.shape[0] // nz
-    for j, part in enumerate(parts):
+    for j, part in zip(order, parts):
         held[j] = part[...]
     z = lax.axis_index("samp")
     for k in range(nz):
@@ -333,30 +343,38 @@
     inputs = [input_points, wave_numbers, offset_angles.reshape(1, features), feature_magnitudes.reshape(1, features)]
     inputs += [response_values.reshape(tall), label, shrinkage_levels.reshape(1, levels)]
     vectors = [((1, features), f32), ((1, features), f32), (tall, f32), (tall, jnp.int32), ((1, levels), f32)]
-    msg, waves, offsets, mag, penalty = pl.pallas_call(
-        functools.partial(pack_kernel, math.sqrt(2.0 / (features * ny)), nz),
+    packed = ((half + extra, depth), bf16)
+    msg, waves, offsets, mag, penalty, response, label = pl.pallas_call(
+        functools.partial(pack_kernel, math.sqrt(2.0 / (features * ny))),
         out_shape=[
-            pltpu.VMEM((half + extra, depth), bf16),
+            pltpu.VMEM(*packed),
             pltpu.VMEM((depth, features), bf16),
             pltpu.VMEM((1, features), f32),
             pltpu.VMEM((1, features), f32),
             pltpu.VMEM((rows, 1), f32),
+            pltpu.VMEM(tall, f32),
+            pltpu.VMEM(tall, jnp.int32),
         ],
-        in_specs=[pl.BlockSpec(memory_space=pltpu.HBM)] * len(inputs) + [pl.BlockSpec(memory_space=pltpu.VMEM)],
+        in_specs=[pl.BlockSpec(memory_space=pltpu.HBM)] * len(inputs),
         scratch_shapes=[pltpu.VMEM((half, depth), bf16)]
         + [pltpu.VMEM(v, d) for v, d in vectors]
         + [pltpu.SemaphoreType.DMA((len(inputs),))],
         compiler_params=pltpu.CompilerParams(vmem_limit_bytes=VMEM_LIMIT),
-    )(*[pltpu.with_memory_space_constraint(v, pltpu.HBM) for v in inputs], other_label)
-
+    )(*[pltpu.with_memory_space_constraint(v, pltpu.HBM) for v in inputs])
+    (msg,) = call(
+        functools.partial(label_kernel, half), [packed], msg, label, other_label, response, aliases={0: 0}
+    )
+
+    order = [j ^ (j >> 1) for j in range(nz)]
     blocks, turned, kepts, moments = [], [], [], None
     tile, tile_t = ((half, features), bf16), ((features, half), bf16)
-    for j, part in enumerate(exchange(msg, "samp", nz)):
+    for j in order:
+        part = flip(msg, "samp", nz, j) if j else msg
         high, low, high_t, low_t, kept, moments = call(
             functools.partial(features_kernel, j == 0),
             [tile, tile, tile_t, tile_t, ((rows, half), f32), ((4, features), f32)],
             part, waves, offsets, *(() if j == 0 else (moments,)),
-            scratch=[pltpu.VMEM((2, 8, features), f32)],
+            scratch=[pltpu.VMEM((2, 8, features), f32), pltpu.VMEM((2, half, LANES), f32)],
             flops=60 * half * features,
         )
         blocks += [high, low]
@@ -375,12 +393,13 @@
             [msg_f, row_s, row_c],
             *exchange(msg, "feat", ny), *kepts, *blocks, *(() if first else (image_rows, sc)),
         )
-        msg, scaled, before, residual, weights, predicted = call(
+        msg, scaled, before, weights, predicted, *rest = call(
             functools.partial(update_kernel, nz, first),
-            [msg_s, row_f, row_f, row_f, row_f, row_s],
+            [msg_s, row_f, row_f, row_f, row_s] + [row_f] * (it < ITERS - 2),
             msg, flip(msg, "fold", nf, 1), sc, penalty, mag, precond, residual, scaled, image_rows, *turned,
             *(() if first else (before, weights, predicted)),
         )
+        residual = rest[0] if rest else None
     msg, image_rows, sc = call(
         functools.partial(last_kernel, ny, nz),
         [msg_s, row_s, row_c],
@@ -391,9 +410,9 @@
         [((rows // 2, features + shard), f32)] * nz,
         msg, flip(msg, "fold", nf, 1), sc, penalty, scaled, before, weights, image_rows, predicted,
     )
-    outs = [outs[0]] + [flip(out, "samp", nz, j) for j, out in enumerate(outs) if j]
+    outs = [flip(out, "samp", nz, j) if j else out for j, out in zip(order, outs)]
     return call(
-        functools.partial(arrange_kernel, nz),
+        functools.partial(arrange_kernel, order),
         [((levels, features), f32), ((levels, shard), f32)],
         *outs,
         scratch=[pltpu.VMEM((nz, rows // 2, features + shard), f32)],

time: 69.2 us -> 65.5 us (0.947)
  Pallas kernels: 31.9 us -> 29.3 us
  waiting for transfers between devices: 21.3 us -> 20.1 us
    pallas_call x12 -> x13, Pallas kernels: 30.6 us -> 28 us  [call(): pl.pallas_call(body, out_shape=outs, scratch_shapes=list(scratch), input_...]
    ppermute x14, waiting for transfers between devices: 21.3 us -> 20.1 us  [flip(): return lax.ppermute(value, axis, [(i, i ^ s) for i in range(n)])]
  transfers between devices with their start and end apart: 14 -> 14, of which waited for: 12 -> 10; matrix products, arithmetic and copies ran while one was open for 0% -> 0% of each run, Pallas kernels for 18% -> 19%
where the time goes in v4:
time: 65.5 us; the launch traced here: 65.4 us
  Pallas kernels  29.3 us (45%)
  waiting for transfers between devices  20.1 us (31%)
  starting transfers between devices  15.2 us (23%)
  between operations  0.7 us (1%)
    pallas_call x13, Pallas kernels, call(): pl.pallas_call(body, out_shape=outs, scratch_shapes=list(scratch), input_...  28 us
    ppermute x14, waiting for transfers between devices, flip(): return lax.ppermute(value, axis, [(i, i ^ s) for i in range(n)])  20.1 us
    ppermute x14, starting transfers between devices, flip(): return lax.ppermute(value, axis, [(i, i ^ s) for i in range(n)])  15.2 us
  transfers between devices with their start and end apart: 14, of which 10 were waited for; matrix products, arithmetic and copies ran while one was open for 0% of the time, Pallas kernels for 19%

profile of v4, /device:TPU:0, one launch (start us, length us, event | category | flops | bytes accessed | tf_op | source)
XLA Modules:
  0.0 65.4 jit_solution(10082555057625498290)
XLA Ops:
  0.6 0.5 collective-permute-start
  1.1 1.3 %shard_map.86 = (bf16[544,128]{1,0:T(8,128)(2,1)S(1)}, bf16[128,2048]{1,0:T(8,128)(2,1)S(1)}, f32[1,2048]{1,0:T(1,128)S(1)}, f32[1,2048]{1,0:T(1,128)S(1)}, f32[...) custom-call(bf16[1024,128]{1,0:T(8,128)(2,1)} %x_hbm.1, bf16[128,2048]{1,0:T(8,128)(2,1)} %w_hbm.1, ...), custom_call_target="tpu_custom_call" | custom-call | tf_op jit(solution)/shard_map/pallas_call | solution.py:347
  2.5 0.0 collective-permute-done.other_label
  2.5 2.7 %collective-permute-start.3 = (bf16[544,128]{1,0:T(8,128)(2,1)S(1)}, bf16[544,128]{1,0:T(8,128)(2,1)S(1)}, u32[]{:S(2)}, u32[]{:S(2)}) collective-permute-start(bf16[544,128]{1,0:T(8,128)(2,1)S(1)} %shard_map.87.msg), channel_id=1, source_target_pairs={{0,2},{2,0},{4,6},{6,4},{1,3},{3,1},{5,7},{7,5},{8,10},{10,8},{12,... | collective-permute-start | bytes 417800 | tf_op jit(solution)/shard_map/ppermute | solution.py:65
  5.2 2.5 %collective-permute-start.2 = (bf16[544,128]{1,0:T(8,128)(2,1)S(1)}, bf16[544,128]{1,0:T(8,128)(2,1)S(1)}, u32[]{:S(2)}, u32[]{:S(2)}) collective-permute-start(bf16[544,128]{1,0:T(8,128)(2,1)S(1)} %shard_map.87.msg), channel_id=1, source_target_pairs={{0,6},{2,4},{4,2},{6,0},{1,7},{3,5},{5,3},{7,1},{8,14},{10,12},{12... | collective-permute-start | bytes 417800 | tf_op jit(solution)/shard_map/ppermute | solution.py:65
  7.7 0.1 collective-permute-start.1
  7.8 3.7 %shard_map.88 = (bf16[512,2048]{1,0:T(8,128)(2,1)S(1)}, bf16[512,2048]{1,0:T(8,128)(2,1)S(1)}, bf16[2048,512]{1,0:T(8,128)(2,1)S(1)}, bf16[2048,512]{1,0:T(8,128...) custom-call(bf16[544,128]{1,0:T(8,128)(2,1)S(1)} %shard_map.87.msg, ...), custom_call_target="tpu_custom_call" | custom-call | flops 62914560 | bytes 671744 | tf_op jit(solution)/shard_map/pallas_call | solution.py:21
  11.5 0.0 collective-permute-done.3.msg
  11.5 3.7 %shard_map.89 = (bf16[512,2048]{1,0:T(8,128)(2,1)S(1)}, bf16[512,2048]{1,0:T(8,128)(2,1)S(1)}, bf16[2048,512]{1,0:T(8,128)(2,1)S(1)}, bf16[2048,512]{1,0:T(8,128...) custom-call(bf16[544,128]{1,0:T(8,128)(2,1)S(1)} %collective-permute-done.3.msg, ...), custom_call_target="tpu_custom_call" | custom-call | flops 62914560 | bytes 704512 | tf_op jit(solution)/shard_map/pallas_call | solution.py:21
  15.2 0.0 collective-permute-done.2.msg
  15.2 3.7 %shard_map.90 = (bf16[512,2048]{1,0:T(8,128)(2,1)S(1)}, bf16[512,2048]{1,0:T(8,128)(2,1)S(1)}, bf16[2048,512]{1,0:T(8,128)(2,1)S(1)}, bf16[2048,512]{1,0:T(8,128...) custom-call(bf16[544,128]{1,0:T(8,128)(2,1)S(1)} %collective-permute-done.2.msg, ...), custom_call_target="tpu_custom_call" | custom-call | flops 62914560 | bytes 704512 | tf_op jit(solution)/shard_map/pallas_call | solution.py:21
  19.0 1.8 %collective-permute-done.1.msg = bf16[544,128]{1,0:T(8,128)(2,1)S(1)} collective-permute-done((bf16[544,128]{1,0:T(8,128)(2,1)S(1)}, bf16[544,128]{1,0:T(8,128)(2,1)S(1)}, u32[]{:S(2)}, u32[]{:S(2)}) %collective-permute-start.1) | collective-permute-done | bytes 139296 | tf_op jit(solution)/shard_map/ppermute | solution.py:65
  20.7 3.9 %shard_map.91 = (bf16[512,2048]{1,0:T(8,128)(2,1)S(1)}, bf16[512,2048]{1,0:T(8,128)(2,1)S(1)}, bf16[2048,512]{1,0:T(8,128)(2,1)S(1)}, bf16[2048,512]{1,0:T(8,128...) custom-call(bf16[544,128]{1,0:T(8,128)(2,1)S(1)} %collective-permute-done.1.msg, ...), custom_call_target="tpu_custom_call" | custom-call | flops 62914560 | bytes 704512 | tf_op jit(solution)/shard_map/pallas_call | solution.py:21
  24.7 0.0 collective-permute-start.4
  24.7 1.2 %collective-permute-done.4.refs_1_ = f32[4,2048]{1,0:T(4,128)S(1)} collective-permute-done((f32[4,2048]{1,0:T(4,128)S(1)}, f32[4,2048]{1,0:T(4,128)S(1)}, u32[]{:S(2)}, u32[]{:S(2)}) %collective-permute-start.4) | collective-permute-done | bytes 32800 | tf_op jit(solution)/shard_map/ppermute | solution.py:65
  25.9 2.3 %shard_map.92 = (f32[8,2176]{1,0:T(8,128)S(1)}, f32[8,2048]{1,0:T(8,128)S(1)}, f32[8,2048]{1,0:T(8,128)S(1)}, f32[8,2048]{1,0:T(8,128)S(1)}) custom-call(f32[4,2048]{1,0:T(4,128)S(1)} %get-tuple-element.69.refs_0_, f32[4,2048]{1,0:T(4,128)S(1)} %collective-permute-done.4.refs_1_, f32[8,1]{1,0:T(8,128)S(1)} %get-tuple-element.70.refs_2_.refs_3_.penalty, ...), custom_call_target="tpu_custom_call" | custom-call | bytes 16850976 | tf_op jit(solution)/shard_map/pallas_call | solution.py:21
  28.2 1.5 %collective-permute-start.5 = (f32[8,2176]{1,0:T(8,128)S(1)}, f32[8,2176]{1,0:T(8,128)S(1)}, u32[]{:S(2)}, u32[]{:S(2)}) collective-permute-start(f32[8,2176]{1,0:T(8,128)S(1)} %get-tuple-element.80.refs_0_), channel_id=1, source_target_pairs={{0,1},{1,0},{2,3},{3,2},{4,5},{5,4},{6,7},{7,6},{8,9},{9,8},{10,11... | collective-permute-start | bytes 208904 | tf_op jit(solution)/shard_map/ppermute | solution.py:65
  29.8 2.8 %collective-permute-done.5.refs_1_ = f32[8,2176]{1,0:T(8,128)S(1)} collective-permute-done((f32[8,2176]{1,0:T(8,128)S(1)}, f32[8,2176]{1,0:T(8,128)S(1)}, u32[]{:S(2)}, u32[]{:S(2)}) %collective-permute-start.5) | collective-permute-done | bytes 69664 | tf_op jit(solution)/shard_map/ppermute | solution.py:65
  32.6 2.3 %shard_map.93 = (f32[8,2176]{1,0:T(8,128)S(1)}, f32[8,2048]{1,0:T(8,128)S(1)}, f32[8,128]{1,0:T(8,128)S(1)}) custom-call(f32[8,2176]{1,0:T(8,128)S(1)} %get-tuple-element.80.refs_0_, f32[8,2176]{1,0:T(8,128)S(1)} %collective-permute-done.5.refs_1_, f32[8,512]{1,0:T(8,128)S(1)} %get-tuple-element.81.refs_2_, f32[8,512]{1,0:T(8,128)S(1)} %get-tuple-element.82.refs_3_, ...), custom_call_target="tpu_custom_call" | custom-call | bytes 16982016 | tf_op jit(solution)/shard_map/pallas_call | solution.py:21
  34.8 0.0 collective-permute-start.6
  34.9 1.3 %collective-permute-done.6.refs_1_ = f32[8,2176]{1,0:T(8,128)S(1)} collective-permute-done((f32[8,2176]{1,0:T(8,128)S(1)}, f32[8,2176]{1,0:T(8,128)S(1)}, u32[]{:S(2)}, u32[]{:S(2)}) %collective-permute-start.6) | collective-permute-done | bytes 69664 | tf_op jit(solution)/shard_map/ppermute | solution.py:65
  36.1 2.4 %shard_map.94 = (f32[8,2176]{1,0:T(8,128)S(1)}, f32[8,2048]{1,0:T(8,128)S(1)}, f32[8,2048]{1,0:T(8,128)S(1)}, f32[8,2048]{1,0:T(8,128)S(1)}, f32[8,2048]{1,0:T(8,128)S(1)}, /*index=5*/f32[8,2048]{1,0:T(8,128)S(1)}) custom-call(f32[8,2176]{1,0:T(8,128)S(1)} %get-tuple-element.93.refs_0_, f32[8,2176]{1,0:T(8,128)S(1)} %collective-permute-done.6.refs_1_, ...), custom_call_target="tpu_custom_call" | custom-call | bytes 17190944 | tf_op jit(solution)/shard_map/pallas_call | solution.py:21
  38.5 1.5 %collective-permute-start.7 = (f32[8,2176]{1,0:T(8,128)S(1)}, f32[8,2176]{1,0:T(8,128)S(1)}, u32[]{:S(2)}, u32[]{:S(2)}) collective-permute-start(f32[8,2176]{1,0:T(8,128)S(1)} %get-tuple-element.99.refs_0_), channel_id=1, source_target_pairs={{0,1},{1,0},{2,3},{3,2},{4,5},{5,4},{6,7},{7,6},{8,9},{9,8},{10,11... | collective-permute-start | bytes 208904 | tf_op jit(solution)/shard_map/ppermute | solution.py:65
  40.1 2.8 %collective-permute-done.7.refs_1_ = f32[8,2176]{1,0:T(8,128)S(1)} collective-permute-done((f32[8,2176]{1,0:T(8,128)S(1)}, f32[8,2176]{1,0:T(8,128)S(1)}, u32[]{:S(2)}, u32[]{:S(2)}) %collective-permute-start.7) | collective-permute-done | bytes 69664 | tf_op jit(solution)/shard_map/ppermute | solution.py:65
  42.9 2.3 %shard_map.95 = (f32[8,2176]{1,0:T(8,128)S(1)}, f32[8,2048]{1,0:T(8,128)S(1)}, f32[8,128]{1,0:T(8,128)S(1)}) custom-call(f32[8,2176]{1,0:T(8,128)S(1)} %get-tuple-element.99.refs_0_, f32[8,2176]{1,0:T(8,128)S(1)} %collective-permute-done.7.refs_1_, f32[8,512]{1,0:T(8,128)S(1)} %get-tuple-element.81.refs_2_, f32[8,512]{1,0:T(8,128)S(1)} %get-tuple-element.82.refs_3_, ...), custom_call_target="tpu_custom_call" | custom-call | bytes 17051648 | tf_op jit(solution)/shard_map/pallas_call | solution.py:21
  45.2 0.0 collective-permute-start.8
  45.2 1.3 %collective-permute-done.8.refs_1_ = f32[8,2176]{1,0:T(8,128)S(1)} collective-permute-done((f32[8,2176]{1,0:T(8,128)S(1)}, f32[8,2176]{1,0:T(8,128)S(1)}, u32[]{:S(2)}, u32[]{:S(2)}) %collective-permute-start.8) | collective-permute-done | bytes 69664 | tf_op jit(solution)/shard_map/ppermute | solution.py:65
  46.5 2.4 %shard_map.96 = (f32[8,2176]{1,0:T(8,128)S(1)}, f32[8,2048]{1,0:T(8,128)S(1)}, f32[8,2048]{1,0:T(8,128)S(1)}, f32[8,2048]{1,0:T(8,128)S(1)}, f32[8,2048]{1,0:T(8,128)S(1)}) custom-call(f32[8,2176]{1,0:T(8,128)S(1)} %get-tuple-element.100.refs_0_, f32[8,2176]{1,0:T(8,128)S(1)} %collective-permute-done.8.refs_1_, ...), custom_call_target="tpu_custom_call" | custom-call | bytes 17387552 | tf_op jit(solution)/shard_map/pallas_call | solution.py:21
  48.9 1.5 %collective-permute-start.9 = (f32[8,2176]{1,0:T(8,128)S(1)}, f32[8,2176]{1,0:T(8,128)S(1)}, u32[]{:S(2)}, u32[]{:S(2)}) collective-permute-start(f32[8,2176]{1,0:T(8,128)S(1)} %get-tuple-element.108.refs_0_), channel_id=1, source_target_pairs={{0,1},{1,0},{2,3},{3,2},{4,5},{5,4},{6,7},{7,6},{8,9},{9,8},{10,11... | collective-permute-start | bytes 208904 | tf_op jit(solution)/shard_map/ppermute | solution.py:65
  50.4 2.8 %collective-permute-done.9.refs_1_ = f32[8,2176]{1,0:T(8,128)S(1)} collective-permute-done((f32[8,2176]{1,0:T(8,128)S(1)}, f32[8,2176]{1,0:T(8,128)S(1)}, u32[]{:S(2)}, u32[]{:S(2)}) %collective-permute-start.9) | collective-permute-done | bytes 69664 | tf_op jit(solution)/shard_map/ppermute | solution.py:65
  53.2 0.2 shard_map.97
  53.4 0.0 collective-permute-start.10
  53.4 1.2 %collective-permute-done.10.got = f32[8,2176]{1,0:T(8,128)S(1)} collective-permute-done((f32[8,2176]{1,0:T(8,128)S(1)}, f32[8,2176]{1,0:T(8,128)S(1)}, u32[]{:S(2)}, u32[]{:S(2)}) %collective-permute-start.10) | collective-permute-done | bytes 69664 | tf_op jit(solution)/shard_map/ppermute | solution.py:65
  54.7 0.2 shard_map.98
  54.9 1.8 %collective-permute-start.11 = (f32[4,3072]{1,0:T(4,128)S(1)}, f32[4,3072]{1,0:T(4,128)S(1)}, u32[]{:S(2)}, u32[]{:S(2)}) collective-permute-start(f32[4,3072]{1,0:T(4,128)S(1)} %get-tuple-element.117), channel_id=1, source_target_pairs={{0,2},{2,0},{4,6},{6,4},{1,3},{3,1},{5,7},{7,5},{8,10},{10,8},{12,... | collective-permute-start | bytes 147464 | tf_op jit(solution)/shard_map/ppermute | solution.py:65
  56.7 3.0 %collective-permute-start.12 = (f32[4,3072]{1,0:T(4,128)S(1)}, f32[4,3072]{1,0:T(4,128)S(1)}, u32[]{:S(2)}, u32[]{:S(2)}) collective-permute-start(f32[4,3072]{1,0:T(4,128)S(1)} %get-tuple-element.118), channel_id=1, source_target_pairs={{0,6},{2,4},{4,2},{6,0},{1,7},{3,5},{5,3},{7,1},{8,14},{10,12},{12... | collective-permute-start | bytes 147464 | tf_op jit(solution)/shard_map/ppermute | solution.py:65
  59.7 0.0 collective-permute-start.13
  59.7 0.0 collective-permute-done.11.refs_1_
  59.7 3.4 %collective-permute-done.12.refs_2_ = f32[4,3072]{1,0:T(4,128)S(1)} collective-permute-done((f32[4,3072]{1,0:T(4,128)S(1)}, f32[4,3072]{1,0:T(4,128)S(1)}, u32[]{:S(2)}, u32[]{:S(2)}) %collective-permute-start.12) | collective-permute-done | bytes 49184 | tf_op jit(solution)/shard_map/ppermute | solution.py:65
  63.1 1.5 %collective-permute-done.13.refs_3_ = f32[4,3072]{1,0:T(4,128)S(1)} collective-permute-done((f32[4,3072]{1,0:T(4,128)S(1)}, f32[4,3072]{1,0:T(4,128)S(1)}, u32[]{:S(2)}, u32[]{:S(2)}) %collective-permute-start.13) | collective-permute-done | bytes 49184 | tf_op jit(solution)/shard_map/ppermute | solution.py:65
  64.6 0.7 %shard_map.99 = (f32[16,2048]{1,0:T(8,128)}, f32[16,1024]{1,0:T(8,128)}) custom-call(f32[4,3072]{1,0:T(4,128)S(1)} %get-tuple-element.116.refs_0_, f32[4,3072]{1,0:T(4,128)S(1)} %collective-permute-done.11.refs_1_, f32[4,3072]{1,0:T(4,128)S(1)} %collective-permute-done.12.refs_2_, f32[4,3072]{1,0:T(4,128)S(1)} %collective-permute-done.13.refs_3_), custom_call_target="tpu_custom_call" | custom-call | bytes 196608 | tf_op jit(solution)/shard_map/pallas_call | solution.py:21
  (1 shorter events, 0.0 us)
Async XLA Ops:
  0.6 1.8 %collective-permute-start = (s32[8,128]{1,0:T(8,128)}, s32[8,128]{1,0:T(8,128)S(1)}, u32[]{:S(2)}, u32[]{:S(2)}) collective-permute-start(s32[8,128]{1,0:T(8,128)} %bitcast.8), channel_id=1, source_target_pairs={{0,8},{8,0},{16,24},{24,16},{1,9},{9,1},{17,25},{25,17},{2,10},{10... | collective-permute-start | bytes 12296 | tf_op jit(solution)/shard_map/ppermute | solution.py:65
  2.5 9.0 %collective-permute-start.3 = (bf16[544,128]{1,0:T(8,128)(2,1)S(1)}, bf16[544,128]{1,0:T(8,128)(2,1)S(1)}, u32[]{:S(2)}, u32[]{:S(2)}) collective-permute-start(bf16[544,128]{1,0:T(8,128)(2,1)S(1)} %shard_map.87.msg), channel_id=1, source_target_pairs={{0,2},{2,0},{4,6},{6,4},{1,3},{3,1},{5,7},{7,5},{8,10},{10,8},{12,... | collective-permute-start | bytes 417800 | tf_op jit(solution)/shard_map/ppermute | solution.py:65
  5.2 10.1 %collective-permute-start.2 = (bf16[544,128]{1,0:T(8,128)(2,1)S(1)}, bf16[544,128]{1,0:T(8,128)(2,1)S(1)}, u32[]{:S(2)}, u32[]{:S(2)}) collective-permute-start(bf16[544,128]{1,0:T(8,128)(2,1)S(1)} %shard_map.87.msg), channel_id=1, source_target_pairs={{0,6},{2,4},{4,2},{6,0},{1,7},{3,5},{5,3},{7,1},{8,14},{10,12},{12... | collective-permute-start | bytes 417800 | tf_op jit(solution)/shard_map/ppermute | solution.py:65
  7.7 13.1 %collective-permute-start.1 = (bf16[544,128]{1,0:T(8,128)(2,1)S(1)}, bf16[544,128]{1,0:T(8,128)(2,1)S(1)}, u32[]{:S(2)}, u32[]{:S(2)}) collective-permute-start(bf16[544,128]{1,0:T(8,128)(2,1)S(1)} %shard_map.87.msg), channel_id=1, source_target_pairs={{0,4},{2,6},{4,0},{6,2},{1,5},{3,7},{5,1},{7,3},{8,12},{10,14},{12... | collective-permute-start | bytes 417800 | tf_op jit(solution)/shard_map/ppermute | solution.py:65
  24.7 1.3 %collective-permute-start.4 = (f32[4,2048]{1,0:T(4,128)S(1)}, f32[4,2048]{1,0:T(4,128)S(1)}, u32[]{:S(2)}, u32[]{:S(2)}) collective-permute-start(f32[4,2048]{1,0:T(4,128)S(1)} %get-tuple-element.69.refs_0_), channel_id=1, source_target_pairs={{0,8},{8,0},{16,24},{24,16},{1,9},{9,1},{17,25},{25,17},{2,10},{10... | collective-permute-start | bytes 98312 | tf_op jit(solution)/shard_map/ppermute | solution.py:65
  28.2 4.3 %collective-permute-start.5 = (f32[8,2176]{1,0:T(8,128)S(1)}, f32[8,2176]{1,0:T(8,128)S(1)}, u32[]{:S(2)}, u32[]{:S(2)}) collective-permute-start(f32[8,2176]{1,0:T(8,128)S(1)} %get-tuple-element.80.refs_0_), channel_id=1, source_target_pairs={{0,1},{1,0},{2,3},{3,2},{4,5},{5,4},{6,7},{7,6},{8,9},{9,8},{10,11... | collective-permute-start | bytes 208904 | tf_op jit(solution)/shard_map/ppermute | solution.py:65
  34.8 1.3 %collective-permute-start.6 = (f32[8,2176]{1,0:T(8,128)S(1)}, f32[8,2176]{1,0:T(8,128)S(1)}, u32[]{:S(2)}, u32[]{:S(2)}) collective-permute-start(f32[8,2176]{1,0:T(8,128)S(1)} %get-tuple-element.93.refs_0_), channel_id=1, source_target_pairs={{0,8},{8,0},{16,24},{24,16},{1,9},{9,1},{17,25},{25,17},{2,10},{10... | collective-permute-start | bytes 208904 | tf_op jit(solution)/shard_map/ppermute | solution.py:65
  38.5 4.3 %collective-permute-start.7 = (f32[8,2176]{1,0:T(8,128)S(1)}, f32[8,2176]{1,0:T(8,128)S(1)}, u32[]{:S(2)}, u32[]{:S(2)}) collective-permute-start(f32[8,2176]{1,0:T(8,128)S(1)} %get-tuple-element.99.refs_0_), channel_id=1, source_target_pairs={{0,1},{1,0},{2,3},{3,2},{4,5},{5,4},{6,7},{7,6},{8,9},{9,8},{10,11... | collective-permute-start | bytes 208904 | tf_op jit(solution)/shard_map/ppermute | solution.py:65
  45.2 1.3 %collective-permute-start.8 = (f32[8,2176]{1,0:T(8,128)S(1)}, f32[8,2176]{1,0:T(8,128)S(1)}, u32[]{:S(2)}, u32[]{:S(2)}) collective-permute-start(f32[8,2176]{1,0:T(8,128)S(1)} %get-tuple-element.100.refs_0_), channel_id=1, source_target_pairs={{0,8},{8,0},{16,24},{24,16},{1,9},{9,1},{17,25},{25,17},{2,10},{10... | collective-permute-start | bytes 208904 | tf_op jit(solution)/shard_map/ppermute | solution.py:65
  48.9 4.3 %collective-permute-start.9 = (f32[8,2176]{1,0:T(8,128)S(1)}, f32[8,2176]{1,0:T(8,128)S(1)}, u32[]{:S(2)}, u32[]{:S(2)}) collective-permute-start(f32[8,2176]{1,0:T(8,128)S(1)} %get-tuple-element.108.refs_0_), channel_id=1, source_target_pairs={{0,1},{1,0},{2,3},{3,2},{4,5},{5,4},{6,7},{7,6},{8,9},{9,8},{10,11... | collective-permute-start | bytes 208904 | tf_op jit(solution)/shard_map/ppermute | solution.py:65
  53.4 1.3 %collective-permute-start.10 = (f32[8,2176]{1,0:T(8,128)S(1)}, f32[8,2176]{1,0:T(8,128)S(1)}, u32[]{:S(2)}, u32[]{:S(2)}) collective-permute-start(f32[8,2176]{1,0:T(8,128)S(1)} %get-tuple-element.110.own), channel_id=1, source_target_pairs={{0,8},{8,0},{16,24},{24,16},{1,9},{9,1},{17,25},{25,17},{2,10},{10... | collective-permute-start | bytes 208904 | tf_op jit(solution)/shard_map/ppermute | solution.py:65
  54.9 4.8 %collective-permute-start.11 = (f32[4,3072]{1,0:T(4,128)S(1)}, f32[4,3072]{1,0:T(4,128)S(1)}, u32[]{:S(2)}, u32[]{:S(2)}) collective-permute-start(f32[4,3072]{1,0:T(4,128)S(1)} %get-tuple-element.117), channel_id=1, source_target_pairs={{0,2},{2,0},{4,6},{6,4},{1,3},{3,1},{5,7},{7,5},{8,10},{10,8},{12,... | collective-permute-start | bytes 147464 | tf_op jit(solution)/shard_map/ppermute | solution.py:65
  56.7 6.4 %collective-permute-start.12 = (f32[4,3072]{1,0:T(4,128)S(1)}, f32[4,3072]{1,0:T(4,128)S(1)}, u32[]{:S(2)}, u32[]{:S(2)}) collective-permute-start(f32[4,3072]{1,0:T(4,128)S(1)} %get-tuple-element.118), channel_id=1, source_target_pairs={{0,6},{2,4},{4,2},{6,0},{1,7},{3,5},{5,3},{7,1},{8,14},{10,12},{12... | collective-permute-start | bytes 147464 | tf_op jit(solution)/shard_map/ppermute | solution.py:65
  59.7 5.0 %collective-permute-start.13 = (f32[4,3072]{1,0:T(4,128)S(1)}, f32[4,3072]{1,0:T(4,128)S(1)}, u32[]{:S(2)}, u32[]{:S(2)}) collective-permute-start(f32[4,3072]{1,0:T(4,128)S(1)} %get-tuple-element.119), channel_id=1, source_target_pairs={{0,4},{2,6},{4,0},{6,2},{1,5},{3,7},{5,1},{7,3},{8,12},{10,14},{12... | collective-permute-start | bytes 147464 | tf_op jit(solution)/shard_map/ppermute | solution.py:65

commit v5 on v4

--- a/solution.py
+++ b/solution.py
@@ -15,8 +15,8 @@
 VMEM_LIMIT = 12 * 2**20
 
 
-def call(body, outs, *args, flops=0, held=True, scratch=(), aliases={}):
-    outs = [pltpu.VMEM(s, d) if held else jax.ShapeDtypeStruct(s, d) for s, d in outs]
+def call(body, outs, *args, flops=0, in_vmem=True, scratch=(), aliases={}):
+    outs = [pltpu.VMEM(s, d) if in_vmem else jax.ShapeDtypeStruct(s, d) for s, d in outs]
     size = sum(math.prod(a.shape) * a.dtype.itemsize for a in args)
     return pl.pallas_call(
         body,
@@ -44,9 +44,15 @@
     high, low = halves(rows)
     n = rows.shape[0]
     both = jnp.concatenate([high.astype(f32), low.astype(f32)], axis=0).astype(bf16)
-    a = jnp.dot(both, high_ref[...], preferred_element_type=f32)
-    b = jnp.dot(high, low_ref[...], preferred_element_type=f32)
-    return a[:n] + a[n:] + b
+    out = jnp.dot(both, high_ref[...], preferred_element_type=f32)
+    out = out + jnp.dot(both, low_ref[...], preferred_element_type=f32)
+    return out[:n] + out[n:]
+
+
+def held(scaled, mag):
+    high, low = halves(scaled * mag)
+    rounded = high.astype(f32) + low.astype(f32)
+    return rounded / mag, rounded
 
 
 def pack_scalars(columns, rows):
@@ -173,63 +179,94 @@
         moment_ref[e : e + 1, :] = square if first else before[e : e + 1, :] + square
 
 
-def send_forward(s, m, blocks, msg, scalars):
-    v = s * m
+def forward(v, blocks, msg):
     at = 0
     for high, low in zip(blocks[::2], blocks[1::2]):
         n = high.shape[1]
         msg[:, at : at + n] = product(v, high, low)
         at += n
-    msg[:, at:] = pack_scalars(scalars, s.shape[0])
-
-
-def begin_kernel(nz, *refs):
-    moments, penalty, mag, blocks = refs[:2], refs[2], refs[3], refs[4 : 4 + 2 * nz]
-    msg, direction, precond, residual = refs[4 + 2 * nz :]
+    return at
+
+
+def send_forward(v, blocks, msg, scalars):
+    at = forward(v, blocks, msg)
+    msg[:, at:] = pack_scalars(scalars, v.shape[0])
+
+
+def forward_kernel(scaled, mag, *refs):
+    forward(scaled[...] * mag[...], refs[:-1], refs[-1])
+
+
+def begin_kernel(count, *refs):
+    moments, penalty, mag, blocks = refs[:2], refs[2], refs[3], refs[4 : 4 + 2 * count]
+    msg, direction, precond, residual = refs[4 + 2 * count :]
     sums = total(moments)
     m = mag[...]
     rows = penalty.shape[0]
     pre = spread(sums[0:2] * (m * m), rows) + penalty[...]
     res = spread(sums[2:4] * m, rows)
-    s = res / pre
+    s, v = held(res / pre, m)
     precond[...] = pre
     residual[...] = res
     direction[...] = s
-    send_forward(s, m, blocks, msg, [row_sum(res * s), row_sum(s * s)])
-
-
-def adjoint_kernel(ny, nz, first, *refs):
-    parts, refs = refs[:ny], refs[ny:]
-    kepts, blocks, refs = refs[:nz], refs[nz : 3 * nz], refs[3 * nz :]
-    sums = total(parts)
+    send_forward(v, blocks, msg, [row_sum(res * s), row_sum(s * s)])
+
+
+def direction_scalars(sc, before_sc):
+    rz, dd = sc[:, 0:1], sc[:, 1:2]
+    if before_sc is None:
+        return rz, dd, jnp.zeros_like(rz)
+    beta = rz / before_sc[:, 0:1]
+    return rz, dd + 2.0 * beta * sc[:, 2:3] + beta * beta * before_sc[:, 1:2], beta
+
+
+def adjoint(image_rows, kepts, blocks):
     half = kepts[0].shape[1]
-    samples = half * nz
-    image_rows, sc = sums[:, :samples], sums[:, samples:]
-    rz, dd = sc[:, 0:1], sc[:, 1:2]
-    beta = jnp.zeros_like(rz)
-    if not first:
-        before, before_sc, refs = refs[0], refs[1], refs[2:]
-        beta = rz / before_sc[:, 0:1]
-        image_rows = image_rows + beta * before[...]
-        dd = dd + 2.0 * beta * sc[:, 2:3] + beta * beta * before_sc[:, 1:2]
-    msg, rows_out, sc_out = refs
-    squares = jnp.zeros_like(dd)
-    adjoint = 0.0
+    squares, out = 0.0, 0.0
     for j, (kept, high, low) in enumerate(zip(kepts, blocks[::2], blocks[1::2])):
         rows = image_rows[:, j * half : (j + 1) * half]
         weighted = rows * kept[...]
         squares = squares + row_sum(weighted * rows)
-        adjoint = adjoint + product(weighted, high, low)
-    msg[:, : adjoint.shape[1]] = adjoint
-    msg[:, adjoint.shape[1] :] = pack_scalars([squares], dd.shape[0])
+        out = out + product(weighted, high, low)
+    return out, squares
+
+
+def adjoint_kernel(ny, count, first, *refs):
+    parts, refs = refs[:ny], refs[ny:]
+    kepts, blocks, refs = refs[:count], refs[count : 3 * count], refs[3 * count :]
+    sums = total(parts)
+    samples = kepts[0].shape[1] * count
+    image_rows, sc = sums[:, :samples], sums[:, samples:]
+    before, before_sc = (None, None) if first else refs[:2]
+    partial, rows_out, sc_out = refs[-3:]
+    rz, dd, beta = direction_scalars(sc, before_sc)
+    if not first:
+        image_rows = image_rows + beta * before[...]
+    out, squares = adjoint(image_rows, kepts, blocks)
+    partial[...] = out
     rows_out[...] = image_rows
-    sc_out[...] = pack_scalars([rz, dd, beta], dd.shape[0])
-
-
-def update_kernel(nz, first, *refs):
+    sc_out[...] = pack_scalars([rz, dd, beta, squares], dd.shape[0])
+
+
+def rest_kernel(ny, count, first, *refs):
+    parts, refs = refs[:ny], refs[ny:]
+    kepts, blocks, refs = refs[:count], refs[count : 3 * count], refs[3 * count :]
+    sc, partial, refs = refs[0], refs[1], refs[2:]
+    image_rows = total(parts)
+    if not first:
+        image_rows = image_rows + sc[:, 2:3] * refs[0][...]
+    msg, rows_out = refs[-2:]
+    out, squares = adjoint(image_rows, kepts, blocks)
+    features = out.shape[1]
+    msg[:, :features] = partial[...] + out
+    msg[:, features:] = pack_scalars([sc[:, 3:4] + squares], out.shape[0])
+    rows_out[...] = image_rows
+
+
+def update_kernel(count, first, *refs):
     parts, refs = refs[:2], refs[2:]
-    sc, penalty, mag, precond, residual, scaled, rows, refs = *refs[:7], refs[7:]
-    blocks, refs = refs[: 2 * nz], refs[2 * nz :]
+    sc, penalty, mag, precond, residual, scaled, rows, rest, refs = *refs[:8], refs[8:]
+    blocks, refs = refs[: 2 * count], refs[2 * count :]
     sums = total(parts)
     features = mag.shape[1]
     lam, m = penalty[...], mag[...]
@@ -241,16 +278,16 @@
         direction = direction + sc[:, 2:3] * before[...]
     image = sums[:, :features] * m + lam * direction
     step = sc[:, 0:1] / (sums[:, features : features + 1] + lam * sc[:, 1:2])
-    moved, fitted = step * direction, step * rows[...]
+    moved, fitted = step * direction, step * jnp.concatenate([rows[...], rest[...]], axis=1)
     weights_out[...] = moved if first else weights[...] + moved
     predicted_out[...] = fitted if first else predicted[...] + fitted
     res = residual[...] - step * image
-    s = res / precond[...]
+    s, v = held(res / precond[...], m)
     for residual_out in refs:
         residual_out[...] = res
     scaled_out[...] = s
     direction_out[...] = direction
-    send_forward(s, m, blocks, msg, [row_sum(res * s), row_sum(s * s), row_sum(s * direction)])
+    send_forward(v, blocks, msg, [row_sum(res * s), row_sum(s * s), row_sum(s * direction)])
 
 
 def fold_rows(value, fold):
@@ -260,15 +297,12 @@
 
 def last_kernel(ny, nz, *refs):
     parts, refs = refs[:ny], refs[ny:]
-    kepts, (before, before_sc, predicted, msg, rows_out, sc_out) = refs[:nz], refs[nz:]
+    kepts, (before, before_rest, before_sc, predicted, msg, rows_out, sc_out) = refs[:nz], refs[nz:]
     sums = total(parts)
     half = kepts[0].shape[1]
     samples = half * nz
-    sc = sums[:, samples:]
-    rz = sc[:, 0:1]
-    beta = rz / before_sc[:, 0:1]
-    image_rows = sums[:, :samples] + beta * before[...]
-    dd = sc[:, 1:2] + 2.0 * beta * sc[:, 2:3] + beta * beta * before_sc[:, 1:2]
+    rz, dd, beta = direction_scalars(sums[:, samples:], before_sc)
+    image_rows = sums[:, :samples] + beta * jnp.concatenate([before[...], before_rest[...]], axis=1)
     squares = jnp.zeros_like(dd)
     for j, kept in enumerate(kepts):
         rows = image_rows[:, j * half : (j + 1) * half]
@@ -380,43 +414,62 @@
         blocks += [high, low]
         turned += [high_t, low_t]
         kepts.append(kept)
+    count, later = nz - 1, 1
+    msg_a, row_a = ((rows, half * count + LANES), f32), ((rows, half * count), f32)
+    row_b = ((rows, half * later), f32)
+    work = 2 * 3 * rows * half * features
     msg, scaled, precond, residual = call(
-        functools.partial(begin_kernel, nz),
-        [msg_s, row_f, row_f, row_f],
-        moments, flip(moments, "fold", nf, 1), penalty, mag, *turned,
-    )
-    before = weights = predicted = image_rows = sc = None
+        functools.partial(begin_kernel, count),
+        [msg_a, row_f, row_f, row_f],
+        moments, flip(moments, "fold", nf, 1), penalty, mag, *turned[: 2 * count],
+        flops=work * count,
+    )
+    before = weights = predicted = sc = rows_a = rows_b = None
     for it in range(ITERS - 1):
-        first = it == 0
-        msg, image_rows, sc = call(
-            functools.partial(adjoint_kernel, ny, nz, first),
-            [msg_f, row_s, row_c],
-            *exchange(msg, "feat", ny), *kepts, *blocks, *(() if first else (image_rows, sc)),
+        first, last = it == 0, it == ITERS - 2
+        parts = exchange(msg, "feat", ny)
+        (msg_b,) = call(forward_kernel, [row_b], scaled, mag, *turned[2 * count :], flops=work * later)
+        parts_b = exchange(msg_b, "feat", ny)
+        partial, new_a, new_sc = call(
+            functools.partial(adjoint_kernel, ny, count, first),
+            [row_f, row_a, row_c],
+            *parts, *kepts[:count], *blocks[: 2 * count], *(() if first else (rows_a, sc)),
+            flops=work * count,
         )
+        msg, rows_b = call(
+            functools.partial(rest_kernel, ny, later, first),
+            [msg_f, row_b],
+            *parts_b, *kepts[count:], *blocks[2 * count :], new_sc, partial, *(() if first else (rows_b,)),
+            flops=work * later,
+        )
+        rows_a, sc = new_a, new_sc
         msg, scaled, before, weights, predicted, *rest = call(
-            functools.partial(update_kernel, nz, first),
-            [msg_s, row_f, row_f, row_f, row_s] + [row_f] * (it < ITERS - 2),
-            msg, flip(msg, "fold", nf, 1), sc, penalty, mag, precond, residual, scaled, image_rows, *turned,
+            functools.partial(update_kernel, nz if last else count, first),
+            [msg_s if last else msg_a, row_f, row_f, row_f, row_s] + [row_f] * (not last),
+            msg, flip(msg, "fold", nf, 1), sc, penalty, mag, precond, residual, scaled, rows_a, rows_b,
+            *(turned if last else turned[: 2 * count]),
             *(() if first else (before, weights, predicted)),
+            flops=work * count,
         )
         residual = rest[0] if rest else None
     msg, image_rows, sc = call(
         functools.partial(last_kernel, ny, nz),
         [msg_s, row_s, row_c],
-        *exchange(msg, "feat", ny), *kepts, image_rows, sc, predicted,
+        *exchange(msg, "feat", ny), *kepts, rows_a, rows_b, sc, predicted,
     )
     outs = call(
         functools.partial(finish_kernel, nz),
         [((rows // 2, features + shard), f32)] * nz,
         msg, flip(msg, "fold", nf, 1), sc, penalty, scaled, before, weights, image_rows, predicted,
     )
-    outs = [flip(out, "samp", nz, j) if j else out for j, out in zip(order, outs)]
+    far_first = [0] + sorted(range(1, nz), key=lambda j: -j.bit_length())
+    outs = [flip(outs[order.index(j)], "samp", nz, j) if j else outs[0] for j in far_first]
     return call(
-        functools.partial(arrange_kernel, order),
+        functools.partial(arrange_kernel, far_first),
         [((levels, features), f32), ((levels, shard), f32)],
         *outs,
         scratch=[pltpu.VMEM((nz, rows // 2, features + shard), f32)],
-        held=False,
+        in_vmem=False,
     )
 
 

time: 65.5 us -> 64 us (0.977)
  waiting for transfers between devices: 20.1 us -> 17.5 us
  starting transfers between devices: 15.2 us -> 15.9 us
    ppermute x14 -> x16, waiting for transfers between devices: 20.1 us -> 17.5 us  [flip(): return lax.ppermute(value, axis, [(i, i ^ s) for i in range(n)])]
    ppermute x14 -> x16, starting transfers between devices: 15.2 us -> 15.9 us  [flip(): return lax.ppermute(value, axis, [(i, i ^ s) for i in range(n)])]
    pallas_call x13 -> x17, Pallas kernels: 28 us -> 28.5 us  [call(): pl.pallas_call(body, out_shape=outs, scratch_shapes=list(scratch), input_...]
  transfers between devices with their start and end apart: 14 -> 16, of which waited for: 10 -> 11; matrix products, arithmetic and copies ran while one was open for 0% -> 0% of each run, Pallas kernels for 19% -> 27%
where the time goes in v5:
time: 64 us; the launch traced here: 63.8 us
  Pallas kernels  29.8 us (47%)
  waiting for transfers between devices  17.5 us (27%)
  starting transfers between devices  15.9 us (25%)
  between operations  0.71 us (1%)
    pallas_call x17, Pallas kernels, call(): pl.pallas_call(body, out_shape=outs, scratch_shapes=list(scratch), input_...  28.5 us
    ppermute x16, waiting for transfers between devices, flip(): return lax.ppermute(value, axis, [(i, i ^ s) for i in range(n)])  17.5 us
    ppermute x16, starting transfers between devices, flip(): return lax.ppermute(value, axis, [(i, i ^ s) for i in range(n)])  15.9 us
    pallas_call x1, Pallas kernels, shards(): pl.pallas_call(functools.partial(pack_kernel, math.sqrt(2.0 / (features *...  1.3 us
  transfers between devices with their start and end apart: 16, of which 11 were waited for; matrix products, arithmetic and copies ran while one was open for 0% of the time, Pallas kernels for 27%

profile of v5, /device:TPU:0, one launch (start us, length us, event | category | flops | bytes accessed | tf_op | source)
XLA Modules:
  0.0 63.8 jit_solution(2678091722233745431)
XLA Ops:
  0.6 0.5 collective-permute-start
  1.1 1.3 %shard_map.86 = (bf16[544,128]{1,0:T(8,128)(2,1)S(1)}, bf16[128,2048]{1,0:T(8,128)(2,1)S(1)}, f32[1,2048]{1,0:T(1,128)S(1)}, f32[1,2048]{1,0:T(1,128)S(1)}, f32[...) custom-call(bf16[1024,128]{1,0:T(8,128)(2,1)} %x_hbm.1, bf16[128,2048]{1,0:T(8,128)(2,1)} %w_hbm.1, ...), custom_call_target="tpu_custom_call" | custom-call | tf_op jit(solution)/shard_map/pallas_call | solution.py:381
  2.5 0.0 collective-permute-done.other_label
  2.5 2.7 %collective-permute-start.3 = (bf16[544,128]{1,0:T(8,128)(2,1)S(1)}, bf16[544,128]{1,0:T(8,128)(2,1)S(1)}, u32[]{:S(2)}, u32[]{:S(2)}) collective-permute-start(bf16[544,128]{1,0:T(8,128)(2,1)S(1)} %shard_map.87.msg), channel_id=1, source_target_pairs={{0,2},{2,0},{4,6},{6,4},{1,3},{3,1},{5,7},{7,5},{8,10},{10,8},{12,... | collective-permute-start | bytes 417800 | tf_op jit(solution)/shard_map/ppermute | solution.py:71
  5.2 2.5 %collective-permute-start.2 = (bf16[544,128]{1,0:T(8,128)(2,1)S(1)}, bf16[544,128]{1,0:T(8,128)(2,1)S(1)}, u32[]{:S(2)}, u32[]{:S(2)}) collective-permute-start(bf16[544,128]{1,0:T(8,128)(2,1)S(1)} %shard_map.87.msg), channel_id=1, source_target_pairs={{0,6},{2,4},{4,2},{6,0},{1,7},{3,5},{5,3},{7,1},{8,14},{10,12},{12... | collective-permute-start | bytes 417800 | tf_op jit(solution)/shard_map/ppermute | solution.py:71
  7.7 0.1 collective-permute-start.1
  7.8 3.7 %shard_map.88 = (bf16[512,2048]{1,0:T(8,128)(2,1)S(1)}, bf16[512,2048]{1,0:T(8,128)(2,1)S(1)}, bf16[2048,512]{1,0:T(8,128)(2,1)S(1)}, bf16[2048,512]{1,0:T(8,128...) custom-call(bf16[544,128]{1,0:T(8,128)(2,1)S(1)} %shard_map.87.msg, ...), custom_call_target="tpu_custom_call" | custom-call | flops 62914560 | bytes 671744 | tf_op jit(solution)/shard_map/pallas_call | solution.py:21
  11.5 0.0 collective-permute-done.3.msg
  11.5 3.7 %shard_map.89 = (bf16[512,2048]{1,0:T(8,128)(2,1)S(1)}, bf16[512,2048]{1,0:T(8,128)(2,1)S(1)}, bf16[2048,512]{1,0:T(8,128)(2,1)S(1)}, bf16[2048,512]{1,0:T(8,128...) custom-call(bf16[544,128]{1,0:T(8,128)(2,1)S(1)} %collective-permute-done.3.msg, ...), custom_call_target="tpu_custom_call" | custom-call | flops 62914560 | bytes 704512 | tf_op jit(solution)/shard_map/pallas_call | solution.py:21
  15.2 0.0 collective-permute-done.2.msg
  15.2 3.8 %shard_map.90 = (bf16[512,2048]{1,0:T(8,128)(2,1)S(1)}, bf16[512,2048]{1,0:T(8,128)(2,1)S(1)}, bf16[2048,512]{1,0:T(8,128)(2,1)S(1)}, bf16[2048,512]{1,0:T(8,128...) custom-call(bf16[544,128]{1,0:T(8,128)(2,1)S(1)} %collective-permute-done.2.msg, ...), custom_call_target="tpu_custom_call" | custom-call | flops 62914560 | bytes 704512 | tf_op jit(solution)/shard_map/pallas_call | solution.py:21
  19.0 1.8 %collective-permute-done.1.msg = bf16[544,128]{1,0:T(8,128)(2,1)S(1)} collective-permute-done((bf16[544,128]{1,0:T(8,128)(2,1)S(1)}, bf16[544,128]{1,0:T(8,128)(2,1)S(1)}, u32[]{:S(2)}, u32[]{:S(2)}) %collective-permute-start.1) | collective-permute-done | bytes 139296 | tf_op jit(solution)/shard_map/ppermute | solution.py:71
  20.7 3.9 %shard_map.91 = (bf16[512,2048]{1,0:T(8,128)(2,1)S(1)}, bf16[512,2048]{1,0:T(8,128)(2,1)S(1)}, bf16[2048,512]{1,0:T(8,128)(2,1)S(1)}, bf16[2048,512]{1,0:T(8,128...) custom-call(bf16[544,128]{1,0:T(8,128)(2,1)S(1)} %collective-permute-done.1.msg, ...), custom_call_target="tpu_custom_call" | custom-call | flops 62914560 | bytes 704512 | tf_op jit(solution)/shard_map/pallas_call | solution.py:21
  24.7 0.0 collective-permute-start.4
  24.7 1.2 %collective-permute-done.4.refs_1_ = f32[4,2048]{1,0:T(4,128)S(1)} collective-permute-done((f32[4,2048]{1,0:T(4,128)S(1)}, f32[4,2048]{1,0:T(4,128)S(1)}, u32[]{:S(2)}, u32[]{:S(2)}) %collective-permute-start.4) | collective-permute-done | bytes 32800 | tf_op jit(solution)/shard_map/ppermute | solution.py:71
  25.9 1.8 %shard_map.92 = (f32[8,1664]{1,0:T(8,128)S(1)}, f32[8,2048]{1,0:T(8,128)S(1)}, f32[8,2048]{1,0:T(8,128)S(1)}, f32[8,2048]{1,0:T(8,128)S(1)}) custom-call(f32[4,2048]{1,0:T(4,128)S(1)} %get-tuple-element.73.refs_0_, f32[4,2048]{1,0:T(4,128)S(1)} %collective-permute-done.4.refs_1_, f32[8,1]{1,0:T(8,128)S(1)} %get-tuple-element.74.refs_2_.refs_3_.penalty, ...), custom_call_target="tpu_custom_call" | custom-call | flops 150994944 | bytes 12656672 | tf_op jit(solution)/shard_map/pallas_call | solution.py:21
  27.7 1.5 %collective-permute-start.6 = (f32[8,1664]{1,0:T(8,128)S(1)}, f32[8,1664]{1,0:T(8,128)S(1)}, u32[]{:S(2)}, u32[]{:S(2)}) collective-permute-start(f32[8,1664]{1,0:T(8,128)S(1)} %get-tuple-element.88.refs_0_), channel_id=1, source_target_pairs={{0,1},{1,0},{2,3},{3,2},{4,5},{5,4},{6,7},{7,6},{8,9},{9,8},{10,11... | collective-permute-start | bytes 159752 | tf_op jit(solution)/shard_map/ppermute | solution.py:71
  29.2 0.6 %shard_map.93.refs_0_ = f32[8,512]{1,0:T(8,128)S(1)} custom-call(f32[8,2048]{1,0:T(8,128)S(1)} %get-tuple-element.82.scaled.refs_7_, f32[1,2048]{1,0:T(1,128)S(1)} %get-tuple-element.75.refs_3_.mag.refs_4_, bf16[2048,512]{1,0:T(8,128)(2,1)S(1)} %get-tuple-element.83.refs_0_.refs_16_, bf16[2048,512]{1,0:T(8,128)(2,1)S(1)} %get-tuple-element.84.refs_1_.refs_17_), custom_call_target="tpu_custom_call" | custom-call | flops 50331648 | bytes 4268032 | tf_op jit(solution)/shard_map/pallas_call | solution.py:21
  29.9 0.5 collective-permute-start.5
  30.4 1.5 %collective-permute-done.6.refs_1_ = f32[8,1664]{1,0:T(8,128)S(1)} collective-permute-done((f32[8,1664]{1,0:T(8,128)S(1)}, f32[8,1664]{1,0:T(8,128)S(1)}, u32[]{:S(2)}, u32[]{:S(2)}) %collective-permute-start.6) | collective-permute-done | bytes 53280 | tf_op jit(solution)/shard_map/ppermute | solution.py:71
  31.8 1.7 %shard_map.94 = (f32[8,2048]{1,0:T(8,128)S(1)}, f32[8,1536]{1,0:T(8,128)S(1)}, f32[8,128]{1,0:T(8,128)S(1)}) custom-call(f32[8,1664]{1,0:T(8,128)S(1)} %get-tuple-element.88.refs_0_, f32[8,1664]{1,0:T(8,128)S(1)} %collective-permute-done.6.refs_1_, f32[8,512]{1,0:T(8,128)S(1)} %get-tuple-element.89.refs_2_, f32[8,512]{1,0:T(8,128)S(1)} %get-tuple-element.90.refs_3_, ...), custom_call_target="tpu_custom_call" | custom-call | flops 150994944 | bytes 12738560 | tf_op jit(solution)/shard_map/pallas_call | solution.py:21
  33.6 0.0 collective-permute-done.5.refs_1_
  33.6 0.6 %shard_map.95 = (f32[8,2176]{1,0:T(8,128)S(1)}, f32[8,512]{1,0:T(8,128)S(1)}) custom-call(f32[8,512]{1,0:T(8,128)S(1)} %shard_map.93.refs_0_, f32[8,512]{1,0:T(8,128)S(1)} %collective-permute-done.5.refs_1_, f32[8,512]{1,0:T(8,128)S(1)} %get-tuple-element.85.refs_2_.refs_5_, bf16[512,2048]{1,0:T(8,128)(2,1)S(1)} %get-tuple-element.86.refs_3_, ...), custom_call_target="tpu_custom_call" | custom-call | flops 50331648 | bytes 4313088 | tf_op jit(solution)/shard_map/pallas_call | solution.py:21
  34.3 0.0 collective-permute-start.7
  34.3 1.2 %collective-permute-done.7.refs_1_ = f32[8,2176]{1,0:T(8,128)S(1)} collective-permute-done((f32[8,2176]{1,0:T(8,128)S(1)}, f32[8,2176]{1,0:T(8,128)S(1)}, u32[]{:S(2)}, u32[]{:S(2)}) %collective-permute-start.7) | collective-permute-done | bytes 69664 | tf_op jit(solution)/shard_map/ppermute | solution.py:71
  35.5 1.9 %shard_map.96 = (f32[8,1664]{1,0:T(8,128)S(1)}, f32[8,2048]{1,0:T(8,128)S(1)}, f32[8,2048]{1,0:T(8,128)S(1)}, f32[8,2048]{1,0:T(8,128)S(1)}, f32[8,2048]{1,0:T(8,128)S(1)}, /*index=5*/f32[8,2048]{1,0:T(8,128)S(1)}) custom-call(f32[8,2176]{1,0:T(8,128)S(1)} %get-tuple-element.100.refs_0_, f32[8,2176]{1,0:T(8,128)S(1)} %collective-permute-done.7.refs_1_, ...), custom_call_target="tpu_custom_call" | custom-call | flops 150994944 | bytes 12996640 | tf_op jit(solution)/shard_map/pallas_call | solution.py:21
  37.4 1.7 %collective-permute-start.9 = (f32[8,1664]{1,0:T(8,128)S(1)}, f32[8,1664]{1,0:T(8,128)S(1)}, u32[]{:S(2)}, u32[]{:S(2)}) collective-permute-start(f32[8,1664]{1,0:T(8,128)S(1)} %get-tuple-element.106.refs_0_), channel_id=1, source_target_pairs={{0,1},{1,0},{2,3},{3,2},{4,5},{5,4},{6,7},{7,6},{8,9},{9,8},{10,11... | collective-permute-start | bytes 159752 | tf_op jit(solution)/shard_map/ppermute | solution.py:71
  39.1 0.6 %shard_map.97.refs_0_ = f32[8,512]{1,0:T(8,128)S(1)} custom-call(f32[8,2048]{1,0:T(8,128)S(1)} %get-tuple-element.105.scaled.refs_7_, f32[1,2048]{1,0:T(1,128)S(1)} %get-tuple-element.75.refs_3_.mag.refs_4_, bf16[2048,512]{1,0:T(8,128)(2,1)S(1)} %get-tuple-element.83.refs_0_.refs_16_, bf16[2048,512]{1,0:T(8,128)(2,1)S(1)} %get-tuple-element.84.refs_1_.refs_17_), custom_call_target="tpu_custom_call" | custom-call | flops 50331648 | bytes 4268032 | tf_op jit(solution)/shard_map/pallas_call | solution.py:21
  39.7 0.4 collective-permute-start.8
  40.1 1.5 %collective-permute-done.9.refs_1_ = f32[8,1664]{1,0:T(8,128)S(1)} collective-permute-done((f32[8,1664]{1,0:T(8,128)S(1)}, f32[8,1664]{1,0:T(8,128)S(1)}, u32[]{:S(2)}, u32[]{:S(2)}) %collective-permute-start.9) | collective-permute-done | bytes 53280 | tf_op jit(solution)/shard_map/ppermute | solution.py:71
  41.6 1.8 %shard_map.98 = (f32[8,2048]{1,0:T(8,128)S(1)}, f32[8,1536]{1,0:T(8,128)S(1)}, f32[8,128]{1,0:T(8,128)S(1)}) custom-call(f32[8,1664]{1,0:T(8,128)S(1)} %get-tuple-element.106.refs_0_, f32[8,1664]{1,0:T(8,128)S(1)} %collective-permute-done.9.refs_1_, f32[8,512]{1,0:T(8,128)S(1)} %get-tuple-element.89.refs_2_, f32[8,512]{1,0:T(8,128)S(1)} %get-tuple-element.90.refs_3_, ...), custom_call_target="tpu_custom_call" | custom-call | flops 150994944 | bytes 12791808 | tf_op jit(solution)/shard_map/pallas_call | solution.py:21
  43.4 0.1 collective-permute-done.8.refs_1_
  43.5 0.7 %shard_map.99 = (f32[8,2176]{1,0:T(8,128)S(1)}, f32[8,512]{1,0:T(8,128)S(1)}) custom-call(f32[8,512]{1,0:T(8,128)S(1)} %shard_map.97.refs_0_, f32[8,512]{1,0:T(8,128)S(1)} %collective-permute-done.8.refs_1_, f32[8,512]{1,0:T(8,128)S(1)} %get-tuple-element.85.refs_2_.refs_5_, bf16[512,2048]{1,0:T(8,128)(2,1)S(1)} %get-tuple-element.86.refs_3_, ...), custom_call_target="tpu_custom_call" | custom-call | flops 50331648 | bytes 4329472 | tf_op jit(solution)/shard_map/pallas_call | solution.py:21
  44.2 0.0 collective-permute-start.10
  44.2 1.2 %collective-permute-done.10.refs_1_ = f32[8,2176]{1,0:T(8,128)S(1)} collective-permute-done((f32[8,2176]{1,0:T(8,128)S(1)}, f32[8,2176]{1,0:T(8,128)S(1)}, u32[]{:S(2)}, u32[]{:S(2)}) %collective-permute-start.10) | collective-permute-done | bytes 69664 | tf_op jit(solution)/shard_map/ppermute | solution.py:71
  45.5 2.4 %shard_map.100 = (f32[8,2176]{1,0:T(8,128)S(1)}, f32[8,2048]{1,0:T(8,128)S(1)}, f32[8,2048]{1,0:T(8,128)S(1)}, f32[8,2048]{1,0:T(8,128)S(1)}, f32[8,2048]{1,0:T(8,128)S(1)}) custom-call(f32[8,2176]{1,0:T(8,128)S(1)} %get-tuple-element.109.refs_0_, f32[8,2176]{1,0:T(8,128)S(1)} %collective-permute-done.10.refs_1_, ...), custom_call_target="tpu_custom_call" | custom-call | flops 150994944 | bytes 17387552 | tf_op jit(solution)/shard_map/pallas_call | solution.py:21
  47.9 1.6 %collective-permute-start.11 = (f32[8,2176]{1,0:T(8,128)S(1)}, f32[8,2176]{1,0:T(8,128)S(1)}, u32[]{:S(2)}, u32[]{:S(2)}) collective-permute-start(f32[8,2176]{1,0:T(8,128)S(1)} %get-tuple-element.116.refs_0_), channel_id=1, source_target_pairs={{0,1},{1,0},{2,3},{3,2},{4,5},{5,4},{6,7},{7,6},{8,9},{9,8},{10,11... | collective-permute-start | bytes 208904 | tf_op jit(solution)/shard_map/ppermute | solution.py:71
  49.5 2.7 %collective-permute-done.11.refs_1_ = f32[8,2176]{1,0:T(8,128)S(1)} collective-permute-done((f32[8,2176]{1,0:T(8,128)S(1)}, f32[8,2176]{1,0:T(8,128)S(1)}, u32[]{:S(2)}, u32[]{:S(2)}) %collective-permute-start.11) | collective-permute-done | bytes 69664 | tf_op jit(solution)/shard_map/ppermute | solution.py:71
  52.2 0.2 shard_map.101
  52.4 0.0 collective-permute-start.12
  52.5 1.2 %collective-permute-done.12.got = f32[8,2176]{1,0:T(8,128)S(1)} collective-permute-done((f32[8,2176]{1,0:T(8,128)S(1)}, f32[8,2176]{1,0:T(8,128)S(1)}, u32[]{:S(2)}, u32[]{:S(2)}) %collective-permute-start.12) | collective-permute-done | bytes 69664 | tf_op jit(solution)/shard_map/ppermute | solution.py:71
  53.7 0.2 shard_map.102
  53.9 3.3 %collective-permute-start.13 = (f32[4,3072]{1,0:T(4,128)S(1)}, f32[4,3072]{1,0:T(4,128)S(1)}, u32[]{:S(2)}, u32[]{:S(2)}) collective-permute-start(f32[4,3072]{1,0:T(4,128)S(1)} %get-tuple-element.125), channel_id=1, source_target_pairs={{0,4},{2,6},{4,0},{6,2},{1,5},{3,7},{5,1},{7,3},{8,12},{10,14},{12... | collective-permute-start | bytes 147464 | tf_op jit(solution)/shard_map/ppermute | solution.py:71
  57.2 0.9 %collective-permute-start.14 = (f32[4,3072]{1,0:T(4,128)S(1)}, f32[4,3072]{1,0:T(4,128)S(1)}, u32[]{:S(2)}, u32[]{:S(2)}) collective-permute-start(f32[4,3072]{1,0:T(4,128)S(1)} %get-tuple-element.126), channel_id=1, source_target_pairs={{0,6},{2,4},{4,2},{6,0},{1,7},{3,5},{5,3},{7,1},{8,14},{10,12},{12... | collective-permute-start | bytes 147464 | tf_op jit(solution)/shard_map/ppermute | solution.py:71
  58.1 0.0 collective-permute-start.15
  58.1 2.6 %collective-permute-done.13.refs_1_ = f32[4,3072]{1,0:T(4,128)S(1)} collective-permute-done((f32[4,3072]{1,0:T(4,128)S(1)}, f32[4,3072]{1,0:T(4,128)S(1)}, u32[]{:S(2)}, u32[]{:S(2)}) %collective-permute-start.13) | collective-permute-done | bytes 49184 | tf_op jit(solution)/shard_map/ppermute | solution.py:71
  60.7 2.4 %collective-permute-done.14.refs_2_ = f32[4,3072]{1,0:T(4,128)S(1)} collective-permute-done((f32[4,3072]{1,0:T(4,128)S(1)}, f32[4,3072]{1,0:T(4,128)S(1)}, u32[]{:S(2)}, u32[]{:S(2)}) %collective-permute-start.14) | collective-permute-done | bytes 49184 | tf_op jit(solution)/shard_map/ppermute | solution.py:71
  63.1 0.7 %shard_map.103 = (f32[16,2048]{1,0:T(8,128)}, f32[16,1024]{1,0:T(8,128)}) custom-call(f32[4,3072]{1,0:T(4,128)S(1)} %get-tuple-element.124.refs_0_, f32[4,3072]{1,0:T(4,128)S(1)} %collective-permute-done.13.refs_1_, f32[4,3072]{1,0:T(4,128)S(1)} %collective-permute-done.14.refs_2_, f32[4,3072]{1,0:T(4,128)S(1)} %collective-permute-done.15.refs_3_), custom_call_target="tpu_custom_call" | custom-call | bytes 196608 | tf_op jit(solution)/shard_map/pallas_call | solution.py:21
  (2 shorter events, 0.0 us)
Async XLA Ops:
  0.6 1.8 %collective-permute-start = (s32[8,128]{1,0:T(8,128)}, s32[8,128]{1,0:T(8,128)S(1)}, u32[]{:S(2)}, u32[]{:S(2)}) collective-permute-start(s32[8,128]{1,0:T(8,128)} %bitcast.8), channel_id=1, source_target_pairs={{0,8},{8,0},{16,24},{24,16},{1,9},{9,1},{17,25},{25,17},{2,10},{10... | collective-permute-start | bytes 12296 | tf_op jit(solution)/shard_map/ppermute | solution.py:71
  2.5 9.0 %collective-permute-start.3 = (bf16[544,128]{1,0:T(8,128)(2,1)S(1)}, bf16[544,128]{1,0:T(8,128)(2,1)S(1)}, u32[]{:S(2)}, u32[]{:S(2)}) collective-permute-start(bf16[544,128]{1,0:T(8,128)(2,1)S(1)} %shard_map.87.msg), channel_id=1, source_target_pairs={{0,2},{2,0},{4,6},{6,4},{1,3},{3,1},{5,7},{7,5},{8,10},{10,8},{12,... | collective-permute-start | bytes 417800 | tf_op jit(solution)/shard_map/ppermute | solution.py:71
  5.2 10.1 %collective-permute-start.2 = (bf16[544,128]{1,0:T(8,128)(2,1)S(1)}, bf16[544,128]{1,0:T(8,128)(2,1)S(1)}, u32[]{:S(2)}, u32[]{:S(2)}) collective-permute-start(bf16[544,128]{1,0:T(8,128)(2,1)S(1)} %shard_map.87.msg), channel_id=1, source_target_pairs={{0,6},{2,4},{4,2},{6,0},{1,7},{3,5},{5,3},{7,1},{8,14},{10,12},{12... | collective-permute-start | bytes 417800 | tf_op jit(solution)/shard_map/ppermute | solution.py:71
  7.7 13.1 %collective-permute-start.1 = (bf16[544,128]{1,0:T(8,128)(2,1)S(1)}, bf16[544,128]{1,0:T(8,128)(2,1)S(1)}, u32[]{:S(2)}, u32[]{:S(2)}) collective-permute-start(bf16[544,128]{1,0:T(8,128)(2,1)S(1)} %shard_map.87.msg), channel_id=1, source_target_pairs={{0,4},{2,6},{4,0},{6,2},{1,5},{3,7},{5,1},{7,3},{8,12},{10,14},{12... | collective-permute-start | bytes 417800 | tf_op jit(solution)/shard_map/ppermute | solution.py:71
  24.7 1.3 %collective-permute-start.4 = (f32[4,2048]{1,0:T(4,128)S(1)}, f32[4,2048]{1,0:T(4,128)S(1)}, u32[]{:S(2)}, u32[]{:S(2)}) collective-permute-start(f32[4,2048]{1,0:T(4,128)S(1)} %get-tuple-element.73.refs_0_), channel_id=1, source_target_pairs={{0,8},{8,0},{16,24},{24,16},{1,9},{9,1},{17,25},{25,17},{2,10},{10... | collective-permute-start | bytes 98312 | tf_op jit(solution)/shard_map/ppermute | solution.py:71
  27.7 4.1 %collective-permute-start.6 = (f32[8,1664]{1,0:T(8,128)S(1)}, f32[8,1664]{1,0:T(8,128)S(1)}, u32[]{:S(2)}, u32[]{:S(2)}) collective-permute-start(f32[8,1664]{1,0:T(8,128)S(1)} %get-tuple-element.88.refs_0_), channel_id=1, source_target_pairs={{0,1},{1,0},{2,3},{3,2},{4,5},{5,4},{6,7},{7,6},{8,9},{9,8},{10,11... | collective-permute-start | bytes 159752 | tf_op jit(solution)/shard_map/ppermute | solution.py:71
  29.9 3.8 %collective-permute-start.5 = (f32[8,512]{1,0:T(8,128)S(1)}, f32[8,512]{1,0:T(8,128)S(1)}, u32[]{:S(2)}, u32[]{:S(2)}) collective-permute-start(f32[8,512]{1,0:T(8,128)S(1)} %shard_map.93.refs_0_), channel_id=1, source_target_pairs={{0,1},{1,0},{2,3},{3,2},{4,5},{5,4},{6,7},{7,6},{8,9},{9,8},{10,11... | collective-permute-start | bytes 49160 | tf_op jit(solution)/shard_map/ppermute | solution.py:71
  34.3 1.3 %collective-permute-start.7 = (f32[8,2176]{1,0:T(8,128)S(1)}, f32[8,2176]{1,0:T(8,128)S(1)}, u32[]{:S(2)}, u32[]{:S(2)}) collective-permute-start(f32[8,2176]{1,0:T(8,128)S(1)} %get-tuple-element.100.refs_0_), channel_id=1, source_target_pairs={{0,8},{8,0},{16,24},{24,16},{1,9},{9,1},{17,25},{25,17},{2,10},{10... | collective-permute-start | bytes 208904 | tf_op jit(solution)/shard_map/ppermute | solution.py:71
  37.4 4.1 %collective-permute-start.9 = (f32[8,1664]{1,0:T(8,128)S(1)}, f32[8,1664]{1,0:T(8,128)S(1)}, u32[]{:S(2)}, u32[]{:S(2)}) collective-permute-start(f32[8,1664]{1,0:T(8,128)S(1)} %get-tuple-element.106.refs_0_), channel_id=1, source_target_pairs={{0,1},{1,0},{2,3},{3,2},{4,5},{5,4},{6,7},{7,6},{8,9},{9,8},{10,11... | collective-permute-start | bytes 159752 | tf_op jit(solution)/shard_map/ppermute | solution.py:71
  39.7 3.8 %collective-permute-start.8 = (f32[8,512]{1,0:T(8,128)S(1)}, f32[8,512]{1,0:T(8,128)S(1)}, u32[]{:S(2)}, u32[]{:S(2)}) collective-permute-start(f32[8,512]{1,0:T(8,128)S(1)} %shard_map.97.refs_0_), channel_id=1, source_target_pairs={{0,1},{1,0},{2,3},{3,2},{4,5},{5,4},{6,7},{7,6},{8,9},{9,8},{10,11... | collective-permute-start | bytes 49160 | tf_op jit(solution)/shard_map/ppermute | solution.py:71
  44.2 1.3 %collective-permute-start.10 = (f32[8,2176]{1,0:T(8,128)S(1)}, f32[8,2176]{1,0:T(8,128)S(1)}, u32[]{:S(2)}, u32[]{:S(2)}) collective-permute-start(f32[8,2176]{1,0:T(8,128)S(1)} %get-tuple-element.109.refs_0_), channel_id=1, source_target_pairs={{0,8},{8,0},{16,24},{24,16},{1,9},{9,1},{17,25},{25,17},{2,10},{10... | collective-permute-start | bytes 208904 | tf_op jit(solution)/shard_map/ppermute | solution.py:71
  47.9 4.3 %collective-permute-start.11 = (f32[8,2176]{1,0:T(8,128)S(1)}, f32[8,2176]{1,0:T(8,128)S(1)}, u32[]{:S(2)}, u32[]{:S(2)}) collective-permute-start(f32[8,2176]{1,0:T(8,128)S(1)} %get-tuple-element.116.refs_0_), channel_id=1, source_target_pairs={{0,1},{1,0},{2,3},{3,2},{4,5},{5,4},{6,7},{7,6},{8,9},{9,8},{10,11... | collective-permute-start | bytes 208904 | tf_op jit(solution)/shard_map/ppermute | solution.py:71
  52.4 1.3 %collective-permute-start.12 = (f32[8,2176]{1,0:T(8,128)S(1)}, f32[8,2176]{1,0:T(8,128)S(1)}, u32[]{:S(2)}, u32[]{:S(2)}) collective-permute-start(f32[8,2176]{1,0:T(8,128)S(1)} %get-tuple-element.118.own), channel_id=1, source_target_pairs={{0,8},{8,0},{16,24},{24,16},{1,9},{9,1},{17,25},{25,17},{2,10},{10... | collective-permute-start | bytes 208904 | tf_op jit(solution)/shard_map/ppermute | solution.py:71
  53.9 6.8 %collective-permute-start.13 = (f32[4,3072]{1,0:T(4,128)S(1)}, f32[4,3072]{1,0:T(4,128)S(1)}, u32[]{:S(2)}, u32[]{:S(2)}) collective-permute-start(f32[4,3072]{1,0:T(4,128)S(1)} %get-tuple-element.125), channel_id=1, source_target_pairs={{0,4},{2,6},{4,0},{6,2},{1,5},{3,7},{5,1},{7,3},{8,12},{10,14},{12... | collective-permute-start | bytes 147464 | tf_op jit(solution)/shard_map/ppermute | solution.py:71
  57.2 5.9 %collective-permute-start.14 = (f32[4,3072]{1,0:T(4,128)S(1)}, f32[4,3072]{1,0:T(4,128)S(1)}, u32[]{:S(2)}, u32[]{:S(2)}) collective-permute-start(f32[4,3072]{1,0:T(4,128)S(1)} %get-tuple-element.126), channel_id=1, source_target_pairs={{0,6},{2,4},{4,2},{6,0},{1,7},{3,5},{5,3},{7,1},{8,14},{10,12},{12... | collective-permute-start | bytes 147464 | tf_op jit(solution)/shard_map/ppermute | solution.py:71
  58.1 5.0 %collective-permute-start.15 = (f32[4,3072]{1,0:T(4,128)S(1)}, f32[4,3072]{1,0:T(4,128)S(1)}, u32[]{:S(2)}, u32[]{:S(2)}) collective-permute-start(f32[4,3072]{1,0:T(4,128)S(1)} %get-tuple-element.127), channel_id=1, source_target_pairs={{0,2},{2,0},{4,6},{6,4},{1,3},{3,1},{5,7},{7,5},{8,10},{10,8},{12,... | collective-permute-start | bytes 147464 | tf_op jit(solution)/shard_map/ppermute | solution.py:71

commit v6 on v5

--- a/solution.py
+++ b/solution.py
@@ -215,20 +215,25 @@
 def direction_scalars(sc, before_sc):
     rz, dd = sc[:, 0:1], sc[:, 1:2]
     if before_sc is None:
-        return rz, dd, jnp.zeros_like(rz)
+        return rz, dd, jnp.zeros_like(rz), jnp.zeros_like(rz)
     beta = rz / before_sc[:, 0:1]
-    return rz, dd + 2.0 * beta * sc[:, 2:3] + beta * beta * before_sc[:, 1:2], beta
-
-
-def adjoint(image_rows, kepts, blocks):
+    dot = sc[:, 2:3] + beta * before_sc[:, 1:2]
+    return rz, dd + beta * (sc[:, 2:3] + dot), beta, dot
+
+
+def adjoint(image_rows, before, kepts, blocks):
     half = kepts[0].shape[1]
-    squares, out = 0.0, 0.0
+    out = 0.0
+    squares = cross = jnp.zeros((image_rows.shape[0], 1), f32)
     for j, (kept, high, low) in enumerate(zip(kepts, blocks[::2], blocks[1::2])):
-        rows = image_rows[:, j * half : (j + 1) * half]
+        at = slice(j * half, (j + 1) * half)
+        rows = image_rows[:, at]
         weighted = rows * kept[...]
         squares = squares + row_sum(weighted * rows)
+        if before is not None:
+            cross = cross + row_sum(weighted * before[:, at])
         out = out + product(weighted, high, low)
-    return out, squares
+    return out, squares, cross
 
 
 def adjoint_kernel(ny, count, first, *refs):
@@ -239,13 +244,14 @@
     image_rows, sc = sums[:, :samples], sums[:, samples:]
     before, before_sc = (None, None) if first else refs[:2]
     partial, rows_out, sc_out = refs[-3:]
-    rz, dd, beta = direction_scalars(sc, before_sc)
+    rz, dd, beta, dot = direction_scalars(sc, before_sc)
     if not first:
-        image_rows = image_rows + beta * before[...]
-    out, squares = adjoint(image_rows, kepts, blocks)
+        before = before[...]
+        image_rows = image_rows + beta * before
+    out, squares, cross = adjoint(image_rows, before, kepts, blocks)
     partial[...] = out
     rows_out[...] = image_rows
-    sc_out[...] = pack_scalars([rz, dd, beta, squares], dd.shape[0])
+    sc_out[...] = pack_scalars([rz, dd, beta, dot, squares, cross], dd.shape[0])
 
 
 def rest_kernel(ny, count, first, *refs):
@@ -253,17 +259,19 @@
     kepts, blocks, refs = refs[:count], refs[count : 3 * count], refs[3 * count :]
     sc, partial, refs = refs[0], refs[1], refs[2:]
     image_rows = total(parts)
+    before = None
     if not first:
-        image_rows = image_rows + sc[:, 2:3] * refs[0][...]
+        before = refs[0][...]
+        image_rows = image_rows + sc[:, 2:3] * before
     msg, rows_out = refs[-2:]
-    out, squares = adjoint(image_rows, kepts, blocks)
+    out, squares, cross = adjoint(image_rows, before, kepts, blocks)
     features = out.shape[1]
     msg[:, :features] = partial[...] + out
-    msg[:, features:] = pack_scalars([sc[:, 3:4] + squares], out.shape[0])
+    msg[:, features:] = pack_scalars([sc[:, 4:5] + squares, sc[:, 5:6] + cross], out.shape[0])
     rows_out[...] = image_rows
 
 
-def update_kernel(count, first, *refs):
+def update_kernel(count, first, last, *refs):
     parts, refs = refs[:2], refs[2:]
     sc, penalty, mag, precond, residual, scaled, rows, rest, refs = *refs[:8], refs[8:]
     blocks, refs = refs[: 2 * count], refs[2 * count :]
@@ -271,22 +279,34 @@
     features = mag.shape[1]
     lam, m = penalty[...], mag[...]
     direction = scaled[...]
-    if not first:
-        (before, weights, predicted), refs = refs[:3], refs[3:]
+    image_rows = jnp.concatenate([rows[...], rest[...]], axis=1)
+    image = sums[:, :features] * m
+    scalars = sums[:, features:]
+    if first:
+        image = image + lam * direction
+    else:
+        (before, weights, predicted, before_image, before_curve, before_rows, before_rest), refs = refs[:7], refs[7:]
+        direction = direction + sc[:, 2:3] * before[...]
+        extra = (scalars[:, 1:2] + lam * sc[:, 3:4]) / before_curve[:, 0:1]
+        image = image + lam * direction - extra * before_image[...]
+        direction = direction - extra * before[...]
+        image_rows = image_rows - extra * jnp.concatenate([before_rows[...], before_rest[...]], axis=1)
     (msg, scaled_out, direction_out, weights_out, predicted_out), refs = refs[:5], refs[5:]
-    if not first:
-        direction = direction + sc[:, 2:3] * before[...]
-    image = sums[:, :features] * m + lam * direction
-    step = sc[:, 0:1] / (sums[:, features : features + 1] + lam * sc[:, 1:2])
-    moved, fitted = step * direction, step * jnp.concatenate([rows[...], rest[...]], axis=1)
+    curve = scalars[:, 0:1] + lam * sc[:, 1:2]
+    step = sc[:, 0:1] / curve
+    moved, fitted = step * direction, step * image_rows
     weights_out[...] = moved if first else weights[...] + moved
     predicted_out[...] = fitted if first else predicted[...] + fitted
     res = residual[...] - step * image
     s, v = held(res / precond[...], m)
-    for residual_out in refs:
-        residual_out[...] = res
     scaled_out[...] = s
     direction_out[...] = direction
+    if last:
+        refs[0][...] = image_rows
+    else:
+        refs[0][...] = res
+        refs[1][...] = image
+        refs[2][...] = pack_scalars([curve], curve.shape[0])
     send_forward(v, blocks, msg, [row_sum(res * s), row_sum(s * s), row_sum(s * direction)])
 
 
@@ -297,12 +317,12 @@
 
 def last_kernel(ny, nz, *refs):
     parts, refs = refs[:ny], refs[ny:]
-    kepts, (before, before_rest, before_sc, predicted, msg, rows_out, sc_out) = refs[:nz], refs[nz:]
+    kepts, (before, before_sc, predicted, msg, rows_out, sc_out) = refs[:nz], refs[nz:]
     sums = total(parts)
     half = kepts[0].shape[1]
     samples = half * nz
-    rz, dd, beta = direction_scalars(sums[:, samples:], before_sc)
-    image_rows = sums[:, :samples] + beta * jnp.concatenate([before[...], before_rest[...]], axis=1)
+    rz, dd, beta, _ = direction_scalars(sums[:, samples:], before_sc)
+    image_rows = sums[:, :samples] + beta * before[...]
     squares = jnp.zeros_like(dd)
     for j, kept in enumerate(kepts):
         rows = image_rows[:, j * half : (j + 1) * half]
@@ -424,7 +444,7 @@
         moments, flip(moments, "fold", nf, 1), penalty, mag, *turned[: 2 * count],
         flops=work * count,
     )
-    before = weights = predicted = sc = rows_a = rows_b = None
+    before = weights = predicted = image = curve = sc = rows_a = rows_b = None
     for it in range(ITERS - 1):
         first, last = it == 0, it == ITERS - 2
         parts = exchange(msg, "feat", ny)
@@ -436,26 +456,27 @@
             *parts, *kepts[:count], *blocks[: 2 * count], *(() if first else (rows_a, sc)),
             flops=work * count,
         )
-        msg, rows_b = call(
+        msg, new_b = call(
             functools.partial(rest_kernel, ny, later, first),
             [msg_f, row_b],
             *parts_b, *kepts[count:], *blocks[2 * count :], new_sc, partial, *(() if first else (rows_b,)),
             flops=work * later,
         )
-        rows_a, sc = new_a, new_sc
+        sc = new_sc
         msg, scaled, before, weights, predicted, *rest = call(
-            functools.partial(update_kernel, nz if last else count, first),
-            [msg_s if last else msg_a, row_f, row_f, row_f, row_s] + [row_f] * (not last),
-            msg, flip(msg, "fold", nf, 1), sc, penalty, mag, precond, residual, scaled, rows_a, rows_b,
+            functools.partial(update_kernel, nz if last else count, first, last),
+            [msg_s if last else msg_a, row_f, row_f, row_f, row_s] + ([row_s] if last else [row_f, row_f, row_c]),
+            msg, flip(msg, "fold", nf, 1), sc, penalty, mag, precond, residual, scaled, new_a, new_b,
             *(turned if last else turned[: 2 * count]),
-            *(() if first else (before, weights, predicted)),
+            *(() if first else (before, weights, predicted, image, curve, rows_a, rows_b)),
             flops=work * count,
         )
-        residual = rest[0] if rest else None
+        rows_a, rows_b = new_a, new_b
+        residual, image, curve = (None, None, None) if last else rest
     msg, image_rows, sc = call(
         functools.partial(last_kernel, ny, nz),
         [msg_s, row_s, row_c],
-        *exchange(msg, "feat", ny), *kepts, rows_a, rows_b, sc, predicted,
+        *exchange(msg, "feat", ny), *kepts, rest[0], sc, predicted,
     )
     outs = call(
         functools.partial(finish_kernel, nz),

time: 64 us -> 64.1 us (level)
  no operation moved by 1% of the time
where the time goes in v6:
time: 64.1 us; the launch traced here: 64 us
  Pallas kernels  30 us (47%)
  waiting for transfers between devices  17.5 us (27%)
  starting transfers between devices  15.8 us (25%)
  between operations  0.71 us (1%)
    pallas_call x17, Pallas kernels, call(): pl.pallas_call(body, out_shape=outs, scratch_shapes=list(scratch), input_...  28.7 us
    ppermute x16, waiting for transfers between devices, flip(): return lax.ppermute(value, axis, [(i, i ^ s) for i in range(n)])  17.5 us
    ppermute x16, starting transfers between devices, flip(): return lax.ppermute(value, axis, [(i, i ^ s) for i in range(n)])  15.8 us
    pallas_call x1, Pallas kernels, shards(): pl.pallas_call(functools.partial(pack_kernel, math.sqrt(2.0 / (features *...  1.3 us
  transfers between devices with their start and end apart: 16, of which 11 were waited for; matrix products, arithmetic and copies ran while one was open for 0% of the time, Pallas kernels for 27%

profile of v6, /device:TPU:0, one launch (start us, length us, event | category | flops | bytes accessed | tf_op | source)
XLA Modules:
  0.0 64.0 jit_solution(522762148549634487)
XLA Ops:
  0.6 0.5 collective-permute-start
  1.1 1.3 %shard_map.86 = (bf16[544,128]{1,0:T(8,128)(2,1)S(1)}, bf16[128,2048]{1,0:T(8,128)(2,1)S(1)}, f32[1,2048]{1,0:T(1,128)S(1)}, f32[1,2048]{1,0:T(1,128)S(1)}, f32[...) custom-call(bf16[1024,128]{1,0:T(8,128)(2,1)} %x_hbm.1, bf16[128,2048]{1,0:T(8,128)(2,1)} %w_hbm.1, ...), custom_call_target="tpu_custom_call" | custom-call | tf_op jit(solution)/shard_map/pallas_call | solution.py:401
  2.5 0.0 collective-permute-done.other_label
  2.5 2.7 %collective-permute-start.3 = (bf16[544,128]{1,0:T(8,128)(2,1)S(1)}, bf16[544,128]{1,0:T(8,128)(2,1)S(1)}, u32[]{:S(2)}, u32[]{:S(2)}) collective-permute-start(bf16[544,128]{1,0:T(8,128)(2,1)S(1)} %shard_map.87.msg), channel_id=1, source_target_pairs={{0,2},{2,0},{4,6},{6,4},{1,3},{3,1},{5,7},{7,5},{8,10},{10,8},{12,... | collective-permute-start | bytes 417800 | tf_op jit(solution)/shard_map/ppermute | solution.py:71
  5.2 2.5 %collective-permute-start.2 = (bf16[544,128]{1,0:T(8,128)(2,1)S(1)}, bf16[544,128]{1,0:T(8,128)(2,1)S(1)}, u32[]{:S(2)}, u32[]{:S(2)}) collective-permute-start(bf16[544,128]{1,0:T(8,128)(2,1)S(1)} %shard_map.87.msg), channel_id=1, source_target_pairs={{0,6},{2,4},{4,2},{6,0},{1,7},{3,5},{5,3},{7,1},{8,14},{10,12},{12... | collective-permute-start | bytes 417800 | tf_op jit(solution)/shard_map/ppermute | solution.py:71
  7.7 0.1 collective-permute-start.1
  7.8 3.7 %shard_map.88 = (bf16[512,2048]{1,0:T(8,128)(2,1)S(1)}, bf16[512,2048]{1,0:T(8,128)(2,1)S(1)}, bf16[2048,512]{1,0:T(8,128)(2,1)S(1)}, bf16[2048,512]{1,0:T(8,128...) custom-call(bf16[544,128]{1,0:T(8,128)(2,1)S(1)} %shard_map.87.msg, ...), custom_call_target="tpu_custom_call" | custom-call | flops 62914560 | bytes 671744 | tf_op jit(solution)/shard_map/pallas_call | solution.py:21
  11.5 0.0 collective-permute-done.3.msg
  11.5 3.7 %shard_map.89 = (bf16[512,2048]{1,0:T(8,128)(2,1)S(1)}, bf16[512,2048]{1,0:T(8,128)(2,1)S(1)}, bf16[2048,512]{1,0:T(8,128)(2,1)S(1)}, bf16[2048,512]{1,0:T(8,128...) custom-call(bf16[544,128]{1,0:T(8,128)(2,1)S(1)} %collective-permute-done.3.msg, ...), custom_call_target="tpu_custom_call" | custom-call | flops 62914560 | bytes 704512 | tf_op jit(solution)/shard_map/pallas_call | solution.py:21
  15.3 3.7 %shard_map.90 = (bf16[512,2048]{1,0:T(8,128)(2,1)S(1)}, bf16[512,2048]{1,0:T(8,128)(2,1)S(1)}, bf16[2048,512]{1,0:T(8,128)(2,1)S(1)}, bf16[2048,512]{1,0:T(8,128...) custom-call(bf16[544,128]{1,0:T(8,128)(2,1)S(1)} %collective-permute-done.2.msg, ...), custom_call_target="tpu_custom_call" | custom-call | flops 62914560 | bytes 704512 | tf_op jit(solution)/shard_map/pallas_call | solution.py:21
  19.0 1.7 %collective-permute-done.1.msg = bf16[544,128]{1,0:T(8,128)(2,1)S(1)} collective-permute-done((bf16[544,128]{1,0:T(8,128)(2,1)S(1)}, bf16[544,128]{1,0:T(8,128)(2,1)S(1)}, u32[]{:S(2)}, u32[]{:S(2)}) %collective-permute-start.1) | collective-permute-done | bytes 139296 | tf_op jit(solution)/shard_map/ppermute | solution.py:71
  20.7 3.9 %shard_map.91 = (bf16[512,2048]{1,0:T(8,128)(2,1)S(1)}, bf16[512,2048]{1,0:T(8,128)(2,1)S(1)}, bf16[2048,512]{1,0:T(8,128)(2,1)S(1)}, bf16[2048,512]{1,0:T(8,128...) custom-call(bf16[544,128]{1,0:T(8,128)(2,1)S(1)} %collective-permute-done.1.msg, ...), custom_call_target="tpu_custom_call" | custom-call | flops 62914560 | bytes 704512 | tf_op jit(solution)/shard_map/pallas_call | solution.py:21
  24.6 0.0 collective-permute-start.4
  24.7 1.2 %collective-permute-done.4.refs_1_ = f32[4,2048]{1,0:T(4,128)S(1)} collective-permute-done((f32[4,2048]{1,0:T(4,128)S(1)}, f32[4,2048]{1,0:T(4,128)S(1)}, u32[]{:S(2)}, u32[]{:S(2)}) %collective-permute-start.4) | collective-permute-done | bytes 32800 | tf_op jit(solution)/shard_map/ppermute | solution.py:71
  25.9 1.8 %shard_map.92 = (f32[8,1664]{1,0:T(8,128)S(1)}, f32[8,2048]{1,0:T(8,128)S(1)}, f32[8,2048]{1,0:T(8,128)S(1)}, f32[8,2048]{1,0:T(8,128)S(1)}) custom-call(f32[4,2048]{1,0:T(4,128)S(1)} %get-tuple-element.76.refs_0_, f32[4,2048]{1,0:T(4,128)S(1)} %collective-permute-done.4.refs_1_, f32[8,1]{1,0:T(8,128)S(1)} %get-tuple-element.77.refs_2_.refs_3_.penalty, ...), custom_call_target="tpu_custom_call" | custom-call | flops 150994944 | bytes 12656672 | tf_op jit(solution)/shard_map/pallas_call | solution.py:21
  27.7 1.5 %collective-permute-start.6 = (f32[8,1664]{1,0:T(8,128)S(1)}, f32[8,1664]{1,0:T(8,128)S(1)}, u32[]{:S(2)}, u32[]{:S(2)}) collective-permute-start(f32[8,1664]{1,0:T(8,128)S(1)} %get-tuple-element.91.refs_0_), channel_id=1, source_target_pairs={{0,1},{1,0},{2,3},{3,2},{4,5},{5,4},{6,7},{7,6},{8,9},{9,8},{10,11... | collective-permute-start | bytes 159752 | tf_op jit(solution)/shard_map/ppermute | solution.py:71
  29.2 0.6 shard_map.93.refs_0_
  29.8 0.5 collective-permute-start.5
  30.4 1.5 %collective-permute-done.6.refs_1_ = f32[8,1664]{1,0:T(8,128)S(1)} collective-permute-done((f32[8,1664]{1,0:T(8,128)S(1)}, f32[8,1664]{1,0:T(8,128)S(1)}, u32[]{:S(2)}, u32[]{:S(2)}) %collective-permute-start.6) | collective-permute-done | bytes 53280 | tf_op jit(solution)/shard_map/ppermute | solution.py:71
  31.8 1.7 %shard_map.94 = (f32[8,2048]{1,0:T(8,128)S(1)}, f32[8,1536]{1,0:T(8,128)S(1)}, f32[8,128]{1,0:T(8,128)S(1)}) custom-call(f32[8,1664]{1,0:T(8,128)S(1)} %get-tuple-element.91.refs_0_, f32[8,1664]{1,0:T(8,128)S(1)} %collective-permute-done.6.refs_1_, f32[8,512]{1,0:T(8,128)S(1)} %get-tuple-element.92.refs_2_, f32[8,512]{1,0:T(8,128)S(1)} %get-tuple-element.93.refs_3_, ...), custom_call_target="tpu_custom_call" | custom-call | flops 150994944 | bytes 12738560 | tf_op jit(solution)/shard_map/pallas_call | solution.py:21
  33.6 0.0 collective-permute-done.5.refs_1_
  33.6 0.6 %shard_map.95 = (f32[8,2176]{1,0:T(8,128)S(1)}, f32[8,512]{1,0:T(8,128)S(1)}) custom-call(f32[8,512]{1,0:T(8,128)S(1)} %shard_map.93.refs_0_, f32[8,512]{1,0:T(8,128)S(1)} %collective-permute-done.5.refs_1_, f32[8,512]{1,0:T(8,128)S(1)} %get-tuple-element.88.refs_2_.refs_5_, bf16[512,2048]{1,0:T(8,128)(2,1)S(1)} %get-tuple-element.89.refs_3_, ...), custom_call_target="tpu_custom_call" | custom-call | flops 50331648 | bytes 4313088 | tf_op jit(solution)/shard_map/pallas_call | solution.py:21
  34.2 0.0 collective-permute-start.7
  34.3 1.2 %collective-permute-done.7.refs_1_ = f32[8,2176]{1,0:T(8,128)S(1)} collective-permute-done((f32[8,2176]{1,0:T(8,128)S(1)}, f32[8,2176]{1,0:T(8,128)S(1)}, u32[]{:S(2)}, u32[]{:S(2)}) %collective-permute-start.7) | collective-permute-done | bytes 69664 | tf_op jit(solution)/shard_map/ppermute | solution.py:71
  35.5 1.9 %shard_map.96 = (f32[8,1664]{1,0:T(8,128)S(1)}, f32[8,2048]{1,0:T(8,128)S(1)}, f32[8,2048]{1,0:T(8,128)S(1)}, f32[8,2048]{1,0:T(8,128)S(1)}, f32[8,2048]{1,0:T(8...) custom-call(f32[8,2176]{1,0:T(8,128)S(1)} %get-tuple-element.103.refs_0_, ...), custom_call_target="tpu_custom_call" | custom-call | flops 150994944 | bytes 12996640 | tf_op jit(solution)/shard_map/pallas_call | solution.py:21
  37.4 1.7 %collective-permute-start.9 = (f32[8,1664]{1,0:T(8,128)S(1)}, f32[8,1664]{1,0:T(8,128)S(1)}, u32[]{:S(2)}, u32[]{:S(2)}) collective-permute-start(f32[8,1664]{1,0:T(8,128)S(1)} %get-tuple-element.109.refs_0_), channel_id=1, source_target_pairs={{0,1},{1,0},{2,3},{3,2},{4,5},{5,4},{6,7},{7,6},{8,9},{9,8},{10,11... | collective-permute-start | bytes 159752 | tf_op jit(solution)/shard_map/ppermute | solution.py:71
  39.1 0.6 %shard_map.97.refs_0_ = f32[8,512]{1,0:T(8,128)S(1)} custom-call(f32[8,2048]{1,0:T(8,128)S(1)} %get-tuple-element.108.scaled.refs_7_, f32[1,2048]{1,0:T(1,128)S(1)} %get-tuple-element.78.refs_3_.mag.refs_4_, bf16[2048,512]{1,0:T(8,128)(2,1)S(1)} %get-tuple-element.86.refs_0_.refs_16_, bf16[2048,512]{1,0:T(8,128)(2,1)S(1)} %get-tuple-element.87.refs_1_.refs_17_), custom_call_target="tpu_custom_call" | custom-call | flops 50331648 | bytes 4268032 | tf_op jit(solution)/shard_map/pallas_call | solution.py:21
  39.7 0.4 collective-permute-start.8
  40.1 1.4 %collective-permute-done.9.refs_1_ = f32[8,1664]{1,0:T(8,128)S(1)} collective-permute-done((f32[8,1664]{1,0:T(8,128)S(1)}, f32[8,1664]{1,0:T(8,128)S(1)}, u32[]{:S(2)}, u32[]{:S(2)}) %collective-permute-start.9) | collective-permute-done | bytes 53280 | tf_op jit(solution)/shard_map/ppermute | solution.py:71
  41.5 1.8 %shard_map.98 = (f32[8,2048]{1,0:T(8,128)S(1)}, f32[8,1536]{1,0:T(8,128)S(1)}, f32[8,128]{1,0:T(8,128)S(1)}) custom-call(f32[8,1664]{1,0:T(8,128)S(1)} %get-tuple-element.109.refs_0_, f32[8,1664]{1,0:T(8,128)S(1)} %collective-permute-done.9.refs_1_, f32[8,512]{1,0:T(8,128)S(1)} %get-tuple-element.92.refs_2_, f32[8,512]{1,0:T(8,128)S(1)} %get-tuple-element.93.refs_3_, ...), custom_call_target="tpu_custom_call" | custom-call | flops 150994944 | bytes 12791808 | tf_op jit(solution)/shard_map/pallas_call | solution.py:21
  43.3 0.2 collective-permute-done.8.refs_1_
  43.5 0.7 %shard_map.99 = (f32[8,2176]{1,0:T(8,128)S(1)}, f32[8,512]{1,0:T(8,128)S(1)}) custom-call(f32[8,512]{1,0:T(8,128)S(1)} %shard_map.97.refs_0_, f32[8,512]{1,0:T(8,128)S(1)} %collective-permute-done.8.refs_1_, f32[8,512]{1,0:T(8,128)S(1)} %get-tuple-element.88.refs_2_.refs_5_, bf16[512,2048]{1,0:T(8,128)(2,1)S(1)} %get-tuple-element.89.refs_3_, ...), custom_call_target="tpu_custom_call" | custom-call | flops 50331648 | bytes 4329472 | tf_op jit(solution)/shard_map/pallas_call | solution.py:21
  44.2 0.0 collective-permute-start.10
  44.2 1.2 %collective-permute-done.10.refs_1_ = f32[8,2176]{1,0:T(8,128)S(1)} collective-permute-done((f32[8,2176]{1,0:T(8,128)S(1)}, f32[8,2176]{1,0:T(8,128)S(1)}, u32[]{:S(2)}, u32[]{:S(2)}) %collective-permute-start.10) | collective-permute-done | bytes 69664 | tf_op jit(solution)/shard_map/ppermute | solution.py:71
  45.5 2.5 %shard_map.100 = (f32[8,2176]{1,0:T(8,128)S(1)}, f32[8,2048]{1,0:T(8,128)S(1)}, f32[8,2048]{1,0:T(8,128)S(1)}, f32[8,2048]{1,0:T(8,128)S(1)}, f32[8,2048]{1,0:T(8,128)S(1)}, /*index=5*/f32[8,2048]{1,0:T(8,128)S(1)}) custom-call(f32[8,2176]{1,0:T(8,128)S(1)} %get-tuple-element.112.refs_0_, f32[8,2176]{1,0:T(8,128)S(1)} %collective-permute-done.10.refs_1_, ...), custom_call_target="tpu_custom_call" | custom-call | flops 150994944 | bytes 17522720 | tf_op jit(solution)/shard_map/pallas_call | solution.py:21
  47.9 1.6 %collective-permute-start.11 = (f32[8,2176]{1,0:T(8,128)S(1)}, f32[8,2176]{1,0:T(8,128)S(1)}, u32[]{:S(2)}, u32[]{:S(2)}) collective-permute-start(f32[8,2176]{1,0:T(8,128)S(1)} %get-tuple-element.121.refs_0_), channel_id=1, source_target_pairs={{0,1},{1,0},{2,3},{3,2},{4,5},{5,4},{6,7},{7,6},{8,9},{9,8},{10,11... | collective-permute-start | bytes 208904 | tf_op jit(solution)/shard_map/ppermute | solution.py:71
  49.6 2.7 %collective-permute-done.11.refs_1_ = f32[8,2176]{1,0:T(8,128)S(1)} collective-permute-done((f32[8,2176]{1,0:T(8,128)S(1)}, f32[8,2176]{1,0:T(8,128)S(1)}, u32[]{:S(2)}, u32[]{:S(2)}) %collective-permute-start.11) | collective-permute-done | bytes 69664 | tf_op jit(solution)/shard_map/ppermute | solution.py:71
  52.3 0.3 shard_map.101
  52.6 0.0 collective-permute-start.12
  52.6 1.2 %collective-permute-done.12.got = f32[8,2176]{1,0:T(8,128)S(1)} collective-permute-done((f32[8,2176]{1,0:T(8,128)S(1)}, f32[8,2176]{1,0:T(8,128)S(1)}, u32[]{:S(2)}, u32[]{:S(2)}) %collective-permute-start.12) | collective-permute-done | bytes 69664 | tf_op jit(solution)/shard_map/ppermute | solution.py:71
  53.9 0.2 shard_map.102
  54.1 3.3 %collective-permute-start.13 = (f32[4,3072]{1,0:T(4,128)S(1)}, f32[4,3072]{1,0:T(4,128)S(1)}, u32[]{:S(2)}, u32[]{:S(2)}) collective-permute-start(f32[4,3072]{1,0:T(4,128)S(1)} %get-tuple-element.131), channel_id=1, source_target_pairs={{0,4},{2,6},{4,0},{6,2},{1,5},{3,7},{5,1},{7,3},{8,12},{10,14},{12... | collective-permute-start | bytes 147464 | tf_op jit(solution)/shard_map/ppermute | solution.py:71
  57.4 0.9 %collective-permute-start.14 = (f32[4,3072]{1,0:T(4,128)S(1)}, f32[4,3072]{1,0:T(4,128)S(1)}, u32[]{:S(2)}, u32[]{:S(2)}) collective-permute-start(f32[4,3072]{1,0:T(4,128)S(1)} %get-tuple-element.132), channel_id=1, source_target_pairs={{0,6},{2,4},{4,2},{6,0},{1,7},{3,5},{5,3},{7,1},{8,14},{10,12},{12... | collective-permute-start | bytes 147464 | tf_op jit(solution)/shard_map/ppermute | solution.py:71
  58.3 0.0 collective-permute-start.15
  58.3 2.6 %collective-permute-done.13.refs_1_ = f32[4,3072]{1,0:T(4,128)S(1)} collective-permute-done((f32[4,3072]{1,0:T(4,128)S(1)}, f32[4,3072]{1,0:T(4,128)S(1)}, u32[]{:S(2)}, u32[]{:S(2)}) %collective-permute-start.13) | collective-permute-done | bytes 49184 | tf_op jit(solution)/shard_map/ppermute | solution.py:71
  60.9 2.4 %collective-permute-done.14.refs_2_ = f32[4,3072]{1,0:T(4,128)S(1)} collective-permute-done((f32[4,3072]{1,0:T(4,128)S(1)}, f32[4,3072]{1,0:T(4,128)S(1)}, u32[]{:S(2)}, u32[]{:S(2)}) %collective-permute-start.14) | collective-permute-done | bytes 49184 | tf_op jit(solution)/shard_map/ppermute | solution.py:71
  63.3 0.0 collective-permute-done.15.refs_3_
  63.3 0.7 %shard_map.103 = (f32[16,2048]{1,0:T(8,128)}, f32[16,1024]{1,0:T(8,128)}) custom-call(f32[4,3072]{1,0:T(4,128)S(1)} %get-tuple-element.130.refs_0_, f32[4,3072]{1,0:T(4,128)S(1)} %collective-permute-done.13.refs_1_, f32[4,3072]{1,0:T(4,128)S(1)} %collective-permute-done.14.refs_2_, f32[4,3072]{1,0:T(4,128)S(1)} %collective-permute-done.15.refs_3_), custom_call_target="tpu_custom_call" | custom-call | bytes 196608 | tf_op jit(solution)/shard_map/pallas_call | solution.py:21
  (2 shorter events, 0.0 us)
Async XLA Ops:
  0.6 1.8 %collective-permute-start = (s32[8,128]{1,0:T(8,128)}, s32[8,128]{1,0:T(8,128)S(1)}, u32[]{:S(2)}, u32[]{:S(2)}) collective-permute-start(s32[8,128]{1,0:T(8,128)} %bitcast.8), channel_id=1, source_target_pairs={{0,8},{8,0},{16,24},{24,16},{1,9},{9,1},{17,25},{25,17},{2,10},{10... | collective-permute-start | bytes 12296 | tf_op jit(solution)/shard_map/ppermute | solution.py:71
  2.5 9.0 %collective-permute-start.3 = (bf16[544,128]{1,0:T(8,128)(2,1)S(1)}, bf16[544,128]{1,0:T(8,128)(2,1)S(1)}, u32[]{:S(2)}, u32[]{:S(2)}) collective-permute-start(bf16[544,128]{1,0:T(8,128)(2,1)S(1)} %shard_map.87.msg), channel_id=1, source_target_pairs={{0,2},{2,0},{4,6},{6,4},{1,3},{3,1},{5,7},{7,5},{8,10},{10,8},{12,... | collective-permute-start | bytes 417800 | tf_op jit(solution)/shard_map/ppermute | solution.py:71
  5.2 10.1 %collective-permute-start.2 = (bf16[544,128]{1,0:T(8,128)(2,1)S(1)}, bf16[544,128]{1,0:T(8,128)(2,1)S(1)}, u32[]{:S(2)}, u32[]{:S(2)}) collective-permute-start(bf16[544,128]{1,0:T(8,128)(2,1)S(1)} %shard_map.87.msg), channel_id=1, source_target_pairs={{0,6},{2,4},{4,2},{6,0},{1,7},{3,5},{5,3},{7,1},{8,14},{10,12},{12... | collective-permute-start | bytes 417800 | tf_op jit(solution)/shard_map/ppermute | solution.py:71
  7.7 13.1 %collective-permute-start.1 = (bf16[544,128]{1,0:T(8,128)(2,1)S(1)}, bf16[544,128]{1,0:T(8,128)(2,1)S(1)}, u32[]{:S(2)}, u32[]{:S(2)}) collective-permute-start(bf16[544,128]{1,0:T(8,128)(2,1)S(1)} %shard_map.87.msg), channel_id=1, source_target_pairs={{0,4},{2,6},{4,0},{6,2},{1,5},{3,7},{5,1},{7,3},{8,12},{10,14},{12... | collective-permute-start | bytes 417800 | tf_op jit(solution)/shard_map/ppermute | solution.py:71
  24.6 1.3 %collective-permute-start.4 = (f32[4,2048]{1,0:T(4,128)S(1)}, f32[4,2048]{1,0:T(4,128)S(1)}, u32[]{:S(2)}, u32[]{:S(2)}) collective-permute-start(f32[4,2048]{1,0:T(4,128)S(1)} %get-tuple-element.76.refs_0_), channel_id=1, source_target_pairs={{0,8},{8,0},{16,24},{24,16},{1,9},{9,1},{17,25},{25,17},{2,10},{10... | collective-permute-start | bytes 98312 | tf_op jit(solution)/shard_map/ppermute | solution.py:71
  27.7 4.1 %collective-permute-start.6 = (f32[8,1664]{1,0:T(8,128)S(1)}, f32[8,1664]{1,0:T(8,128)S(1)}, u32[]{:S(2)}, u32[]{:S(2)}) collective-permute-start(f32[8,1664]{1,0:T(8,128)S(1)} %get-tuple-element.91.refs_0_), channel_id=1, source_target_pairs={{0,1},{1,0},{2,3},{3,2},{4,5},{5,4},{6,7},{7,6},{8,9},{9,8},{10,11... | collective-permute-start | bytes 159752 | tf_op jit(solution)/shard_map/ppermute | solution.py:71
  29.8 3.8 %collective-permute-start.5 = (f32[8,512]{1,0:T(8,128)S(1)}, f32[8,512]{1,0:T(8,128)S(1)}, u32[]{:S(2)}, u32[]{:S(2)}) collective-permute-start(f32[8,512]{1,0:T(8,128)S(1)} %shard_map.93.refs_0_), channel_id=1, source_target_pairs={{0,1},{1,0},{2,3},{3,2},{4,5},{5,4},{6,7},{7,6},{8,9},{9,8},{10,11... | collective-permute-start | bytes 49160 | tf_op jit(solution)/shard_map/ppermute | solution.py:71
  34.2 1.3 %collective-permute-start.7 = (f32[8,2176]{1,0:T(8,128)S(1)}, f32[8,2176]{1,0:T(8,128)S(1)}, u32[]{:S(2)}, u32[]{:S(2)}) collective-permute-start(f32[8,2176]{1,0:T(8,128)S(1)} %get-tuple-element.103.refs_0_), channel_id=1, source_target_pairs={{0,8},{8,0},{16,24},{24,16},{1,9},{9,1},{17,25},{25,17},{2,10},{10... | collective-permute-start | bytes 208904 | tf_op jit(solution)/shard_map/ppermute | solution.py:71
  37.4 4.1 %collective-permute-start.9 = (f32[8,1664]{1,0:T(8,128)S(1)}, f32[8,1664]{1,0:T(8,128)S(1)}, u32[]{:S(2)}, u32[]{:S(2)}) collective-permute-start(f32[8,1664]{1,0:T(8,128)S(1)} %get-tuple-element.109.refs_0_), channel_id=1, source_target_pairs={{0,1},{1,0},{2,3},{3,2},{4,5},{5,4},{6,7},{7,6},{8,9},{9,8},{10,11... | collective-permute-start | bytes 159752 | tf_op jit(solution)/shard_map/ppermute | solution.py:71
  39.7 3.8 %collective-permute-start.8 = (f32[8,512]{1,0:T(8,128)S(1)}, f32[8,512]{1,0:T(8,128)S(1)}, u32[]{:S(2)}, u32[]{:S(2)}) collective-permute-start(f32[8,512]{1,0:T(8,128)S(1)} %shard_map.97.refs_0_), channel_id=1, source_target_pairs={{0,1},{1,0},{2,3},{3,2},{4,5},{5,4},{6,7},{7,6},{8,9},{9,8},{10,11... | collective-permute-start | bytes 49160 | tf_op jit(solution)/shard_map/ppermute | solution.py:71
  44.2 1.3 %collective-permute-start.10 = (f32[8,2176]{1,0:T(8,128)S(1)}, f32[8,2176]{1,0:T(8,128)S(1)}, u32[]{:S(2)}, u32[]{:S(2)}) collective-permute-start(f32[8,2176]{1,0:T(8,128)S(1)} %get-tuple-element.112.refs_0_), channel_id=1, source_target_pairs={{0,8},{8,0},{16,24},{24,16},{1,9},{9,1},{17,25},{25,17},{2,10},{10... | collective-permute-start | bytes 208904 | tf_op jit(solution)/shard_map/ppermute | solution.py:71
  47.9 4.3 %collective-permute-start.11 = (f32[8,2176]{1,0:T(8,128)S(1)}, f32[8,2176]{1,0:T(8,128)S(1)}, u32[]{:S(2)}, u32[]{:S(2)}) collective-permute-start(f32[8,2176]{1,0:T(8,128)S(1)} %get-tuple-element.121.refs_0_), channel_id=1, source_target_pairs={{0,1},{1,0},{2,3},{3,2},{4,5},{5,4},{6,7},{7,6},{8,9},{9,8},{10,11... | collective-permute-start | bytes 208904 | tf_op jit(solution)/shard_map/ppermute | solution.py:71
  52.6 1.3 %collective-permute-start.12 = (f32[8,2176]{1,0:T(8,128)S(1)}, f32[8,2176]{1,0:T(8,128)S(1)}, u32[]{:S(2)}, u32[]{:S(2)}) collective-permute-start(f32[8,2176]{1,0:T(8,128)S(1)} %get-tuple-element.124.own), channel_id=1, source_target_pairs={{0,8},{8,0},{16,24},{24,16},{1,9},{9,1},{17,25},{25,17},{2,10},{10... | collective-permute-start | bytes 208904 | tf_op jit(solution)/shard_map/ppermute | solution.py:71
  54.1 6.8 %collective-permute-start.13 = (f32[4,3072]{1,0:T(4,128)S(1)}, f32[4,3072]{1,0:T(4,128)S(1)}, u32[]{:S(2)}, u32[]{:S(2)}) collective-permute-start(f32[4,3072]{1,0:T(4,128)S(1)} %get-tuple-element.131), channel_id=1, source_target_pairs={{0,4},{2,6},{4,0},{6,2},{1,5},{3,7},{5,1},{7,3},{8,12},{10,14},{12... | collective-permute-start | bytes 147464 | tf_op jit(solution)/shard_map/ppermute | solution.py:71
  57.4 5.9 %collective-permute-start.14 = (f32[4,3072]{1,0:T(4,128)S(1)}, f32[4,3072]{1,0:T(4,128)S(1)}, u32[]{:S(2)}, u32[]{:S(2)}) collective-permute-start(f32[4,3072]{1,0:T(4,128)S(1)} %get-tuple-element.132), channel_id=1, source_target_pairs={{0,6},{2,4},{4,2},{6,0},{1,7},{3,5},{5,3},{7,1},{8,14},{10,12},{12... | collective-permute-start | bytes 147464 | tf_op jit(solution)/shard_map/ppermute | solution.py:71
  58.3 5.0 %collective-permute-start.15 = (f32[4,3072]{1,0:T(4,128)S(1)}, f32[4,3072]{1,0:T(4,128)S(1)}, u32[]{:S(2)}, u32[]{:S(2)}) collective-permute-start(f32[4,3072]{1,0:T(4,128)S(1)} %get-tuple-element.133), channel_id=1, source_target_pairs={{0,2},{2,0},{4,6},{6,4},{1,3},{3,1},{5,7},{7,5},{8,10},{10,8},{12,... | collective-permute-start | bytes 147464 | tf_op jit(solution)/shard_map/ppermute | solution.py:71

commit v7 on v6

--- a/solution.py
+++ b/solution.py
@@ -8,11 +8,12 @@
 from jax.experimental.pallas import tpu as pltpu
 from jax.sharding import PartitionSpec as P
 
-f32, bf16 = jnp.float32, jnp.bfloat16
+f32, bf16, f8 = jnp.float32, jnp.bfloat16, jnp.float8_e4m3fn
 TURN = 1.0 / (2.0 * math.pi)
 SINE = (-6.283164044377446, 41.337142378931674, -81.34076911271806, 70.99343519544783)
 LANES = 128
 VMEM_LIMIT = 12 * 2**20
+LOW_SCALE = 512.0
 
 
 def call(body, outs, *args, flops=0, in_vmem=True, scratch=(), aliases={}):
@@ -40,13 +41,22 @@
     return high, (value - high.astype(f32)).astype(bf16)
 
 
-def product(rows, high_ref, low_ref):
+def split(rows):
     high, low = halves(rows)
-    n = rows.shape[0]
     both = jnp.concatenate([high.astype(f32), low.astype(f32)], axis=0).astype(bf16)
+    scale = 256.0 / jnp.maximum(jnp.max(jnp.abs(rows), axis=1, keepdims=True), 1e-30)
+    scaled = rows * scale
+    coarse = scaled.astype(f8).astype(f32)
+    small = jnp.concatenate([coarse, (scaled - coarse) * 16.0], axis=0).astype(f8)
+    return both, small, 1.0 / (scale * LOW_SCALE)
+
+
+def product(parts, high_ref, low_ref):
+    both, small, back = parts
+    n = back.shape[0]
     out = jnp.dot(both, high_ref[...], preferred_element_type=f32)
-    out = out + jnp.dot(both, low_ref[...], preferred_element_type=f32)
-    return out[:n] + out[n:]
+    fine = jnp.dot(small, low_ref[...], preferred_element_type=f32)
+    return out[:n] + out[n:] + (fine[:n] + fine[n:] * 0.0625) * back
 
 
 def held(scaled, mag):
@@ -128,12 +138,11 @@
     own = (mine(label[...]) != 0).astype(f32)
     other = (mine(other_label[...]) != 0).astype(f32)
     y = mine(response[...])
-    high, middle = halves(y)
-    y = y - high.astype(f32)
-    middle, low = halves(y)
+    high, low = halves(y)
     aux = [jnp.where(c == 0, own, other), jnp.where(c == 0, other, own)]
-    aux += [v.astype(f32) for v in (high, middle, low)]
-    aux += [jnp.zeros((msg.shape[0] - half - 5 * n, LANES), f32)]
+    aux += [v.astype(f32) for v in (high, low)]
+    if msg.shape[0] - half > 4 * n:
+        aux += [jnp.zeros((msg.shape[0] - half - 4 * n, LANES), f32)]
     msg[half:, :] = jnp.concatenate(aux, axis=0).astype(bf16)
 
 
@@ -145,7 +154,7 @@
     aux = msg[samples:, :].astype(f32)
     kept = jnp.concatenate([as_row(aux[e * n : (e + 1) * n]) for e in (0, 1)], axis=0)
     kept_ref[...] = spread(kept, kept_ref.shape[0])
-    y = (aux[2 * n : 3 * n] + aux[3 * n : 4 * n]) + aux[4 * n : 5 * n]
+    y = aux[2 * n : 3 * n] + aux[3 * n : 4 * n]
     y_high, y_low = halves(kept * as_row(y))
     y_both = jnp.concatenate([y_high.astype(f32), y_low.astype(f32)], axis=0).astype(bf16)
     columns = jnp.concatenate([kept, jnp.zeros((6, samples), f32)], axis=0).T
@@ -164,9 +173,10 @@
         c = c * q
         high, low = halves(c)
         high_ref[:, j : j + cb] = high
-        low_ref[:, j : j + cb] = low
+        small = ((c - high.astype(f32)) * LOW_SCALE).astype(f8)
+        low_ref[:, j : j + cb] = small
         high_t[j : j + cb, :] = high.T
-        low_t[j : j + cb, :] = low.T
+        low_t[j : j + cb, :] = small.T
         square = c * c
         for e in (0, 1):
             part = square * jnp.concatenate([mask[e]] * (cb // LANES), axis=1)
@@ -180,10 +190,10 @@
 
 
 def forward(v, blocks, msg):
-    at = 0
+    at, parts = 0, split(v)
     for high, low in zip(blocks[::2], blocks[1::2]):
         n = high.shape[1]
-        msg[:, at : at + n] = product(v, high, low)
+        msg[:, at : at + n] = product(parts, high, low)
         at += n
     return at
 
@@ -232,7 +242,7 @@
         squares = squares + row_sum(weighted * rows)
         if before is not None:
             cross = cross + row_sum(weighted * before[:, at])
-        out = out + product(weighted, high, low)
+        out = out + product(split(weighted), high, low)
     return out, squares, cross
 
 
@@ -388,7 +398,7 @@
     half, rows = shard // 2, 2 * (levels // nz)
     samples = half * nz
     tall = (shard // LANES, LANES)
-    extra = pl.cdiv(5 * half // LANES, 16) * 16
+    extra = pl.cdiv(4 * half // LANES, 16) * 16
     row_f, row_s, row_c = ((rows, features), f32), ((rows, samples), f32), ((rows, LANES), f32)
     msg_f, msg_s = ((rows, features + LANES), f32), ((rows, samples + LANES), f32)
 
@@ -421,12 +431,13 @@
 
     order = [j ^ (j >> 1) for j in range(nz)]
     blocks, turned, kepts, moments = [], [], [], None
-    tile, tile_t = ((half, features), bf16), ((features, half), bf16)
+    shapes = (half, features), (features, half)
+    tiles = [(shape, kind) for shape in shapes for kind in (bf16, f8)]
     for j in order:
         part = flip(msg, "samp", nz, j) if j else msg
         high, low, high_t, low_t, kept, moments = call(
             functools.partial(features_kernel, j == 0),
-            [tile, tile, tile_t, tile_t, ((rows, half), f32), ((4, features), f32)],
+            [*tiles, ((rows, half), f32), ((4, features), f32)],
             part, waves, offsets, *(() if j == 0 else (moments,)),
             scratch=[pltpu.VMEM((2, 8, features), f32), pltpu.VMEM((2, half, LANES), f32)],
             flops=60 * half * features,

time: 64.1 us -> 62.3 us (0.972)
  Pallas kernels: 30 us -> 27.7 us
    pallas_call x17, Pallas kernels: 28.7 us -> 26.4 us  [call(): pl.pallas_call(body, out_shape=outs, scratch_shapes=list(scratch), input_...]
  transfers between devices with their start and end apart: 16 -> 16, of which waited for: 11 -> 12; matrix products, arithmetic and copies ran while one was open for 0% -> 0% of each run, Pallas kernels for 27% -> 27%
where the time goes in v7:
time: 62.3 us; the launch traced here: 62.1 us
  Pallas kernels  27.7 us (44%)
  waiting for transfers between devices  17.6 us (28%)
  starting transfers between devices  16.1 us (26%)
  between operations  0.73 us (1%)
    pallas_call x17, Pallas kernels, call(): pl.pallas_call(body, out_shape=outs, scratch_shapes=list(scratch), input_...  26.4 us
    ppermute x16, waiting for transfers between devices, flip(): return lax.ppermute(value, axis, [(i, i ^ s) for i in range(n)])  17.6 us
    ppermute x16, starting transfers between devices, flip(): return lax.ppermute(value, axis, [(i, i ^ s) for i in range(n)])  16.1 us
    pallas_call x1, Pallas kernels, shards(): pl.pallas_call(functools.partial(pack_kernel, math.sqrt(2.0 / (features *...  1.3 us
  transfers between devices with their start and end apart: 16, of which 12 were waited for; matrix products, arithmetic and copies ran while one was open for 0% of the time, Pallas kernels for 27%

profile of v7, /device:TPU:0, one launch (start us, length us, event | category | flops | bytes accessed | tf_op | source)
XLA Modules:
  0.0 62.1 jit_solution(3037786207636803390)
XLA Ops:
  0.6 0.5 collective-permute-start
  1.1 1.3 %shard_map.86 = (bf16[528,128]{1,0:T(8,128)(2,1)S(1)}, bf16[128,2048]{1,0:T(8,128)(2,1)S(1)}, f32[1,2048]{1,0:T(1,128)S(1)}, f32[1,2048]{1,0:T(1,128)S(1)}, f32[...) custom-call(bf16[1024,128]{1,0:T(8,128)(2,1)} %x_hbm.1, bf16[128,2048]{1,0:T(8,128)(2,1)} %w_hbm.1, ...), custom_call_target="tpu_custom_call" | custom-call | tf_op jit(solution)/shard_map/pallas_call | solution.py:411
  2.5 0.0 collective-permute-done.other_label
  2.5 2.7 %collective-permute-start.3 = (bf16[528,128]{1,0:T(8,128)(2,1)S(1)}, bf16[528,128]{1,0:T(8,128)(2,1)S(1)}, u32[]{:S(2)}, u32[]{:S(2)}) collective-permute-start(bf16[528,128]{1,0:T(8,128)(2,1)S(1)} %shard_map.87.msg), channel_id=1, source_target_pairs={{0,2},{2,0},{4,6},{6,4},{1,3},{3,1},{5,7},{7,5},{8,10},{10,8},{12,... | collective-permute-start | bytes 405512 | tf_op jit(solution)/shard_map/ppermute | solution.py:81
  5.2 2.5 %collective-permute-start.2 = (bf16[528,128]{1,0:T(8,128)(2,1)S(1)}, bf16[528,128]{1,0:T(8,128)(2,1)S(1)}, u32[]{:S(2)}, u32[]{:S(2)}) collective-permute-start(bf16[528,128]{1,0:T(8,128)(2,1)S(1)} %shard_map.87.msg), channel_id=1, source_target_pairs={{0,6},{2,4},{4,2},{6,0},{1,7},{3,5},{5,3},{7,1},{8,14},{10,12},{12... | collective-permute-start | bytes 405512 | tf_op jit(solution)/shard_map/ppermute | solution.py:81
  7.7 0.1 collective-permute-start.1
  7.8 3.8 %shard_map.88 = (bf16[512,2048]{1,0:T(8,128)(2,1)S(1)}, f8e4m3fn[512,2048]{1,0:T(32,128)(4,1)S(1)}, bf16[2048,512]{1,0:T(8,128)(2,1)S(1)}, f8e4m3fn[2048,512]{1,...) custom-call(bf16[528,128]{1,0:T(8,128)(2,1)S(1)} %shard_map.87.msg, ...), custom_call_target="tpu_custom_call" | custom-call | flops 62914560 | bytes 667648 | tf_op jit(solution)/shard_map/pallas_call | solution.py:22
  11.6 0.0 collective-permute-done.3.msg
  11.6 3.8 %shard_map.89 = (bf16[512,2048]{1,0:T(8,128)(2,1)S(1)}, f8e4m3fn[512,2048]{1,0:T(32,128)(4,1)S(1)}, bf16[2048,512]{1,0:T(8,128)(2,1)S(1)}, f8e4m3fn[2048,512]{1,...) custom-call(bf16[528,128]{1,0:T(8,128)(2,1)S(1)} %collective-permute-done.3.msg, ...), custom_call_target="tpu_custom_call" | custom-call | flops 62914560 | bytes 700416 | tf_op jit(solution)/shard_map/pallas_call | solution.py:22
  15.4 0.0 collective-permute-done.2.msg
  15.4 3.8 %shard_map.90 = (bf16[512,2048]{1,0:T(8,128)(2,1)S(1)}, f8e4m3fn[512,2048]{1,0:T(32,128)(4,1)S(1)}, bf16[2048,512]{1,0:T(8,128)(2,1)S(1)}, f8e4m3fn[2048,512]{1,...) custom-call(bf16[528,128]{1,0:T(8,128)(2,1)S(1)} %collective-permute-done.2.msg, ...), custom_call_target="tpu_custom_call" | custom-call | flops 62914560 | bytes 700416 | tf_op jit(solution)/shard_map/pallas_call | solution.py:22
  19.2 1.2 %collective-permute-done.1.msg = bf16[528,128]{1,0:T(8,128)(2,1)S(1)} collective-permute-done((bf16[528,128]{1,0:T(8,128)(2,1)S(1)}, bf16[528,128]{1,0:T(8,128)(2,1)S(1)}, u32[]{:S(2)}, u32[]{:S(2)}) %collective-permute-start.1) | collective-permute-done | bytes 135200 | tf_op jit(solution)/shard_map/ppermute | solution.py:81
  20.4 4.0 %shard_map.91 = (bf16[512,2048]{1,0:T(8,128)(2,1)S(1)}, f8e4m3fn[512,2048]{1,0:T(32,128)(4,1)S(1)}, bf16[2048,512]{1,0:T(8,128)(2,1)S(1)}, f8e4m3fn[2048,512]{1,...) custom-call(bf16[528,128]{1,0:T(8,128)(2,1)S(1)} %collective-permute-done.1.msg, ...), custom_call_target="tpu_custom_call" | custom-call | flops 62914560 | bytes 700416 | tf_op jit(solution)/shard_map/pallas_call | solution.py:22
  24.3 0.0 collective-permute-start.4
  24.4 1.2 %collective-permute-done.4.refs_1_ = f32[4,2048]{1,0:T(4,128)S(1)} collective-permute-done((f32[4,2048]{1,0:T(4,128)S(1)}, f32[4,2048]{1,0:T(4,128)S(1)}, u32[]{:S(2)}, u32[]{:S(2)}) %collective-permute-start.4) | collective-permute-done | bytes 32800 | tf_op jit(solution)/shard_map/ppermute | solution.py:81
  25.6 1.4 %shard_map.92 = (f32[8,1664]{1,0:T(8,128)S(1)}, f32[8,2048]{1,0:T(8,128)S(1)}, f32[8,2048]{1,0:T(8,128)S(1)}, f32[8,2048]{1,0:T(8,128)S(1)}) custom-call(f32[4,2048]{1,0:T(4,128)S(1)} %get-tuple-element.76.refs_0_, f32[4,2048]{1,0:T(4,128)S(1)} %collective-permute-done.4.refs_1_, f32[8,1]{1,0:T(8,128)S(1)} %get-tuple-element.77.refs_2_.refs_3_.penalty, ...), custom_call_target="tpu_custom_call" | custom-call | flops 150994944 | bytes 9510944 | tf_op jit(solution)/shard_map/pallas_call | solution.py:22
  27.0 1.6 %collective-permute-start.6 = (f32[8,1664]{1,0:T(8,128)S(1)}, f32[8,1664]{1,0:T(8,128)S(1)}, u32[]{:S(2)}, u32[]{:S(2)}) collective-permute-start(f32[8,1664]{1,0:T(8,128)S(1)} %get-tuple-element.91.refs_0_), channel_id=1, source_target_pairs={{0,1},{1,0},{2,3},{3,2},{4,5},{5,4},{6,7},{7,6},{8,9},{9,8},{10,11... | collective-permute-start | bytes 159752 | tf_op jit(solution)/shard_map/ppermute | solution.py:81
  28.6 0.5 shard_map.93.refs_0_
  29.1 0.6 collective-permute-start.5
  29.7 1.5 %collective-permute-done.6.refs_1_ = f32[8,1664]{1,0:T(8,128)S(1)} collective-permute-done((f32[8,1664]{1,0:T(8,128)S(1)}, f32[8,1664]{1,0:T(8,128)S(1)}, u32[]{:S(2)}, u32[]{:S(2)}) %collective-permute-start.6) | collective-permute-done | bytes 53280 | tf_op jit(solution)/shard_map/ppermute | solution.py:81
  31.2 1.4 %shard_map.94 = (f32[8,2048]{1,0:T(8,128)S(1)}, f32[8,1536]{1,0:T(8,128)S(1)}, f32[8,128]{1,0:T(8,128)S(1)}) custom-call(f32[8,1664]{1,0:T(8,128)S(1)} %get-tuple-element.91.refs_0_, f32[8,1664]{1,0:T(8,128)S(1)} %collective-permute-done.6.refs_1_, f32[8,512]{1,0:T(8,128)S(1)} %get-tuple-element.92.refs_2_, f32[8,512]{1,0:T(8,128)S(1)} %get-tuple-element.93.refs_3_, ...), custom_call_target="tpu_custom_call" | custom-call | flops 150994944 | bytes 9592832 | tf_op jit(solution)/shard_map/pallas_call | solution.py:22
  32.6 0.3 collective-permute-done.5.refs_1_
  32.9 0.5 shard_map.95
  33.4 0.1 collective-permute-start.7
  33.5 1.2 %collective-permute-done.7.refs_1_ = f32[8,2176]{1,0:T(8,128)S(1)} collective-permute-done((f32[8,2176]{1,0:T(8,128)S(1)}, f32[8,2176]{1,0:T(8,128)S(1)}, u32[]{:S(2)}, u32[]{:S(2)}) %collective-permute-start.7) | collective-permute-done | bytes 69664 | tf_op jit(solution)/shard_map/ppermute | solution.py:81
  34.7 1.5 %shard_map.96 = (f32[8,1664]{1,0:T(8,128)S(1)}, f32[8,2048]{1,0:T(8,128)S(1)}, f32[8,2048]{1,0:T(8,128)S(1)}, f32[8,2048]{1,0:T(8,128)S(1)}, f32[8,2048]{1,0:T(8...) custom-call(f32[8,2176]{1,0:T(8,128)S(1)} %get-tuple-element.103.refs_0_, ...), custom_call_target="tpu_custom_call" | custom-call | flops 150994944 | bytes 9850912 | tf_op jit(solution)/shard_map/pallas_call | solution.py:22
  36.2 1.4 %collective-permute-start.9 = (f32[8,1664]{1,0:T(8,128)S(1)}, f32[8,1664]{1,0:T(8,128)S(1)}, u32[]{:S(2)}, u32[]{:S(2)}) collective-permute-start(f32[8,1664]{1,0:T(8,128)S(1)} %get-tuple-element.109.refs_0_), channel_id=1, source_target_pairs={{0,1},{1,0},{2,3},{3,2},{4,5},{5,4},{6,7},{7,6},{8,9},{9,8},{10,11... | collective-permute-start | bytes 159752 | tf_op jit(solution)/shard_map/ppermute | solution.py:81
  37.7 0.5 shard_map.97.refs_0_
  38.2 0.7 %collective-permute-start.8 = (f32[8,512]{1,0:T(8,128)S(1)}, f32[8,512]{1,0:T(8,128)S(1)}, u32[]{:S(2)}, u32[]{:S(2)}) collective-permute-start(f32[8,512]{1,0:T(8,128)S(1)} %shard_map.97.refs_0_), channel_id=1, source_target_pairs={{0,1},{1,0},{2,3},{3,2},{4,5},{5,4},{6,7},{7,6},{8,9},{9,8},{10,11... | collective-permute-start | bytes 49160 | tf_op jit(solution)/shard_map/ppermute | solution.py:81
  38.9 1.5 %collective-permute-done.9.refs_1_ = f32[8,1664]{1,0:T(8,128)S(1)} collective-permute-done((f32[8,1664]{1,0:T(8,128)S(1)}, f32[8,1664]{1,0:T(8,128)S(1)}, u32[]{:S(2)}, u32[]{:S(2)}) %collective-permute-start.9) | collective-permute-done | bytes 53280 | tf_op jit(solution)/shard_map/ppermute | solution.py:81
  40.4 1.4 %shard_map.98 = (f32[8,2048]{1,0:T(8,128)S(1)}, f32[8,1536]{1,0:T(8,128)S(1)}, f32[8,128]{1,0:T(8,128)S(1)}) custom-call(f32[8,1664]{1,0:T(8,128)S(1)} %get-tuple-element.109.refs_0_, f32[8,1664]{1,0:T(8,128)S(1)} %collective-permute-done.9.refs_1_, f32[8,512]{1,0:T(8,128)S(1)} %get-tuple-element.92.refs_2_, f32[8,512]{1,0:T(8,128)S(1)} %get-tuple-element.93.refs_3_, ...), custom_call_target="tpu_custom_call" | custom-call | flops 150994944 | bytes 9646080 | tf_op jit(solution)/shard_map/pallas_call | solution.py:22
  41.8 0.2 collective-permute-done.8.refs_1_
  42.0 0.6 shard_map.99
  42.6 0.1 collective-permute-start.10
  42.6 1.2 %collective-permute-done.10.refs_1_ = f32[8,2176]{1,0:T(8,128)S(1)} collective-permute-done((f32[8,2176]{1,0:T(8,128)S(1)}, f32[8,2176]{1,0:T(8,128)S(1)}, u32[]{:S(2)}, u32[]{:S(2)}) %collective-permute-start.10) | collective-permute-done | bytes 69664 | tf_op jit(solution)/shard_map/ppermute | solution.py:81
  43.9 1.9 %shard_map.100 = (f32[8,2176]{1,0:T(8,128)S(1)}, f32[8,2048]{1,0:T(8,128)S(1)}, f32[8,2048]{1,0:T(8,128)S(1)}, f32[8,2048]{1,0:T(8,128)S(1)}, f32[8,2048]{1,0:T(8,128)S(1)}, /*index=5*/f32[8,2048]{1,0:T(8,128)S(1)}) custom-call(f32[8,2176]{1,0:T(8,128)S(1)} %get-tuple-element.112.refs_0_, f32[8,2176]{1,0:T(8,128)S(1)} %collective-permute-done.10.refs_1_, ...), custom_call_target="tpu_custom_call" | custom-call | flops 150994944 | bytes 13328416 | tf_op jit(solution)/shard_map/pallas_call | solution.py:22
  45.8 1.5 %collective-permute-start.11 = (f32[8,2176]{1,0:T(8,128)S(1)}, f32[8,2176]{1,0:T(8,128)S(1)}, u32[]{:S(2)}, u32[]{:S(2)}) collective-permute-start(f32[8,2176]{1,0:T(8,128)S(1)} %get-tuple-element.121.refs_0_), channel_id=1, source_target_pairs={{0,1},{1,0},{2,3},{3,2},{4,5},{5,4},{6,7},{7,6},{8,9},{9,8},{10,11... | collective-permute-start | bytes 208904 | tf_op jit(solution)/shard_map/ppermute | solution.py:81
  47.3 2.9 %collective-permute-done.11.refs_1_ = f32[8,2176]{1,0:T(8,128)S(1)} collective-permute-done((f32[8,2176]{1,0:T(8,128)S(1)}, f32[8,2176]{1,0:T(8,128)S(1)}, u32[]{:S(2)}, u32[]{:S(2)}) %collective-permute-start.11) | collective-permute-done | bytes 69664 | tf_op jit(solution)/shard_map/ppermute | solution.py:81
  50.2 0.3 shard_map.101
  50.5 0.0 collective-permute-start.12
  50.6 1.2 %collective-permute-done.12.got = f32[8,2176]{1,0:T(8,128)S(1)} collective-permute-done((f32[8,2176]{1,0:T(8,128)S(1)}, f32[8,2176]{1,0:T(8,128)S(1)}, u32[]{:S(2)}, u32[]{:S(2)}) %collective-permute-start.12) | collective-permute-done | bytes 69664 | tf_op jit(solution)/shard_map/ppermute | solution.py:81
  51.8 0.2 shard_map.102
  52.0 3.5 %collective-permute-start.13 = (f32[4,3072]{1,0:T(4,128)S(1)}, f32[4,3072]{1,0:T(4,128)S(1)}, u32[]{:S(2)}, u32[]{:S(2)}) collective-permute-start(f32[4,3072]{1,0:T(4,128)S(1)} %get-tuple-element.131), channel_id=1, source_target_pairs={{0,4},{2,6},{4,0},{6,2},{1,5},{3,7},{5,1},{7,3},{8,12},{10,14},{12... | collective-permute-start | bytes 147464 | tf_op jit(solution)/shard_map/ppermute | solution.py:81
  55.5 0.9 %collective-permute-start.14 = (f32[4,3072]{1,0:T(4,128)S(1)}, f32[4,3072]{1,0:T(4,128)S(1)}, u32[]{:S(2)}, u32[]{:S(2)}) collective-permute-start(f32[4,3072]{1,0:T(4,128)S(1)} %get-tuple-element.132), channel_id=1, source_target_pairs={{0,6},{2,4},{4,2},{6,0},{1,7},{3,5},{5,3},{7,1},{8,14},{10,12},{12... | collective-permute-start | bytes 147464 | tf_op jit(solution)/shard_map/ppermute | solution.py:81
  56.4 0.0 collective-permute-start.15
  56.4 2.6 %collective-permute-done.13.refs_1_ = f32[4,3072]{1,0:T(4,128)S(1)} collective-permute-done((f32[4,3072]{1,0:T(4,128)S(1)}, f32[4,3072]{1,0:T(4,128)S(1)}, u32[]{:S(2)}, u32[]{:S(2)}) %collective-permute-start.13) | collective-permute-done | bytes 49184 | tf_op jit(solution)/shard_map/ppermute | solution.py:81
  59.0 2.4 %collective-permute-done.14.refs_2_ = f32[4,3072]{1,0:T(4,128)S(1)} collective-permute-done((f32[4,3072]{1,0:T(4,128)S(1)}, f32[4,3072]{1,0:T(4,128)S(1)}, u32[]{:S(2)}, u32[]{:S(2)}) %collective-permute-start.14) | collective-permute-done | bytes 49184 | tf_op jit(solution)/shard_map/ppermute | solution.py:81
  61.4 0.7 %shard_map.103 = (f32[16,2048]{1,0:T(8,128)}, f32[16,1024]{1,0:T(8,128)}) custom-call(f32[4,3072]{1,0:T(4,128)S(1)} %get-tuple-element.130.refs_0_, f32[4,3072]{1,0:T(4,128)S(1)} %collective-permute-done.13.refs_1_, f32[4,3072]{1,0:T(4,128)S(1)} %collective-permute-done.14.refs_2_, f32[4,3072]{1,0:T(4,128)S(1)} %collective-permute-done.15.refs_3_), custom_call_target="tpu_custom_call" | custom-call | bytes 196608 | tf_op jit(solution)/shard_map/pallas_call | solution.py:22
  (2 shorter events, 0.0 us)
Async XLA Ops:
  0.6 1.8 %collective-permute-start = (s32[8,128]{1,0:T(8,128)}, s32[8,128]{1,0:T(8,128)S(1)}, u32[]{:S(2)}, u32[]{:S(2)}) collective-permute-start(s32[8,128]{1,0:T(8,128)} %bitcast.8), channel_id=1, source_target_pairs={{0,8},{8,0},{16,24},{24,16},{1,9},{9,1},{17,25},{25,17},{2,10},{10... | collective-permute-start | bytes 12296 | tf_op jit(solution)/shard_map/ppermute | solution.py:81
  2.5 9.1 %collective-permute-start.3 = (bf16[528,128]{1,0:T(8,128)(2,1)S(1)}, bf16[528,128]{1,0:T(8,128)(2,1)S(1)}, u32[]{:S(2)}, u32[]{:S(2)}) collective-permute-start(bf16[528,128]{1,0:T(8,128)(2,1)S(1)} %shard_map.87.msg), channel_id=1, source_target_pairs={{0,2},{2,0},{4,6},{6,4},{1,3},{3,1},{5,7},{7,5},{8,10},{10,8},{12,... | collective-permute-start | bytes 405512 | tf_op jit(solution)/shard_map/ppermute | solution.py:81
  5.2 10.2 %collective-permute-start.2 = (bf16[528,128]{1,0:T(8,128)(2,1)S(1)}, bf16[528,128]{1,0:T(8,128)(2,1)S(1)}, u32[]{:S(2)}, u32[]{:S(2)}) collective-permute-start(bf16[528,128]{1,0:T(8,128)(2,1)S(1)} %shard_map.87.msg), channel_id=1, source_target_pairs={{0,6},{2,4},{4,2},{6,0},{1,7},{3,5},{5,3},{7,1},{8,14},{10,12},{12... | collective-permute-start | bytes 405512 | tf_op jit(solution)/shard_map/ppermute | solution.py:81
  7.7 12.7 %collective-permute-start.1 = (bf16[528,128]{1,0:T(8,128)(2,1)S(1)}, bf16[528,128]{1,0:T(8,128)(2,1)S(1)}, u32[]{:S(2)}, u32[]{:S(2)}) collective-permute-start(bf16[528,128]{1,0:T(8,128)(2,1)S(1)} %shard_map.87.msg), channel_id=1, source_target_pairs={{0,4},{2,6},{4,0},{6,2},{1,5},{3,7},{5,1},{7,3},{8,12},{10,14},{12... | collective-permute-start | bytes 405512 | tf_op jit(solution)/shard_map/ppermute | solution.py:81
  24.3 1.2 %collective-permute-start.4 = (f32[4,2048]{1,0:T(4,128)S(1)}, f32[4,2048]{1,0:T(4,128)S(1)}, u32[]{:S(2)}, u32[]{:S(2)}) collective-permute-start(f32[4,2048]{1,0:T(4,128)S(1)} %get-tuple-element.76.refs_0_), channel_id=1, source_target_pairs={{0,8},{8,0},{16,24},{24,16},{1,9},{9,1},{17,25},{25,17},{2,10},{10... | collective-permute-start | bytes 98312 | tf_op jit(solution)/shard_map/ppermute | solution.py:81
  27.0 4.2 %collective-permute-start.6 = (f32[8,1664]{1,0:T(8,128)S(1)}, f32[8,1664]{1,0:T(8,128)S(1)}, u32[]{:S(2)}, u32[]{:S(2)}) collective-permute-start(f32[8,1664]{1,0:T(8,128)S(1)} %get-tuple-element.91.refs_0_), channel_id=1, source_target_pairs={{0,1},{1,0},{2,3},{3,2},{4,5},{5,4},{6,7},{7,6},{8,9},{9,8},{10,11... | collective-permute-start | bytes 159752 | tf_op jit(solution)/shard_map/ppermute | solution.py:81
  29.1 3.8 %collective-permute-start.5 = (f32[8,512]{1,0:T(8,128)S(1)}, f32[8,512]{1,0:T(8,128)S(1)}, u32[]{:S(2)}, u32[]{:S(2)}) collective-permute-start(f32[8,512]{1,0:T(8,128)S(1)} %shard_map.93.refs_0_), channel_id=1, source_target_pairs={{0,1},{1,0},{2,3},{3,2},{4,5},{5,4},{6,7},{7,6},{8,9},{9,8},{10,11... | collective-permute-start | bytes 49160 | tf_op jit(solution)/shard_map/ppermute | solution.py:81
  33.4 1.3 %collective-permute-start.7 = (f32[8,2176]{1,0:T(8,128)S(1)}, f32[8,2176]{1,0:T(8,128)S(1)}, u32[]{:S(2)}, u32[]{:S(2)}) collective-permute-start(f32[8,2176]{1,0:T(8,128)S(1)} %get-tuple-element.103.refs_0_), channel_id=1, source_target_pairs={{0,8},{8,0},{16,24},{24,16},{1,9},{9,1},{17,25},{25,17},{2,10},{10... | collective-permute-start | bytes 208904 | tf_op jit(solution)/shard_map/ppermute | solution.py:81
  36.2 4.2 %collective-permute-start.9 = (f32[8,1664]{1,0:T(8,128)S(1)}, f32[8,1664]{1,0:T(8,128)S(1)}, u32[]{:S(2)}, u32[]{:S(2)}) collective-permute-start(f32[8,1664]{1,0:T(8,128)S(1)} %get-tuple-element.109.refs_0_), channel_id=1, source_target_pairs={{0,1},{1,0},{2,3},{3,2},{4,5},{5,4},{6,7},{7,6},{8,9},{9,8},{10,11... | collective-permute-start | bytes 159752 | tf_op jit(solution)/shard_map/ppermute | solution.py:81
  38.2 3.8 %collective-permute-start.8 = (f32[8,512]{1,0:T(8,128)S(1)}, f32[8,512]{1,0:T(8,128)S(1)}, u32[]{:S(2)}, u32[]{:S(2)}) collective-permute-start(f32[8,512]{1,0:T(8,128)S(1)} %shard_map.97.refs_0_), channel_id=1, source_target_pairs={{0,1},{1,0},{2,3},{3,2},{4,5},{5,4},{6,7},{7,6},{8,9},{9,8},{10,11... | collective-permute-start | bytes 49160 | tf_op jit(solution)/shard_map/ppermute | solution.py:81
  42.6 1.3 %collective-permute-start.10 = (f32[8,2176]{1,0:T(8,128)S(1)}, f32[8,2176]{1,0:T(8,128)S(1)}, u32[]{:S(2)}, u32[]{:S(2)}) collective-permute-start(f32[8,2176]{1,0:T(8,128)S(1)} %get-tuple-element.112.refs_0_), channel_id=1, source_target_pairs={{0,8},{8,0},{16,24},{24,16},{1,9},{9,1},{17,25},{25,17},{2,10},{10... | collective-permute-start | bytes 208904 | tf_op jit(solution)/shard_map/ppermute | solution.py:81
  45.8 4.4 %collective-permute-start.11 = (f32[8,2176]{1,0:T(8,128)S(1)}, f32[8,2176]{1,0:T(8,128)S(1)}, u32[]{:S(2)}, u32[]{:S(2)}) collective-permute-start(f32[8,2176]{1,0:T(8,128)S(1)} %get-tuple-element.121.refs_0_), channel_id=1, source_target_pairs={{0,1},{1,0},{2,3},{3,2},{4,5},{5,4},{6,7},{7,6},{8,9},{9,8},{10,11... | collective-permute-start | bytes 208904 | tf_op jit(solution)/shard_map/ppermute | solution.py:81
  50.5 1.3 %collective-permute-start.12 = (f32[8,2176]{1,0:T(8,128)S(1)}, f32[8,2176]{1,0:T(8,128)S(1)}, u32[]{:S(2)}, u32[]{:S(2)}) collective-permute-start(f32[8,2176]{1,0:T(8,128)S(1)} %get-tuple-element.124.own), channel_id=1, source_target_pairs={{0,8},{8,0},{16,24},{24,16},{1,9},{9,1},{17,25},{25,17},{2,10},{10... | collective-permute-start | bytes 208904 | tf_op jit(solution)/shard_map/ppermute | solution.py:81
  52.0 7.0 %collective-permute-start.13 = (f32[4,3072]{1,0:T(4,128)S(1)}, f32[4,3072]{1,0:T(4,128)S(1)}, u32[]{:S(2)}, u32[]{:S(2)}) collective-permute-start(f32[4,3072]{1,0:T(4,128)S(1)} %get-tuple-element.131), channel_id=1, source_target_pairs={{0,4},{2,6},{4,0},{6,2},{1,5},{3,7},{5,1},{7,3},{8,12},{10,14},{12... | collective-permute-start | bytes 147464 | tf_op jit(solution)/shard_map/ppermute | solution.py:81
  55.5 5.9 %collective-permute-start.14 = (f32[4,3072]{1,0:T(4,128)S(1)}, f32[4,3072]{1,0:T(4,128)S(1)}, u32[]{:S(2)}, u32[]{:S(2)}) collective-permute-start(f32[4,3072]{1,0:T(4,128)S(1)} %get-tuple-element.132), channel_id=1, source_target_pairs={{0,6},{2,4},{4,2},{6,0},{1,7},{3,5},{5,3},{7,1},{8,14},{10,12},{12... | collective-permute-start | bytes 147464 | tf_op jit(solution)/shard_map/ppermute | solution.py:81
  56.4 5.0 %collective-permute-start.15 = (f32[4,3072]{1,0:T(4,128)S(1)}, f32[4,3072]{1,0:T(4,128)S(1)}, u32[]{:S(2)}, u32[]{:S(2)}) collective-permute-start(f32[4,3072]{1,0:T(4,128)S(1)} %get-tuple-element.133), channel_id=1, source_target_pairs={{0,2},{2,0},{4,6},{6,4},{1,3},{3,1},{5,7},{7,5},{8,10},{10,8},{12,... | collective-permute-start | bytes 147464 | tf_op jit(solution)/shard_map/ppermute | solution.py:81

commit v8 on v7

--- a/solution.py
+++ b/solution.py
@@ -429,7 +429,7 @@
         functools.partial(label_kernel, half), [packed], msg, label, other_label, response, aliases={0: 0}
     )
 
-    order = [j ^ (j >> 1) for j in range(nz)]
+    order = [0] + [j for i in range(1, nz // 2 + 1) for j in sorted({nz - i, i}, reverse=True)]
     blocks, turned, kepts, moments = [], [], [], None
     shapes = (half, features), (features, half)
     tiles = [(shape, kind) for shape in shapes for kind in (bf16, f8)]
@@ -494,7 +494,7 @@
         [((rows // 2, features + shard), f32)] * nz,
         msg, flip(msg, "fold", nf, 1), sc, penalty, scaled, before, weights, image_rows, predicted,
     )
-    far_first = [0] + sorted(range(1, nz), key=lambda j: -j.bit_length())
+    far_first = [0, *range(nz - 1, 0, -1)]
     outs = [flip(outs[order.index(j)], "samp", nz, j) if j else outs[0] for j in far_first]
     return call(
         functools.partial(arrange_kernel, far_first),

time: 62.3 us -> 61.2 us (0.982)
  waiting for transfers between devices: 17.6 us -> 16.3 us
    ppermute x16, waiting for transfers between devices: 17.6 us -> 16.3 us  [flip(): return lax.ppermute(value, axis, [(i, i ^ s) for i in range(n)])]
  transfers between devices with their start and end apart: 16 -> 16, of which waited for: 12 -> 10; matrix products, arithmetic and copies ran while one was open for 0% -> 0% of each run, Pallas kernels for 27% -> 27%
where the time goes in v8:
time: 61.2 us; the launch traced here: 61 us
  Pallas kernels  27.7 us (45%)
  starting transfers between devices  16.3 us (27%)
  waiting for transfers between devices  16.3 us (27%)
  between operations  0.73 us (1%)
    pallas_call x17, Pallas kernels, call(): pl.pallas_call(body, out_shape=outs, scratch_shapes=list(scratch), input_...  26.4 us
    ppermute x16, waiting for transfers between devices, flip(): return lax.ppermute(value, axis, [(i, i ^ s) for i in range(n)])  16.3 us
    ppermute x16, starting transfers between devices, flip(): return lax.ppermute(value, axis, [(i, i ^ s) for i in range(n)])  16.3 us
    pallas_call x1, Pallas kernels, shards(): pl.pallas_call(functools.partial(pack_kernel, math.sqrt(2.0 / (features *...  1.3 us
  transfers between devices with their start and end apart: 16, of which 10 were waited for; matrix products, arithmetic and copies ran while one was open for 0% of the time, Pallas kernels for 27%

profile of v8, /device:TPU:0, one launch (start us, length us, event | category | flops | bytes accessed | tf_op | source)
XLA Modules:
  0.0 61.0 jit_solution(13918340853096348126)
XLA Ops:
  0.6 0.5 collective-permute-start
  1.1 1.3 %shard_map.86 = (bf16[528,128]{1,0:T(8,128)(2,1)S(1)}, bf16[128,2048]{1,0:T(8,128)(2,1)S(1)}, f32[1,2048]{1,0:T(1,128)S(1)}, f32[1,2048]{1,0:T(1,128)S(1)}, f32[...) custom-call(bf16[1024,128]{1,0:T(8,128)(2,1)} %x_hbm.1, bf16[128,2048]{1,0:T(8,128)(2,1)} %w_hbm.1, ...), custom_call_target="tpu_custom_call" | custom-call | tf_op jit(solution)/shard_map/pallas_call | solution.py:411
  2.5 0.0 collective-permute-done.other_label
  2.5 4.7 %collective-permute-start.3 = (bf16[528,128]{1,0:T(8,128)(2,1)S(1)}, bf16[528,128]{1,0:T(8,128)(2,1)S(1)}, u32[]{:S(2)}, u32[]{:S(2)}) collective-permute-start(bf16[528,128]{1,0:T(8,128)(2,1)S(1)} %shard_map.87.msg), channel_id=1, source_target_pairs={{0,6},{2,4},{4,2},{6,0},{1,7},{3,5},{5,3},{7,1},{8,14},{10,12},{12... | collective-permute-start | bytes 405512 | tf_op jit(solution)/shard_map/ppermute | solution.py:81
  7.2 0.0 collective-permute-start.2
  7.2 0.6 %collective-permute-start.1 = (bf16[528,128]{1,0:T(8,128)(2,1)S(1)}, bf16[528,128]{1,0:T(8,128)(2,1)S(1)}, u32[]{:S(2)}, u32[]{:S(2)}) collective-permute-start(bf16[528,128]{1,0:T(8,128)(2,1)S(1)} %shard_map.87.msg), channel_id=1, source_target_pairs={{0,4},{2,6},{4,0},{6,2},{1,5},{3,7},{5,1},{7,3},{8,12},{10,14},{12... | collective-permute-start | bytes 405512 | tf_op jit(solution)/shard_map/ppermute | solution.py:81
  7.8 3.8 %shard_map.88 = (bf16[512,2048]{1,0:T(8,128)(2,1)S(1)}, f8e4m3fn[512,2048]{1,0:T(32,128)(4,1)S(1)}, bf16[2048,512]{1,0:T(8,128)(2,1)S(1)}, f8e4m3fn[2048,512]{1,...) custom-call(bf16[528,128]{1,0:T(8,128)(2,1)S(1)} %shard_map.87.msg, ...), custom_call_target="tpu_custom_call" | custom-call | flops 62914560 | bytes 667648 | tf_op jit(solution)/shard_map/pallas_call | solution.py:22
  11.6 0.0 collective-permute-done.3.msg
  11.7 3.8 %shard_map.89 = (bf16[512,2048]{1,0:T(8,128)(2,1)S(1)}, f8e4m3fn[512,2048]{1,0:T(32,128)(4,1)S(1)}, bf16[2048,512]{1,0:T(8,128)(2,1)S(1)}, f8e4m3fn[2048,512]{1,...) custom-call(bf16[528,128]{1,0:T(8,128)(2,1)S(1)} %collective-permute-done.3.msg, ...), custom_call_target="tpu_custom_call" | custom-call | flops 62914560 | bytes 700416 | tf_op jit(solution)/shard_map/pallas_call | solution.py:22
  15.5 0.0 collective-permute-done.2.msg
  15.5 3.8 %shard_map.90 = (bf16[512,2048]{1,0:T(8,128)(2,1)S(1)}, f8e4m3fn[512,2048]{1,0:T(32,128)(4,1)S(1)}, bf16[2048,512]{1,0:T(8,128)(2,1)S(1)}, f8e4m3fn[2048,512]{1,...) custom-call(bf16[528,128]{1,0:T(8,128)(2,1)S(1)} %collective-permute-done.2.msg, ...), custom_call_target="tpu_custom_call" | custom-call | flops 62914560 | bytes 700416 | tf_op jit(solution)/shard_map/pallas_call | solution.py:22
  19.3 0.0 collective-permute-done.1.msg
  19.3 4.0 %shard_map.91 = (bf16[512,2048]{1,0:T(8,128)(2,1)S(1)}, f8e4m3fn[512,2048]{1,0:T(32,128)(4,1)S(1)}, bf16[2048,512]{1,0:T(8,128)(2,1)S(1)}, f8e4m3fn[2048,512]{1,...) custom-call(bf16[528,128]{1,0:T(8,128)(2,1)S(1)} %collective-permute-done.1.msg, ...), custom_call_target="tpu_custom_call" | custom-call | flops 62914560 | bytes 700416 | tf_op jit(solution)/shard_map/pallas_call | solution.py:22
  23.3 0.0 collective-permute-start.4
  23.4 1.2 %collective-permute-done.4.refs_1_ = f32[4,2048]{1,0:T(4,128)S(1)} collective-permute-done((f32[4,2048]{1,0:T(4,128)S(1)}, f32[4,2048]{1,0:T(4,128)S(1)}, u32[]{:S(2)}, u32[]{:S(2)}) %collective-permute-start.4) | collective-permute-done | bytes 32800 | tf_op jit(solution)/shard_map/ppermute | solution.py:81
  24.5 1.4 %shard_map.92 = (f32[8,1664]{1,0:T(8,128)S(1)}, f32[8,2048]{1,0:T(8,128)S(1)}, f32[8,2048]{1,0:T(8,128)S(1)}, f32[8,2048]{1,0:T(8,128)S(1)}) custom-call(f32[4,2048]{1,0:T(4,128)S(1)} %get-tuple-element.76.refs_0_, f32[4,2048]{1,0:T(4,128)S(1)} %collective-permute-done.4.refs_1_, f32[8,1]{1,0:T(8,128)S(1)} %get-tuple-element.77.refs_2_.refs_3_.penalty, ...), custom_call_target="tpu_custom_call" | custom-call | flops 150994944 | bytes 9510944 | tf_op jit(solution)/shard_map/pallas_call | solution.py:22
  25.9 1.7 %collective-permute-start.6 = (f32[8,1664]{1,0:T(8,128)S(1)}, f32[8,1664]{1,0:T(8,128)S(1)}, u32[]{:S(2)}, u32[]{:S(2)}) collective-permute-start(f32[8,1664]{1,0:T(8,128)S(1)} %get-tuple-element.91.refs_0_), channel_id=1, source_target_pairs={{0,1},{1,0},{2,3},{3,2},{4,5},{5,4},{6,7},{7,6},{8,9},{9,8},{10,11... | collective-permute-start | bytes 159752 | tf_op jit(solution)/shard_map/ppermute | solution.py:81
  27.7 0.5 shard_map.93.refs_0_
  28.2 0.4 collective-permute-start.5
  28.6 1.5 %collective-permute-done.6.refs_1_ = f32[8,1664]{1,0:T(8,128)S(1)} collective-permute-done((f32[8,1664]{1,0:T(8,128)S(1)}, f32[8,1664]{1,0:T(8,128)S(1)}, u32[]{:S(2)}, u32[]{:S(2)}) %collective-permute-start.6) | collective-permute-done | bytes 53280 | tf_op jit(solution)/shard_map/ppermute | solution.py:81
  30.1 1.4 %shard_map.94 = (f32[8,2048]{1,0:T(8,128)S(1)}, f32[8,1536]{1,0:T(8,128)S(1)}, f32[8,128]{1,0:T(8,128)S(1)}) custom-call(f32[8,1664]{1,0:T(8,128)S(1)} %get-tuple-element.91.refs_0_, f32[8,1664]{1,0:T(8,128)S(1)} %collective-permute-done.6.refs_1_, f32[8,512]{1,0:T(8,128)S(1)} %get-tuple-element.92.refs_2_, f32[8,512]{1,0:T(8,128)S(1)} %get-tuple-element.93.refs_3_, ...), custom_call_target="tpu_custom_call" | custom-call | flops 150994944 | bytes 9592832 | tf_op jit(solution)/shard_map/pallas_call | solution.py:22
  31.5 0.5 collective-permute-done.5.refs_1_
  32.0 0.5 shard_map.95
  32.5 0.1 collective-permute-start.7
  32.6 1.2 %collective-permute-done.7.refs_1_ = f32[8,2176]{1,0:T(8,128)S(1)} collective-permute-done((f32[8,2176]{1,0:T(8,128)S(1)}, f32[8,2176]{1,0:T(8,128)S(1)}, u32[]{:S(2)}, u32[]{:S(2)}) %collective-permute-start.7) | collective-permute-done | bytes 69664 | tf_op jit(solution)/shard_map/ppermute | solution.py:81
  33.8 1.5 %shard_map.96 = (f32[8,1664]{1,0:T(8,128)S(1)}, f32[8,2048]{1,0:T(8,128)S(1)}, f32[8,2048]{1,0:T(8,128)S(1)}, f32[8,2048]{1,0:T(8,128)S(1)}, f32[8,2048]{1,0:T(8...) custom-call(f32[8,2176]{1,0:T(8,128)S(1)} %get-tuple-element.103.refs_0_, ...), custom_call_target="tpu_custom_call" | custom-call | flops 150994944 | bytes 9850912 | tf_op jit(solution)/shard_map/pallas_call | solution.py:22
  35.3 1.3 %collective-permute-start.9 = (f32[8,1664]{1,0:T(8,128)S(1)}, f32[8,1664]{1,0:T(8,128)S(1)}, u32[]{:S(2)}, u32[]{:S(2)}) collective-permute-start(f32[8,1664]{1,0:T(8,128)S(1)} %get-tuple-element.109.refs_0_), channel_id=1, source_target_pairs={{0,1},{1,0},{2,3},{3,2},{4,5},{5,4},{6,7},{7,6},{8,9},{9,8},{10,11... | collective-permute-start | bytes 159752 | tf_op jit(solution)/shard_map/ppermute | solution.py:81
  36.6 0.5 shard_map.97.refs_0_
  37.1 0.9 %collective-permute-start.8 = (f32[8,512]{1,0:T(8,128)S(1)}, f32[8,512]{1,0:T(8,128)S(1)}, u32[]{:S(2)}, u32[]{:S(2)}) collective-permute-start(f32[8,512]{1,0:T(8,128)S(1)} %shard_map.97.refs_0_), channel_id=1, source_target_pairs={{0,1},{1,0},{2,3},{3,2},{4,5},{5,4},{6,7},{7,6},{8,9},{9,8},{10,11... | collective-permute-start | bytes 49160 | tf_op jit(solution)/shard_map/ppermute | solution.py:81
  38.0 1.5 %collective-permute-done.9.refs_1_ = f32[8,1664]{1,0:T(8,128)S(1)} collective-permute-done((f32[8,1664]{1,0:T(8,128)S(1)}, f32[8,1664]{1,0:T(8,128)S(1)}, u32[]{:S(2)}, u32[]{:S(2)}) %collective-permute-start.9) | collective-permute-done | bytes 53280 | tf_op jit(solution)/shard_map/ppermute | solution.py:81
  39.5 1.4 %shard_map.98 = (f32[8,2048]{1,0:T(8,128)S(1)}, f32[8,1536]{1,0:T(8,128)S(1)}, f32[8,128]{1,0:T(8,128)S(1)}) custom-call(f32[8,1664]{1,0:T(8,128)S(1)} %get-tuple-element.109.refs_0_, f32[8,1664]{1,0:T(8,128)S(1)} %collective-permute-done.9.refs_1_, f32[8,512]{1,0:T(8,128)S(1)} %get-tuple-element.92.refs_2_, f32[8,512]{1,0:T(8,128)S(1)} %get-tuple-element.93.refs_3_, ...), custom_call_target="tpu_custom_call" | custom-call | flops 150994944 | bytes 9646080 | tf_op jit(solution)/shard_map/pallas_call | solution.py:22
  40.9 0.0 collective-permute-done.8.refs_1_
  40.9 0.6 shard_map.99
  41.5 0.1 collective-permute-start.10
  41.6 1.2 %collective-permute-done.10.refs_1_ = f32[8,2176]{1,0:T(8,128)S(1)} collective-permute-done((f32[8,2176]{1,0:T(8,128)S(1)}, f32[8,2176]{1,0:T(8,128)S(1)}, u32[]{:S(2)}, u32[]{:S(2)}) %collective-permute-start.10) | collective-permute-done | bytes 69664 | tf_op jit(solution)/shard_map/ppermute | solution.py:81
  42.9 1.9 %shard_map.100 = (f32[8,2176]{1,0:T(8,128)S(1)}, f32[8,2048]{1,0:T(8,128)S(1)}, f32[8,2048]{1,0:T(8,128)S(1)}, f32[8,2048]{1,0:T(8,128)S(1)}, f32[8,2048]{1,0:T(8,128)S(1)}, /*index=5*/f32[8,2048]{1,0:T(8,128)S(1)}) custom-call(f32[8,2176]{1,0:T(8,128)S(1)} %get-tuple-element.112.refs_0_, f32[8,2176]{1,0:T(8,128)S(1)} %collective-permute-done.10.refs_1_, ...), custom_call_target="tpu_custom_call" | custom-call | flops 150994944 | bytes 13328416 | tf_op jit(solution)/shard_map/pallas_call | solution.py:22
  44.8 1.5 %collective-permute-start.11 = (f32[8,2176]{1,0:T(8,128)S(1)}, f32[8,2176]{1,0:T(8,128)S(1)}, u32[]{:S(2)}, u32[]{:S(2)}) collective-permute-start(f32[8,2176]{1,0:T(8,128)S(1)} %get-tuple-element.121.refs_0_), channel_id=1, source_target_pairs={{0,1},{1,0},{2,3},{3,2},{4,5},{5,4},{6,7},{7,6},{8,9},{9,8},{10,11... | collective-permute-start | bytes 208904 | tf_op jit(solution)/shard_map/ppermute | solution.py:81
  46.3 2.9 %collective-permute-done.11.refs_1_ = f32[8,2176]{1,0:T(8,128)S(1)} collective-permute-done((f32[8,2176]{1,0:T(8,128)S(1)}, f32[8,2176]{1,0:T(8,128)S(1)}, u32[]{:S(2)}, u32[]{:S(2)}) %collective-permute-start.11) | collective-permute-done | bytes 69664 | tf_op jit(solution)/shard_map/ppermute | solution.py:81
  49.2 0.3 shard_map.101
  49.5 0.0 collective-permute-start.12
  49.5 1.2 %collective-permute-done.12.got = f32[8,2176]{1,0:T(8,128)S(1)} collective-permute-done((f32[8,2176]{1,0:T(8,128)S(1)}, f32[8,2176]{1,0:T(8,128)S(1)}, u32[]{:S(2)}, u32[]{:S(2)}) %collective-permute-start.12) | collective-permute-done | bytes 69664 | tf_op jit(solution)/shard_map/ppermute | solution.py:81
  50.8 0.2 shard_map.102
  51.0 3.8 %collective-permute-start.13 = (f32[4,3072]{1,0:T(4,128)S(1)}, f32[4,3072]{1,0:T(4,128)S(1)}, u32[]{:S(2)}, u32[]{:S(2)}) collective-permute-start(f32[4,3072]{1,0:T(4,128)S(1)} %get-tuple-element.131), channel_id=1, source_target_pairs={{0,6},{2,4},{4,2},{6,0},{1,7},{3,5},{5,3},{7,1},{8,14},{10,12},{12... | collective-permute-start | bytes 147464 | tf_op jit(solution)/shard_map/ppermute | solution.py:81
  54.8 0.5 collective-permute-start.14
  55.3 0.2 collective-permute-start.15
  55.4 1.6 %collective-permute-done.13.refs_1_ = f32[4,3072]{1,0:T(4,128)S(1)} collective-permute-done((f32[4,3072]{1,0:T(4,128)S(1)}, f32[4,3072]{1,0:T(4,128)S(1)}, u32[]{:S(2)}, u32[]{:S(2)}) %collective-permute-start.13) | collective-permute-done | bytes 49184 | tf_op jit(solution)/shard_map/ppermute | solution.py:81
  57.0 3.3 %collective-permute-done.14.refs_2_ = f32[4,3072]{1,0:T(4,128)S(1)} collective-permute-done((f32[4,3072]{1,0:T(4,128)S(1)}, f32[4,3072]{1,0:T(4,128)S(1)}, u32[]{:S(2)}, u32[]{:S(2)}) %collective-permute-start.14) | collective-permute-done | bytes 49184 | tf_op jit(solution)/shard_map/ppermute | solution.py:81
  60.3 0.7 %shard_map.103 = (f32[16,2048]{1,0:T(8,128)}, f32[16,1024]{1,0:T(8,128)}) custom-call(f32[4,3072]{1,0:T(4,128)S(1)} %get-tuple-element.130.refs_0_, f32[4,3072]{1,0:T(4,128)S(1)} %collective-permute-done.13.refs_1_, f32[4,3072]{1,0:T(4,128)S(1)} %collective-permute-done.14.refs_2_, f32[4,3072]{1,0:T(4,128)S(1)} %collective-permute-done.15.refs_3_), custom_call_target="tpu_custom_call" | custom-call | bytes 196608 | tf_op jit(solution)/shard_map/pallas_call | solution.py:22
  (2 shorter events, 0.0 us)
Async XLA Ops:
  0.6 1.8 %collective-permute-start = (s32[8,128]{1,0:T(8,128)}, s32[8,128]{1,0:T(8,128)S(1)}, u32[]{:S(2)}, u32[]{:S(2)}) collective-permute-start(s32[8,128]{1,0:T(8,128)} %bitcast.8), channel_id=1, source_target_pairs={{0,8},{8,0},{16,24},{24,16},{1,9},{9,1},{17,25},{25,17},{2,10},{10... | collective-permute-start | bytes 12296 | tf_op jit(solution)/shard_map/ppermute | solution.py:81
  2.5 9.2 %collective-permute-start.3 = (bf16[528,128]{1,0:T(8,128)(2,1)S(1)}, bf16[528,128]{1,0:T(8,128)(2,1)S(1)}, u32[]{:S(2)}, u32[]{:S(2)}) collective-permute-start(bf16[528,128]{1,0:T(8,128)(2,1)S(1)} %shard_map.87.msg), channel_id=1, source_target_pairs={{0,6},{2,4},{4,2},{6,0},{1,7},{3,5},{5,3},{7,1},{8,14},{10,12},{12... | collective-permute-start | bytes 405512 | tf_op jit(solution)/shard_map/ppermute | solution.py:81
  7.2 8.3 %collective-permute-start.2 = (bf16[528,128]{1,0:T(8,128)(2,1)S(1)}, bf16[528,128]{1,0:T(8,128)(2,1)S(1)}, u32[]{:S(2)}, u32[]{:S(2)}) collective-permute-start(bf16[528,128]{1,0:T(8,128)(2,1)S(1)} %shard_map.87.msg), channel_id=1, source_target_pairs={{0,2},{2,0},{4,6},{6,4},{1,3},{3,1},{5,7},{7,5},{8,10},{10,8},{12,... | collective-permute-start | bytes 405512 | tf_op jit(solution)/shard_map/ppermute | solution.py:81
  7.2 12.1 %collective-permute-start.1 = (bf16[528,128]{1,0:T(8,128)(2,1)S(1)}, bf16[528,128]{1,0:T(8,128)(2,1)S(1)}, u32[]{:S(2)}, u32[]{:S(2)}) collective-permute-start(bf16[528,128]{1,0:T(8,128)(2,1)S(1)} %shard_map.87.msg), channel_id=1, source_target_pairs={{0,4},{2,6},{4,0},{6,2},{1,5},{3,7},{5,1},{7,3},{8,12},{10,14},{12... | collective-permute-start | bytes 405512 | tf_op jit(solution)/shard_map/ppermute | solution.py:81
  23.3 1.2 %collective-permute-start.4 = (f32[4,2048]{1,0:T(4,128)S(1)}, f32[4,2048]{1,0:T(4,128)S(1)}, u32[]{:S(2)}, u32[]{:S(2)}) collective-permute-start(f32[4,2048]{1,0:T(4,128)S(1)} %get-tuple-element.76.refs_0_), channel_id=1, source_target_pairs={{0,8},{8,0},{16,24},{24,16},{1,9},{9,1},{17,25},{25,17},{2,10},{10... | collective-permute-start | bytes 98312 | tf_op jit(solution)/shard_map/ppermute | solution.py:81
  25.9 4.2 %collective-permute-start.6 = (f32[8,1664]{1,0:T(8,128)S(1)}, f32[8,1664]{1,0:T(8,128)S(1)}, u32[]{:S(2)}, u32[]{:S(2)}) collective-permute-start(f32[8,1664]{1,0:T(8,128)S(1)} %get-tuple-element.91.refs_0_), channel_id=1, source_target_pairs={{0,1},{1,0},{2,3},{3,2},{4,5},{5,4},{6,7},{7,6},{8,9},{9,8},{10,11... | collective-permute-start | bytes 159752 | tf_op jit(solution)/shard_map/ppermute | solution.py:81
  28.2 3.8 %collective-permute-start.5 = (f32[8,512]{1,0:T(8,128)S(1)}, f32[8,512]{1,0:T(8,128)S(1)}, u32[]{:S(2)}, u32[]{:S(2)}) collective-permute-start(f32[8,512]{1,0:T(8,128)S(1)} %shard_map.93.refs_0_), channel_id=1, source_target_pairs={{0,1},{1,0},{2,3},{3,2},{4,5},{5,4},{6,7},{7,6},{8,9},{9,8},{10,11... | collective-permute-start | bytes 49160 | tf_op jit(solution)/shard_map/ppermute | solution.py:81
  32.5 1.3 %collective-permute-start.7 = (f32[8,2176]{1,0:T(8,128)S(1)}, f32[8,2176]{1,0:T(8,128)S(1)}, u32[]{:S(2)}, u32[]{:S(2)}) collective-permute-start(f32[8,2176]{1,0:T(8,128)S(1)} %get-tuple-element.103.refs_0_), channel_id=1, source_target_pairs={{0,8},{8,0},{16,24},{24,16},{1,9},{9,1},{17,25},{25,17},{2,10},{10... | collective-permute-start | bytes 208904 | tf_op jit(solution)/shard_map/ppermute | solution.py:81
  35.3 4.2 %collective-permute-start.9 = (f32[8,1664]{1,0:T(8,128)S(1)}, f32[8,1664]{1,0:T(8,128)S(1)}, u32[]{:S(2)}, u32[]{:S(2)}) collective-permute-start(f32[8,1664]{1,0:T(8,128)S(1)} %get-tuple-element.109.refs_0_), channel_id=1, source_target_pairs={{0,1},{1,0},{2,3},{3,2},{4,5},{5,4},{6,7},{7,6},{8,9},{9,8},{10,11... | collective-permute-start | bytes 159752 | tf_op jit(solution)/shard_map/ppermute | solution.py:81
  37.1 3.8 %collective-permute-start.8 = (f32[8,512]{1,0:T(8,128)S(1)}, f32[8,512]{1,0:T(8,128)S(1)}, u32[]{:S(2)}, u32[]{:S(2)}) collective-permute-start(f32[8,512]{1,0:T(8,128)S(1)} %shard_map.97.refs_0_), channel_id=1, source_target_pairs={{0,1},{1,0},{2,3},{3,2},{4,5},{5,4},{6,7},{7,6},{8,9},{9,8},{10,11... | collective-permute-start | bytes 49160 | tf_op jit(solution)/shard_map/ppermute | solution.py:81
  41.5 1.3 %collective-permute-start.10 = (f32[8,2176]{1,0:T(8,128)S(1)}, f32[8,2176]{1,0:T(8,128)S(1)}, u32[]{:S(2)}, u32[]{:S(2)}) collective-permute-start(f32[8,2176]{1,0:T(8,128)S(1)} %get-tuple-element.112.refs_0_), channel_id=1, source_target_pairs={{0,8},{8,0},{16,24},{24,16},{1,9},{9,1},{17,25},{25,17},{2,10},{10... | collective-permute-start | bytes 208904 | tf_op jit(solution)/shard_map/ppermute | solution.py:81
  44.8 4.4 %collective-permute-start.11 = (f32[8,2176]{1,0:T(8,128)S(1)}, f32[8,2176]{1,0:T(8,128)S(1)}, u32[]{:S(2)}, u32[]{:S(2)}) collective-permute-start(f32[8,2176]{1,0:T(8,128)S(1)} %get-tuple-element.121.refs_0_), channel_id=1, source_target_pairs={{0,1},{1,0},{2,3},{3,2},{4,5},{5,4},{6,7},{7,6},{8,9},{9,8},{10,11... | collective-permute-start | bytes 208904 | tf_op jit(solution)/shard_map/ppermute | solution.py:81
  49.5 1.3 %collective-permute-start.12 = (f32[8,2176]{1,0:T(8,128)S(1)}, f32[8,2176]{1,0:T(8,128)S(1)}, u32[]{:S(2)}, u32[]{:S(2)}) collective-permute-start(f32[8,2176]{1,0:T(8,128)S(1)} %get-tuple-element.124.own), channel_id=1, source_target_pairs={{0,8},{8,0},{16,24},{24,16},{1,9},{9,1},{17,25},{25,17},{2,10},{10... | collective-permute-start | bytes 208904 | tf_op jit(solution)/shard_map/ppermute | solution.py:81
  51.0 6.0 %collective-permute-start.13 = (f32[4,3072]{1,0:T(4,128)S(1)}, f32[4,3072]{1,0:T(4,128)S(1)}, u32[]{:S(2)}, u32[]{:S(2)}) collective-permute-start(f32[4,3072]{1,0:T(4,128)S(1)} %get-tuple-element.131), channel_id=1, source_target_pairs={{0,6},{2,4},{4,2},{6,0},{1,7},{3,5},{5,3},{7,1},{8,14},{10,12},{12... | collective-permute-start | bytes 147464 | tf_op jit(solution)/shard_map/ppermute | solution.py:81
  54.8 5.5 %collective-permute-start.14 = (f32[4,3072]{1,0:T(4,128)S(1)}, f32[4,3072]{1,0:T(4,128)S(1)}, u32[]{:S(2)}, u32[]{:S(2)}) collective-permute-start(f32[4,3072]{1,0:T(4,128)S(1)} %get-tuple-element.132), channel_id=1, source_target_pairs={{0,4},{2,6},{4,0},{6,2},{1,5},{3,7},{5,1},{7,3},{8,12},{10,14},{12... | collective-permute-start | bytes 147464 | tf_op jit(solution)/shard_map/ppermute | solution.py:81
  55.3 5.0 %collective-permute-start.15 = (f32[4,3072]{1,0:T(4,128)S(1)}, f32[4,3072]{1,0:T(4,128)S(1)}, u32[]{:S(2)}, u32[]{:S(2)}) collective-permute-start(f32[4,3072]{1,0:T(4,128)S(1)} %get-tuple-element.133), channel_id=1, source_target_pairs={{0,2},{2,0},{4,6},{6,4},{1,3},{3,1},{5,7},{7,5},{8,10},{10,8},{12,... | collective-permute-start | bytes 147464 | tf_op jit(solution)/shard_map/ppermute | solution.py:81

commit v9 on v8

--- a/solution.py
+++ b/solution.py
@@ -13,7 +13,7 @@
 SINE = (-6.283164044377446, 41.337142378931674, -81.34076911271806, 70.99343519544783)
 LANES = 128
 VMEM_LIMIT = 12 * 2**20
-LOW_SCALE = 512.0
+RAISE = 512.0
 
 
 def call(body, outs, *args, flops=0, in_vmem=True, scratch=(), aliases={}):
@@ -48,7 +48,7 @@
     scaled = rows * scale
     coarse = scaled.astype(f8).astype(f32)
     small = jnp.concatenate([coarse, (scaled - coarse) * 16.0], axis=0).astype(f8)
-    return both, small, 1.0 / (scale * LOW_SCALE)
+    return both, small, 1.0 / scale
 
 
 def product(parts, high_ref, low_ref):
@@ -102,12 +102,12 @@
 def pack_kernel(
     scale, x_hbm, w_hbm, offset_hbm, mag_hbm, response_hbm, label_hbm, penalty_hbm,
     msg, w_ref, offset_ref, mag_ref, penalty_ref, response_out, label_out,
-    points, offset_in, mag_in, response_ref, label_ref, penalty_in, sems,
+    offset_in, mag_in, response_ref, label_ref, penalty_in, sems,
 ):
-    half = points.shape[0]
+    half = x_hbm.shape[0] // 2
     c = core()
     pairs = [
-        (x_hbm.at[pl.ds(pl.multiple_of(c * half, half), half), :], points),
+        (x_hbm.at[pl.ds(pl.multiple_of(c * half, half), half), :], msg.at[pl.ds(0, half), :]),
         (label_hbm, label_ref), (response_hbm, response_ref), (w_hbm, w_ref),
         (offset_hbm, offset_in), (mag_hbm, mag_in), (penalty_hbm, penalty_in),
     ]
@@ -116,12 +116,11 @@
         copy.start()
     for copy in copies:
         copy.wait()
-    msg[:half, :] = points[...]
     msg[half:, :] = jnp.zeros_like(msg[half:, :])
     label_out[...] = label_ref[...]
     response_out[...] = response_ref[...]
     offset_ref[...] = offset_in[...] * TURN
-    mag_ref[...] = mag_in[...] * scale
+    mag_ref[...] = mag_in[...] * (scale / RAISE)
     levels, rows = penalty_in.shape[1], penalty_ref.shape[0]
     row, column = [lax.broadcasted_iota(jnp.int32, (rows, levels), a) for a in (0, 1)]
     chosen = column == lax.axis_index("samp") * (rows // 2) + lax.rem(row, rows // 2)
@@ -167,13 +166,13 @@
         r = t - jnp.round(t)
         q = jnp.abs(r) - 0.25
         u = q * q
-        c = jnp.full_like(u, SINE[-1])
+        c = jnp.full_like(u, SINE[-1] * RAISE)
         for k in SINE[-2::-1]:
-            c = c * u + k
+            c = c * u + k * RAISE
         c = c * q
         high, low = halves(c)
         high_ref[:, j : j + cb] = high
-        small = ((c - high.astype(f32)) * LOW_SCALE).astype(f8)
+        small = (c - high.astype(f32)).astype(f8)
         low_ref[:, j : j + cb] = small
         high_t[j : j + cb, :] = high.T
         low_t[j : j + cb, :] = small.T
@@ -420,8 +419,7 @@
             pltpu.VMEM(tall, jnp.int32),
         ],
         in_specs=[pl.BlockSpec(memory_space=pltpu.HBM)] * len(inputs),
-        scratch_shapes=[pltpu.VMEM((half, depth), bf16)]
-        + [pltpu.VMEM(v, d) for v, d in vectors]
+        scratch_shapes=[pltpu.VMEM(v, d) for v, d in vectors]
         + [pltpu.SemaphoreType.DMA((len(inputs),))],
         compiler_params=pltpu.CompilerParams(vmem_limit_bytes=VMEM_LIMIT),
     )(*[pltpu.with_memory_space_constraint(v, pltpu.HBM) for v in inputs])

time: 61.2 us -> 60.8 us (level)
  transfers between devices with their start and end apart: 16 -> 16, of which waited for: 10 -> 13; matrix products, arithmetic and copies ran while one was open for 0% -> 0% of each run, Pallas kernels for 27% -> 27%
where the time goes in v9:
time: 60.8 us; the launch traced here: 60.7 us
  Pallas kernels  27.2 us (45%)
  waiting for transfers between devices  16.5 us (27%)
  starting transfers between devices  16.3 us (27%)
  between operations  0.73 us (1%)
    pallas_call x17, Pallas kernels, call(): pl.pallas_call(body, out_shape=outs, scratch_shapes=list(scratch), input_...  25.9 us
    ppermute x16, waiting for transfers between devices, flip(): return lax.ppermute(value, axis, [(i, i ^ s) for i in range(n)])  16.5 us
    ppermute x16, starting transfers between devices, flip(): return lax.ppermute(value, axis, [(i, i ^ s) for i in range(n)])  16.3 us
    pallas_call x1, Pallas kernels, shards(): pl.pallas_call(functools.partial(pack_kernel, math.sqrt(2.0 / (features *...  1.29 us
  transfers between devices with their start and end apart: 16, of which 13 were waited for; matrix products, arithmetic and copies ran while one was open for 0% of the time, Pallas kernels for 27%

profile of v9, /device:TPU:0, one launch (start us, length us, event | category | flops | bytes accessed | tf_op | source)
XLA Modules:
  0.0 60.7 jit_solution(7628532558654219737)
XLA Ops:
  0.6 0.5 collective-permute-start
  1.1 1.3 %shard_map.86 = (bf16[528,128]{1,0:T(8,128)(2,1)S(1)}, bf16[128,2048]{1,0:T(8,128)(2,1)S(1)}, f32[1,2048]{1,0:T(1,128)S(1)}, f32[1,2048]{1,0:T(1,128)S(1)}, f32[...) custom-call(bf16[1024,128]{1,0:T(8,128)(2,1)} %x_hbm.1, bf16[128,2048]{1,0:T(8,128)(2,1)} %w_hbm.1, ...), custom_call_target="tpu_custom_call" | custom-call | tf_op jit(solution)/shard_map/pallas_call | solution.py:410
  2.5 0.0 collective-permute-done.other_label
  2.5 4.7 %collective-permute-start.3 = (bf16[528,128]{1,0:T(8,128)(2,1)S(1)}, bf16[528,128]{1,0:T(8,128)(2,1)S(1)}, u32[]{:S(2)}, u32[]{:S(2)}) collective-permute-start(bf16[528,128]{1,0:T(8,128)(2,1)S(1)} %shard_map.87.msg), channel_id=1, source_target_pairs={{0,6},{2,4},{4,2},{6,0},{1,7},{3,5},{5,3},{7,1},{8,14},{10,12},{12... | collective-permute-start | bytes 405512 | tf_op jit(solution)/shard_map/ppermute | solution.py:81
  7.2 0.0 collective-permute-start.2
  7.2 0.6 %collective-permute-start.1 = (bf16[528,128]{1,0:T(8,128)(2,1)S(1)}, bf16[528,128]{1,0:T(8,128)(2,1)S(1)}, u32[]{:S(2)}, u32[]{:S(2)}) collective-permute-start(bf16[528,128]{1,0:T(8,128)(2,1)S(1)} %shard_map.87.msg), channel_id=1, source_target_pairs={{0,4},{2,6},{4,0},{6,2},{1,5},{3,7},{5,1},{7,3},{8,12},{10,14},{12... | collective-permute-start | bytes 405512 | tf_op jit(solution)/shard_map/ppermute | solution.py:81
  7.8 3.7 %shard_map.88 = (bf16[512,2048]{1,0:T(8,128)(2,1)S(1)}, f8e4m3fn[512,2048]{1,0:T(32,128)(4,1)S(1)}, bf16[2048,512]{1,0:T(8,128)(2,1)S(1)}, f8e4m3fn[2048,512]{1,...) custom-call(bf16[528,128]{1,0:T(8,128)(2,1)S(1)} %shard_map.87.msg, ...), custom_call_target="tpu_custom_call" | custom-call | flops 62914560 | bytes 667648 | tf_op jit(solution)/shard_map/pallas_call | solution.py:22
  11.5 0.2 collective-permute-done.3.msg
  11.7 3.7 %shard_map.89 = (bf16[512,2048]{1,0:T(8,128)(2,1)S(1)}, f8e4m3fn[512,2048]{1,0:T(32,128)(4,1)S(1)}, bf16[2048,512]{1,0:T(8,128)(2,1)S(1)}, f8e4m3fn[2048,512]{1,...) custom-call(bf16[528,128]{1,0:T(8,128)(2,1)S(1)} %collective-permute-done.3.msg, ...), custom_call_target="tpu_custom_call" | custom-call | flops 62914560 | bytes 700416 | tf_op jit(solution)/shard_map/pallas_call | solution.py:22
  15.4 0.0 collective-permute-done.2.msg
  15.4 3.7 %shard_map.90 = (bf16[512,2048]{1,0:T(8,128)(2,1)S(1)}, f8e4m3fn[512,2048]{1,0:T(32,128)(4,1)S(1)}, bf16[2048,512]{1,0:T(8,128)(2,1)S(1)}, f8e4m3fn[2048,512]{1,...) custom-call(bf16[528,128]{1,0:T(8,128)(2,1)S(1)} %collective-permute-done.2.msg, ...), custom_call_target="tpu_custom_call" | custom-call | flops 62914560 | bytes 700416 | tf_op jit(solution)/shard_map/pallas_call | solution.py:22
  19.1 0.2 collective-permute-done.1.msg
  19.3 3.9 %shard_map.91 = (bf16[512,2048]{1,0:T(8,128)(2,1)S(1)}, f8e4m3fn[512,2048]{1,0:T(32,128)(4,1)S(1)}, bf16[2048,512]{1,0:T(8,128)(2,1)S(1)}, f8e4m3fn[2048,512]{1,...) custom-call(bf16[528,128]{1,0:T(8,128)(2,1)S(1)} %collective-permute-done.1.msg, ...), custom_call_target="tpu_custom_call" | custom-call | flops 62914560 | bytes 700416 | tf_op jit(solution)/shard_map/pallas_call | solution.py:22
  23.1 0.0 collective-permute-start.4
  23.2 1.2 %collective-permute-done.4.refs_1_ = f32[4,2048]{1,0:T(4,128)S(1)} collective-permute-done((f32[4,2048]{1,0:T(4,128)S(1)}, f32[4,2048]{1,0:T(4,128)S(1)}, u32[]{:S(2)}, u32[]{:S(2)}) %collective-permute-start.4) | collective-permute-done | bytes 32800 | tf_op jit(solution)/shard_map/ppermute | solution.py:81
  24.4 1.4 %shard_map.92 = (f32[8,1664]{1,0:T(8,128)S(1)}, f32[8,2048]{1,0:T(8,128)S(1)}, f32[8,2048]{1,0:T(8,128)S(1)}, f32[8,2048]{1,0:T(8,128)S(1)}) custom-call(f32[4,2048]{1,0:T(4,128)S(1)} %get-tuple-element.76.refs_0_, f32[4,2048]{1,0:T(4,128)S(1)} %collective-permute-done.4.refs_1_, f32[8,1]{1,0:T(8,128)S(1)} %get-tuple-element.77.refs_2_.refs_3_.penalty, ...), custom_call_target="tpu_custom_call" | custom-call | flops 150994944 | bytes 9510944 | tf_op jit(solution)/shard_map/pallas_call | solution.py:22
  25.8 1.6 %collective-permute-start.6 = (f32[8,1664]{1,0:T(8,128)S(1)}, f32[8,1664]{1,0:T(8,128)S(1)}, u32[]{:S(2)}, u32[]{:S(2)}) collective-permute-start(f32[8,1664]{1,0:T(8,128)S(1)} %get-tuple-element.91.refs_0_), channel_id=1, source_target_pairs={{0,1},{1,0},{2,3},{3,2},{4,5},{5,4},{6,7},{7,6},{8,9},{9,8},{10,11... | collective-permute-start | bytes 159752 | tf_op jit(solution)/shard_map/ppermute | solution.py:81
  27.4 0.5 shard_map.93.refs_0_
  27.9 0.6 collective-permute-start.5
  28.5 1.5 %collective-permute-done.6.refs_1_ = f32[8,1664]{1,0:T(8,128)S(1)} collective-permute-done((f32[8,1664]{1,0:T(8,128)S(1)}, f32[8,1664]{1,0:T(8,128)S(1)}, u32[]{:S(2)}, u32[]{:S(2)}) %collective-permute-start.6) | collective-permute-done | bytes 53280 | tf_op jit(solution)/shard_map/ppermute | solution.py:81
  30.0 1.4 %shard_map.94 = (f32[8,2048]{1,0:T(8,128)S(1)}, f32[8,1536]{1,0:T(8,128)S(1)}, f32[8,128]{1,0:T(8,128)S(1)}) custom-call(f32[8,1664]{1,0:T(8,128)S(1)} %get-tuple-element.91.refs_0_, f32[8,1664]{1,0:T(8,128)S(1)} %collective-permute-done.6.refs_1_, f32[8,512]{1,0:T(8,128)S(1)} %get-tuple-element.92.refs_2_, f32[8,512]{1,0:T(8,128)S(1)} %get-tuple-element.93.refs_3_, ...), custom_call_target="tpu_custom_call" | custom-call | flops 150994944 | bytes 9592832 | tf_op jit(solution)/shard_map/pallas_call | solution.py:22
  31.3 0.3 collective-permute-done.5.refs_1_
  31.7 0.5 shard_map.95
  32.2 0.1 collective-permute-start.7
  32.3 1.2 %collective-permute-done.7.refs_1_ = f32[8,2176]{1,0:T(8,128)S(1)} collective-permute-done((f32[8,2176]{1,0:T(8,128)S(1)}, f32[8,2176]{1,0:T(8,128)S(1)}, u32[]{:S(2)}, u32[]{:S(2)}) %collective-permute-start.7) | collective-permute-done | bytes 69664 | tf_op jit(solution)/shard_map/ppermute | solution.py:81
  33.5 1.5 %shard_map.96 = (f32[8,1664]{1,0:T(8,128)S(1)}, f32[8,2048]{1,0:T(8,128)S(1)}, f32[8,2048]{1,0:T(8,128)S(1)}, f32[8,2048]{1,0:T(8,128)S(1)}, f32[8,2048]{1,0:T(8...) custom-call(f32[8,2176]{1,0:T(8,128)S(1)} %get-tuple-element.103.refs_0_, ...), custom_call_target="tpu_custom_call" | custom-call | flops 150994944 | bytes 9850912 | tf_op jit(solution)/shard_map/pallas_call | solution.py:22
  35.0 1.4 %collective-permute-start.9 = (f32[8,1664]{1,0:T(8,128)S(1)}, f32[8,1664]{1,0:T(8,128)S(1)}, u32[]{:S(2)}, u32[]{:S(2)}) collective-permute-start(f32[8,1664]{1,0:T(8,128)S(1)} %get-tuple-element.109.refs_0_), channel_id=1, source_target_pairs={{0,1},{1,0},{2,3},{3,2},{4,5},{5,4},{6,7},{7,6},{8,9},{9,8},{10,11... | collective-permute-start | bytes 159752 | tf_op jit(solution)/shard_map/ppermute | solution.py:81
  36.5 0.5 shard_map.97.refs_0_
  37.0 0.7 %collective-permute-start.8 = (f32[8,512]{1,0:T(8,128)S(1)}, f32[8,512]{1,0:T(8,128)S(1)}, u32[]{:S(2)}, u32[]{:S(2)}) collective-permute-start(f32[8,512]{1,0:T(8,128)S(1)} %shard_map.97.refs_0_), channel_id=1, source_target_pairs={{0,1},{1,0},{2,3},{3,2},{4,5},{5,4},{6,7},{7,6},{8,9},{9,8},{10,11... | collective-permute-start | bytes 49160 | tf_op jit(solution)/shard_map/ppermute | solution.py:81
  37.7 1.5 %collective-permute-done.9.refs_1_ = f32[8,1664]{1,0:T(8,128)S(1)} collective-permute-done((f32[8,1664]{1,0:T(8,128)S(1)}, f32[8,1664]{1,0:T(8,128)S(1)}, u32[]{:S(2)}, u32[]{:S(2)}) %collective-permute-start.9) | collective-permute-done | bytes 53280 | tf_op jit(solution)/shard_map/ppermute | solution.py:81
  39.2 1.4 %shard_map.98 = (f32[8,2048]{1,0:T(8,128)S(1)}, f32[8,1536]{1,0:T(8,128)S(1)}, f32[8,128]{1,0:T(8,128)S(1)}) custom-call(f32[8,1664]{1,0:T(8,128)S(1)} %get-tuple-element.109.refs_0_, f32[8,1664]{1,0:T(8,128)S(1)} %collective-permute-done.9.refs_1_, f32[8,512]{1,0:T(8,128)S(1)} %get-tuple-element.92.refs_2_, f32[8,512]{1,0:T(8,128)S(1)} %get-tuple-element.93.refs_3_, ...), custom_call_target="tpu_custom_call" | custom-call | flops 150994944 | bytes 9646080 | tf_op jit(solution)/shard_map/pallas_call | solution.py:22
  40.6 0.2 collective-permute-done.8.refs_1_
  40.8 0.6 shard_map.99
  41.4 0.1 collective-permute-start.10
  41.4 1.2 %collective-permute-done.10.refs_1_ = f32[8,2176]{1,0:T(8,128)S(1)} collective-permute-done((f32[8,2176]{1,0:T(8,128)S(1)}, f32[8,2176]{1,0:T(8,128)S(1)}, u32[]{:S(2)}, u32[]{:S(2)}) %collective-permute-start.10) | collective-permute-done | bytes 69664 | tf_op jit(solution)/shard_map/ppermute | solution.py:81
  42.7 1.9 %shard_map.100 = (f32[8,2176]{1,0:T(8,128)S(1)}, f32[8,2048]{1,0:T(8,128)S(1)}, f32[8,2048]{1,0:T(8,128)S(1)}, f32[8,2048]{1,0:T(8,128)S(1)}, f32[8,2048]{1,0:T(8,128)S(1)}, /*index=5*/f32[8,2048]{1,0:T(8,128)S(1)}) custom-call(f32[8,2176]{1,0:T(8,128)S(1)} %get-tuple-element.112.refs_0_, f32[8,2176]{1,0:T(8,128)S(1)} %collective-permute-done.10.refs_1_, ...), custom_call_target="tpu_custom_call" | custom-call | flops 150994944 | bytes 13328416 | tf_op jit(solution)/shard_map/pallas_call | solution.py:22
  44.6 1.5 %collective-permute-start.11 = (f32[8,2176]{1,0:T(8,128)S(1)}, f32[8,2176]{1,0:T(8,128)S(1)}, u32[]{:S(2)}, u32[]{:S(2)}) collective-permute-start(f32[8,2176]{1,0:T(8,128)S(1)} %get-tuple-element.121.refs_0_), channel_id=1, source_target_pairs={{0,1},{1,0},{2,3},{3,2},{4,5},{5,4},{6,7},{7,6},{8,9},{9,8},{10,11... | collective-permute-start | bytes 208904 | tf_op jit(solution)/shard_map/ppermute | solution.py:81
  46.1 2.9 %collective-permute-done.11.refs_1_ = f32[8,2176]{1,0:T(8,128)S(1)} collective-permute-done((f32[8,2176]{1,0:T(8,128)S(1)}, f32[8,2176]{1,0:T(8,128)S(1)}, u32[]{:S(2)}, u32[]{:S(2)}) %collective-permute-start.11) | collective-permute-done | bytes 69664 | tf_op jit(solution)/shard_map/ppermute | solution.py:81
  49.0 0.3 shard_map.101
  49.3 0.0 collective-permute-start.12
  49.4 1.2 %collective-permute-done.12.got = f32[8,2176]{1,0:T(8,128)S(1)} collective-permute-done((f32[8,2176]{1,0:T(8,128)S(1)}, f32[8,2176]{1,0:T(8,128)S(1)}, u32[]{:S(2)}, u32[]{:S(2)}) %collective-permute-start.12) | collective-permute-done | bytes 69664 | tf_op jit(solution)/shard_map/ppermute | solution.py:81
  50.6 0.2 shard_map.102
  50.8 3.6 %collective-permute-start.13 = (f32[4,3072]{1,0:T(4,128)S(1)}, f32[4,3072]{1,0:T(4,128)S(1)}, u32[]{:S(2)}, u32[]{:S(2)}) collective-permute-start(f32[4,3072]{1,0:T(4,128)S(1)} %get-tuple-element.131), channel_id=1, source_target_pairs={{0,6},{2,4},{4,2},{6,0},{1,7},{3,5},{5,3},{7,1},{8,14},{10,12},{12... | collective-permute-start | bytes 147464 | tf_op jit(solution)/shard_map/ppermute | solution.py:81
  54.5 0.5 collective-permute-start.14
  55.0 0.3 collective-permute-start.15
  55.3 1.6 %collective-permute-done.13.refs_1_ = f32[4,3072]{1,0:T(4,128)S(1)} collective-permute-done((f32[4,3072]{1,0:T(4,128)S(1)}, f32[4,3072]{1,0:T(4,128)S(1)}, u32[]{:S(2)}, u32[]{:S(2)}) %collective-permute-start.13) | collective-permute-done | bytes 49184 | tf_op jit(solution)/shard_map/ppermute | solution.py:81
  56.8 3.2 %collective-permute-done.14.refs_2_ = f32[4,3072]{1,0:T(4,128)S(1)} collective-permute-done((f32[4,3072]{1,0:T(4,128)S(1)}, f32[4,3072]{1,0:T(4,128)S(1)}, u32[]{:S(2)}, u32[]{:S(2)}) %collective-permute-start.14) | collective-permute-done | bytes 49184 | tf_op jit(solution)/shard_map/ppermute | solution.py:81
  60.0 0.7 %shard_map.103 = (f32[16,2048]{1,0:T(8,128)}, f32[16,1024]{1,0:T(8,128)}) custom-call(f32[4,3072]{1,0:T(4,128)S(1)} %get-tuple-element.130.refs_0_, f32[4,3072]{1,0:T(4,128)S(1)} %collective-permute-done.13.refs_1_, f32[4,3072]{1,0:T(4,128)S(1)} %collective-permute-done.14.refs_2_, f32[4,3072]{1,0:T(4,128)S(1)} %collective-permute-done.15.refs_3_), custom_call_target="tpu_custom_call" | custom-call | bytes 196608 | tf_op jit(solution)/shard_map/pallas_call | solution.py:22
  (2 shorter events, 0.0 us)
Async XLA Ops:
  0.6 1.8 %collective-permute-start = (s32[8,128]{1,0:T(8,128)}, s32[8,128]{1,0:T(8,128)S(1)}, u32[]{:S(2)}, u32[]{:S(2)}) collective-permute-start(s32[8,128]{1,0:T(8,128)} %bitcast.8), channel_id=1, source_target_pairs={{0,8},{8,0},{16,24},{24,16},{1,9},{9,1},{17,25},{25,17},{2,10},{10... | collective-permute-start | bytes 12296 | tf_op jit(solution)/shard_map/ppermute | solution.py:81
  2.5 9.2 %collective-permute-start.3 = (bf16[528,128]{1,0:T(8,128)(2,1)S(1)}, bf16[528,128]{1,0:T(8,128)(2,1)S(1)}, u32[]{:S(2)}, u32[]{:S(2)}) collective-permute-start(bf16[528,128]{1,0:T(8,128)(2,1)S(1)} %shard_map.87.msg), channel_id=1, source_target_pairs={{0,6},{2,4},{4,2},{6,0},{1,7},{3,5},{5,3},{7,1},{8,14},{10,12},{12... | collective-permute-start | bytes 405512 | tf_op jit(solution)/shard_map/ppermute | solution.py:81
  7.2 8.2 %collective-permute-start.2 = (bf16[528,128]{1,0:T(8,128)(2,1)S(1)}, bf16[528,128]{1,0:T(8,128)(2,1)S(1)}, u32[]{:S(2)}, u32[]{:S(2)}) collective-permute-start(bf16[528,128]{1,0:T(8,128)(2,1)S(1)} %shard_map.87.msg), channel_id=1, source_target_pairs={{0,2},{2,0},{4,6},{6,4},{1,3},{3,1},{5,7},{7,5},{8,10},{10,8},{12,... | collective-permute-start | bytes 405512 | tf_op jit(solution)/shard_map/ppermute | solution.py:81
  7.2 12.1 %collective-permute-start.1 = (bf16[528,128]{1,0:T(8,128)(2,1)S(1)}, bf16[528,128]{1,0:T(8,128)(2,1)S(1)}, u32[]{:S(2)}, u32[]{:S(2)}) collective-permute-start(bf16[528,128]{1,0:T(8,128)(2,1)S(1)} %shard_map.87.msg), channel_id=1, source_target_pairs={{0,4},{2,6},{4,0},{6,2},{1,5},{3,7},{5,1},{7,3},{8,12},{10,14},{12... | collective-permute-start | bytes 405512 | tf_op jit(solution)/shard_map/ppermute | solution.py:81
  23.1 1.2 %collective-permute-start.4 = (f32[4,2048]{1,0:T(4,128)S(1)}, f32[4,2048]{1,0:T(4,128)S(1)}, u32[]{:S(2)}, u32[]{:S(2)}) collective-permute-start(f32[4,2048]{1,0:T(4,128)S(1)} %get-tuple-element.76.refs_0_), channel_id=1, source_target_pairs={{0,8},{8,0},{16,24},{24,16},{1,9},{9,1},{17,25},{25,17},{2,10},{10... | collective-permute-start | bytes 98312 | tf_op jit(solution)/shard_map/ppermute | solution.py:81
  25.8 4.2 %collective-permute-start.6 = (f32[8,1664]{1,0:T(8,128)S(1)}, f32[8,1664]{1,0:T(8,128)S(1)}, u32[]{:S(2)}, u32[]{:S(2)}) collective-permute-start(f32[8,1664]{1,0:T(8,128)S(1)} %get-tuple-element.91.refs_0_), channel_id=1, source_target_pairs={{0,1},{1,0},{2,3},{3,2},{4,5},{5,4},{6,7},{7,6},{8,9},{9,8},{10,11... | collective-permute-start | bytes 159752 | tf_op jit(solution)/shard_map/ppermute | solution.py:81
  27.9 3.8 %collective-permute-start.5 = (f32[8,512]{1,0:T(8,128)S(1)}, f32[8,512]{1,0:T(8,128)S(1)}, u32[]{:S(2)}, u32[]{:S(2)}) collective-permute-start(f32[8,512]{1,0:T(8,128)S(1)} %shard_map.93.refs_0_), channel_id=1, source_target_pairs={{0,1},{1,0},{2,3},{3,2},{4,5},{5,4},{6,7},{7,6},{8,9},{9,8},{10,11... | collective-permute-start | bytes 49160 | tf_op jit(solution)/shard_map/ppermute | solution.py:81
  32.2 1.3 %collective-permute-start.7 = (f32[8,2176]{1,0:T(8,128)S(1)}, f32[8,2176]{1,0:T(8,128)S(1)}, u32[]{:S(2)}, u32[]{:S(2)}) collective-permute-start(f32[8,2176]{1,0:T(8,128)S(1)} %get-tuple-element.103.refs_0_), channel_id=1, source_target_pairs={{0,8},{8,0},{16,24},{24,16},{1,9},{9,1},{17,25},{25,17},{2,10},{10... | collective-permute-start | bytes 208904 | tf_op jit(solution)/shard_map/ppermute | solution.py:81
  35.0 4.2 %collective-permute-start.9 = (f32[8,1664]{1,0:T(8,128)S(1)}, f32[8,1664]{1,0:T(8,128)S(1)}, u32[]{:S(2)}, u32[]{:S(2)}) collective-permute-start(f32[8,1664]{1,0:T(8,128)S(1)} %get-tuple-element.109.refs_0_), channel_id=1, source_target_pairs={{0,1},{1,0},{2,3},{3,2},{4,5},{5,4},{6,7},{7,6},{8,9},{9,8},{10,11... | collective-permute-start | bytes 159752 | tf_op jit(solution)/shard_map/ppermute | solution.py:81
  37.0 3.8 %collective-permute-start.8 = (f32[8,512]{1,0:T(8,128)S(1)}, f32[8,512]{1,0:T(8,128)S(1)}, u32[]{:S(2)}, u32[]{:S(2)}) collective-permute-start(f32[8,512]{1,0:T(8,128)S(1)} %shard_map.97.refs_0_), channel_id=1, source_target_pairs={{0,1},{1,0},{2,3},{3,2},{4,5},{5,4},{6,7},{7,6},{8,9},{9,8},{10,11... | collective-permute-start | bytes 49160 | tf_op jit(solution)/shard_map/ppermute | solution.py:81
  41.4 1.3 %collective-permute-start.10 = (f32[8,2176]{1,0:T(8,128)S(1)}, f32[8,2176]{1,0:T(8,128)S(1)}, u32[]{:S(2)}, u32[]{:S(2)}) collective-permute-start(f32[8,2176]{1,0:T(8,128)S(1)} %get-tuple-element.112.refs_0_), channel_id=1, source_target_pairs={{0,8},{8,0},{16,24},{24,16},{1,9},{9,1},{17,25},{25,17},{2,10},{10... | collective-permute-start | bytes 208904 | tf_op jit(solution)/shard_map/ppermute | solution.py:81
  44.6 4.4 %collective-permute-start.11 = (f32[8,2176]{1,0:T(8,128)S(1)}, f32[8,2176]{1,0:T(8,128)S(1)}, u32[]{:S(2)}, u32[]{:S(2)}) collective-permute-start(f32[8,2176]{1,0:T(8,128)S(1)} %get-tuple-element.121.refs_0_), channel_id=1, source_target_pairs={{0,1},{1,0},{2,3},{3,2},{4,5},{5,4},{6,7},{7,6},{8,9},{9,8},{10,11... | collective-permute-start | bytes 208904 | tf_op jit(solution)/shard_map/ppermute | solution.py:81
  49.3 1.3 %collective-permute-start.12 = (f32[8,2176]{1,0:T(8,128)S(1)}, f32[8,2176]{1,0:T(8,128)S(1)}, u32[]{:S(2)}, u32[]{:S(2)}) collective-permute-start(f32[8,2176]{1,0:T(8,128)S(1)} %get-tuple-element.124.own), channel_id=1, source_target_pairs={{0,8},{8,0},{16,24},{24,16},{1,9},{9,1},{17,25},{25,17},{2,10},{10... | collective-permute-start | bytes 208904 | tf_op jit(solution)/shard_map/ppermute | solution.py:81
  50.8 6.0 %collective-permute-start.13 = (f32[4,3072]{1,0:T(4,128)S(1)}, f32[4,3072]{1,0:T(4,128)S(1)}, u32[]{:S(2)}, u32[]{:S(2)}) collective-permute-start(f32[4,3072]{1,0:T(4,128)S(1)} %get-tuple-element.131), channel_id=1, source_target_pairs={{0,6},{2,4},{4,2},{6,0},{1,7},{3,5},{5,3},{7,1},{8,14},{10,12},{12... | collective-permute-start | bytes 147464 | tf_op jit(solution)/shard_map/ppermute | solution.py:81
  54.5 5.5 %collective-permute-start.14 = (f32[4,3072]{1,0:T(4,128)S(1)}, f32[4,3072]{1,0:T(4,128)S(1)}, u32[]{:S(2)}, u32[]{:S(2)}) collective-permute-start(f32[4,3072]{1,0:T(4,128)S(1)} %get-tuple-element.132), channel_id=1, source_target_pairs={{0,4},{2,6},{4,0},{6,2},{1,5},{3,7},{5,1},{7,3},{8,12},{10,14},{12... | collective-permute-start | bytes 147464 | tf_op jit(solution)/shard_map/ppermute | solution.py:81
  55.0 5.0 %collective-permute-start.15 = (f32[4,3072]{1,0:T(4,128)S(1)}, f32[4,3072]{1,0:T(4,128)S(1)}, u32[]{:S(2)}, u32[]{:S(2)}) collective-permute-start(f32[4,3072]{1,0:T(4,128)S(1)} %get-tuple-element.133), channel_id=1, source_target_pairs={{0,2},{2,0},{4,6},{6,4},{1,3},{3,1},{5,7},{7,5},{8,10},{10,8},{12,... | collective-permute-start | bytes 147464 | tf_op jit(solution)/shard_map/ppermute | solution.py:81

commit v10 on v9

--- a/solution.py
+++ b/solution.py
@@ -181,7 +181,8 @@
             part = square * jnp.concatenate([mask[e]] * (cb // LANES), axis=1)
             acc[e, :, j : j + cb] = part.reshape(samples // 8, 8, cb).sum(0)
         side = jnp.dot(y_both, high, preferred_element_type=f32)
-        side = side[:2] + side[2:] + jnp.dot(y_high, low, preferred_element_type=f32)
+        fine = jnp.dot(y_both, low, preferred_element_type=f32)
+        side = side[:2] + side[2:] + (fine[:2] + fine[2:])
         moment_ref[2:4, j : j + cb] = side if first else before[2:4, j : j + cb] + side
     for e in (0, 1):
         square = jnp.sum(acc[e], axis=0, keepdims=True)

time: 60.8 us -> 60.8 us (level)
  no operation moved by 1% of the time
where the time goes in v10:
time: 60.8 us; the launch traced here: 60.7 us
  Pallas kernels  27.2 us (45%)
  waiting for transfers between devices  16.5 us (27%)
  starting transfers between devices  16.3 us (27%)
  between operations  0.73 us (1%)
    pallas_call x17, Pallas kernels, call(): pl.pallas_call(body, out_shape=outs, scratch_shapes=list(scratch), input_...  25.9 us
    ppermute x16, waiting for transfers between devices, flip(): return lax.ppermute(value, axis, [(i, i ^ s) for i in range(n)])  16.5 us
    ppermute x16, starting transfers between devices, flip(): return lax.ppermute(value, axis, [(i, i ^ s) for i in range(n)])  16.3 us
    pallas_call x1, Pallas kernels, shards(): pl.pallas_call(functools.partial(pack_kernel, math.sqrt(2.0 / (features *...  1.29 us
  transfers between devices with their start and end apart: 16, of which 13 were waited for; matrix products, arithmetic and copies ran while one was open for 0% of the time, Pallas kernels for 27%

profile of v10, /device:TPU:0, one launch (start us, length us, event | category | flops | bytes accessed | tf_op | source)
XLA Modules:
  0.0 60.7 jit_solution(12670308869845579526)
XLA Ops:
  0.6 0.5 collective-permute-start
  1.1 1.3 %shard_map.86 = (bf16[528,128]{1,0:T(8,128)(2,1)S(1)}, bf16[128,2048]{1,0:T(8,128)(2,1)S(1)}, f32[1,2048]{1,0:T(1,128)S(1)}, f32[1,2048]{1,0:T(1,128)S(1)}, f32[...) custom-call(bf16[1024,128]{1,0:T(8,128)(2,1)} %x_hbm.1, bf16[128,2048]{1,0:T(8,128)(2,1)} %w_hbm.1, ...), custom_call_target="tpu_custom_call" | custom-call | tf_op jit(solution)/shard_map/pallas_call | solution.py:411
  2.5 0.0 collective-permute-done.other_label
  2.5 4.7 %collective-permute-start.3 = (bf16[528,128]{1,0:T(8,128)(2,1)S(1)}, bf16[528,128]{1,0:T(8,128)(2,1)S(1)}, u32[]{:S(2)}, u32[]{:S(2)}) collective-permute-start(bf16[528,128]{1,0:T(8,128)(2,1)S(1)} %shard_map.87.msg), channel_id=1, source_target_pairs={{0,6},{2,4},{4,2},{6,0},{1,7},{3,5},{5,3},{7,1},{8,14},{10,12},{12... | collective-permute-start | bytes 405512 | tf_op jit(solution)/shard_map/ppermute | solution.py:81
  7.2 0.0 collective-permute-start.2
  7.2 0.6 %collective-permute-start.1 = (bf16[528,128]{1,0:T(8,128)(2,1)S(1)}, bf16[528,128]{1,0:T(8,128)(2,1)S(1)}, u32[]{:S(2)}, u32[]{:S(2)}) collective-permute-start(bf16[528,128]{1,0:T(8,128)(2,1)S(1)} %shard_map.87.msg), channel_id=1, source_target_pairs={{0,4},{2,6},{4,0},{6,2},{1,5},{3,7},{5,1},{7,3},{8,12},{10,14},{12... | collective-permute-start | bytes 405512 | tf_op jit(solution)/shard_map/ppermute | solution.py:81
  7.8 3.7 %shard_map.88 = (bf16[512,2048]{1,0:T(8,128)(2,1)S(1)}, f8e4m3fn[512,2048]{1,0:T(32,128)(4,1)S(1)}, bf16[2048,512]{1,0:T(8,128)(2,1)S(1)}, f8e4m3fn[2048,512]{1,...) custom-call(bf16[528,128]{1,0:T(8,128)(2,1)S(1)} %shard_map.87.msg, ...), custom_call_target="tpu_custom_call" | custom-call | flops 62914560 | bytes 667648 | tf_op jit(solution)/shard_map/pallas_call | solution.py:22
  11.5 0.2 collective-permute-done.3.msg
  11.7 3.7 %shard_map.89 = (bf16[512,2048]{1,0:T(8,128)(2,1)S(1)}, f8e4m3fn[512,2048]{1,0:T(32,128)(4,1)S(1)}, bf16[2048,512]{1,0:T(8,128)(2,1)S(1)}, f8e4m3fn[2048,512]{1,...) custom-call(bf16[528,128]{1,0:T(8,128)(2,1)S(1)} %collective-permute-done.3.msg, ...), custom_call_target="tpu_custom_call" | custom-call | flops 62914560 | bytes 700416 | tf_op jit(solution)/shard_map/pallas_call | solution.py:22
  15.4 0.0 collective-permute-done.2.msg
  15.4 3.7 %shard_map.90 = (bf16[512,2048]{1,0:T(8,128)(2,1)S(1)}, f8e4m3fn[512,2048]{1,0:T(32,128)(4,1)S(1)}, bf16[2048,512]{1,0:T(8,128)(2,1)S(1)}, f8e4m3fn[2048,512]{1,...) custom-call(bf16[528,128]{1,0:T(8,128)(2,1)S(1)} %collective-permute-done.2.msg, ...), custom_call_target="tpu_custom_call" | custom-call | flops 62914560 | bytes 700416 | tf_op jit(solution)/shard_map/pallas_call | solution.py:22
  19.1 0.2 collective-permute-done.1.msg
  19.3 3.9 %shard_map.91 = (bf16[512,2048]{1,0:T(8,128)(2,1)S(1)}, f8e4m3fn[512,2048]{1,0:T(32,128)(4,1)S(1)}, bf16[2048,512]{1,0:T(8,128)(2,1)S(1)}, f8e4m3fn[2048,512]{1,...) custom-call(bf16[528,128]{1,0:T(8,128)(2,1)S(1)} %collective-permute-done.1.msg, ...), custom_call_target="tpu_custom_call" | custom-call | flops 62914560 | bytes 700416 | tf_op jit(solution)/shard_map/pallas_call | solution.py:22
  23.1 0.0 collective-permute-start.4
  23.2 1.2 %collective-permute-done.4.refs_1_ = f32[4,2048]{1,0:T(4,128)S(1)} collective-permute-done((f32[4,2048]{1,0:T(4,128)S(1)}, f32[4,2048]{1,0:T(4,128)S(1)}, u32[]{:S(2)}, u32[]{:S(2)}) %collective-permute-start.4) | collective-permute-done | bytes 32800 | tf_op jit(solution)/shard_map/ppermute | solution.py:81
  24.4 1.4 %shard_map.92 = (f32[8,1664]{1,0:T(8,128)S(1)}, f32[8,2048]{1,0:T(8,128)S(1)}, f32[8,2048]{1,0:T(8,128)S(1)}, f32[8,2048]{1,0:T(8,128)S(1)}) custom-call(f32[4,2048]{1,0:T(4,128)S(1)} %get-tuple-element.76.refs_0_, f32[4,2048]{1,0:T(4,128)S(1)} %collective-permute-done.4.refs_1_, f32[8,1]{1,0:T(8,128)S(1)} %get-tuple-element.77.refs_2_.refs_3_.penalty, ...), custom_call_target="tpu_custom_call" | custom-call | flops 150994944 | bytes 9510944 | tf_op jit(solution)/shard_map/pallas_call | solution.py:22
  25.8 1.6 %collective-permute-start.6 = (f32[8,1664]{1,0:T(8,128)S(1)}, f32[8,1664]{1,0:T(8,128)S(1)}, u32[]{:S(2)}, u32[]{:S(2)}) collective-permute-start(f32[8,1664]{1,0:T(8,128)S(1)} %get-tuple-element.91.refs_0_), channel_id=1, source_target_pairs={{0,1},{1,0},{2,3},{3,2},{4,5},{5,4},{6,7},{7,6},{8,9},{9,8},{10,11... | collective-permute-start | bytes 159752 | tf_op jit(solution)/shard_map/ppermute | solution.py:81
  27.4 0.5 shard_map.93.refs_0_
  27.9 0.6 collective-permute-start.5
  28.4 1.5 %collective-permute-done.6.refs_1_ = f32[8,1664]{1,0:T(8,128)S(1)} collective-permute-done((f32[8,1664]{1,0:T(8,128)S(1)}, f32[8,1664]{1,0:T(8,128)S(1)}, u32[]{:S(2)}, u32[]{:S(2)}) %collective-permute-start.6) | collective-permute-done | bytes 53280 | tf_op jit(solution)/shard_map/ppermute | solution.py:81
  30.0 1.4 %shard_map.94 = (f32[8,2048]{1,0:T(8,128)S(1)}, f32[8,1536]{1,0:T(8,128)S(1)}, f32[8,128]{1,0:T(8,128)S(1)}) custom-call(f32[8,1664]{1,0:T(8,128)S(1)} %get-tuple-element.91.refs_0_, f32[8,1664]{1,0:T(8,128)S(1)} %collective-permute-done.6.refs_1_, f32[8,512]{1,0:T(8,128)S(1)} %get-tuple-element.92.refs_2_, f32[8,512]{1,0:T(8,128)S(1)} %get-tuple-element.93.refs_3_, ...), custom_call_target="tpu_custom_call" | custom-call | flops 150994944 | bytes 9592832 | tf_op jit(solution)/shard_map/pallas_call | solution.py:22
  31.3 0.3 collective-permute-done.5.refs_1_
  31.7 0.5 shard_map.95
  32.2 0.1 collective-permute-start.7
  32.3 1.2 %collective-permute-done.7.refs_1_ = f32[8,2176]{1,0:T(8,128)S(1)} collective-permute-done((f32[8,2176]{1,0:T(8,128)S(1)}, f32[8,2176]{1,0:T(8,128)S(1)}, u32[]{:S(2)}, u32[]{:S(2)}) %collective-permute-start.7) | collective-permute-done | bytes 69664 | tf_op jit(solution)/shard_map/ppermute | solution.py:81
  33.5 1.5 %shard_map.96 = (f32[8,1664]{1,0:T(8,128)S(1)}, f32[8,2048]{1,0:T(8,128)S(1)}, f32[8,2048]{1,0:T(8,128)S(1)}, f32[8,2048]{1,0:T(8,128)S(1)}, f32[8,2048]{1,0:T(8...) custom-call(f32[8,2176]{1,0:T(8,128)S(1)} %get-tuple-element.103.refs_0_, ...), custom_call_target="tpu_custom_call" | custom-call | flops 150994944 | bytes 9850912 | tf_op jit(solution)/shard_map/pallas_call | solution.py:22
  35.0 1.4 %collective-permute-start.9 = (f32[8,1664]{1,0:T(8,128)S(1)}, f32[8,1664]{1,0:T(8,128)S(1)}, u32[]{:S(2)}, u32[]{:S(2)}) collective-permute-start(f32[8,1664]{1,0:T(8,128)S(1)} %get-tuple-element.109.refs_0_), channel_id=1, source_target_pairs={{0,1},{1,0},{2,3},{3,2},{4,5},{5,4},{6,7},{7,6},{8,9},{9,8},{10,11... | collective-permute-start | bytes 159752 | tf_op jit(solution)/shard_map/ppermute | solution.py:81
  36.4 0.5 shard_map.97.refs_0_
  37.0 0.7 %collective-permute-start.8 = (f32[8,512]{1,0:T(8,128)S(1)}, f32[8,512]{1,0:T(8,128)S(1)}, u32[]{:S(2)}, u32[]{:S(2)}) collective-permute-start(f32[8,512]{1,0:T(8,128)S(1)} %shard_map.97.refs_0_), channel_id=1, source_target_pairs={{0,1},{1,0},{2,3},{3,2},{4,5},{5,4},{6,7},{7,6},{8,9},{9,8},{10,11... | collective-permute-start | bytes 49160 | tf_op jit(solution)/shard_map/ppermute | solution.py:81
  37.7 1.5 %collective-permute-done.9.refs_1_ = f32[8,1664]{1,0:T(8,128)S(1)} collective-permute-done((f32[8,1664]{1,0:T(8,128)S(1)}, f32[8,1664]{1,0:T(8,128)S(1)}, u32[]{:S(2)}, u32[]{:S(2)}) %collective-permute-start.9) | collective-permute-done | bytes 53280 | tf_op jit(solution)/shard_map/ppermute | solution.py:81
  39.2 1.4 %shard_map.98 = (f32[8,2048]{1,0:T(8,128)S(1)}, f32[8,1536]{1,0:T(8,128)S(1)}, f32[8,128]{1,0:T(8,128)S(1)}) custom-call(f32[8,1664]{1,0:T(8,128)S(1)} %get-tuple-element.109.refs_0_, f32[8,1664]{1,0:T(8,128)S(1)} %collective-permute-done.9.refs_1_, f32[8,512]{1,0:T(8,128)S(1)} %get-tuple-element.92.refs_2_, f32[8,512]{1,0:T(8,128)S(1)} %get-tuple-element.93.refs_3_, ...), custom_call_target="tpu_custom_call" | custom-call | flops 150994944 | bytes 9646080 | tf_op jit(solution)/shard_map/pallas_call | solution.py:22
  40.6 0.2 collective-permute-done.8.refs_1_
  40.8 0.6 shard_map.99
  41.4 0.1 collective-permute-start.10
  41.4 1.2 %collective-permute-done.10.refs_1_ = f32[8,2176]{1,0:T(8,128)S(1)} collective-permute-done((f32[8,2176]{1,0:T(8,128)S(1)}, f32[8,2176]{1,0:T(8,128)S(1)}, u32[]{:S(2)}, u32[]{:S(2)}) %collective-permute-start.10) | collective-permute-done | bytes 69664 | tf_op jit(solution)/shard_map/ppermute | solution.py:81
  42.7 1.9 %shard_map.100 = (f32[8,2176]{1,0:T(8,128)S(1)}, f32[8,2048]{1,0:T(8,128)S(1)}, f32[8,2048]{1,0:T(8,128)S(1)}, f32[8,2048]{1,0:T(8,128)S(1)}, f32[8,2048]{1,0:T(8,128)S(1)}, /*index=5*/f32[8,2048]{1,0:T(8,128)S(1)}) custom-call(f32[8,2176]{1,0:T(8,128)S(1)} %get-tuple-element.112.refs_0_, f32[8,2176]{1,0:T(8,128)S(1)} %collective-permute-done.10.refs_1_, ...), custom_call_target="tpu_custom_call" | custom-call | flops 150994944 | bytes 13328416 | tf_op jit(solution)/shard_map/pallas_call | solution.py:22
  44.6 1.5 %collective-permute-start.11 = (f32[8,2176]{1,0:T(8,128)S(1)}, f32[8,2176]{1,0:T(8,128)S(1)}, u32[]{:S(2)}, u32[]{:S(2)}) collective-permute-start(f32[8,2176]{1,0:T(8,128)S(1)} %get-tuple-element.121.refs_0_), channel_id=1, source_target_pairs={{0,1},{1,0},{2,3},{3,2},{4,5},{5,4},{6,7},{7,6},{8,9},{9,8},{10,11... | collective-permute-start | bytes 208904 | tf_op jit(solution)/shard_map/ppermute | solution.py:81
  46.1 2.9 %collective-permute-done.11.refs_1_ = f32[8,2176]{1,0:T(8,128)S(1)} collective-permute-done((f32[8,2176]{1,0:T(8,128)S(1)}, f32[8,2176]{1,0:T(8,128)S(1)}, u32[]{:S(2)}, u32[]{:S(2)}) %collective-permute-start.11) | collective-permute-done | bytes 69664 | tf_op jit(solution)/shard_map/ppermute | solution.py:81
  49.0 0.3 shard_map.101
  49.3 0.0 collective-permute-start.12
  49.4 1.2 %collective-permute-done.12.got = f32[8,2176]{1,0:T(8,128)S(1)} collective-permute-done((f32[8,2176]{1,0:T(8,128)S(1)}, f32[8,2176]{1,0:T(8,128)S(1)}, u32[]{:S(2)}, u32[]{:S(2)}) %collective-permute-start.12) | collective-permute-done | bytes 69664 | tf_op jit(solution)/shard_map/ppermute | solution.py:81
  50.6 0.2 shard_map.102
  50.8 3.6 %collective-permute-start.13 = (f32[4,3072]{1,0:T(4,128)S(1)}, f32[4,3072]{1,0:T(4,128)S(1)}, u32[]{:S(2)}, u32[]{:S(2)}) collective-permute-start(f32[4,3072]{1,0:T(4,128)S(1)} %get-tuple-element.131), channel_id=1, source_target_pairs={{0,6},{2,4},{4,2},{6,0},{1,7},{3,5},{5,3},{7,1},{8,14},{10,12},{12... | collective-permute-start | bytes 147464 | tf_op jit(solution)/shard_map/ppermute | solution.py:81
  54.5 0.5 collective-permute-start.14
  54.9 0.3 collective-permute-start.15
  55.3 1.6 %collective-permute-done.13.refs_1_ = f32[4,3072]{1,0:T(4,128)S(1)} collective-permute-done((f32[4,3072]{1,0:T(4,128)S(1)}, f32[4,3072]{1,0:T(4,128)S(1)}, u32[]{:S(2)}, u32[]{:S(2)}) %collective-permute-start.13) | collective-permute-done | bytes 49184 | tf_op jit(solution)/shard_map/ppermute | solution.py:81
  56.8 3.2 %collective-permute-done.14.refs_2_ = f32[4,3072]{1,0:T(4,128)S(1)} collective-permute-done((f32[4,3072]{1,0:T(4,128)S(1)}, f32[4,3072]{1,0:T(4,128)S(1)}, u32[]{:S(2)}, u32[]{:S(2)}) %collective-permute-start.14) | collective-permute-done | bytes 49184 | tf_op jit(solution)/shard_map/ppermute | solution.py:81
  60.0 0.7 %shard_map.103 = (f32[16,2048]{1,0:T(8,128)}, f32[16,1024]{1,0:T(8,128)}) custom-call(f32[4,3072]{1,0:T(4,128)S(1)} %get-tuple-element.130.refs_0_, f32[4,3072]{1,0:T(4,128)S(1)} %collective-permute-done.13.refs_1_, f32[4,3072]{1,0:T(4,128)S(1)} %collective-permute-done.14.refs_2_, f32[4,3072]{1,0:T(4,128)S(1)} %collective-permute-done.15.refs_3_), custom_call_target="tpu_custom_call" | custom-call | bytes 196608 | tf_op jit(solution)/shard_map/pallas_call | solution.py:22
  (2 shorter events, 0.0 us)
Async XLA Ops:
  0.6 1.8 %collective-permute-start = (s32[8,128]{1,0:T(8,128)}, s32[8,128]{1,0:T(8,128)S(1)}, u32[]{:S(2)}, u32[]{:S(2)}) collective-permute-start(s32[8,128]{1,0:T(8,128)} %bitcast.8), channel_id=1, source_target_pairs={{0,8},{8,0},{16,24},{24,16},{1,9},{9,1},{17,25},{25,17},{2,10},{10... | collective-permute-start | bytes 12296 | tf_op jit(solution)/shard_map/ppermute | solution.py:81
  2.5 9.2 %collective-permute-start.3 = (bf16[528,128]{1,0:T(8,128)(2,1)S(1)}, bf16[528,128]{1,0:T(8,128)(2,1)S(1)}, u32[]{:S(2)}, u32[]{:S(2)}) collective-permute-start(bf16[528,128]{1,0:T(8,128)(2,1)S(1)} %shard_map.87.msg), channel_id=1, source_target_pairs={{0,6},{2,4},{4,2},{6,0},{1,7},{3,5},{5,3},{7,1},{8,14},{10,12},{12... | collective-permute-start | bytes 405512 | tf_op jit(solution)/shard_map/ppermute | solution.py:81
  7.2 8.2 %collective-permute-start.2 = (bf16[528,128]{1,0:T(8,128)(2,1)S(1)}, bf16[528,128]{1,0:T(8,128)(2,1)S(1)}, u32[]{:S(2)}, u32[]{:S(2)}) collective-permute-start(bf16[528,128]{1,0:T(8,128)(2,1)S(1)} %shard_map.87.msg), channel_id=1, source_target_pairs={{0,2},{2,0},{4,6},{6,4},{1,3},{3,1},{5,7},{7,5},{8,10},{10,8},{12,... | collective-permute-start | bytes 405512 | tf_op jit(solution)/shard_map/ppermute | solution.py:81
  7.2 12.1 %collective-permute-start.1 = (bf16[528,128]{1,0:T(8,128)(2,1)S(1)}, bf16[528,128]{1,0:T(8,128)(2,1)S(1)}, u32[]{:S(2)}, u32[]{:S(2)}) collective-permute-start(bf16[528,128]{1,0:T(8,128)(2,1)S(1)} %shard_map.87.msg), channel_id=1, source_target_pairs={{0,4},{2,6},{4,0},{6,2},{1,5},{3,7},{5,1},{7,3},{8,12},{10,14},{12... | collective-permute-start | bytes 405512 | tf_op jit(solution)/shard_map/ppermute | solution.py:81
  23.1 1.2 %collective-permute-start.4 = (f32[4,2048]{1,0:T(4,128)S(1)}, f32[4,2048]{1,0:T(4,128)S(1)}, u32[]{:S(2)}, u32[]{:S(2)}) collective-permute-start(f32[4,2048]{1,0:T(4,128)S(1)} %get-tuple-element.76.refs_0_), channel_id=1, source_target_pairs={{0,8},{8,0},{16,24},{24,16},{1,9},{9,1},{17,25},{25,17},{2,10},{10... | collective-permute-start | bytes 98312 | tf_op jit(solution)/shard_map/ppermute | solution.py:81
  25.8 4.2 %collective-permute-start.6 = (f32[8,1664]{1,0:T(8,128)S(1)}, f32[8,1664]{1,0:T(8,128)S(1)}, u32[]{:S(2)}, u32[]{:S(2)}) collective-permute-start(f32[8,1664]{1,0:T(8,128)S(1)} %get-tuple-element.91.refs_0_), channel_id=1, source_target_pairs={{0,1},{1,0},{2,3},{3,2},{4,5},{5,4},{6,7},{7,6},{8,9},{9,8},{10,11... | collective-permute-start | bytes 159752 | tf_op jit(solution)/shard_map/ppermute | solution.py:81
  27.9 3.8 %collective-permute-start.5 = (f32[8,512]{1,0:T(8,128)S(1)}, f32[8,512]{1,0:T(8,128)S(1)}, u32[]{:S(2)}, u32[]{:S(2)}) collective-permute-start(f32[8,512]{1,0:T(8,128)S(1)} %shard_map.93.refs_0_), channel_id=1, source_target_pairs={{0,1},{1,0},{2,3},{3,2},{4,5},{5,4},{6,7},{7,6},{8,9},{9,8},{10,11... | collective-permute-start | bytes 49160 | tf_op jit(solution)/shard_map/ppermute | solution.py:81
  32.2 1.3 %collective-permute-start.7 = (f32[8,2176]{1,0:T(8,128)S(1)}, f32[8,2176]{1,0:T(8,128)S(1)}, u32[]{:S(2)}, u32[]{:S(2)}) collective-permute-start(f32[8,2176]{1,0:T(8,128)S(1)} %get-tuple-element.103.refs_0_), channel_id=1, source_target_pairs={{0,8},{8,0},{16,24},{24,16},{1,9},{9,1},{17,25},{25,17},{2,10},{10... | collective-permute-start | bytes 208904 | tf_op jit(solution)/shard_map/ppermute | solution.py:81
  35.0 4.2 %collective-permute-start.9 = (f32[8,1664]{1,0:T(8,128)S(1)}, f32[8,1664]{1,0:T(8,128)S(1)}, u32[]{:S(2)}, u32[]{:S(2)}) collective-permute-start(f32[8,1664]{1,0:T(8,128)S(1)} %get-tuple-element.109.refs_0_), channel_id=1, source_target_pairs={{0,1},{1,0},{2,3},{3,2},{4,5},{5,4},{6,7},{7,6},{8,9},{9,8},{10,11... | collective-permute-start | bytes 159752 | tf_op jit(solution)/shard_map/ppermute | solution.py:81
  37.0 3.8 %collective-permute-start.8 = (f32[8,512]{1,0:T(8,128)S(1)}, f32[8,512]{1,0:T(8,128)S(1)}, u32[]{:S(2)}, u32[]{:S(2)}) collective-permute-start(f32[8,512]{1,0:T(8,128)S(1)} %shard_map.97.refs_0_), channel_id=1, source_target_pairs={{0,1},{1,0},{2,3},{3,2},{4,5},{5,4},{6,7},{7,6},{8,9},{9,8},{10,11... | collective-permute-start | bytes 49160 | tf_op jit(solution)/shard_map/ppermute | solution.py:81
  41.4 1.3 %collective-permute-start.10 = (f32[8,2176]{1,0:T(8,128)S(1)}, f32[8,2176]{1,0:T(8,128)S(1)}, u32[]{:S(2)}, u32[]{:S(2)}) collective-permute-start(f32[8,2176]{1,0:T(8,128)S(1)} %get-tuple-element.112.refs_0_), channel_id=1, source_target_pairs={{0,8},{8,0},{16,24},{24,16},{1,9},{9,1},{17,25},{25,17},{2,10},{10... | collective-permute-start | bytes 208904 | tf_op jit(solution)/shard_map/ppermute | solution.py:81
  44.6 4.4 %collective-permute-start.11 = (f32[8,2176]{1,0:T(8,128)S(1)}, f32[8,2176]{1,0:T(8,128)S(1)}, u32[]{:S(2)}, u32[]{:S(2)}) collective-permute-start(f32[8,2176]{1,0:T(8,128)S(1)} %get-tuple-element.121.refs_0_), channel_id=1, source_target_pairs={{0,1},{1,0},{2,3},{3,2},{4,5},{5,4},{6,7},{7,6},{8,9},{9,8},{10,11... | collective-permute-start | bytes 208904 | tf_op jit(solution)/shard_map/ppermute | solution.py:81
  49.3 1.3 %collective-permute-start.12 = (f32[8,2176]{1,0:T(8,128)S(1)}, f32[8,2176]{1,0:T(8,128)S(1)}, u32[]{:S(2)}, u32[]{:S(2)}) collective-permute-start(f32[8,2176]{1,0:T(8,128)S(1)} %get-tuple-element.124.own), channel_id=1, source_target_pairs={{0,8},{8,0},{16,24},{24,16},{1,9},{9,1},{17,25},{25,17},{2,10},{10... | collective-permute-start | bytes 208904 | tf_op jit(solution)/shard_map/ppermute | solution.py:81
  50.8 6.0 %collective-permute-start.13 = (f32[4,3072]{1,0:T(4,128)S(1)}, f32[4,3072]{1,0:T(4,128)S(1)}, u32[]{:S(2)}, u32[]{:S(2)}) collective-permute-start(f32[4,3072]{1,0:T(4,128)S(1)} %get-tuple-element.131), channel_id=1, source_target_pairs={{0,6},{2,4},{4,2},{6,0},{1,7},{3,5},{5,3},{7,1},{8,14},{10,12},{12... | collective-permute-start | bytes 147464 | tf_op jit(solution)/shard_map/ppermute | solution.py:81
  54.5 5.5 %collective-permute-start.14 = (f32[4,3072]{1,0:T(4,128)S(1)}, f32[4,3072]{1,0:T(4,128)S(1)}, u32[]{:S(2)}, u32[]{:S(2)}) collective-permute-start(f32[4,3072]{1,0:T(4,128)S(1)} %get-tuple-element.132), channel_id=1, source_target_pairs={{0,4},{2,6},{4,0},{6,2},{1,5},{3,7},{5,1},{7,3},{8,12},{10,14},{12... | collective-permute-start | bytes 147464 | tf_op jit(solution)/shard_map/ppermute | solution.py:81
  54.9 5.0 %collective-permute-start.15 = (f32[4,3072]{1,0:T(4,128)S(1)}, f32[4,3072]{1,0:T(4,128)S(1)}, u32[]{:S(2)}, u32[]{:S(2)}) collective-permute-start(f32[4,3072]{1,0:T(4,128)S(1)} %get-tuple-element.133), channel_id=1, source_target_pairs={{0,2},{2,0},{4,6},{6,4},{1,3},{3,1},{5,7},{7,5},{8,10},{10,8},{12,... | collective-permute-start | bytes 147464 | tf_op jit(solution)/shard_map/ppermute | solution.py:81

commit v11 on v9

--- a/solution.py
+++ b/solution.py
@@ -188,6 +188,18 @@
         moment_ref[e : e + 1, :] = square if first else before[e : e + 1, :] + square
 
 
+def window(refs, each, axis, low, high):
+    out, at = [], 0
+    for i in range(0, len(refs), each):
+        size = refs[i].shape[axis]
+        a, b = max(low - at, 0), min(high - at, size)
+        if a < b:
+            take = (slice(None), slice(a, b)) if axis else (slice(a, b), slice(None))
+            out += [r.at[take] for r in refs[i : i + each]]
+        at += size
+    return out
+
+
 def forward(v, blocks, msg):
     at, parts = 0, split(v)
     for high, low in zip(blocks[::2], blocks[1::2]):
@@ -202,13 +214,14 @@
     msg[:, at:] = pack_scalars(scalars, v.shape[0])
 
 
-def forward_kernel(scaled, mag, *refs):
-    forward(scaled[...] * mag[...], refs[:-1], refs[-1])
-
-
-def begin_kernel(count, *refs):
-    moments, penalty, mag, blocks = refs[:2], refs[2], refs[3], refs[4 : 4 + 2 * count]
-    msg, direction, precond, residual = refs[4 + 2 * count :]
+def forward_kernel(skip, scaled, mag, *refs):
+    forward(scaled[...] * mag[...], window(refs[:-1], 2, 1, skip, refs[0].shape[1]), refs[-1])
+
+
+def begin_kernel(nz, cut, *refs):
+    moments, penalty, mag, blocks = refs[:2], refs[2], refs[3], refs[4 : 4 + 2 * nz]
+    msg, direction, precond, residual = refs[4 + 2 * nz :]
+    blocks = window(blocks, 2, 1, 0, cut)
     sums = total(moments)
     m = mag[...]
     rows = penalty.shape[0]
@@ -231,11 +244,11 @@
 
 
 def adjoint(image_rows, before, kepts, blocks):
-    half = kepts[0].shape[1]
-    out = 0.0
+    start, out = 0, 0.0
     squares = cross = jnp.zeros((image_rows.shape[0], 1), f32)
-    for j, (kept, high, low) in enumerate(zip(kepts, blocks[::2], blocks[1::2])):
-        at = slice(j * half, (j + 1) * half)
+    for kept, high, low in zip(kepts, blocks[::2], blocks[1::2]):
+        at = slice(start, start + kept.shape[1])
+        start = at.stop
         rows = image_rows[:, at]
         weighted = rows * kept[...]
         squares = squares + row_sum(weighted * rows)
@@ -245,12 +258,12 @@
     return out, squares, cross
 
 
-def adjoint_kernel(ny, count, first, *refs):
+def adjoint_kernel(ny, nz, cut, first, *refs):
     parts, refs = refs[:ny], refs[ny:]
-    kepts, blocks, refs = refs[:count], refs[count : 3 * count], refs[3 * count :]
+    kepts, blocks, refs = refs[:nz], refs[nz : 3 * nz], refs[3 * nz :]
+    kepts, blocks = window(kepts, 1, 1, 0, cut), window(blocks, 2, 0, 0, cut)
     sums = total(parts)
-    samples = kepts[0].shape[1] * count
-    image_rows, sc = sums[:, :samples], sums[:, samples:]
+    image_rows, sc = sums[:, :cut], sums[:, cut:]
     before, before_sc = (None, None) if first else refs[:2]
     partial, rows_out, sc_out = refs[-3:]
     rz, dd, beta, dot = direction_scalars(sc, before_sc)
@@ -263,9 +276,10 @@
     sc_out[...] = pack_scalars([rz, dd, beta, dot, squares, cross], dd.shape[0])
 
 
-def rest_kernel(ny, count, first, *refs):
+def rest_kernel(ny, skip, first, *refs):
     parts, refs = refs[:ny], refs[ny:]
-    kepts, blocks, refs = refs[:count], refs[count : 3 * count], refs[3 * count :]
+    half = refs[0].shape[1]
+    kepts, blocks, refs = window(refs[:1], 1, 1, skip, half), window(refs[1:3], 2, 0, skip, half), refs[3:]
     sc, partial, refs = refs[0], refs[1], refs[2:]
     image_rows = total(parts)
     before = None
@@ -280,10 +294,10 @@
     rows_out[...] = image_rows
 
 
-def update_kernel(count, first, last, *refs):
+def update_kernel(nz, cut, first, last, *refs):
     parts, refs = refs[:2], refs[2:]
     sc, penalty, mag, precond, residual, scaled, rows, rest, refs = *refs[:8], refs[8:]
-    blocks, refs = refs[: 2 * count], refs[2 * count :]
+    blocks, refs = window(refs[: 2 * nz], 2, 1, 0, cut), refs[2 * nz :]
     sums = total(parts)
     features = mag.shape[1]
     lam, m = penalty[...], mag[...]
@@ -443,42 +457,43 @@
         blocks += [high, low]
         turned += [high_t, low_t]
         kepts.append(kept)
-    count, later = nz - 1, 1
-    msg_a, row_a = ((rows, half * count + LANES), f32), ((rows, half * count), f32)
-    row_b = ((rows, half * later), f32)
-    work = 2 * 3 * rows * half * features
+    skip = half // 2
+    cut = samples - half + skip
+    msg_a, row_a = ((rows, cut + LANES), f32), ((rows, cut), f32)
+    row_b = ((rows, samples - cut), f32)
+    work, work_b = 6 * rows * cut * features, 6 * rows * (samples - cut) * features
     msg, scaled, precond, residual = call(
-        functools.partial(begin_kernel, count),
+        functools.partial(begin_kernel, nz, cut),
         [msg_a, row_f, row_f, row_f],
-        moments, flip(moments, "fold", nf, 1), penalty, mag, *turned[: 2 * count],
-        flops=work * count,
+        moments, flip(moments, "fold", nf, 1), penalty, mag, *turned,
+        flops=work,
     )
     before = weights = predicted = image = curve = sc = rows_a = rows_b = None
     for it in range(ITERS - 1):
         first, last = it == 0, it == ITERS - 2
         parts = exchange(msg, "feat", ny)
-        (msg_b,) = call(forward_kernel, [row_b], scaled, mag, *turned[2 * count :], flops=work * later)
+        (msg_b,) = call(functools.partial(forward_kernel, skip), [row_b], scaled, mag, *turned[-2:], flops=work_b)
         parts_b = exchange(msg_b, "feat", ny)
         partial, new_a, new_sc = call(
-            functools.partial(adjoint_kernel, ny, count, first),
+            functools.partial(adjoint_kernel, ny, nz, cut, first),
             [row_f, row_a, row_c],
-            *parts, *kepts[:count], *blocks[: 2 * count], *(() if first else (rows_a, sc)),
-            flops=work * count,
+            *parts, *kepts, *blocks, *(() if first else (rows_a, sc)),
+            flops=work,
         )
         msg, new_b = call(
-            functools.partial(rest_kernel, ny, later, first),
+            functools.partial(rest_kernel, ny, skip, first),
             [msg_f, row_b],
-            *parts_b, *kepts[count:], *blocks[2 * count :], new_sc, partial, *(() if first else (rows_b,)),
-            flops=work * later,
+            *parts_b, kepts[-1], *blocks[-2:], new_sc, partial, *(() if first else (rows_b,)),
+            flops=work_b,
         )
         sc = new_sc
         msg, scaled, before, weights, predicted, *rest = call(
-            functools.partial(update_kernel, nz if last else count, first, last),
+            functools.partial(update_kernel, nz, samples if last else cut, first, last),
             [msg_s if last else msg_a, row_f, row_f, row_f, row_s] + ([row_s] if last else [row_f, row_f, row_c]),
             msg, flip(msg, "fold", nf, 1), sc, penalty, mag, precond, residual, scaled, new_a, new_b,
-            *(turned if last else turned[: 2 * count]),
+            *turned,
             *(() if first else (before, weights, predicted, image, curve, rows_a, rows_b)),
-            flops=work * count,
+            flops=work,
         )
         rows_a, rows_b = new_a, new_b
         residual, image, curve = (None, None, None) if last else rest

time: 60.8 us -> 60.9 us (level)
  transfers between devices with their start and end apart: 16 -> 16, of which waited for: 13 -> 12; matrix products, arithmetic and copies ran while one was open for 0% -> 0% of each run, Pallas kernels for 27% -> 27%
where the time goes in v11:
time: 60.9 us; the launch traced here: 60.7 us
  Pallas kernels  27.1 us (44%)
  starting transfers between devices  16.4 us (27%)
  waiting for transfers between devices  16.4 us (27%)
  between operations  0.77 us (1%)
    pallas_call x17, Pallas kernels, call(): pl.pallas_call(body, out_shape=outs, scratch_shapes=list(scratch), input_...  25.8 us
    ppermute x16, starting transfers between devices, flip(): return lax.ppermute(value, axis, [(i, i ^ s) for i in range(n)])  16.4 us
    ppermute x16, waiting for transfers between devices, flip(): return lax.ppermute(value, axis, [(i, i ^ s) for i in range(n)])  16.4 us
    pallas_call x1, Pallas kernels, shards(): pl.pallas_call(functools.partial(pack_kernel, math.sqrt(2.0 / (features *...  1.29 us
  transfers between devices with their start and end apart: 16, of which 12 were waited for; matrix products, arithmetic and copies ran while one was open for 0% of the time, Pallas kernels for 27%

profile of v11, /device:TPU:0, one launch (start us, length us, event | category | flops | bytes accessed | tf_op | source)
XLA Modules:
  0.0 60.7 jit_solution(5953908222085056245)
XLA Ops:
  0.6 0.5 collective-permute-start
  1.1 1.3 %shard_map.86 = (bf16[528,128]{1,0:T(8,128)(2,1)S(1)}, bf16[128,2048]{1,0:T(8,128)(2,1)S(1)}, f32[1,2048]{1,0:T(1,128)S(1)}, f32[1,2048]{1,0:T(1,128)S(1)}, f32[...) custom-call(bf16[1024,128]{1,0:T(8,128)(2,1)} %x_hbm.1, bf16[128,2048]{1,0:T(8,128)(2,1)} %w_hbm.1, ...), custom_call_target="tpu_custom_call" | custom-call | tf_op jit(solution)/shard_map/pallas_call | solution.py:424
  2.5 0.0 collective-permute-done.other_label
  2.5 4.7 %collective-permute-start.3 = (bf16[528,128]{1,0:T(8,128)(2,1)S(1)}, bf16[528,128]{1,0:T(8,128)(2,1)S(1)}, u32[]{:S(2)}, u32[]{:S(2)}) collective-permute-start(bf16[528,128]{1,0:T(8,128)(2,1)S(1)} %shard_map.87.msg), channel_id=1, source_target_pairs={{0,6},{2,4},{4,2},{6,0},{1,7},{3,5},{5,3},{7,1},{8,14},{10,12},{12... | collective-permute-start | bytes 405512 | tf_op jit(solution)/shard_map/ppermute | solution.py:81
  7.2 0.0 collective-permute-start.2
  7.2 0.6 %collective-permute-start.1 = (bf16[528,128]{1,0:T(8,128)(2,1)S(1)}, bf16[528,128]{1,0:T(8,128)(2,1)S(1)}, u32[]{:S(2)}, u32[]{:S(2)}) collective-permute-start(bf16[528,128]{1,0:T(8,128)(2,1)S(1)} %shard_map.87.msg), channel_id=1, source_target_pairs={{0,4},{2,6},{4,0},{6,2},{1,5},{3,7},{5,1},{7,3},{8,12},{10,14},{12... | collective-permute-start | bytes 405512 | tf_op jit(solution)/shard_map/ppermute | solution.py:81
  7.8 3.7 %shard_map.88 = (bf16[512,2048]{1,0:T(8,128)(2,1)S(1)}, f8e4m3fn[512,2048]{1,0:T(32,128)(4,1)S(1)}, bf16[2048,512]{1,0:T(8,128)(2,1)S(1)}, f8e4m3fn[2048,512]{1,...) custom-call(bf16[528,128]{1,0:T(8,128)(2,1)S(1)} %shard_map.87.msg, ...), custom_call_target="tpu_custom_call" | custom-call | flops 62914560 | bytes 667648 | tf_op jit(solution)/shard_map/pallas_call | solution.py:22
  11.5 0.2 collective-permute-done.3.msg
  11.7 3.7 %shard_map.89 = (bf16[512,2048]{1,0:T(8,128)(2,1)S(1)}, f8e4m3fn[512,2048]{1,0:T(32,128)(4,1)S(1)}, bf16[2048,512]{1,0:T(8,128)(2,1)S(1)}, f8e4m3fn[2048,512]{1,...) custom-call(bf16[528,128]{1,0:T(8,128)(2,1)S(1)} %collective-permute-done.3.msg, ...), custom_call_target="tpu_custom_call" | custom-call | flops 62914560 | bytes 700416 | tf_op jit(solution)/shard_map/pallas_call | solution.py:22
  15.4 0.1 collective-permute-done.2.msg
  15.4 3.7 %shard_map.90 = (bf16[512,2048]{1,0:T(8,128)(2,1)S(1)}, f8e4m3fn[512,2048]{1,0:T(32,128)(4,1)S(1)}, bf16[2048,512]{1,0:T(8,128)(2,1)S(1)}, f8e4m3fn[2048,512]{1,...) custom-call(bf16[528,128]{1,0:T(8,128)(2,1)S(1)} %collective-permute-done.2.msg, ...), custom_call_target="tpu_custom_call" | custom-call | flops 62914560 | bytes 700416 | tf_op jit(solution)/shard_map/pallas_call | solution.py:22
  19.1 0.2 collective-permute-done.1.msg
  19.3 3.9 %shard_map.91 = (bf16[512,2048]{1,0:T(8,128)(2,1)S(1)}, f8e4m3fn[512,2048]{1,0:T(32,128)(4,1)S(1)}, bf16[2048,512]{1,0:T(8,128)(2,1)S(1)}, f8e4m3fn[2048,512]{1,...) custom-call(bf16[528,128]{1,0:T(8,128)(2,1)S(1)} %collective-permute-done.1.msg, ...), custom_call_target="tpu_custom_call" | custom-call | flops 62914560 | bytes 700416 | tf_op jit(solution)/shard_map/pallas_call | solution.py:22
  23.1 0.0 collective-permute-start.4
  23.2 1.2 %collective-permute-done.4.refs_1_ = f32[4,2048]{1,0:T(4,128)S(1)} collective-permute-done((f32[4,2048]{1,0:T(4,128)S(1)}, f32[4,2048]{1,0:T(4,128)S(1)}, u32[]{:S(2)}, u32[]{:S(2)}) %collective-permute-start.4) | collective-permute-done | bytes 32800 | tf_op jit(solution)/shard_map/ppermute | solution.py:81
  24.4 1.6 %shard_map.92 = (f32[8,1920]{1,0:T(8,128)S(1)}, f32[8,2048]{1,0:T(8,128)S(1)}, f32[8,2048]{1,0:T(8,128)S(1)}, f32[8,2048]{1,0:T(8,128)S(1)}) custom-call(f32[4,2048]{1,0:T(4,128)S(1)} %get-tuple-element.76.refs_0_, f32[4,2048]{1,0:T(4,128)S(1)} %collective-permute-done.4.refs_1_, f32[8,1]{1,0:T(8,128)S(1)} %get-tuple-element.77.refs_2_.refs_3_.penalty, ...), custom_call_target="tpu_custom_call" | custom-call | flops 176160768 | bytes 12656672 | tf_op jit(solution)/shard_map/pallas_call | solution.py:22
  26.0 1.6 %collective-permute-start.6 = (f32[8,1920]{1,0:T(8,128)S(1)}, f32[8,1920]{1,0:T(8,128)S(1)}, u32[]{:S(2)}, u32[]{:S(2)}) collective-permute-start(f32[8,1920]{1,0:T(8,128)S(1)} %get-tuple-element.91.refs_0_), channel_id=1, source_target_pairs={{0,1},{1,0},{2,3},{3,2},{4,5},{5,4},{6,7},{7,6},{8,9},{9,8},{10,11... | collective-permute-start | bytes 184328 | tf_op jit(solution)/shard_map/ppermute | solution.py:81
  27.6 0.3 shard_map.93.refs_0_
  27.9 0.6 collective-permute-start.5
  28.5 1.8 %collective-permute-done.6.refs_1_ = f32[8,1920]{1,0:T(8,128)S(1)} collective-permute-done((f32[8,1920]{1,0:T(8,128)S(1)}, f32[8,1920]{1,0:T(8,128)S(1)}, u32[]{:S(2)}, u32[]{:S(2)}) %collective-permute-start.6) | collective-permute-done | bytes 61472 | tf_op jit(solution)/shard_map/ppermute | solution.py:81
  30.3 1.6 %shard_map.94 = (f32[8,2048]{1,0:T(8,128)S(1)}, f32[8,1792]{1,0:T(8,128)S(1)}, f32[8,128]{1,0:T(8,128)S(1)}) custom-call(f32[8,1920]{1,0:T(8,128)S(1)} %get-tuple-element.91.refs_0_, f32[8,1920]{1,0:T(8,128)S(1)} %collective-permute-done.6.refs_1_, f32[8,512]{1,0:T(8,128)S(1)} %get-tuple-element.92.refs_2_, f32[8,512]{1,0:T(8,128)S(1)} %get-tuple-element.93.refs_3_, ...), custom_call_target="tpu_custom_call" | custom-call | flops 176160768 | bytes 12771328 | tf_op jit(solution)/shard_map/pallas_call | solution.py:22
  31.8 0.0 collective-permute-done.5.refs_1_
  31.8 0.3 shard_map.95
  32.1 0.1 collective-permute-start.7
  32.2 1.2 %collective-permute-done.7.refs_1_ = f32[8,2176]{1,0:T(8,128)S(1)} collective-permute-done((f32[8,2176]{1,0:T(8,128)S(1)}, f32[8,2176]{1,0:T(8,128)S(1)}, u32[]{:S(2)}, u32[]{:S(2)}) %collective-permute-start.7) | collective-permute-done | bytes 69664 | tf_op jit(solution)/shard_map/ppermute | solution.py:81
  33.5 1.7 %shard_map.96 = (f32[8,1920]{1,0:T(8,128)S(1)}, f32[8,2048]{1,0:T(8,128)S(1)}, f32[8,2048]{1,0:T(8,128)S(1)}, f32[8,2048]{1,0:T(8,128)S(1)}, f32[8,2048]{1,0:T(8...) custom-call(f32[8,2176]{1,0:T(8,128)S(1)} %get-tuple-element.103.refs_0_, ...), custom_call_target="tpu_custom_call" | custom-call | flops 176160768 | bytes 12996640 | tf_op jit(solution)/shard_map/pallas_call | solution.py:22
  35.2 1.6 %collective-permute-start.9 = (f32[8,1920]{1,0:T(8,128)S(1)}, f32[8,1920]{1,0:T(8,128)S(1)}, u32[]{:S(2)}, u32[]{:S(2)}) collective-permute-start(f32[8,1920]{1,0:T(8,128)S(1)} %get-tuple-element.109.refs_0_), channel_id=1, source_target_pairs={{0,1},{1,0},{2,3},{3,2},{4,5},{5,4},{6,7},{7,6},{8,9},{9,8},{10,11... | collective-permute-start | bytes 184328 | tf_op jit(solution)/shard_map/ppermute | solution.py:81
  36.7 0.3 shard_map.97.refs_0_
  37.1 0.6 collective-permute-start.8
  37.7 1.8 %collective-permute-done.9.refs_1_ = f32[8,1920]{1,0:T(8,128)S(1)} collective-permute-done((f32[8,1920]{1,0:T(8,128)S(1)}, f32[8,1920]{1,0:T(8,128)S(1)}, u32[]{:S(2)}, u32[]{:S(2)}) %collective-permute-start.9) | collective-permute-done | bytes 61472 | tf_op jit(solution)/shard_map/ppermute | solution.py:81
  39.4 1.6 %shard_map.98 = (f32[8,2048]{1,0:T(8,128)S(1)}, f32[8,1792]{1,0:T(8,128)S(1)}, f32[8,128]{1,0:T(8,128)S(1)}) custom-call(f32[8,1920]{1,0:T(8,128)S(1)} %get-tuple-element.109.refs_0_, f32[8,1920]{1,0:T(8,128)S(1)} %collective-permute-done.9.refs_1_, f32[8,512]{1,0:T(8,128)S(1)} %get-tuple-element.92.refs_2_, f32[8,512]{1,0:T(8,128)S(1)} %get-tuple-element.93.refs_3_, ...), custom_call_target="tpu_custom_call" | custom-call | flops 176160768 | bytes 12832768 | tf_op jit(solution)/shard_map/pallas_call | solution.py:22
  41.0 0.0 collective-permute-done.8.refs_1_
  41.1 0.4 shard_map.99
  41.4 0.1 collective-permute-start.10
  41.5 1.2 %collective-permute-done.10.refs_1_ = f32[8,2176]{1,0:T(8,128)S(1)} collective-permute-done((f32[8,2176]{1,0:T(8,128)S(1)}, f32[8,2176]{1,0:T(8,128)S(1)}, u32[]{:S(2)}, u32[]{:S(2)}) %collective-permute-start.10) | collective-permute-done | bytes 69664 | tf_op jit(solution)/shard_map/ppermute | solution.py:81
  42.8 1.9 %shard_map.100 = (f32[8,2176]{1,0:T(8,128)S(1)}, f32[8,2048]{1,0:T(8,128)S(1)}, f32[8,2048]{1,0:T(8,128)S(1)}, f32[8,2048]{1,0:T(8,128)S(1)}, f32[8,2048]{1,0:T(8,128)S(1)}, /*index=5*/f32[8,2048]{1,0:T(8,128)S(1)}) custom-call(f32[8,2176]{1,0:T(8,128)S(1)} %get-tuple-element.112.refs_0_, f32[8,2176]{1,0:T(8,128)S(1)} %collective-permute-done.10.refs_1_, ...), custom_call_target="tpu_custom_call" | custom-call | flops 176160768 | bytes 13328416 | tf_op jit(solution)/shard_map/pallas_call | solution.py:22
  44.7 1.6 %collective-permute-start.11 = (f32[8,2176]{1,0:T(8,128)S(1)}, f32[8,2176]{1,0:T(8,128)S(1)}, u32[]{:S(2)}, u32[]{:S(2)}) collective-permute-start(f32[8,2176]{1,0:T(8,128)S(1)} %get-tuple-element.121.refs_0_), channel_id=1, source_target_pairs={{0,1},{1,0},{2,3},{3,2},{4,5},{5,4},{6,7},{7,6},{8,9},{9,8},{10,11... | collective-permute-start | bytes 208904 | tf_op jit(solution)/shard_map/ppermute | solution.py:81
  46.3 2.8 %collective-permute-done.11.refs_1_ = f32[8,2176]{1,0:T(8,128)S(1)} collective-permute-done((f32[8,2176]{1,0:T(8,128)S(1)}, f32[8,2176]{1,0:T(8,128)S(1)}, u32[]{:S(2)}, u32[]{:S(2)}) %collective-permute-start.11) | collective-permute-done | bytes 69664 | tf_op jit(solution)/shard_map/ppermute | solution.py:81
  49.1 0.3 shard_map.101
  49.4 0.0 collective-permute-start.12
  49.4 1.2 %collective-permute-done.12.got = f32[8,2176]{1,0:T(8,128)S(1)} collective-permute-done((f32[8,2176]{1,0:T(8,128)S(1)}, f32[8,2176]{1,0:T(8,128)S(1)}, u32[]{:S(2)}, u32[]{:S(2)}) %collective-permute-start.12) | collective-permute-done | bytes 69664 | tf_op jit(solution)/shard_map/ppermute | solution.py:81
  50.7 0.2 shard_map.102
  50.9 3.6 %collective-permute-start.13 = (f32[4,3072]{1,0:T(4,128)S(1)}, f32[4,3072]{1,0:T(4,128)S(1)}, u32[]{:S(2)}, u32[]{:S(2)}) collective-permute-start(f32[4,3072]{1,0:T(4,128)S(1)} %get-tuple-element.131), channel_id=1, source_target_pairs={{0,6},{2,4},{4,2},{6,0},{1,7},{3,5},{5,3},{7,1},{8,14},{10,12},{12... | collective-permute-start | bytes 147464 | tf_op jit(solution)/shard_map/ppermute | solution.py:81
  54.5 0.5 collective-permute-start.14
  55.0 0.3 collective-permute-start.15
  55.3 1.6 %collective-permute-done.13.refs_1_ = f32[4,3072]{1,0:T(4,128)S(1)} collective-permute-done((f32[4,3072]{1,0:T(4,128)S(1)}, f32[4,3072]{1,0:T(4,128)S(1)}, u32[]{:S(2)}, u32[]{:S(2)}) %collective-permute-start.13) | collective-permute-done | bytes 49184 | tf_op jit(solution)/shard_map/ppermute | solution.py:81
  56.9 3.1 %collective-permute-done.14.refs_2_ = f32[4,3072]{1,0:T(4,128)S(1)} collective-permute-done((f32[4,3072]{1,0:T(4,128)S(1)}, f32[4,3072]{1,0:T(4,128)S(1)}, u32[]{:S(2)}, u32[]{:S(2)}) %collective-permute-start.14) | collective-permute-done | bytes 49184 | tf_op jit(solution)/shard_map/ppermute | solution.py:81
  60.0 0.7 %shard_map.103 = (f32[16,2048]{1,0:T(8,128)}, f32[16,1024]{1,0:T(8,128)}) custom-call(f32[4,3072]{1,0:T(4,128)S(1)} %get-tuple-element.130.refs_0_, f32[4,3072]{1,0:T(4,128)S(1)} %collective-permute-done.13.refs_1_, f32[4,3072]{1,0:T(4,128)S(1)} %collective-permute-done.14.refs_2_, f32[4,3072]{1,0:T(4,128)S(1)} %collective-permute-done.15.refs_3_), custom_call_target="tpu_custom_call" | custom-call | bytes 196608 | tf_op jit(solution)/shard_map/pallas_call | solution.py:22
  (2 shorter events, 0.0 us)
Async XLA Ops:
  0.6 1.8 %collective-permute-start = (s32[8,128]{1,0:T(8,128)}, s32[8,128]{1,0:T(8,128)S(1)}, u32[]{:S(2)}, u32[]{:S(2)}) collective-permute-start(s32[8,128]{1,0:T(8,128)} %bitcast.8), channel_id=1, source_target_pairs={{0,8},{8,0},{16,24},{24,16},{1,9},{9,1},{17,25},{25,17},{2,10},{10... | collective-permute-start | bytes 12296 | tf_op jit(solution)/shard_map/ppermute | solution.py:81
  2.5 9.2 %collective-permute-start.3 = (bf16[528,128]{1,0:T(8,128)(2,1)S(1)}, bf16[528,128]{1,0:T(8,128)(2,1)S(1)}, u32[]{:S(2)}, u32[]{:S(2)}) collective-permute-start(bf16[528,128]{1,0:T(8,128)(2,1)S(1)} %shard_map.87.msg), channel_id=1, source_target_pairs={{0,6},{2,4},{4,2},{6,0},{1,7},{3,5},{5,3},{7,1},{8,14},{10,12},{12... | collective-permute-start | bytes 405512 | tf_op jit(solution)/shard_map/ppermute | solution.py:81
  7.2 8.2 %collective-permute-start.2 = (bf16[528,128]{1,0:T(8,128)(2,1)S(1)}, bf16[528,128]{1,0:T(8,128)(2,1)S(1)}, u32[]{:S(2)}, u32[]{:S(2)}) collective-permute-start(bf16[528,128]{1,0:T(8,128)(2,1)S(1)} %shard_map.87.msg), channel_id=1, source_target_pairs={{0,2},{2,0},{4,6},{6,4},{1,3},{3,1},{5,7},{7,5},{8,10},{10,8},{12,... | collective-permute-start | bytes 405512 | tf_op jit(solution)/shard_map/ppermute | solution.py:81
  7.2 12.1 %collective-permute-start.1 = (bf16[528,128]{1,0:T(8,128)(2,1)S(1)}, bf16[528,128]{1,0:T(8,128)(2,1)S(1)}, u32[]{:S(2)}, u32[]{:S(2)}) collective-permute-start(bf16[528,128]{1,0:T(8,128)(2,1)S(1)} %shard_map.87.msg), channel_id=1, source_target_pairs={{0,4},{2,6},{4,0},{6,2},{1,5},{3,7},{5,1},{7,3},{8,12},{10,14},{12... | collective-permute-start | bytes 405512 | tf_op jit(solution)/shard_map/ppermute | solution.py:81
  23.1 1.2 %collective-permute-start.4 = (f32[4,2048]{1,0:T(4,128)S(1)}, f32[4,2048]{1,0:T(4,128)S(1)}, u32[]{:S(2)}, u32[]{:S(2)}) collective-permute-start(f32[4,2048]{1,0:T(4,128)S(1)} %get-tuple-element.76.refs_0_), channel_id=1, source_target_pairs={{0,8},{8,0},{16,24},{24,16},{1,9},{9,1},{17,25},{25,17},{2,10},{10... | collective-permute-start | bytes 98312 | tf_op jit(solution)/shard_map/ppermute | solution.py:81
  26.0 4.3 %collective-permute-start.6 = (f32[8,1920]{1,0:T(8,128)S(1)}, f32[8,1920]{1,0:T(8,128)S(1)}, u32[]{:S(2)}, u32[]{:S(2)}) collective-permute-start(f32[8,1920]{1,0:T(8,128)S(1)} %get-tuple-element.91.refs_0_), channel_id=1, source_target_pairs={{0,1},{1,0},{2,3},{3,2},{4,5},{5,4},{6,7},{7,6},{8,9},{9,8},{10,11... | collective-permute-start | bytes 184328 | tf_op jit(solution)/shard_map/ppermute | solution.py:81
  27.9 3.9 %collective-permute-start.5 = (f32[8,256]{1,0:T(8,128)S(1)}, f32[8,256]{1,0:T(8,128)S(1)}, u32[]{:S(2)}, u32[]{:S(2)}) collective-permute-start(f32[8,256]{1,0:T(8,128)S(1)} %shard_map.93.refs_0_), channel_id=1, source_target_pairs={{0,1},{1,0},{2,3},{3,2},{4,5},{5,4},{6,7},{7,6},{8,9},{9,8},{10,11... | collective-permute-start | bytes 24584 | tf_op jit(solution)/shard_map/ppermute | solution.py:81
  32.1 1.3 %collective-permute-start.7 = (f32[8,2176]{1,0:T(8,128)S(1)}, f32[8,2176]{1,0:T(8,128)S(1)}, u32[]{:S(2)}, u32[]{:S(2)}) collective-permute-start(f32[8,2176]{1,0:T(8,128)S(1)} %get-tuple-element.103.refs_0_), channel_id=1, source_target_pairs={{0,8},{8,0},{16,24},{24,16},{1,9},{9,1},{17,25},{25,17},{2,10},{10... | collective-permute-start | bytes 208904 | tf_op jit(solution)/shard_map/ppermute | solution.py:81
  35.2 4.3 %collective-permute-start.9 = (f32[8,1920]{1,0:T(8,128)S(1)}, f32[8,1920]{1,0:T(8,128)S(1)}, u32[]{:S(2)}, u32[]{:S(2)}) collective-permute-start(f32[8,1920]{1,0:T(8,128)S(1)} %get-tuple-element.109.refs_0_), channel_id=1, source_target_pairs={{0,1},{1,0},{2,3},{3,2},{4,5},{5,4},{6,7},{7,6},{8,9},{9,8},{10,11... | collective-permute-start | bytes 184328 | tf_op jit(solution)/shard_map/ppermute | solution.py:81
  37.1 4.0 %collective-permute-start.8 = (f32[8,256]{1,0:T(8,128)S(1)}, f32[8,256]{1,0:T(8,128)S(1)}, u32[]{:S(2)}, u32[]{:S(2)}) collective-permute-start(f32[8,256]{1,0:T(8,128)S(1)} %shard_map.97.refs_0_), channel_id=1, source_target_pairs={{0,1},{1,0},{2,3},{3,2},{4,5},{5,4},{6,7},{7,6},{8,9},{9,8},{10,11... | collective-permute-start | bytes 24584 | tf_op jit(solution)/shard_map/ppermute | solution.py:81
  41.4 1.3 %collective-permute-start.10 = (f32[8,2176]{1,0:T(8,128)S(1)}, f32[8,2176]{1,0:T(8,128)S(1)}, u32[]{:S(2)}, u32[]{:S(2)}) collective-permute-start(f32[8,2176]{1,0:T(8,128)S(1)} %get-tuple-element.112.refs_0_), channel_id=1, source_target_pairs={{0,8},{8,0},{16,24},{24,16},{1,9},{9,1},{17,25},{25,17},{2,10},{10... | collective-permute-start | bytes 208904 | tf_op jit(solution)/shard_map/ppermute | solution.py:81
  44.7 4.4 %collective-permute-start.11 = (f32[8,2176]{1,0:T(8,128)S(1)}, f32[8,2176]{1,0:T(8,128)S(1)}, u32[]{:S(2)}, u32[]{:S(2)}) collective-permute-start(f32[8,2176]{1,0:T(8,128)S(1)} %get-tuple-element.121.refs_0_), channel_id=1, source_target_pairs={{0,1},{1,0},{2,3},{3,2},{4,5},{5,4},{6,7},{7,6},{8,9},{9,8},{10,11... | collective-permute-start | bytes 208904 | tf_op jit(solution)/shard_map/ppermute | solution.py:81
  49.4 1.3 %collective-permute-start.12 = (f32[8,2176]{1,0:T(8,128)S(1)}, f32[8,2176]{1,0:T(8,128)S(1)}, u32[]{:S(2)}, u32[]{:S(2)}) collective-permute-start(f32[8,2176]{1,0:T(8,128)S(1)} %get-tuple-element.124.own), channel_id=1, source_target_pairs={{0,8},{8,0},{16,24},{24,16},{1,9},{9,1},{17,25},{25,17},{2,10},{10... | collective-permute-start | bytes 208904 | tf_op jit(solution)/shard_map/ppermute | solution.py:81
  50.9 6.0 %collective-permute-start.13 = (f32[4,3072]{1,0:T(4,128)S(1)}, f32[4,3072]{1,0:T(4,128)S(1)}, u32[]{:S(2)}, u32[]{:S(2)}) collective-permute-start(f32[4,3072]{1,0:T(4,128)S(1)} %get-tuple-element.131), channel_id=1, source_target_pairs={{0,6},{2,4},{4,2},{6,0},{1,7},{3,5},{5,3},{7,1},{8,14},{10,12},{12... | collective-permute-start | bytes 147464 | tf_op jit(solution)/shard_map/ppermute | solution.py:81
  54.5 5.5 %collective-permute-start.14 = (f32[4,3072]{1,0:T(4,128)S(1)}, f32[4,3072]{1,0:T(4,128)S(1)}, u32[]{:S(2)}, u32[]{:S(2)}) collective-permute-start(f32[4,3072]{1,0:T(4,128)S(1)} %get-tuple-element.132), channel_id=1, source_target_pairs={{0,4},{2,6},{4,0},{6,2},{1,5},{3,7},{5,1},{7,3},{8,12},{10,14},{12... | collective-permute-start | bytes 147464 | tf_op jit(solution)/shard_map/ppermute | solution.py:81
  55.0 5.0 %collective-permute-start.15 = (f32[4,3072]{1,0:T(4,128)S(1)}, f32[4,3072]{1,0:T(4,128)S(1)}, u32[]{:S(2)}, u32[]{:S(2)}) collective-permute-start(f32[4,3072]{1,0:T(4,128)S(1)} %get-tuple-element.133), channel_id=1, source_target_pairs={{0,2},{2,0},{4,6},{6,4},{1,3},{3,1},{5,7},{7,5},{8,10},{10,8},{12,... | collective-permute-start | bytes 147464 | tf_op jit(solution)/shard_map/ppermute | solution.py:81
